TPU v7x, 512 devices: a whole 4x8x8 slice. The times are simulated.
512 devices in a mesh: blk: 32 (over z, x), tok: 16 (over y, core).
Axes of the slice: x: 4, y: 8, z: 8, core: 2. Of those that a mesh axis runs over, the one named last changes fastest.
Arguments:
- activations: bfloat16 [6144, 16384], P('tok', 'blk'), may hold values from -6 to 6
- weights: bfloat16 [6, 64, 2, 256, 256], P(None, 'blk', None, 'tok'), may hold values from -0.25 to 0.25
- matchings: int32 [6, 64], replicated, may hold values from 0 to 63, as said below
- cotangent: bfloat16 [6144, 16384], P('tok', 'blk'), may hold values from -6 to 6
Outputs:
- output: bfloat16 [6144, 16384], P('tok', 'blk')
- input_grad: bfloat16 [6144, 16384], P('tok', 'blk')
- weight_grad: float32 [6, 64, 2, 256, 256], P(None, 'blk', None, 'tok')
Inputs may be any that keep to these rules, and one draw needn't show every extreme that they name: matchings[s] sends each block i either to itself or to i XOR 2^s, and the two blocks of each such pair make the same choice.
All inputs are finite; a program needn't handle non-finite values.
Results may differ from a plain program's by a relative error of at most 0.03.
Values may be sent and summed in bfloat16 or wider, within the bound.
No kernel may reach another device: no remote copies, remote signals or barrier semaphores. Data moves between devices by JAX's collectives and lax.ppermute only.
A program may use at most 64 MiB of HBM per device.

v0:
```python
import jax
import jax.numpy as jnp
from jax import lax
from jax.sharding import PartitionSpec as P


def partner(value, axis, bit):
    mask = 2**bit
    pairs = [(source, source ^ mask) for source in range(lax.axis_size(axis))]
    return lax.ppermute(value, axis, pairs)


def local_partner(value, section):
    rows, count, width = value.shape
    span = 1 << section
    shaped = value.reshape(rows, count // (2 * span), 2, span, width)
    return shaped[:, :, ::-1].reshape(rows, count, width)


def forward_partner(value, section, local_bits):
    if section < local_bits:
        return local_partner(value, section)
    return partner(value, "blk", section - local_bits)


def backward_partner(value, section, local_bits):
    if section < local_bits:
        return local_partner(value, section)
    return partner(value, "blk", section - local_bits)


def body(activations, weights, matchings, cotangent):
    rows = activations.shape[0]
    per_dev = weights.shape[1]
    width = weights.shape[4]
    sections = weights.shape[0]
    local_bits = per_dev.bit_length() - 1
    first_block = lax.axis_index("blk") * per_dev
    ident = first_block + jnp.arange(per_dev, dtype=jnp.int32)

    def swapped(section):
        owned = lax.dynamic_slice_in_dim(matchings[section], first_block, per_dev)
        return (owned != ident)[None, :, None]

    value = activations.reshape(rows, per_dev, width)
    saved = []
    final = None
    for section in range(sections):
        other = forward_partner(value, section, local_bits)
        flipped = swapped(section)
        first_in = jnp.where(flipped, other, value)
        second_in = jnp.where(flipped, value, other)
        saved.append((first_in, second_in))
        full = lax.all_gather(weights[section], "tok", axis=2, tiled=True)
        mixed = jnp.einsum("tjk,jkl->tjl", first_in, full[:, 0], preferred_element_type=jnp.float32)
        mixed = mixed + jnp.einsum(
            "tjk,jkl->tjl", second_in, full[:, 1], preferred_element_type=jnp.float32
        )
        if section < sections - 1:
            value = mixed.astype(jnp.bfloat16)
        else:
            final = mixed
    result = jax.nn.gelu(final).astype(jnp.bfloat16)
    back_fn = jax.vjp(jax.nn.gelu, final)[1]
    grad_now = back_fn(cotangent.reshape(rows, per_dev, width).astype(jnp.float32))[0].astype(
        jnp.bfloat16
    )
    terms = [None] * sections
    for section in reversed(range(sections)):
        first_in, second_in = saved[section]
        term = jnp.stack(
            [
                jnp.einsum("tjk,tjl->jkl", first_in, grad_now, preferred_element_type=jnp.float32),
                jnp.einsum("tjk,tjl->jkl", second_in, grad_now, preferred_element_type=jnp.float32),
            ],
            axis=1,
        )
        terms[section] = term
        full = lax.all_gather(weights[section], "tok", axis=2, tiled=True)
        grad_first = jnp.einsum(
            "tjl,jkl->tjk", grad_now, full[:, 0], preferred_element_type=jnp.float32
        )
        grad_second = jnp.einsum(
            "tjl,jkl->tjk", grad_now, full[:, 1], preferred_element_type=jnp.float32
        )
        flipped = swapped(section)
        kept = jnp.where(flipped, grad_second, grad_first)
        sent = jnp.where(flipped, grad_first, grad_second).astype(jnp.bfloat16)
        grad_now = (kept + backward_partner(sent, section, local_bits).astype(jnp.float32)).astype(
            jnp.bfloat16
        )
    weight_grad = lax.psum_scatter(
        jnp.stack(terms).astype(jnp.bfloat16), "tok", scatter_dimension=3, tiled=True
    ).astype(jnp.float32)
    return (
        result.reshape(rows, per_dev * width),
        grad_now.reshape(rows, per_dev * width),
        weight_grad,
    )


def solution(mesh):
    placed = (P("tok", "blk"), P(None, "blk", None, "tok", None), P(), P("tok", "blk"))
    return jax.shard_map(
        body,
        mesh=mesh,
        in_specs=placed,
        out_specs=(P("tok", "blk"), P("tok", "blk"), P(None, "blk", None, "tok", None)),
        check_vma=False,
    )
```

profile of v0, /device:TPU:1, one launch (start us, length us, event | category | flops | bytes accessed | tf_op | source)
XLA Modules:
  0.0 313.9 jit_solution(14981670406129750478)
XLA Ops:
  7.2 1.4 fusion.79
  8.6 1.5 fusion.78
  10.1 1.2 copy.88
  11.3 22.4 %all-gather = bf16[1,2,2,256,256]{4,3,1,2,0:T(8,128)(2,1)S(1)} all-gather(bf16[1,2,2,16,256]{4,3,1,2,0:T(8,128)(2,1)S(1)} %copy.90), channel_id=2, replica_groups=mesh['blk'=32,'tok'=16] {'tok'}, dimensions={3}, use_global_device_ids=true | all-gather | bytes 557056 | tf_op jit(solution)/shard_map/all_gather | solution.py:54
  34.8 1.9 collective-permute-start
  36.9 17.4 %all-gather.1 = bf16[1,2,2,256,256]{4,3,1,2,0:T(8,128)(2,1)S(1)} all-gather(bf16[1,2,2,16,256]{4,3,1,2,0:T(8,128)(2,1)S(1)} %copy.91), channel_id=3, replica_groups=mesh['blk'=32,'tok'=16] {'tok'}, dimensions={3}, use_global_device_ids=true | all-gather | bytes 557056 | tf_op jit(solution)/shard_map/all_gather | solution.py:54
  54.9 2.7 collective-permute-start.1
  57.8 17.0 %all-gather.2 = bf16[1,2,2,256,256]{4,3,1,2,0:T(8,128)(2,1)S(1)} all-gather(bf16[1,2,2,16,256]{4,3,1,2,0:T(8,128)(2,1)S(1)} %copy.92), channel_id=4, replica_groups=mesh['blk'=32,'tok'=16] {'tok'}, dimensions={3}, use_global_device_ids=true | all-gather | bytes 557056 | tf_op jit(solution)/shard_map/all_gather | solution.py:54
  75.4 4.0 %collective-permute-start.2 = (bf16[384,2,256]{2,0,1:T(8,128)(2,1)S(1)}, bf16[384,2,256]{2,0,1:T(8,128)(2,1)S(1)}, u32[]{:S(2)}, u32[]{:S(2)}) collective-permute-start(bf16[384,2,256]{2,0,1:T(8,128)(2,1)S(1)} %fusion.8), channel_id=1, source_target_pairs={{0,64},{16,80},{32,96},{48,112},{64,0},{80,16},{96,32},{112,48},{1... | collective-permute-start | bytes 1179656 | tf_op jit(solution)/shard_map/ppermute | solution.py:10
  79.5 16.6 %all-gather.3 = bf16[1,2,2,256,256]{4,3,1,2,0:T(8,128)(2,1)S(1)} all-gather(bf16[1,2,2,16,256]{4,3,1,2,0:T(8,128)(2,1)S(1)} %copy.93), channel_id=5, replica_groups=mesh['blk'=32,'tok'=16] {'tok'}, dimensions={3}, use_global_device_ids=true | all-gather | bytes 557056 | tf_op jit(solution)/shard_map/all_gather | solution.py:54
  96.9 5.8 %collective-permute-start.3 = (bf16[384,2,256]{2,0,1:T(8,128)(2,1)S(1)}, bf16[384,2,256]{2,0,1:T(8,128)(2,1)S(1)}, u32[]{:S(2)}, u32[]{:S(2)}) collective-permute-start(bf16[384,2,256]{2,0,1:T(8,128)(2,1)S(1)} %fusion.7), channel_id=1, source_target_pairs={{0,128},{16,144},{32,160},{48,176},{64,192},{80,208},{96,224},{112... | collective-permute-start | bytes 1179656 | tf_op jit(solution)/shard_map/ppermute | solution.py:10
  102.8 17.0 %all-gather.4 = bf16[1,2,2,256,256]{4,3,1,2,0:T(8,128)(2,1)S(1)} all-gather(bf16[1,2,2,16,256]{4,3,1,2,0:T(8,128)(2,1)S(1)} %copy.94), channel_id=6, replica_groups=mesh['blk'=32,'tok'=16] {'tok'}, dimensions={3}, use_global_device_ids=true | all-gather | bytes 557056 | tf_op jit(solution)/shard_map/all_gather | solution.py:54
  120.8 8.7 %collective-permute-start.4 = (bf16[384,2,256]{2,0,1:T(8,128)(2,1)S(1)}, bf16[384,2,256]{2,0,1:T(8,128)(2,1)}, u32[]{:S(2)}, u32[]{:S(2)}) collective-permute-start(bf16[384,2,256]{2,0,1:T(8,128)(2,1)S(1)} %fusion.6), channel_id=1, source_target_pairs={{0,256},{16,272},{32,288},{48,304},{64,320},{80,336},{96,352},{112... | collective-permute-start | bytes 1179656 | tf_op jit(solution)/shard_map/ppermute | solution.py:10
  129.6 18.7 %all-gather.5 = bf16[1,2,2,256,256]{4,2,1,0,3:T(2,128)(2,1)} all-gather(bf16[1,2,2,16,256]{4,2,1,0,3:T(2,128)(2,1)S(1)} %copy.95), channel_id=7, replica_groups=mesh['blk'=32,'tok'=16] {'tok'}, dimensions={3}, use_global_device_ids=true | all-gather | bytes 557056 | tf_op jit(solution)/shard_map/all_gather | solution.py:54
  148.3 2.0 copy.49
  150.4 2.0 copy.50
  152.4 0.6 fusion.67
  153.1 1.4 fusion.65
  154.5 3.0 fusion.29
  158.3 1.9 collective-permute-start.5
  160.2 20.0 %collective-permute-done.5 = bf16[384,2,256]{2,0,1:T(8,128)(2,1)S(1)} collective-permute-done((bf16[384,2,256]{2,0,1:T(8,128)(2,1)S(1)}, bf16[384,2,256]{2,0,1:T(8,128)(2,1)S(1)}, u32[]{:S(2)}, u32[]{:S(2)}) %collective-permute-start.5) | collective-permute-done | bytes 393248 | tf_op jit(solution)/shard_map/ppermute | solution.py:10
  181.3 1.9 collective-permute-start.6
  183.2 1.4 fusion.22
  184.6 18.6 %collective-permute-done.6 = bf16[384,2,256]{2,0,1:T(8,128)(2,1)S(1)} collective-permute-done((bf16[384,2,256]{2,0,1:T(8,128)(2,1)S(1)}, bf16[384,2,256]{2,0,1:T(8,128)(2,1)S(1)}, u32[]{:S(2)}, u32[]{:S(2)}) %collective-permute-start.6) | collective-permute-done | bytes 393248 | tf_op jit(solution)/shard_map/ppermute | solution.py:10
  204.2 2.1 collective-permute-start.7
  206.3 1.4 fusion.21
  207.7 0.4 fusion.20
  208.1 0.4 fusion.19
  208.6 7.9 %collective-permute-done.7 = bf16[384,2,256]{2,0,1:T(8,128)(2,1)S(1)} collective-permute-done((bf16[384,2,256]{2,0,1:T(8,128)(2,1)S(1)}, bf16[384,2,256]{2,0,1:T(8,128)(2,1)S(1)}, u32[]{:S(2)}, u32[]{:S(2)}) %collective-permute-start.7) | collective-permute-done | bytes 393248 | tf_op jit(solution)/shard_map/ppermute | solution.py:10
  217.4 2.7 collective-permute-start.8
  220.1 0.4 fusion.18
  220.6 0.4 fusion.17
  221.0 0.4 fusion.16
  221.4 8.8 %collective-permute-done.8 = bf16[384,2,256]{2,0,1:T(8,128)(2,1)S(1)} collective-permute-done((bf16[384,2,256]{2,0,1:T(8,128)(2,1)S(1)}, bf16[384,2,256]{2,0,1:T(8,128)(2,1)S(1)}, u32[]{:S(2)}, u32[]{:S(2)}) %collective-permute-start.8) | collective-permute-done | bytes 393248 | tf_op jit(solution)/shard_map/ppermute | solution.py:10
  231.2 2.1 collective-permute-start.9
  233.3 0.4 fusion.15
  234.1 0.4 fusion.13
  234.6 7.0 %collective-permute-done.9 = bf16[384,2,256]{2,0,1:T(8,128)(2,1)S(1)} collective-permute-done((bf16[384,2,256]{2,0,1:T(8,128)(2,1)S(1)}, bf16[384,2,256]{2,0,1:T(8,128)(2,1)S(1)}, u32[]{:S(2)}, u32[]{:S(2)}) %collective-permute-start.9) | collective-permute-done | bytes 393248 | tf_op jit(solution)/shard_map/ppermute | solution.py:10
  242.4 0.8 fusion.36
  243.2 0.8 fusion.37
  244.1 0.8 fusion.38
  244.9 0.8 fusion.39
  245.7 0.8 fusion.40
  246.6 0.8 fusion.41
  247.4 0.9 copy.67
  249.3 0.9 copy.68
  250.3 55.1 %reduce-scatter.2.cloned.1.call-done = bf16[6,2,2,16,256]{4,3,1,2,0:T(8,128)(2,1)} async-done(((bf16[6,2,2,256,256]{4,3,1,2,0:T(8,128)(2,1)}), bf16[6,2,2,16,256]{4,3,1,2,0:T(8,128)(2,1)}) %reduce-scatter.2.cloned.1.call-update) | async-done | bytes 196624 | tf_op jit(solution)/shard_map/reduce_scatter | solution.py:92
  305.3 1.7 copy.69
  (94 shorter events, 11.2 us)
Async XLA Ops:
  7.2 298.2 %reduce-scatter.2.cloned.1.call-start = ((), (), s32[]{:S(2)}) async-start(), calls=%async_computation.1 | async-start | bytes 3342336 | tf_op jit(solution)/shard_map/reduce_scatter | solution.py:92
  33.7 20.5 %copy-start = (bf16[1,2,2,256,256]{4,3,1,2,0:T(8,128)(2,1)}, bf16[1,2,2,256,256]{4,3,1,2,0:T(8,128)(2,1)S(1)}, u32[]{:S(2)}) copy-start(bf16[1,2,2,256,256]{4,3,1,2,0:T(8,128)(2,1)S(1)} %all-gather) | copy-start | bytes 1572868
  33.8 2.9 copy-start.17
  34.2 20.8 %copy-start.10 = (bf16[384,2,256]{0,2,1:T(8,128)(2,1)}, bf16[384,2,256]{0,2,1:T(8,128)(2,1)S(1)}, u32[]{:S(2)}) copy-start(bf16[384,2,256]{0,2,1:T(8,128)(2,1)S(1)} %get-tuple-element.9) | copy-start | bytes 1179652
  34.2 20.8 %copy-start.12 = (bf16[384,2,256]{0,2,1:T(8,128)(2,1)}, bf16[384,2,256]{0,2,1:T(8,128)(2,1)S(1)}, u32[]{:S(2)}) copy-start(bf16[384,2,256]{0,2,1:T(8,128)(2,1)S(1)} %get-tuple-element.10) | copy-start | bytes 1179652
  34.8 19.4 %collective-permute-start = (bf16[384,2,256]{2,0,1:T(8,128)(2,1)S(1)}, bf16[384,2,256]{2,0,1:T(8,128)(2,1)S(1)}, u32[]{:S(2)}, u32[]{:S(2)}) collective-permute-start(bf16[384,2,256]{2,0,1:T(8,128)(2,1)S(1)} %fusion.10), channel_id=1, source_target_pairs={{0,16},{16,0},{32,48},{48,32},{64,80},{80,64},{96,112},{112,96},{1... | collective-permute-start | bytes 1179656 | tf_op jit(solution)/shard_map/ppermute | solution.py:10
  54.2 20.5 %copy-start.2 = (bf16[1,2,2,256,256]{4,3,1,2,0:T(8,128)(2,1)}, bf16[1,2,2,256,256]{4,3,1,2,0:T(8,128)(2,1)S(1)}, u32[]{:S(2)}) copy-start(bf16[1,2,2,256,256]{4,3,1,2,0:T(8,128)(2,1)S(1)} %all-gather.1) | copy-start | bytes 1572868
  54.9 19.8 %collective-permute-start.1 = (bf16[384,2,256]{2,0,1:T(8,128)(2,1)S(1)}, bf16[384,2,256]{2,0,1:T(8,128)(2,1)S(1)}, u32[]{:S(2)}, u32[]{:S(2)}) collective-permute-start(bf16[384,2,256]{2,0,1:T(8,128)(2,1)S(1)} %fusion.9), channel_id=1, source_target_pairs={{0,32},{16,48},{32,0},{48,16},{64,96},{80,112},{96,64},{112,80},{1... | collective-permute-start | bytes 1179656 | tf_op jit(solution)/shard_map/ppermute | solution.py:10
  74.8 21.7 %copy-start.4 = (bf16[1,2,2,256,256]{4,3,1,2,0:T(8,128)(2,1)}, bf16[1,2,2,256,256]{4,3,1,2,0:T(8,128)(2,1)S(1)}, u32[]{:S(2)}) copy-start(bf16[1,2,2,256,256]{4,3,1,2,0:T(8,128)(2,1)S(1)} %all-gather.2) | copy-start | bytes 1572868
  75.4 20.7 %collective-permute-start.2 = (bf16[384,2,256]{2,0,1:T(8,128)(2,1)S(1)}, bf16[384,2,256]{2,0,1:T(8,128)(2,1)S(1)}, u32[]{:S(2)}, u32[]{:S(2)}) collective-permute-start(bf16[384,2,256]{2,0,1:T(8,128)(2,1)S(1)} %fusion.8), channel_id=1, source_target_pairs={{0,64},{16,80},{32,96},{48,112},{64,0},{80,16},{96,32},{112,48},{1... | collective-permute-start | bytes 1179656 | tf_op jit(solution)/shard_map/ppermute | solution.py:10
  96.2 24.3 %copy-start.6 = (bf16[1,2,2,256,256]{4,3,1,2,0:T(8,128)(2,1)}, bf16[1,2,2,256,256]{4,3,1,2,0:T(8,128)(2,1)S(1)}, u32[]{:S(2)}) copy-start(bf16[1,2,2,256,256]{4,3,1,2,0:T(8,128)(2,1)S(1)} %all-gather.3) | copy-start | bytes 1572868
  96.5 33.0 %copy-start.16 = (bf16[1,2,2,16,256]{4,3,2,1,0:T(8,128)(2,1)S(1)}, bf16[1,2,2,16,256]{4,3,2,1,0:T(8,128)(2,1)}, u32[]{:S(2)}) copy-start(bf16[1,2,2,16,256]{4,3,2,1,0:T(8,128)(2,1)} %get-tuple-element.17) | copy-start | bytes 98308
  96.9 23.3 %collective-permute-start.3 = (bf16[384,2,256]{2,0,1:T(8,128)(2,1)S(1)}, bf16[384,2,256]{2,0,1:T(8,128)(2,1)S(1)}, u32[]{:S(2)}, u32[]{:S(2)}) collective-permute-start(bf16[384,2,256]{2,0,1:T(8,128)(2,1)S(1)} %fusion.7), channel_id=1, source_target_pairs={{0,128},{16,144},{32,160},{48,176},{64,192},{80,208},{96,224},{112... | collective-permute-start | bytes 1179656 | tf_op jit(solution)/shard_map/ppermute | solution.py:10
  119.8 1.0 copy-start.8
  120.8 32.2 %collective-permute-start.4 = (bf16[384,2,256]{2,0,1:T(8,128)(2,1)S(1)}, bf16[384,2,256]{2,0,1:T(8,128)(2,1)}, u32[]{:S(2)}, u32[]{:S(2)}) collective-permute-start(bf16[384,2,256]{2,0,1:T(8,128)(2,1)S(1)} %fusion.6), channel_id=1, source_target_pairs={{0,256},{16,272},{32,288},{48,304},{64,320},{80,336},{96,352},{112... | collective-permute-start | bytes 1179656 | tf_op jit(solution)/shard_map/ppermute | solution.py:10
  154.5 3.0 copy-start.14
  157.8 22.7 %copy-start.9 = (bf16[1,2,2,256,256]{4,3,1,2,0:T(8,128)(2,1)S(1)}, bf16[1,2,2,256,256]{4,3,1,2,0:T(8,128)(2,1)}, u32[]{:S(2)}) copy-start(bf16[1,2,2,256,256]{4,3,1,2,0:T(8,128)(2,1)} %copy-done.8) | copy-start | bytes 1572868
  158.3 22.0 %collective-permute-start.5 = (bf16[384,2,256]{2,0,1:T(8,128)(2,1)S(1)}, bf16[384,2,256]{2,0,1:T(8,128)(2,1)S(1)}, u32[]{:S(2)}, u32[]{:S(2)}) collective-permute-start(bf16[384,2,256]{2,0,1:T(8,128)(2,1)S(1)} %fusion.42), channel_id=1, source_target_pairs={{0,256},{16,272},{32,288},{48,304},{64,320},{80,336},{96,352},{112... | collective-permute-start | bytes 1179656 | tf_op jit(solution)/shard_map/ppermute | solution.py:10
  181.1 22.3 %copy-start.7 = (bf16[1,2,2,256,256]{4,3,1,2,0:T(8,128)(2,1)S(1)}, bf16[1,2,2,256,256]{4,3,1,2,0:T(8,128)(2,1)}, u32[]{:S(2)}) copy-start(bf16[1,2,2,256,256]{4,3,1,2,0:T(8,128)(2,1)} %copy-done.6) | copy-start | bytes 1572868
  181.3 22.0 %collective-permute-start.6 = (bf16[384,2,256]{2,0,1:T(8,128)(2,1)S(1)}, bf16[384,2,256]{2,0,1:T(8,128)(2,1)S(1)}, u32[]{:S(2)}, u32[]{:S(2)}) collective-permute-start(bf16[384,2,256]{2,0,1:T(8,128)(2,1)S(1)} %fusion.43), channel_id=1, source_target_pairs={{0,128},{16,144},{32,160},{48,176},{64,192},{80,208},{96,224},{112... | collective-permute-start | bytes 1179656 | tf_op jit(solution)/shard_map/ppermute | solution.py:10
  204.2 12.4 %copy-start.5 = (bf16[1,2,2,256,256]{4,3,1,2,0:T(8,128)(2,1)S(1)}, bf16[1,2,2,256,256]{4,3,1,2,0:T(8,128)(2,1)}, u32[]{:S(2)}) copy-start(bf16[1,2,2,256,256]{4,3,1,2,0:T(8,128)(2,1)} %copy-done.4) | copy-start | bytes 1572868
  204.2 12.2 %collective-permute-start.7 = (bf16[384,2,256]{2,0,1:T(8,128)(2,1)S(1)}, bf16[384,2,256]{2,0,1:T(8,128)(2,1)S(1)}, u32[]{:S(2)}, u32[]{:S(2)}) collective-permute-start(bf16[384,2,256]{2,0,1:T(8,128)(2,1)S(1)} %fusion.44), channel_id=1, source_target_pairs={{0,64},{16,80},{32,96},{48,112},{64,0},{80,16},{96,32},{112,48},{1... | collective-permute-start | bytes 1179656 | tf_op jit(solution)/shard_map/ppermute | solution.py:10
  217.4 13.0 %copy-start.3 = (bf16[1,2,2,256,256]{4,3,1,2,0:T(8,128)(2,1)S(1)}, bf16[1,2,2,256,256]{4,3,1,2,0:T(8,128)(2,1)}, u32[]{:S(2)}) copy-start(bf16[1,2,2,256,256]{4,3,1,2,0:T(8,128)(2,1)} %copy-done.2) | copy-start | bytes 1572868
  217.4 12.8 %collective-permute-start.8 = (bf16[384,2,256]{2,0,1:T(8,128)(2,1)S(1)}, bf16[384,2,256]{2,0,1:T(8,128)(2,1)S(1)}, u32[]{:S(2)}, u32[]{:S(2)}) collective-permute-start(bf16[384,2,256]{2,0,1:T(8,128)(2,1)S(1)} %fusion.45), channel_id=1, source_target_pairs={{0,32},{16,48},{32,0},{48,16},{64,96},{80,112},{96,64},{112,80},{1... | collective-permute-start | bytes 1179656 | tf_op jit(solution)/shard_map/ppermute | solution.py:10
  231.2 10.6 %copy-start.11 = (bf16[384,2,256]{0,2,1:T(8,128)(2,1)S(1)}, bf16[384,2,256]{0,2,1:T(8,128)(2,1)}, u32[]{:S(2)}) copy-start(bf16[384,2,256]{0,2,1:T(8,128)(2,1)} %copy-done.10) | copy-start | bytes 1179652
  231.2 10.4 %collective-permute-start.9 = (bf16[384,2,256]{2,0,1:T(8,128)(2,1)S(1)}, bf16[384,2,256]{2,0,1:T(8,128)(2,1)S(1)}, u32[]{:S(2)}, u32[]{:S(2)}) collective-permute-start(bf16[384,2,256]{2,0,1:T(8,128)(2,1)S(1)} %fusion.46), channel_id=1, source_target_pairs={{0,16},{16,0},{32,48},{48,32},{64,80},{80,64},{96,112},{112,96},{1... | collective-permute-start | bytes 1179656 | tf_op jit(solution)/shard_map/ppermute | solution.py:10
  233.7 8.4 %copy-start.13 = (bf16[384,2,256]{0,2,1:T(8,128)(2,1)S(1)}, bf16[384,2,256]{0,2,1:T(8,128)(2,1)}, u32[]{:S(2)}) copy-start(bf16[384,2,256]{0,2,1:T(8,128)(2,1)} %copy-done.12) | copy-start | bytes 1179652
  244.9 2.5 copy-start.15
  245.7 2.6 copy-start.1
  247.4 1.6 copy-start.18
Sparse Core Ops, SparseCore 0:
  247.6 57.7 reduce-scatter.1
where the time goes:
time: 316 us; the launch traced here: 314 us
  waiting for transfers between devices  118 us (37%)
  blocking collectives  109 us (34%)
  starting transfers between devices  33.8 us (11%)
  matrix products  18 us (6%)
  between operations  14.7 us (5%)
  local copies, waits for them, and re-layouts  11.8 us (4%)
  other arithmetic  8.5 us (3%)
    all_gather x6, blocking collectives, body(): full = lax.all_gather(weights[section], 'tok', axis=2, tiled=True)  109 us
    ppermute x10, waiting for transfers between devices, partner(): return lax.ppermute(value, axis, pairs)  62.7 us
    reduce_scatter x1, waiting for transfers between devices, body(): lax.psum_scatter(jnp.stack(terms).astype(jnp.bfloat16), 'tok', scatter_di...  55.1 us
    ppermute x10, starting transfers between devices, partner(): return lax.ppermute(value, axis, pairs)  33.8 us
  transfers between devices with their start and end apart: 11, of which 7 were waited for; matrix products, arithmetic and copies ran while one was open for 4% of the time, Pallas kernels for 0%

commit v1 on v0

v1 whole, which is shorter than its diff:
```python
import jax
import jax.numpy as jnp
from jax import lax
from jax.sharding import PartitionSpec as P


def partner(value, axis, bit):
    mask = 2**bit
    pairs = [(source, source ^ mask) for source in range(lax.axis_size(axis))]
    return lax.ppermute(value, axis, pairs)


def local_partner(value, section):
    count, rows, width = value.shape
    span = 1 << section
    shaped = value.reshape(count // (2 * span), 2, span, rows, width)
    return shaped[:, ::-1].reshape(count, rows, width)


def exchange(value, section, local_bits):
    if section < local_bits:
        return local_partner(value, section)
    return partner(value, "blk", section - local_bits)


def scatter_sum(terms, axis):
    count, per_dev, both, depth, width = terms.shape
    size = lax.axis_size(axis)
    parts = terms.reshape(count, per_dev, both, size, depth // size, width)
    parts = jnp.moveaxis(parts, 3, 0)
    parts = lax.all_to_all(parts, axis, 0, 0)
    return jnp.sum(parts.astype(jnp.float32), axis=0)


EARLY = 2


def body(activations, weights, matchings, cotangent):
    rows = activations.shape[0]
    sections, per_dev, _, _, width = weights.shape
    local_bits = per_dev.bit_length() - 1
    first_block = lax.axis_index("blk") * per_dev
    ident = first_block + jnp.arange(per_dev, dtype=jnp.int32)
    owned = lax.dynamic_slice_in_dim(matchings, first_block, per_dev, axis=1)
    flips = (owned != ident)[:, :, None, None]

    rest = lax.all_gather(weights[EARLY:], "tok", axis=3, tiled=True)
    full = [
        lax.all_gather(weights[s], "tok", axis=2, tiled=True) if s < EARLY else rest[s - EARLY]
        for s in range(sections)
    ]

    value = jnp.stack([activations[:, j * width : (j + 1) * width] for j in range(per_dev)])
    saved = []
    final = None
    for section in range(sections):
        other = exchange(value, section, local_bits)
        flipped = flips[section]
        first_in = jnp.where(flipped, other, value)
        second_in = jnp.where(flipped, value, other)
        saved.append((first_in, second_in))
        mixed = jnp.einsum("jtk,jkl->jtl", first_in, full[section][:, 0], preferred_element_type=jnp.float32)
        mixed = mixed + jnp.einsum(
            "jtk,jkl->jtl", second_in, full[section][:, 1], preferred_element_type=jnp.float32
        )
        if section < sections - 1:
            value = mixed.astype(jnp.bfloat16)
        else:
            final = mixed
    result = jax.nn.gelu(final).astype(jnp.bfloat16)
    back_fn = jax.vjp(jax.nn.gelu, final)[1]
    cotan = jnp.stack([cotangent[:, j * width : (j + 1) * width] for j in range(per_dev)])
    grad_now = back_fn(cotan.astype(jnp.float32))[0].astype(jnp.bfloat16)
    terms = [None] * sections
    late = None
    for section in reversed(range(sections)):
        first_in, second_in = saved[section]
        terms[section] = jnp.stack(
            [
                jnp.einsum("jtk,jtl->jkl", first_in, grad_now, preferred_element_type=jnp.float32),
                jnp.einsum("jtk,jtl->jkl", second_in, grad_now, preferred_element_type=jnp.float32),
            ],
            axis=1,
        ).astype(jnp.bfloat16)
        if section == EARLY:
            late = lax.psum_scatter(jnp.stack(terms[EARLY:]), "tok", scatter_dimension=3, tiled=True)
        grad_first = jnp.einsum(
            "jtl,jkl->jtk", grad_now, full[section][:, 0], preferred_element_type=jnp.float32
        )
        grad_second = jnp.einsum(
            "jtl,jkl->jtk", grad_now, full[section][:, 1], preferred_element_type=jnp.float32
        )
        flipped = flips[section]
        kept = jnp.where(flipped, grad_second, grad_first)
        sent = jnp.where(flipped, grad_first, grad_second).astype(jnp.bfloat16)
        grad_now = (kept + exchange(sent, section, local_bits).astype(jnp.float32)).astype(jnp.bfloat16)
    first = scatter_sum(jnp.stack(terms[:EARLY]), "tok")
    weight_grad = jnp.concatenate([first, late.astype(jnp.float32)])
    return (
        jnp.concatenate([result[j] for j in range(per_dev)], axis=1),
        jnp.concatenate([grad_now[j] for j in range(per_dev)], axis=1),
        weight_grad,
    )


def solution(mesh):
    placed = (P("tok", "blk"), P(None, "blk", None, "tok", None), P(), P("tok", "blk"))
    return jax.shard_map(
        body,
        mesh=mesh,
        in_specs=placed,
        out_specs=(P("tok", "blk"), P("tok", "blk"), P(None, "blk", None, "tok", None)),
        check_vma=False,
    )
```

time: 316 us -> 283 us (0.90)
  blocking collectives: 109 us -> 41.3 us
  starting transfers between devices: 33.8 us -> 52.2 us
  waiting for transfers between devices: 118 us -> 132 us
  other arithmetic: 8.5 us -> 5.34 us
    all_gather x6 -> x2, blocking collectives: 109 us -> 41.3 us  [body(): lax.all_gather(weights[s], 'tok', axis=2, tiled=True)]
    reduce_scatter x1, waiting for transfers between devices: 55.1 us -> 8.35 us  [body(): lax.psum_scatter(jnp.stack(terms[EARLY:]), 'tok', scatter_dimension=3, ti...]
    ppermute x10, waiting for transfers between devices: 62.7 us -> 96.5 us  [partner(): return lax.ppermute(value, axis, pairs)]
    all_to_all x0 -> x1, waiting for transfers between devices: none -> 27.1 us  [scatter_sum(): parts = lax.all_to_all(parts, axis, 0, 0)]
    all_to_all x0 -> x1, starting transfers between devices: none -> 9.61 us  [scatter_sum(): parts = lax.all_to_all(parts, axis, 0, 0)]
    ppermute x10, starting transfers between devices: 33.8 us -> 42.6 us  [partner(): return lax.ppermute(value, axis, pairs)]
    unnamed x5 -> x0, other arithmetic: 4.15 us -> none
    unnamed x47 -> x52, local copies, waits for them, and re-layouts: 3.72 us -> 7.64 us
  transfers between devices with their start and end apart: 11 -> 13, of which waited for: 7 -> 11; matrix products, arithmetic and copies ran while one was open for 4% -> 9% of each run, Pallas kernels for 0% -> 0%
where the time goes in v1:
time: 283 us; the launch traced here: 279 us
  waiting for transfers between devices  132 us (47%)
  starting transfers between devices  52.2 us (18%)
  blocking collectives  41.3 us (15%)
  matrix products  18.7 us (7%)
  between operations  14.7 us (5%)
  local copies, waits for them, and re-layouts  14.2 us (5%)
  other arithmetic  5.34 us (2%)
    ppermute x10, waiting for transfers between devices, partner(): return lax.ppermute(value, axis, pairs)  96.5 us
    ppermute x10, starting transfers between devices, partner(): return lax.ppermute(value, axis, pairs)  42.6 us
    all_gather x2, blocking collectives, body(): lax.all_gather(weights[s], 'tok', axis=2, tiled=True)  41.3 us
    all_to_all x1, waiting for transfers between devices, scatter_sum(): parts = lax.all_to_all(parts, axis, 0, 0)  27.1 us
    all_to_all x1, starting transfers between devices, scatter_sum(): parts = lax.all_to_all(parts, axis, 0, 0)  9.61 us
    reduce_scatter x1, waiting for transfers between devices, body(): lax.psum_scatter(jnp.stack(terms[EARLY:]), 'tok', scatter_dimension=3, ti...  8.35 us
    unnamed x52, local copies, waits for them, and re-layouts  7.64 us
  transfers between devices with their start and end apart: 13, of which 11 were waited for; matrix products, arithmetic and copies ran while one was open for 9% of the time, Pallas kernels for 0%

profile of v1, /device:TPU:1, one launch (start us, length us, event | category | flops | bytes accessed | tf_op | source)
XLA Modules:
  0.0 278.6 jit_solution(12180917436595408731)
XLA Ops:
  7.2 0.9 slice.137
  8.1 0.7 copy.92
  8.9 0.8 fusion.43
  9.7 1.1 fusion.42
  11.2 0.5 slice_bitcast_fusion.49
  11.7 22.4 %all-gather = bf16[1,2,2,256,256]{4,3,1,2,0:T(8,128)(2,1)S(1)} all-gather(bf16[1,2,2,16,256]{4,3,1,2,0:T(8,128)(2,1)S(1)} %copy.90), channel_id=2, replica_groups=mesh['blk'=32,'tok'=16] {'tok'}, dimensions={3}, use_global_device_ids=true | all-gather | bytes 557056 | tf_op jit(solution)/shard_map/all_gather | solution.py:49
  35.5 1.9 collective-permute-start
  37.4 18.9 %all-gather.1 = bf16[1,2,2,256,256]{4,3,1,2,0:T(8,128)(2,1)S(1)} all-gather(bf16[1,2,2,16,256]{4,3,1,2,0:T(8,128)(2,1)S(1)} %copy.91), channel_id=3, replica_groups=mesh['blk'=32,'tok'=16] {'tok'}, dimensions={3}, use_global_device_ids=true | all-gather | bytes 557056 | tf_op jit(solution)/shard_map/all_gather | solution.py:49
  57.0 3.5 %collective-permute-start.1 = (bf16[2,384,256]{2,1,0:T(8,128)(2,1)S(1)}, bf16[2,384,256]{2,1,0:T(8,128)(2,1)S(1)}, u32[]{:S(2)}, u32[]{:S(2)}) collective-permute-start(bf16[2,384,256]{2,1,0:T(8,128)(2,1)S(1)} %fusion.1), channel_id=1, source_target_pairs={{0,32},{16,48},{32,0},{48,16},{64,96},{80,112},{96,64},{112,80},{1... | collective-permute-start | bytes 1179656 | tf_op jit(solution)/shard_map/ppermute | solution.py:10
  60.5 2.5 slice_bitcast_fusion.3
  62.9 8.0 %collective-permute-done.1 = bf16[2,384,256]{2,1,0:T(8,128)(2,1)S(1)} collective-permute-done((bf16[2,384,256]{2,1,0:T(8,128)(2,1)S(1)}, bf16[2,384,256]{2,1,0:T(8,128)(2,1)S(1)}, u32[]{:S(2)}, u32[]{:S(2)}) %collective-permute-start.1) | collective-permute-done | bytes 393248 | tf_op jit(solution)/shard_map/ppermute | solution.py:10
  71.6 2.6 collective-permute-start.2
  74.2 8.9 %collective-permute-done.2 = bf16[2,384,256]{2,1,0:T(8,128)(2,1)S(1)} collective-permute-done((bf16[2,384,256]{2,1,0:T(8,128)(2,1)S(1)}, bf16[2,384,256]{2,1,0:T(8,128)(2,1)S(1)}, u32[]{:S(2)}, u32[]{:S(2)}) %collective-permute-start.2) | collective-permute-done | bytes 393248 | tf_op jit(solution)/shard_map/ppermute | solution.py:10
  83.8 3.9 %collective-permute-start.3 = (bf16[2,384,256]{2,1,0:T(8,128)(2,1)S(1)}, bf16[2,384,256]{2,1,0:T(8,128)(2,1)S(1)}, u32[]{:S(2)}, u32[]{:S(2)}) collective-permute-start(bf16[2,384,256]{2,1,0:T(8,128)(2,1)S(1)} %fusion.3), channel_id=1, source_target_pairs={{0,128},{16,144},{32,160},{48,176},{64,192},{80,208},{96,224},{112... | collective-permute-start | bytes 1179656 | tf_op jit(solution)/shard_map/ppermute | solution.py:10
  87.7 17.8 %collective-permute-done.3 = bf16[2,384,256]{2,1,0:T(8,128)(2,1)S(1)} collective-permute-done((bf16[2,384,256]{2,1,0:T(8,128)(2,1)S(1)}, bf16[2,384,256]{2,1,0:T(8,128)(2,1)S(1)}, u32[]{:S(2)}, u32[]{:S(2)}) %collective-permute-start.3) | collective-permute-done | bytes 393248 | tf_op jit(solution)/shard_map/ppermute | solution.py:10
  106.2 9.6 %collective-permute-start.4 = (bf16[2,384,256]{2,1,0:T(8,128)(2,1)S(1)}, bf16[2,384,256]{2,1,0:T(8,128)(2,1)}, u32[]{:S(2)}, u32[]{:S(2)}) collective-permute-start(bf16[2,384,256]{2,1,0:T(8,128)(2,1)S(1)} %fusion.4), channel_id=1, source_target_pairs={{0,256},{16,272},{32,288},{48,304},{64,320},{80,336},{96,352},{112... | collective-permute-start | bytes 1179656 | tf_op jit(solution)/shard_map/ppermute | solution.py:10
  115.8 0.8 fusion.41
  116.6 1.7 copy.93
  118.3 1.7 copy.94
  120.1 9.8 %collective-permute-done.4 = bf16[2,384,256]{2,1,0:T(8,128)(2,1)} collective-permute-done((bf16[2,384,256]{2,1,0:T(8,128)(2,1)S(1)}, bf16[2,384,256]{2,1,0:T(8,128)(2,1)}, u32[]{:S(2)}, u32[]{:S(2)}) %collective-permute-start.4) | collective-permute-done | bytes 393248 | tf_op jit(solution)/shard_map/ppermute | solution.py:10
  129.9 1.4 fusion.40
  131.3 2.9 %fusion.15 = (bf16[2,384,256]{1,2,0:T(8,128)(2,1)S(1)}, bf16[2,384,256]{1,2,0:T(8,128)(2,1)}) fusion(bf16[1,384,256]{1,2,0:T(8,128)(2,1)} %bitcast.161, bf16[1,384,256]{1,2,0:T(8,128)(2,1)} %bitcast.160, f32[2,384,256]{1,2,0:T(8,128)S(1)} %fusion.40, bf16[2,2,256,256]{3,2,0,1:T(8,128)(2,1)} %get-tuple-element.10, ...), kind=kOutput, calls=%fused_computation.41 | convolution fusion | flops 105775104 | bytes 3015168 | tf_op jit(solution)/shard_map/jtk,jkl->jtl/dot_general | solution.py:62
  134.9 6.6 %collective-permute-start.5 = (bf16[2,384,256]{2,1,0:T(8,128)(2,1)S(1)}, bf16[2,384,256]{2,1,0:T(8,128)(2,1)S(1)}, u32[]{:S(2)}, u32[]{:S(2)}) collective-permute-start(bf16[2,384,256]{2,1,0:T(8,128)(2,1)S(1)} %get-tuple-element.33), channel_id=1, source_target_pairs={{0,256},{16,272},{32,288},{48,304},{64,320},{80,336},{96,352},{112... | collective-permute-start | bytes 1179656 | tf_op jit(solution)/shard_map/ppermute | solution.py:10
  141.5 18.0 %collective-permute-done.5 = bf16[2,384,256]{2,1,0:T(8,128)(2,1)S(1)} collective-permute-done((bf16[2,384,256]{2,1,0:T(8,128)(2,1)S(1)}, bf16[2,384,256]{2,1,0:T(8,128)(2,1)S(1)}, u32[]{:S(2)}, u32[]{:S(2)}) %collective-permute-start.5) | collective-permute-done | bytes 393248 | tf_op jit(solution)/shard_map/ppermute | solution.py:10
  160.3 1.9 collective-permute-start.6
  162.2 1.4 fusion.12
  163.7 1.4 fusion.11
  165.5 15.4 %collective-permute-done.6 = bf16[2,384,256]{2,1,0:T(8,128)(2,1)S(1)} collective-permute-done((bf16[2,384,256]{2,1,0:T(8,128)(2,1)S(1)}, bf16[2,384,256]{2,1,0:T(8,128)(2,1)S(1)}, u32[]{:S(2)}, u32[]{:S(2)}) %collective-permute-start.6) | collective-permute-done | bytes 393248 | tf_op jit(solution)/shard_map/ppermute | solution.py:10
  181.8 1.9 collective-permute-start.7
  183.7 0.4 fusion.9
  184.1 0.4 fusion.8
  184.6 0.4 fusion.7
  185.0 7.2 %collective-permute-done.7 = bf16[2,384,256]{2,1,0:T(8,128)(2,1)S(1)} collective-permute-done((bf16[2,384,256]{2,1,0:T(8,128)(2,1)S(1)}, bf16[2,384,256]{2,1,0:T(8,128)(2,1)S(1)}, u32[]{:S(2)}, u32[]{:S(2)}) %collective-permute-start.7) | collective-permute-done | bytes 393248 | tf_op jit(solution)/shard_map/ppermute | solution.py:10
  192.7 1.0 select_convert_fusion.2
  193.7 3.9 %collective-permute-start.8 = (bf16[2,384,256]{2,1,0:T(8,128)(2,1)}, bf16[2,384,256]{2,1,0:T(8,128)(2,1)S(1)}, u32[]{:S(2)}, u32[]{:S(2)}) collective-permute-start(bf16[2,384,256]{2,1,0:T(8,128)(2,1)} %get-tuple-element.39), channel_id=1, source_target_pairs={{0,32},{16,48},{32,0},{48,16},{64,96},{80,112},{96,64},{112,80},{1... | collective-permute-start | bytes 1179656 | tf_op jit(solution)/shard_map/ppermute | solution.py:10
  198.0 0.4 fusion.5
  198.5 1.5 maximum_maximum_fusion
  200.0 4.9 %collective-permute-done.8 = bf16[2,384,256]{2,1,0:T(8,128)(2,1)S(1)} collective-permute-done((bf16[2,384,256]{2,1,0:T(8,128)(2,1)}, bf16[2,384,256]{2,1,0:T(8,128)(2,1)S(1)}, u32[]{:S(2)}, u32[]{:S(2)}) %collective-permute-start.8) | collective-permute-done | bytes 393248 | tf_op jit(solution)/shard_map/ppermute | solution.py:10
  205.7 6.8 %collective-permute-start.9 = (bf16[2,384,256]{2,1,0:T(8,128)(2,1)S(1)}, bf16[2,384,256]{2,1,0:T(8,128)(2,1)S(1)}, u32[]{:S(2)}, u32[]{:S(2)}) collective-permute-start(bf16[2,384,256]{2,1,0:T(8,128)(2,1)S(1)} %get-tuple-element.41), channel_id=1, source_target_pairs={{0,16},{16,0},{32,48},{48,32},{64,80},{80,64},{96,112},{112,96},{1... | collective-permute-start | bytes 1179656 | tf_op jit(solution)/shard_map/ppermute | solution.py:10
  213.4 6.5 %collective-permute-done.9 = bf16[2,384,256]{2,1,0:T(8,128)(2,1)S(1)} collective-permute-done((bf16[2,384,256]{2,1,0:T(8,128)(2,1)S(1)}, bf16[2,384,256]{2,1,0:T(8,128)(2,1)S(1)}, u32[]{:S(2)}, u32[]{:S(2)}) %collective-permute-start.9) | collective-permute-done | bytes 393248 | tf_op jit(solution)/shard_map/ppermute | solution.py:10
  220.7 1.1 copy_bitcast_fusion
  221.8 9.6 %all-to-all-start = ((bf16[16,2,2,2,16,256]{5,4,2,3,1,0:T(8,128)(2,1)}), bf16[16,2,2,2,16,256]{5,4,2,3,1,0:T(8,128)(2,1)S(1)}, u32[]{:S(2)}, u32[]{:S(2)}) async-start(bf16[16,2,2,2,16,256]{5,4,2,3,1,0:T(8,128)(2,1)} %copy_bitcast_fusion), calls=%async_computation | async-start | bytes 2097152 | tf_op jit(solution)/shard_map/all_to_all | solution.py:31
  231.6 0.9 copy.64
  233.4 0.9 copy.65
  234.3 27.1 %all-to-all-done = bf16[16,2,2,2,16,256]{5,4,2,3,1,0:T(8,128)(2,1)S(1)} async-done(((bf16[16,2,2,2,16,256]{5,4,2,3,1,0:T(8,128)(2,1)}), bf16[16,2,2,2,16,256]{5,4,2,3,1,0:T(8,128)(2,1)S(1)}, u32[]{:S(2)}, u32[]{:S(2)}) %all-to-all-start) | async-done | bytes 1048608 | tf_op jit(solution)/shard_map/all_to_all | solution.py:31
  261.7 8.3 %reduce-scatter.2.cloned.1.call-done = bf16[4,2,2,16,256]{4,3,1,2,0:T(8,128)(2,1)} async-done(((bf16[4,2,2,256,256]{4,3,1,2,0:T(8,128)(2,1)}), bf16[4,2,2,16,256]{4,3,1,2,0:T(8,128)(2,1)}) %reduce-scatter.2.cloned.1.call-update) | async-done | bytes 131088 | tf_op jit(solution)/shard_map/reduce_scatter | solution.py:86
  270.0 0.9 convert_element_type.161
  271.0 0.8 copy.66
  (95 shorter events, 11.6 us)
Async XLA Ops:
  7.2 4.0 %copy-start.20 = (s32[6,64]{1,0:T(8,128)S(1)}, s32[6,64]{1,0:T(8,128)}, u32[]{:S(2)}) copy-start(s32[6,64]{1,0:T(8,128)} %param.6) | copy-start | bytes 4612
  7.2 53.3 %all-gather.4.cloned.1.call-start = ((), (), s32[]{:S(2)}) async-start(), calls=%async_computation.2 | async-start | bytes 2228224 | tf_op jit(solution)/shard_map/all_gather | solution.py:47
  8.8 261.2 %reduce-scatter.2.cloned.1.call-start = ((), (), s32[]{:S(2)}) async-start(), calls=%async_computation.3 | async-start | bytes 2228224 | tf_op jit(solution)/shard_map/reduce_scatter | solution.py:86
  11.7 23.7 %copy-start.18 = (pred[2]{0:T(512)(128)(4,1)}, pred[2]{0:T(512)(128)(4,1)S(1)}, u32[]{:S(2)}) copy-start(pred[2]{0:T(512)(128)(4,1)S(1)} %get-tuple-element.28) | copy-start | bytes 10
  34.2 1.3 copy-start
  34.4 0.8 copy-start.12
  34.4 22.2 %copy-start.10 = (bf16[2,384,256]{1,2,0:T(8,128)(2,1)}, bf16[2,384,256]{1,2,0:T(8,128)(2,1)S(1)}, u32[]{:S(2)}) copy-start(bf16[2,384,256]{1,2,0:T(8,128)(2,1)S(1)} %get-tuple-element.15) | copy-start | bytes 1179652
  35.5 20.8 %collective-permute-start = (bf16[2,384,256]{2,1,0:T(8,128)(2,1)S(1)}, bf16[2,384,256]{2,1,0:T(8,128)(2,1)S(1)}, u32[]{:S(2)}, u32[]{:S(2)}) collective-permute-start(bf16[2,384,256]{2,1,0:T(8,128)(2,1)S(1)} %fusion), channel_id=1, source_target_pairs={{0,16},{16,0},{32,48},{48,32},{64,80},{80,64},{96,112},{112,96},{1... | collective-permute-start | bytes 1179656 | tf_op jit(solution)/shard_map/ppermute | solution.py:10
  56.3 6.6 %copy-start.2 = (bf16[1,2,2,256,256]{4,3,1,2,0:T(8,128)(2,1)}, bf16[1,2,2,256,256]{4,3,1,2,0:T(8,128)(2,1)S(1)}, u32[]{:S(2)}) copy-start(bf16[1,2,2,256,256]{4,3,1,2,0:T(8,128)(2,1)S(1)} %all-gather.1) | copy-start | bytes 1572868
  57.0 14.0 %collective-permute-start.1 = (bf16[2,384,256]{2,1,0:T(8,128)(2,1)S(1)}, bf16[2,384,256]{2,1,0:T(8,128)(2,1)S(1)}, u32[]{:S(2)}, u32[]{:S(2)}) collective-permute-start(bf16[2,384,256]{2,1,0:T(8,128)(2,1)S(1)} %fusion.1), channel_id=1, source_target_pairs={{0,32},{16,48},{32,0},{48,16},{64,96},{80,112},{96,64},{112,80},{1... | collective-permute-start | bytes 1179656 | tf_op jit(solution)/shard_map/ppermute | solution.py:10
  62.9 20.5 %copy-start.4 = (bf16[2,2,256,256]{3,2,0,1:T(8,128)(2,1)}, bf16[2,2,256,256]{3,2,0,1:T(8,128)(2,1)S(1)}, u32[]{:S(2)}) copy-start(bf16[2,2,256,256]{3,2,0,1:T(8,128)(2,1)S(1)} %get-tuple-element.9) | copy-start | bytes 1572868
  62.9 20.5 %copy-start.6 = (bf16[2,2,256,256]{3,2,0,1:T(8,128)(2,1)}, bf16[2,2,256,256]{3,2,0,1:T(8,128)(2,1)S(1)}, u32[]{:S(2)}) copy-start(bf16[2,2,256,256]{3,2,0,1:T(8,128)(2,1)S(1)} %get-tuple-element.12) | copy-start | bytes 1572868
  62.9 42.9 %copy-start.8 = (bf16[2,2,256,256]{3,2,0,1:T(8,128)(2,1)}, bf16[2,2,256,256]{3,2,0,1:T(8,128)(2,1)S(1)}, u32[]{:S(2)}) copy-start(bf16[2,2,256,256]{3,2,0,1:T(8,128)(2,1)S(1)} %get-tuple-element.11) | copy-start | bytes 1572868
  71.6 11.6 %collective-permute-start.2 = (bf16[2,384,256]{2,1,0:T(8,128)(2,1)S(1)}, bf16[2,384,256]{2,1,0:T(8,128)(2,1)S(1)}, u32[]{:S(2)}, u32[]{:S(2)}) collective-permute-start(bf16[2,384,256]{2,1,0:T(8,128)(2,1)S(1)} %fusion.2), channel_id=1, source_target_pairs={{0,64},{16,80},{32,96},{48,112},{64,0},{80,16},{96,32},{112,48},{1... | collective-permute-start | bytes 1179656 | tf_op jit(solution)/shard_map/ppermute | solution.py:10
  83.8 32.0 %copy-start.15 = (bf16[384,512]{1,0:T(8,128)(2,1)S(1)}, bf16[384,512]{1,0:T(8,128)(2,1)}, u32[]{:S(2)}) copy-start(bf16[384,512]{1,0:T(8,128)(2,1)} %param.7) | copy-start | bytes 1179652
  83.8 21.7 %collective-permute-start.3 = (bf16[2,384,256]{2,1,0:T(8,128)(2,1)S(1)}, bf16[2,384,256]{2,1,0:T(8,128)(2,1)S(1)}, u32[]{:S(2)}, u32[]{:S(2)}) collective-permute-start(bf16[2,384,256]{2,1,0:T(8,128)(2,1)S(1)} %fusion.3), channel_id=1, source_target_pairs={{0,128},{16,144},{32,160},{48,176},{64,192},{80,208},{96,224},{112... | collective-permute-start | bytes 1179656 | tf_op jit(solution)/shard_map/ppermute | solution.py:10
  106.2 23.7 %collective-permute-start.4 = (bf16[2,384,256]{2,1,0:T(8,128)(2,1)S(1)}, bf16[2,384,256]{2,1,0:T(8,128)(2,1)}, u32[]{:S(2)}, u32[]{:S(2)}) collective-permute-start(bf16[2,384,256]{2,1,0:T(8,128)(2,1)S(1)} %fusion.4), channel_id=1, source_target_pairs={{0,256},{16,272},{32,288},{48,304},{64,320},{80,336},{96,352},{112... | collective-permute-start | bytes 1179656 | tf_op jit(solution)/shard_map/ppermute | solution.py:10
  131.3 2.9 %copy-start.14 = (bf16[2,2,256,256]{3,2,0,1:T(8,128)(2,1)S(1)}, bf16[2,2,256,256]{3,2,0,1:T(8,128)(2,1)}, u32[]{:S(2)}) copy-start(bf16[2,2,256,256]{3,2,0,1:T(8,128)(2,1)} %get-tuple-element.10) | copy-start | bytes 1572868
  131.3 3.2 %copy-start.17 = (pred[2]{0:T(512)(128)(4,1)S(1)}, pred[2]{0:T(512)(128)(4,1)}, u32[]{:S(2)}) copy-start(pred[2]{0:T(512)(128)(4,1)} %get-tuple-element.27) | copy-start | bytes 10
  134.6 25.1 %copy-start.9 = (bf16[2,2,256,256]{3,2,0,1:T(8,128)(2,1)S(1)}, bf16[2,2,256,256]{3,2,0,1:T(8,128)(2,1)}, u32[]{:S(2)}) copy-start(bf16[2,2,256,256]{3,2,0,1:T(8,128)(2,1)} %copy-done.8) | copy-start | bytes 1572868
  134.9 24.6 %collective-permute-start.5 = (bf16[2,384,256]{2,1,0:T(8,128)(2,1)S(1)}, bf16[2,384,256]{2,1,0:T(8,128)(2,1)S(1)}, u32[]{:S(2)}, u32[]{:S(2)}) collective-permute-start(bf16[2,384,256]{2,1,0:T(8,128)(2,1)S(1)} %get-tuple-element.33), channel_id=1, source_target_pairs={{0,256},{16,272},{32,288},{48,304},{64,320},{80,336},{96,352},{112... | collective-permute-start | bytes 1179656 | tf_op jit(solution)/shard_map/ppermute | solution.py:10
  160.3 20.6 %collective-permute-start.6 = (bf16[2,384,256]{2,1,0:T(8,128)(2,1)S(1)}, bf16[2,384,256]{2,1,0:T(8,128)(2,1)S(1)}, u32[]{:S(2)}, u32[]{:S(2)}) collective-permute-start(bf16[2,384,256]{2,1,0:T(8,128)(2,1)S(1)} %get-tuple-element.35), channel_id=1, source_target_pairs={{0,128},{16,144},{32,160},{48,176},{64,192},{80,208},{96,224},{112... | collective-permute-start | bytes 1179656 | tf_op jit(solution)/shard_map/ppermute | solution.py:10
  165.1 16.1 %copy-start.7 = (bf16[2,2,256,256]{3,2,0,1:T(8,128)(2,1)S(1)}, bf16[2,2,256,256]{3,2,0,1:T(8,128)(2,1)}, u32[]{:S(2)}) copy-start(bf16[2,2,256,256]{3,2,0,1:T(8,128)(2,1)} %copy-done.6) | copy-start | bytes 1572868
  181.8 10.4 %collective-permute-start.7 = (bf16[2,384,256]{2,1,0:T(8,128)(2,1)S(1)}, bf16[2,384,256]{2,1,0:T(8,128)(2,1)S(1)}, u32[]{:S(2)}, u32[]{:S(2)}) collective-permute-start(bf16[2,384,256]{2,1,0:T(8,128)(2,1)S(1)} %get-tuple-element.37), channel_id=1, source_target_pairs={{0,64},{16,80},{32,96},{48,112},{64,0},{80,16},{96,32},{112,48},{1... | collective-permute-start | bytes 1179656 | tf_op jit(solution)/shard_map/ppermute | solution.py:10
  184.6 7.8 %copy-start.5 = (bf16[2,2,256,256]{3,2,0,1:T(8,128)(2,1)S(1)}, bf16[2,2,256,256]{3,2,0,1:T(8,128)(2,1)}, u32[]{:S(2)}) copy-start(bf16[2,2,256,256]{3,2,0,1:T(8,128)(2,1)} %copy-done.4) | copy-start | bytes 1572868
  193.7 11.2 %collective-permute-start.8 = (bf16[2,384,256]{2,1,0:T(8,128)(2,1)}, bf16[2,384,256]{2,1,0:T(8,128)(2,1)S(1)}, u32[]{:S(2)}, u32[]{:S(2)}) collective-permute-start(bf16[2,384,256]{2,1,0:T(8,128)(2,1)} %get-tuple-element.39), channel_id=1, source_target_pairs={{0,32},{16,48},{32,0},{48,16},{64,96},{80,112},{96,64},{112,80},{1... | collective-permute-start | bytes 1179656 | tf_op jit(solution)/shard_map/ppermute | solution.py:10
  200.0 5.2 %copy-start.3 = (bf16[1,2,2,256,256]{4,3,1,2,0:T(8,128)(2,1)S(1)}, bf16[1,2,2,256,256]{4,3,1,2,0:T(8,128)(2,1)}, u32[]{:S(2)}) copy-start(bf16[1,2,2,256,256]{4,3,1,2,0:T(8,128)(2,1)} %copy-done.2) | copy-start | bytes 1572868
  205.7 14.1 %collective-permute-start.9 = (bf16[2,384,256]{2,1,0:T(8,128)(2,1)S(1)}, bf16[2,384,256]{2,1,0:T(8,128)(2,1)S(1)}, u32[]{:S(2)}, u32[]{:S(2)}) collective-permute-start(bf16[2,384,256]{2,1,0:T(8,128)(2,1)S(1)} %get-tuple-element.41), channel_id=1, source_target_pairs={{0,16},{16,0},{32,48},{48,32},{64,80},{80,64},{96,112},{112,96},{1... | collective-permute-start | bytes 1179656 | tf_op jit(solution)/shard_map/ppermute | solution.py:10
  212.9 7.1 %copy-start.11 = (bf16[2,384,256]{1,2,0:T(8,128)(2,1)S(1)}, bf16[2,384,256]{1,2,0:T(8,128)(2,1)}, u32[]{:S(2)}) copy-start(bf16[2,384,256]{1,2,0:T(8,128)(2,1)} %copy-done.10) | copy-start | bytes 1179652
  213.0 7.4 %copy-start.13 = (bf16[2,384,256]{1,2,0:T(8,128)(2,1)S(1)}, bf16[2,384,256]{1,2,0:T(8,128)(2,1)}, u32[]{:S(2)}) copy-start(bf16[2,384,256]{1,2,0:T(8,128)(2,1)} %copy-done.12) | copy-start | bytes 1179652
  220.7 10.8 %copy-start.16 = (bf16[2,384,256]{1,2,0:T(8,128)(2,1)S(1)}, bf16[2,384,256]{1,2,0:T(8,128)(2,1)}, u32[]{:S(2)}) copy-start(bf16[2,384,256]{1,2,0:T(8,128)(2,1)} %get-tuple-element.14) | copy-start | bytes 1179652
  221.8 10.7 %copy-start.1 = (bf16[1,2,2,256,256]{4,3,1,2,0:T(8,128)(2,1)S(1)}, bf16[1,2,2,256,256]{4,3,1,2,0:T(8,128)(2,1)}, u32[]{:S(2)}) copy-start(bf16[1,2,2,256,256]{4,3,1,2,0:T(8,128)(2,1)} %copy-done) | copy-start | bytes 1572868
  221.8 39.7 %all-to-all-start = ((bf16[16,2,2,2,16,256]{5,4,2,3,1,0:T(8,128)(2,1)}), bf16[16,2,2,2,16,256]{5,4,2,3,1,0:T(8,128)(2,1)S(1)}, u32[]{:S(2)}, u32[]{:S(2)}) async-start(bf16[16,2,2,2,16,256]{5,4,2,3,1,0:T(8,128)(2,1)} %copy_bitcast_fusion), calls=%async_computation | async-start | bytes 2097152 | tf_op jit(solution)/shard_map/all_to_all | solution.py:31
  231.4 1.4 copy-start.19
Sparse Core Ops, SparseCore 0:
  10.7 48.1 all-gather.3
  200.1 69.8 reduce-scatter.1

commit v2 on v1

v2 whole, which is shorter than its diff:
```python
import jax
import jax.numpy as jnp
import numpy as np
from jax import lax
from jax.sharding import PartitionSpec as P


TRADED = {4: 3, 5: 4}
GATHERS = ((1, 2, 3), (4, 5))
SCATTERS = ((4, 5), (2, 3), (0, 1))


def flip(value, bit):
    mask = 1 << bit
    pairs = [(source, source ^ mask) for source in range(lax.axis_size("blk"))]
    return lax.ppermute(value, "blk", pairs)


def mine(bit):
    return (lax.axis_index("blk") >> bit) & 1


def trade(value, bit, axis=0):
    one = mine(bit) == 1
    low = lax.index_in_dim(value, 0, axis, keepdims=False)
    high = lax.index_in_dim(value, 1, axis, keepdims=False)
    keep = jnp.where(one, high, low)
    came = flip(jnp.where(one, low, high), bit)
    return jnp.stack([jnp.where(one, came, keep), jnp.where(one, keep, came)], axis)


def partner(value, section):
    if section == 0 or section in TRADED:
        return value[::-1]
    return flip(value, section - 1)


def owned_tables(sections):
    weight = np.zeros((5, sections, 1), np.int32)
    local = np.zeros((sections, 2), np.int32)
    place = {b + 1: b for b in range(5)}
    here = 0
    for section in range(sections):
        if section in TRADED:
            bit = TRADED[section]
            place[here] = bit
            del place[bit + 1]
            here = bit + 1
        for number, bit in place.items():
            weight[bit, section, 0] = 1 << number
        local[section] = np.arange(2) << here
    return weight, local


def swapped_blocks(matchings):
    sections, blocks = matchings.shape
    weight, local = owned_tables(sections)
    owned = sum((mine(bit) * weight[bit] for bit in range(5)), jnp.asarray(local))
    every = jnp.arange(blocks, dtype=jnp.int32)
    hit = (every == owned[:, :, None]) & (matchings != every)[:, None, :]
    return jnp.any(hit, axis=2)[:, :, None, None]


def scatter_sum(terms):
    count, per_dev, both, depth, width = terms.shape
    size = lax.axis_size("tok")
    core = lax.axis_index("tok") & 1
    parts = terms.reshape(count, per_dev, both, size // 2, 2, depth // size, width)
    parts = jnp.moveaxis(parts, (3, 4), (0, 1))
    even, odd = parts[:, 0], parts[:, 1]
    pairs = [(source, source ^ 1) for source in range(size)]
    came = lax.ppermute(jnp.where(core == 1, even, odd), "tok", pairs)
    kept = jnp.where(core == 1, odd, even)
    chip = (kept.astype(jnp.float32) + came.astype(jnp.float32)).astype(jnp.bfloat16)
    groups = [list(range(c, size, 2)) for c in range(2)]
    chip = lax.all_to_all(chip, "tok", 0, 0, axis_index_groups=groups)
    return jnp.sum(chip.astype(jnp.float32), axis=0)


def body(activations, weights, matchings, cotangent):
    rows = activations.shape[0]
    sections, per_dev, _, _, width = weights.shape

    flips = swapped_blocks(matchings)

    def split(array):
        return jnp.stack([array[:, j * width : (j + 1) * width] for j in range(per_dev)])

    def join(blocks):
        return jnp.concatenate([blocks[j] for j in range(per_dev)], axis=1)

    shards = {s: weights[s] for s in range(4)}
    moved = trade(weights[4:6], TRADED[4], axis=1)
    shards[4] = moved[0]
    shards[5] = trade(moved[1], TRADED[5])
    full = [None] * sections
    full[0] = lax.all_gather(shards[0], "tok", axis=2, tiled=True)
    for group in GATHERS:
        gathered = lax.all_gather(jnp.stack([shards[s] for s in group]), "tok", axis=3, tiled=True)
        for place, s in enumerate(group):
            full[s] = gathered[place]

    value = split(activations)
    saved = []
    for section in range(sections):
        if section in TRADED:
            value = trade(value, TRADED[section])
        flipped = flips[section]
        other = partner(value, section)
        first_in = jnp.where(flipped, other, value)
        second_in = jnp.where(flipped, value, other)
        saved.append((first_in, second_in, flipped))
        both = full[section]
        mixed = jnp.einsum("jtk,jkl->jtl", first_in, both[:, 0], preferred_element_type=jnp.float32)
        mixed = mixed + jnp.einsum(
            "jtk,jkl->jtl", second_in, both[:, 1], preferred_element_type=jnp.float32
        )
        if section < sections - 1:
            value = mixed.astype(jnp.bfloat16)
        if section == 0:
            cotan = split(lax.optimization_barrier((cotangent, value))[0])
            for at in sorted(TRADED):
                cotan = trade(cotan, TRADED[at])
    result = jax.nn.gelu(mixed).astype(jnp.bfloat16)
    back_fn = jax.vjp(jax.nn.gelu, mixed)[1]
    grad = back_fn(cotan.astype(jnp.float32))[0].astype(jnp.bfloat16)
    terms = [None] * sections
    totals = [None] * sections
    for section in reversed(range(sections)):
        first_in, second_in, flipped = saved[section]
        both = full[section]
        if section == 0:
            grad = lax.optimization_barrier((grad, totals[2]))[0]
        grad_first = jnp.einsum("jtl,jkl->jtk", grad, both[:, 0], preferred_element_type=jnp.float32)
        grad_second = jnp.einsum("jtl,jkl->jtk", grad, both[:, 1], preferred_element_type=jnp.float32)
        kept = jnp.where(flipped, grad_second, grad_first)
        sent = jnp.where(flipped, grad_first, grad_second).astype(jnp.bfloat16)
        term = jnp.stack(
            [
                jnp.einsum("jtk,jtl->jkl", part, grad, preferred_element_type=jnp.float32)
                for part in (first_in, second_in)
            ],
            axis=1,
        ).astype(jnp.bfloat16)
        terms[section] = term
        for group in SCATTERS:
            if section == min(group):
                summed = scatter_sum(jnp.stack([terms[s] for s in group]))
                for place, s in enumerate(group):
                    totals[s] = summed[place]
        if section == 2:
            sent = lax.optimization_barrier((sent, totals[4]))[0]
        grad = (kept + partner(sent, section).astype(jnp.float32)).astype(jnp.bfloat16)
        if section in TRADED:
            grad = trade(grad, TRADED[section])
    for at in sorted(TRADED, reverse=True):
        result = trade(result, TRADED[at])
    totals[5] = trade(totals[5], TRADED[5])
    moved = trade(jnp.stack(totals[4:6]), TRADED[4], axis=1)
    weight_grad = jnp.concatenate([jnp.stack(totals[:4]), moved])
    return join(result), join(grad), weight_grad


def solution(mesh):
    placed = (P("tok", "blk"), P(None, "blk", None, "tok", None), P(), P("tok", "blk"))
    return jax.shard_map(
        body,
        mesh=mesh,
        in_specs=placed,
        out_specs=(P("tok", "blk"), P("tok", "blk"), P(None, "blk", None, "tok", None)),
        check_vma=False,
    )
```

time: 283 us -> 282 us (level); the launches traced: 279 us -> 280 us
  starting transfers between devices: 52.2 us -> 106 us
  waiting for transfers between devices: 132 us -> 87.4 us
  blocking collectives: 41.3 us -> 19.8 us
  other arithmetic: 5.34 us -> 19.9 us
  local copies, waits for them, and re-layouts: 14.2 us -> 10.6 us
    ppermute x10 -> x21, starting transfers between devices: 42.6 us -> 90 us  [the longest x18 77.9 us: flip(): return lax.ppermute(value, 'blk', pairs)]
    ppermute x10 -> x21, waiting for transfers between devices: 96.5 us -> 51.4 us  [the longest x18 51.4 us: flip(): return lax.ppermute(value, 'blk', pairs)]
    all_gather x2 -> x1, blocking collectives: 41.3 us -> 19.8 us  [body(): full[0] = lax.all_gather(shards[0], 'tok', axis=2, tiled=True)]
    all_gather x1 -> x2, waiting for transfers between devices: 0.02 us -> 15.6 us  [body(): lax.all_gather(jnp.stack([shards[s] for s in group]), 'tok', axis=3, tile...]
    reduce_scatter x1 -> x0, waiting for transfers between devices: 8.35 us -> none  [body(): lax.psum_scatter(jnp.stack(terms[EARLY:]), 'tok', scatter_dimension=3, ti...]
    all_to_all x1 -> x3, waiting for transfers between devices: 27.1 us -> 20.4 us  [scatter_sum(): chip = lax.all_to_all(chip, 'tok', 0, 0, axis_index_groups=groups)]
    select_n x0 -> x17, other arithmetic: none -> 6.22 us  [the longest x12 4.4 us: trade(): came = flip(jnp.where(one, low, high), bit)]
    all_to_all x1 -> x3, starting transfers between devices: 9.61 us -> 15.7 us  [scatter_sum(): chip = lax.all_to_all(chip, 'tok', 0, 0, axis_index_groups=groups)]
  transfers between devices with their start and end apart: 13 -> 26, of which waited for: 11 -> 12; matrix products, arithmetic and copies ran while one was open for 9% -> 16% of each run, Pallas kernels for 0% -> 0%
where the time goes in v2:
time: 282 us; the launch traced here: 280 us
  starting transfers between devices  106 us (38%)
  waiting for transfers between devices  87.4 us (31%)
  matrix products  21.5 us (8%)
  other arithmetic  19.9 us (7%)
  blocking collectives  19.8 us (7%)
  between operations  15.2 us (5%)
  local copies, waits for them, and re-layouts  10.6 us (4%)
    ppermute x18, starting transfers between devices, flip(): return lax.ppermute(value, 'blk', pairs)  77.9 us
    ppermute x18, waiting for transfers between devices, flip(): return lax.ppermute(value, 'blk', pairs)  51.4 us
    all_to_all x3, waiting for transfers between devices, scatter_sum(): chip = lax.all_to_all(chip, 'tok', 0, 0, axis_index_groups=groups)  20.4 us
    all_gather x1, blocking collectives, body(): full[0] = lax.all_gather(shards[0], 'tok', axis=2, tiled=True)  19.8 us
    all_to_all x3, starting transfers between devices, scatter_sum(): chip = lax.all_to_all(chip, 'tok', 0, 0, axis_index_groups=groups)  15.7 us
    all_gather x2, waiting for transfers between devices, body(): lax.all_gather(jnp.stack([shards[s] for s in group]), 'tok', axis=3, tile...  15.6 us
    ppermute x3, starting transfers between devices, scatter_sum(): came = lax.ppermute(jnp.where(core == 1, even, odd), 'tok', pairs)  12.2 us
    dot_general x12, matrix products, body(): jnp.einsum('jtk,jtl->jkl', part, grad, preferred_element_type=jnp.float32)  7.97 us
  transfers between devices with their start and end apart: 26, of which 12 were waited for; matrix products, arithmetic and copies ran while one was open for 16% of the time, Pallas kernels for 0%

profile of v2, /device:TPU:1, one launch (start us, length us, event | category | flops | bytes accessed | tf_op | source)
XLA Modules:
  0.0 280.4 jit_solution(15084069306590261357)
XLA Ops:
  8.1 6.6 %collective-permute-start.4 = (bf16[2,2,16,256]{3,2,1,0:T(8,128)(2,1)S(1)}, bf16[2,2,16,256]{3,2,1,0:T(8,128)(2,1)S(1)}, u32[]{:S(2)}, u32[]{:S(2)}) collective-permute-start(bf16[2,2,16,256]{3,2,1,0:T(8,128)(2,1)S(1)} %fusion.47), channel_id=1, source_target_pairs={{0,128},{16,144},{32,160},{48,176},{64,192},{80,208},{96,224},{112... | collective-permute-start | bytes 98312 | tf_op jit(solution)/shard_map/ppermute | solution.py:16
  19.6 19.8 %all-gather = bf16[1,2,2,256,256]{4,3,1,2,0:T(8,128)(2,1)S(1)} all-gather(bf16[1,2,2,16,256]{4,3,1,2,0:T(8,128)(2,1)S(1)} %copy.174), channel_id=2, replica_groups=mesh['blk'=32,'tok'=16] {'tok'}, dimensions={3}, use_global_device_ids=true | all-gather | bytes 557056 | tf_op jit(solution)/shard_map/all_gather | solution.py:97
  40.9 9.0 %collective-permute-start.5 = (bf16[2,16,256]{2,1,0:T(8,128)(2,1)S(1)}, bf16[2,16,256]{2,1,0:T(8,128)(2,1)S(1)}, u32[]{:S(2)}, u32[]{:S(2)}) collective-permute-start(bf16[2,16,256]{2,1,0:T(8,128)(2,1)S(1)} %select_bitcast_fusion.12), channel_id=1, source_target_pairs={{0,256},{16,272},{32,288},{48,304},{64,320},{80,336},{96,352},{112... | collective-permute-start | bytes 49160 | tf_op jit(solution)/shard_map/ppermute | solution.py:16
  50.2 3.4 %collective-permute-start = (bf16[2,384,256]{2,1,0:T(8,128)(2,1)S(1)}, bf16[2,384,256]{2,1,0:T(8,128)(2,1)S(1)}, u32[]{:S(2)}, u32[]{:S(2)}) collective-permute-start(bf16[2,384,256]{2,1,0:T(8,128)(2,1)S(1)} %fusion), channel_id=1, source_target_pairs={{0,16},{16,0},{32,48},{48,32},{64,80},{80,64},{96,112},{112,96},{1... | collective-permute-start | bytes 1179656 | tf_op jit(solution)/shard_map/ppermute | solution.py:16
  54.2 7.1 %all-gather.4.cloned.1.call-done = bf16[3,2,2,256,256]{4,3,1,2,0:T(8,128)(2,1)} async-done(((bf16[3,2,2,16,256]{4,3,1,2,0:T(8,128)(2,1)}), bf16[3,2,2,256,256]{4,3,1,2,0:T(8,128)(2,1)}) %all-gather.4.cloned.1.call-update) | async-done | bytes 1572880 | tf_op jit(solution)/shard_map/all_gather | solution.py:99
  61.3 2.3 slice_bitcast_fusion.4
  65.0 4.6 %collective-permute-start.1 = (bf16[2,384,256]{2,1,0:T(8,128)(2,1)S(1)}, bf16[2,384,256]{2,1,0:T(8,128)(2,1)S(1)}, u32[]{:S(2)}, u32[]{:S(2)}) collective-permute-start(bf16[2,384,256]{2,1,0:T(8,128)(2,1)S(1)} %fusion.1), channel_id=1, source_target_pairs={{0,32},{16,48},{32,0},{48,16},{64,96},{80,112},{96,64},{112,80},{1... | collective-permute-start | bytes 1179656 | tf_op jit(solution)/shard_map/ppermute | solution.py:16
  71.0 4.3 %collective-permute-start.9 = (bf16[384,256]{1,0:T(8,128)(2,1)}, bf16[384,256]{1,0:T(8,128)(2,1)}, u32[]{:S(2)}, u32[]{:S(2)}) collective-permute-start(bf16[384,256]{1,0:T(8,128)(2,1)} %broadcast_select_fusion.16), channel_id=1, source_target_pairs={{0,128},{16,144},{32,160},{48,176},{64,192},{80,208},{96,224},{112... | collective-permute-start | bytes 589832 | tf_op jit(solution)/shard_map/ppermute | solution.py:16
  75.4 3.5 %collective-permute-done.1 = bf16[2,384,256]{2,1,0:T(8,128)(2,1)S(1)} collective-permute-done((bf16[2,384,256]{2,1,0:T(8,128)(2,1)S(1)}, bf16[2,384,256]{2,1,0:T(8,128)(2,1)S(1)}, u32[]{:S(2)}, u32[]{:S(2)}) %collective-permute-start.1) | collective-permute-done | bytes 393248 | tf_op jit(solution)/shard_map/ppermute | solution.py:16
  80.9 3.5 %collective-permute-start.2 = (bf16[2,384,256]{2,1,0:T(8,128)(2,1)S(1)}, bf16[2,384,256]{2,1,0:T(8,128)(2,1)}, u32[]{:S(2)}, u32[]{:S(2)}) collective-permute-start(bf16[2,384,256]{2,1,0:T(8,128)(2,1)S(1)} %fusion.2), channel_id=1, source_target_pairs={{0,64},{16,80},{32,96},{48,112},{64,0},{80,16},{96,32},{112,48},{1... | collective-permute-start | bytes 1179656 | tf_op jit(solution)/shard_map/ppermute | solution.py:16
  84.4 2.0 broadcast_select_fusion.12
  86.4 8.3 %collective-permute-start.10 = (bf16[384,256]{1,0:T(8,128)(2,1)}, bf16[384,256]{1,0:T(8,128)(2,1)}, u32[]{:S(2)}, u32[]{:S(2)}) collective-permute-start(bf16[384,256]{1,0:T(8,128)(2,1)} %get-tuple-element.20), channel_id=1, source_target_pairs={{0,256},{16,272},{32,288},{48,304},{64,320},{80,336},{96,352},{112... | collective-permute-start | bytes 589832 | tf_op jit(solution)/shard_map/ppermute | solution.py:16
  94.7 1.4 fusion.29
  96.1 1.3 fusion.3
  98.3 2.3 collective-permute-start.3
  100.6 8.5 %all-gather.6.cloned.1.call-done = bf16[2,2,2,256,256]{4,3,1,2,0:T(8,128)(2,1)} async-done(((bf16[2,2,2,16,256]{4,3,1,2,0:T(8,128)(2,1)}), bf16[2,2,2,256,256]{4,3,1,2,0:T(8,128)(2,1)}) %all-gather.6.cloned.1.call-update) | async-done | bytes 1048592 | tf_op jit(solution)/shard_map/all_gather | solution.py:99
  109.1 1.3 slice_bitcast_fusion
  110.3 3.8 %collective-permute-done.3 = bf16[384,256]{1,0:T(8,128)(2,1)S(1)} collective-permute-done((bf16[384,256]{1,0:T(8,128)(2,1)}, bf16[384,256]{1,0:T(8,128)(2,1)S(1)}, u32[]{:S(2)}, u32[]{:S(2)}) %collective-permute-start.3) | collective-permute-done | bytes 196640 | tf_op jit(solution)/shard_map/ppermute | solution.py:16
  115.1 3.9 %collective-permute-start.6 = (bf16[384,256]{1,0:T(8,128)(2,1)S(1)}, bf16[384,256]{1,0:T(8,128)(2,1)S(1)}, u32[]{:S(2)}, u32[]{:S(2)}) collective-permute-start(bf16[384,256]{1,0:T(8,128)(2,1)S(1)} %select_bitcast_fusion.8), channel_id=1, source_target_pairs={{0,256},{16,272},{32,288},{48,304},{64,320},{80,336},{96,352},{112... | collective-permute-start | bytes 589832 | tf_op jit(solution)/shard_map/ppermute | solution.py:16
  120.0 11.5 %collective-permute-done.6 = bf16[384,256]{1,0:T(8,128)(2,1)S(1)} collective-permute-done((bf16[384,256]{1,0:T(8,128)(2,1)S(1)}, bf16[384,256]{1,0:T(8,128)(2,1)S(1)}, u32[]{:S(2)}, u32[]{:S(2)}) %collective-permute-start.6) | collective-permute-done | bytes 196640 | tf_op jit(solution)/shard_map/ppermute | solution.py:16
  133.6 3.9 %collective-permute-start.7 = (bf16[384,256]{1,0:T(8,128)(2,1)S(1)}, bf16[384,256]{1,0:T(8,128)(2,1)S(1)}, u32[]{:S(2)}, u32[]{:S(2)}) collective-permute-start(bf16[384,256]{1,0:T(8,128)(2,1)S(1)} %select_bitcast_fusion.7), channel_id=1, source_target_pairs={{0,256},{16,272},{32,288},{48,304},{64,320},{80,336},{96,352},{112... | collective-permute-start | bytes 589832 | tf_op jit(solution)/shard_map/ppermute | solution.py:16
  138.0 5.3 %collective-permute-start.11 = (bf16[384,256]{1,0:T(8,128)(2,1)S(1)}, bf16[384,256]{1,0:T(8,128)(2,1)S(1)}, u32[]{:S(2)}, u32[]{:S(2)}) collective-permute-start(bf16[384,256]{1,0:T(8,128)(2,1)S(1)} %select_bitcast_fusion.4), channel_id=1, source_target_pairs={{0,256},{16,272},{32,288},{48,304},{64,320},{80,336},{96,352},{112... | collective-permute-start | bytes 589832 | tf_op jit(solution)/shard_map/ppermute | solution.py:16
  143.7 10.4 %collective-permute-done.11 = bf16[384,256]{1,0:T(8,128)(2,1)S(1)} collective-permute-done((bf16[384,256]{1,0:T(8,128)(2,1)S(1)}, bf16[384,256]{1,0:T(8,128)(2,1)S(1)}, u32[]{:S(2)}, u32[]{:S(2)}) %collective-permute-start.11) | collective-permute-done | bytes 196640 | tf_op jit(solution)/shard_map/ppermute | solution.py:16
  155.2 1.9 collective-permute-start.8
  157.7 4.3 %collective-permute-start.12 = (bf16[384,256]{1,0:T(8,128)(2,1)S(1)}, bf16[384,256]{1,0:T(8,128)(2,1)S(1)}, u32[]{:S(2)}, u32[]{:S(2)}) collective-permute-start(bf16[384,256]{1,0:T(8,128)(2,1)S(1)} %select_bitcast_fusion.3), channel_id=1, source_target_pairs={{0,128},{16,144},{32,160},{48,176},{64,192},{80,208},{96,224},{112... | collective-permute-start | bytes 589832 | tf_op jit(solution)/shard_map/ppermute | solution.py:16
  162.2 3.7 %collective-permute-start.18 = (bf16[8,2,2,2,16,256]{5,4,2,3,1,0:T(8,128)(2,1)S(1)}, bf16[8,2,2,2,16,256]{5,4,2,3,1,0:T(8,128)(2,1)S(1)}, u32[]{:S(2)}, u32[]{:S(2)}) collective-permute-start(bf16[8,2,2,2,16,256]{5,4,2,3,1,0:T(8,128)(2,1)S(1)} %select_bitcast_fusion), channel_id=1, source_target_pairs={{0,1},{1,0},{2,3},{3,2},{4,5},{5,4},{6,7},{7,6},{8,9},{9,8},{10,11... | collective-permute-start | bytes 1572872 | tf_op jit(solution)/shard_map/ppermute | solution.py:72
  165.9 10.2 %collective-permute-done.12 = bf16[384,256]{1,0:T(8,128)(2,1)S(1)} collective-permute-done((bf16[384,256]{1,0:T(8,128)(2,1)S(1)}, bf16[384,256]{1,0:T(8,128)(2,1)S(1)}, u32[]{:S(2)}, u32[]{:S(2)}) %collective-permute-start.12) | collective-permute-done | bytes 196640 | tf_op jit(solution)/shard_map/ppermute | solution.py:16
  176.4 1.3 select_convert_fusion.3
  177.7 1.9 collective-permute-start.13
  179.7 2.1 convolution_convert_fusion.5
  181.8 2.2 convolution_convert_fusion.4
  185.9 5.9 %all-to-all-start.2 = ((bf16[8,2,2,2,16,256]{5,4,2,3,1,0:T(8,128)(2,1)}), bf16[8,2,2,2,16,256]{5,4,2,3,1,0:T(8,128)(2,1)}, u32[]{:S(2)}, u32[]{:S(2)}) async-start(bf16[8,2,2,2,16,256]{5,4,2,3,1,0:T(8,128)(2,1)} %fusion.5), calls=%async_computation.2 | async-start | bytes 1048576 | tf_op jit(solution)/shard_map/all_to_all | solution.py:76
  191.8 1.5 add_convert_fusion.3
  193.9 3.1 %collective-permute-start.14 = (bf16[2,384,256]{2,1,0:T(8,128)(2,1)S(1)}, bf16[2,384,256]{2,1,0:T(8,128)(2,1)S(1)}, u32[]{:S(2)}, u32[]{:S(2)}) collective-permute-start(bf16[2,384,256]{2,1,0:T(8,128)(2,1)S(1)} %get-tuple-element.69), channel_id=1, source_target_pairs={{0,32},{16,48},{32,0},{48,16},{64,96},{80,112},{96,64},{112,80},{1... | collective-permute-start | bytes 1179656 | tf_op jit(solution)/shard_map/ppermute | solution.py:16
  198.2 3.6 %collective-permute-start.17 = (bf16[8,2,2,2,16,256]{5,4,2,3,1,0:T(8,128)(2,1)S(1)}, bf16[8,2,2,2,16,256]{5,4,2,3,1,0:T(8,128)(2,1)S(1)}, u32[]{:S(2)}, u32[]{:S(2)}) collective-permute-start(bf16[8,2,2,2,16,256]{5,4,2,3,1,0:T(8,128)(2,1)S(1)} %select_bitcast_fusion.1), channel_id=1, source_target_pairs={{0,1},{1,0},{2,3},{3,2},{4,5},{5,4},{6,7},{7,6},{8,9},{9,8},{10,11... | collective-permute-start | bytes 1572872 | tf_op jit(solution)/shard_map/ppermute | solution.py:72
  201.8 5.2 %collective-permute-done.14 = bf16[2,384,256]{2,1,0:T(8,128)(2,1)S(1)} collective-permute-done((bf16[2,384,256]{2,1,0:T(8,128)(2,1)S(1)}, bf16[2,384,256]{2,1,0:T(8,128)(2,1)S(1)}, u32[]{:S(2)}, u32[]{:S(2)}) %collective-permute-start.14) | collective-permute-done | bytes 393248 | tf_op jit(solution)/shard_map/ppermute | solution.py:16
  207.9 2.7 collective-permute-start.15
  212.6 5.8 %collective-permute-done.15 = bf16[2,384,256]{2,1,0:T(8,128)(2,1)S(1)} collective-permute-done((bf16[2,384,256]{2,1,0:T(8,128)(2,1)S(1)}, bf16[2,384,256]{2,1,0:T(8,128)(2,1)S(1)}, u32[]{:S(2)}, u32[]{:S(2)}) %collective-permute-start.15) | collective-permute-done | bytes 393248 | tf_op jit(solution)/shard_map/ppermute | solution.py:16
  220.7 4.9 %collective-permute-start.16 = (bf16[8,2,2,2,16,256]{5,4,2,3,1,0:T(8,128)(2,1)}, bf16[8,2,2,2,16,256]{5,4,2,3,1,0:T(8,128)(2,1)}, u32[]{:S(2)}, u32[]{:S(2)}) collective-permute-start(bf16[8,2,2,2,16,256]{5,4,2,3,1,0:T(8,128)(2,1)} %select_bitcast_fusion.2), channel_id=1, source_target_pairs={{0,1},{1,0},{2,3},{3,2},{4,5},{5,4},{6,7},{7,6},{8,9},{9,8},{10,11... | collective-permute-start | bytes 1572872 | tf_op jit(solution)/shard_map/ppermute | solution.py:72
  227.0 6.4 %all-to-all-start.1 = ((bf16[8,2,2,2,16,256]{5,4,2,3,1,0:T(8,128)(2,1)}), bf16[8,2,2,2,16,256]{5,4,2,3,1,0:T(8,128)(2,1)S(1)}, u32[]{:S(2)}, u32[]{:S(2)}) async-start(bf16[8,2,2,2,16,256]{5,4,2,3,1,0:T(8,128)(2,1)} %fusion.6), calls=%async_computation.1 | async-start | bytes 1048576 | tf_op jit(solution)/shard_map/all_to_all | solution.py:76
  233.3 1.2 add_convert_fusion
  234.5 1.1 convert_reduce_fusion
  235.7 4.9 %collective-permute-start.19 = (f32[2,16,256]{2,1,0:T(8,128)S(1)}, f32[2,16,256]{2,1,0:T(8,128)S(1)}, u32[]{:S(2)}, u32[]{:S(2)}) collective-permute-start(f32[2,16,256]{2,1,0:T(8,128)S(1)} %select_bitcast_fusion.11), channel_id=1, source_target_pairs={{0,256},{16,272},{32,288},{48,304},{64,320},{80,336},{96,352},{112... | collective-permute-start | bytes 98312 | tf_op jit(solution)/shard_map/ppermute | solution.py:16
  240.6 2.1 fusion.7
  242.7 8.6 %all-to-all-done.1 = bf16[8,2,2,2,16,256]{5,4,2,3,1,0:T(8,128)(2,1)S(1)} async-done(((bf16[8,2,2,2,16,256]{5,4,2,3,1,0:T(8,128)(2,1)}), bf16[8,2,2,2,16,256]{5,4,2,3,1,0:T(8,128)(2,1)S(1)}, u32[]{:S(2)}, u32[]{:S(2)}) %all-to-all-start.1) | async-done | bytes 524320 | tf_op jit(solution)/shard_map/all_to_all | solution.py:76
  251.3 3.5 %all-to-all-start = ((bf16[8,2,2,2,16,256]{5,4,2,3,1,0:T(8,128)(2,1)}), bf16[8,2,2,2,16,256]{5,4,2,3,1,0:T(8,128)(2,1)S(1)}, u32[]{:S(2)}, u32[]{:S(2)}) async-start(bf16[8,2,2,2,16,256]{5,4,2,3,1,0:T(8,128)(2,1)} %fusion.7), calls=%async_computation | async-start | bytes 1048576 | tf_op jit(solution)/shard_map/all_to_all | solution.py:76
  254.9 3.9 %collective-permute-start.20 = (f32[2,2,16,256]{3,2,1,0:T(8,128)S(1)}, f32[2,2,16,256]{3,2,1,0:T(8,128)S(1)}, u32[]{:S(2)}, u32[]{:S(2)}) collective-permute-start(f32[2,2,16,256]{3,2,1,0:T(8,128)S(1)} %select_bitcast_fusion.10), channel_id=1, source_target_pairs={{0,128},{16,144},{32,160},{48,176},{64,192},{80,208},{96,224},{112... | collective-permute-start | bytes 196616 | tf_op jit(solution)/shard_map/ppermute | solution.py:16
  260.9 11.8 %all-to-all-done = bf16[8,2,2,2,16,256]{5,4,2,3,1,0:T(8,128)(2,1)S(1)} async-done(((bf16[8,2,2,2,16,256]{5,4,2,3,1,0:T(8,128)(2,1)}), bf16[8,2,2,2,16,256]{5,4,2,3,1,0:T(8,128)(2,1)S(1)}, u32[]{:S(2)}, u32[]{:S(2)}) %all-to-all-start) | async-done | bytes 524320 | tf_op jit(solution)/shard_map/all_to_all | solution.py:76
  (180 shorter events, 33.5 us)
Async XLA Ops:
  7.2 11.3 %copy-start.32 = (s32[6,1]{0,1:T(1,128)S(1)}, s32[6,1]{0,1:T(1,128)}, u32[]{:S(2)}) copy-start(s32[6,1]{0,1:T(1,128)} %constant.52.clone) | copy-start | bytes 76
  7.2 11.3 %copy-start.33 = (s32[6,1]{0,1:T(1,128)S(1)}, s32[6,1]{0,1:T(1,128)}, u32[]{:S(2)}) copy-start(s32[6,1]{0,1:T(1,128)} %constant.51.clone) | copy-start | bytes 76
  7.2 11.3 %copy-start.31 = (s32[6,2]{0,1:T(2,128)S(1)}, s32[6,2]{0,1:T(2,128)}, u32[]{:S(2)}) copy-start(s32[6,2]{0,1:T(2,128)} %constant.47.clone) | copy-start | bytes 148
  7.2 11.3 %copy-start.30 = (s32[6,64]{1,0:T(8,128)S(1)}, s32[6,64]{1,0:T(8,128)}, u32[]{:S(2)}) copy-start(s32[6,64]{1,0:T(8,128)} %param.12) | copy-start | bytes 4612
  7.2 54.1 %all-gather.4.cloned.1.call-start = ((), (), s32[]{:S(2)}) async-start(), calls=%async_computation.3 | async-start | bytes 1671168 | tf_op jit(solution)/shard_map/all_gather | solution.py:99
  8.1 32.0 %collective-permute-start.4 = (bf16[2,2,16,256]{3,2,1,0:T(8,128)(2,1)S(1)}, bf16[2,2,16,256]{3,2,1,0:T(8,128)(2,1)S(1)}, u32[]{:S(2)}, u32[]{:S(2)}) collective-permute-start(bf16[2,2,16,256]{3,2,1,0:T(8,128)(2,1)S(1)} %fusion.47), channel_id=1, source_target_pairs={{0,128},{16,144},{32,160},{48,176},{64,192},{80,208},{96,224},{112... | collective-permute-start | bytes 98312 | tf_op jit(solution)/shard_map/ppermute | solution.py:16
  16.3 92.8 %all-gather.6.cloned.1.call-start = ((), (), s32[]{:S(2)}) async-start(), calls=%async_computation.4 | async-start | bytes 1114112 | tf_op jit(solution)/shard_map/all_gather | solution.py:99
  19.6 20.4 %copy-start.26 = (pred[2]{0:T(512)(128)(4,1)}, pred[2]{0:T(512)(128)(4,1)S(1)}, u32[]{:S(2)}) copy-start(pred[2]{0:T(512)(128)(4,1)S(1)} %get-tuple-element.15) | copy-start | bytes 10
  19.6 44.0 %copy-start.22 = (pred[2]{0:T(512)(128)(4,1)}, pred[2]{0:T(512)(128)(4,1)S(1)}, u32[]{:S(2)}) copy-start(pred[2]{0:T(512)(128)(4,1)S(1)} %get-tuple-element.16) | copy-start | bytes 10
  39.7 10.2 %copy-start.10 = (bf16[2,384,256]{1,2,0:T(8,128)(2,1)}, bf16[2,384,256]{1,2,0:T(8,128)(2,1)S(1)}, u32[]{:S(2)}) copy-start(bf16[2,384,256]{1,2,0:T(8,128)(2,1)S(1)} %get-tuple-element.50) | copy-start | bytes 1179652
  39.7 10.2 %copy-start.6 = (bf16[2,384,256]{1,2,0:T(8,128)(2,1)}, bf16[2,384,256]{1,2,0:T(8,128)(2,1)S(1)}, u32[]{:S(2)}) copy-start(bf16[2,384,256]{1,2,0:T(8,128)(2,1)S(1)} %get-tuple-element.49) | copy-start | bytes 1179652
  40.8 13.4 %copy-start.15 = (bf16[2,2,16,256]{3,2,1,0:T(8,128)(2,1)}, bf16[2,2,16,256]{3,2,1,0:T(8,128)(2,1)S(1)}, u32[]{:S(2)}) copy-start(bf16[2,2,16,256]{3,2,1,0:T(8,128)(2,1)S(1)} %get-tuple-element.55) | copy-start | bytes 98308
  40.8 13.4 %copy-start.17 = (bf16[2,2,16,256]{3,2,1,0:T(8,128)(2,1)}, bf16[2,2,16,256]{3,2,1,0:T(8,128)(2,1)S(1)}, u32[]{:S(2)}) copy-start(bf16[2,2,16,256]{3,2,1,0:T(8,128)(2,1)S(1)} %get-tuple-element.56) | copy-start | bytes 98308
  40.9 12.7 %collective-permute-start.5 = (bf16[2,16,256]{2,1,0:T(8,128)(2,1)S(1)}, bf16[2,16,256]{2,1,0:T(8,128)(2,1)S(1)}, u32[]{:S(2)}, u32[]{:S(2)}) collective-permute-start(bf16[2,16,256]{2,1,0:T(8,128)(2,1)S(1)} %select_bitcast_fusion.12), channel_id=1, source_target_pairs={{0,256},{16,272},{32,288},{48,304},{64,320},{80,336},{96,352},{112... | collective-permute-start | bytes 49160 | tf_op jit(solution)/shard_map/ppermute | solution.py:16
  50.2 13.4 %collective-permute-start = (bf16[2,384,256]{2,1,0:T(8,128)(2,1)S(1)}, bf16[2,384,256]{2,1,0:T(8,128)(2,1)S(1)}, u32[]{:S(2)}, u32[]{:S(2)}) collective-permute-start(bf16[2,384,256]{2,1,0:T(8,128)(2,1)S(1)} %fusion), channel_id=1, source_target_pairs={{0,16},{16,0},{32,48},{48,32},{64,80},{80,64},{96,112},{112,96},{1... | collective-permute-start | bytes 1179656 | tf_op jit(solution)/shard_map/ppermute | solution.py:16
  63.6 16.3 %copy-start = (bf16[2,2,256,256]{3,2,0,1:T(8,128)(2,1)}, bf16[2,2,256,256]{3,2,0,1:T(8,128)(2,1)S(1)}, u32[]{:S(2)}) copy-start(bf16[2,2,256,256]{3,2,0,1:T(8,128)(2,1)S(1)} %get-tuple-element.28) | copy-start | bytes 1572868
  63.9 5.7 %copy-start.16 = (bf16[2,2,16,256]{3,2,1,0:T(8,128)(2,1)S(1)}, bf16[2,2,16,256]{3,2,1,0:T(8,128)(2,1)}, u32[]{:S(2)}) copy-start(bf16[2,2,16,256]{3,2,1,0:T(8,128)(2,1)} %copy-done.15) | copy-start | bytes 98308
  64.0 6.4 %copy-start.12 = (bf16[384,512]{1,0:T(8,128)(2,1)S(1)}, bf16[384,512]{1,0:T(8,128)(2,1)}, u32[]{:S(2)}) copy-start(bf16[384,512]{1,0:T(8,128)(2,1)} %param.13) | copy-start | bytes 1179652
  65.0 13.9 %collective-permute-start.1 = (bf16[2,384,256]{2,1,0:T(8,128)(2,1)S(1)}, bf16[2,384,256]{2,1,0:T(8,128)(2,1)S(1)}, u32[]{:S(2)}, u32[]{:S(2)}) collective-permute-start(bf16[2,384,256]{2,1,0:T(8,128)(2,1)S(1)} %fusion.1), channel_id=1, source_target_pairs={{0,32},{16,48},{32,0},{48,16},{64,96},{80,112},{96,64},{112,80},{1... | collective-permute-start | bytes 1179656 | tf_op jit(solution)/shard_map/ppermute | solution.py:16
  71.0 13.4 %collective-permute-start.9 = (bf16[384,256]{1,0:T(8,128)(2,1)}, bf16[384,256]{1,0:T(8,128)(2,1)}, u32[]{:S(2)}, u32[]{:S(2)}) collective-permute-start(bf16[384,256]{1,0:T(8,128)(2,1)} %broadcast_select_fusion.16), channel_id=1, source_target_pairs={{0,128},{16,144},{32,160},{48,176},{64,192},{80,208},{96,224},{112... | collective-permute-start | bytes 589832 | tf_op jit(solution)/shard_map/ppermute | solution.py:16
  79.9 14.8 %copy-start.25 = (pred[2]{0:T(512)(128)(4,1)S(1)}, pred[2]{0:T(512)(128)(4,1)}, u32[]{:S(2)}) copy-start(pred[2]{0:T(512)(128)(4,1)} %get-tuple-element.18) | copy-start | bytes 10
  80.9 16.6 %copy-start.4 = (bf16[2,384,256]{2,1,0:T(8,128)(2,1)}, bf16[2,384,256]{2,1,0:T(8,128)(2,1)S(1)}, u32[]{:S(2)}) copy-start(bf16[2,384,256]{2,1,0:T(8,128)(2,1)S(1)} %fusion.2) | copy-start | bytes 1179652
  80.9 15.2 %copy-start.2 = (bf16[2,2,256,256]{3,2,0,1:T(8,128)(2,1)S(1)}, bf16[2,2,256,256]{3,2,0,1:T(8,128)(2,1)}, u32[]{:S(2)}) copy-start(bf16[2,2,256,256]{3,2,0,1:T(8,128)(2,1)} %get-tuple-element.27) | copy-start | bytes 1572868
  80.9 13.8 %collective-permute-start.2 = (bf16[2,384,256]{2,1,0:T(8,128)(2,1)S(1)}, bf16[2,384,256]{2,1,0:T(8,128)(2,1)}, u32[]{:S(2)}, u32[]{:S(2)}) collective-permute-start(bf16[2,384,256]{2,1,0:T(8,128)(2,1)S(1)} %fusion.2), channel_id=1, source_target_pairs={{0,64},{16,80},{32,96},{48,112},{64,0},{80,16},{96,32},{112,48},{1... | collective-permute-start | bytes 1179656 | tf_op jit(solution)/shard_map/ppermute | solution.py:16
  86.4 32.6 %collective-permute-start.10 = (bf16[384,256]{1,0:T(8,128)(2,1)}, bf16[384,256]{1,0:T(8,128)(2,1)}, u32[]{:S(2)}, u32[]{:S(2)}) collective-permute-start(bf16[384,256]{1,0:T(8,128)(2,1)} %get-tuple-element.20), channel_id=1, source_target_pairs={{0,256},{16,272},{32,288},{48,304},{64,320},{80,336},{96,352},{112... | collective-permute-start | bytes 589832 | tf_op jit(solution)/shard_map/ppermute | solution.py:16
  98.3 16.0 %copy-start.28 = (pred[2]{0:T(512)(128)(4,1)S(1)}, pred[2]{0:T(512)(128)(4,1)}, u32[]{:S(2)}) copy-start(pred[2]{0:T(512)(128)(4,1)} %get-tuple-element.19) | copy-start | bytes 10
  98.3 15.9 %collective-permute-start.3 = (bf16[384,256]{1,0:T(8,128)(2,1)}, bf16[384,256]{1,0:T(8,128)(2,1)S(1)}, u32[]{:S(2)}, u32[]{:S(2)}) collective-permute-start(bf16[384,256]{1,0:T(8,128)(2,1)} %select_bitcast_fusion.9), channel_id=1, source_target_pairs={{0,128},{16,144},{32,160},{48,176},{64,192},{80,208},{96,224},{112... | collective-permute-start | bytes 589832 | tf_op jit(solution)/shard_map/ppermute | solution.py:16
  100.6 13.6 %copy-start.9 = (bf16[2,384,256]{2,1,0:T(8,128)(2,1)S(1)}, bf16[2,384,256]{2,1,0:T(8,128)(2,1)}, u32[]{:S(2)}) copy-start(bf16[2,384,256]{2,1,0:T(8,128)(2,1)} %copy-done.8) | copy-start | bytes 1179652
  115.0 16.6 %copy-start.29 = (pred[2]{0:T(512)(128)(4,1)S(1)}, pred[2]{0:T(512)(128)(4,1)}, u32[]{:S(2)}) copy-start(pred[2]{0:T(512)(128)(4,1)} %get-tuple-element.14) | copy-start | bytes 10
  115.1 16.5 %collective-permute-start.6 = (bf16[384,256]{1,0:T(8,128)(2,1)S(1)}, bf16[384,256]{1,0:T(8,128)(2,1)S(1)}, u32[]{:S(2)}, u32[]{:S(2)}) collective-permute-start(bf16[384,256]{1,0:T(8,128)(2,1)S(1)} %select_bitcast_fusion.8), channel_id=1, source_target_pairs={{0,256},{16,272},{32,288},{48,304},{64,320},{80,336},{96,352},{112... | collective-permute-start | bytes 589832 | tf_op jit(solution)/shard_map/ppermute | solution.py:16
  133.6 21.5 %collective-permute-start.7 = (bf16[384,256]{1,0:T(8,128)(2,1)S(1)}, bf16[384,256]{1,0:T(8,128)(2,1)S(1)}, u32[]{:S(2)}, u32[]{:S(2)}) collective-permute-start(bf16[384,256]{1,0:T(8,128)(2,1)S(1)} %select_bitcast_fusion.7), channel_id=1, source_target_pairs={{0,256},{16,272},{32,288},{48,304},{64,320},{80,336},{96,352},{112... | collective-permute-start | bytes 589832 | tf_op jit(solution)/shard_map/ppermute | solution.py:16
  138.0 16.0 %collective-permute-start.11 = (bf16[384,256]{1,0:T(8,128)(2,1)S(1)}, bf16[384,256]{1,0:T(8,128)(2,1)S(1)}, u32[]{:S(2)}, u32[]{:S(2)}) collective-permute-start(bf16[384,256]{1,0:T(8,128)(2,1)S(1)} %select_bitcast_fusion.4), channel_id=1, source_target_pairs={{0,256},{16,272},{32,288},{48,304},{64,320},{80,336},{96,352},{112... | collective-permute-start | bytes 589832 | tf_op jit(solution)/shard_map/ppermute | solution.py:16
  155.2 28.8 %collective-permute-start.8 = (bf16[384,256]{1,0:T(8,128)(2,1)S(1)}, bf16[384,256]{1,0:T(8,128)(2,1)S(1)}, u32[]{:S(2)}, u32[]{:S(2)}) collective-permute-start(bf16[384,256]{1,0:T(8,128)(2,1)S(1)} %get-tuple-element.23), channel_id=1, source_target_pairs={{0,128},{16,144},{32,160},{48,176},{64,192},{80,208},{96,224},{112... | collective-permute-start | bytes 589832 | tf_op jit(solution)/shard_map/ppermute | solution.py:16
  157.7 18.4 %collective-permute-start.12 = (bf16[384,256]{1,0:T(8,128)(2,1)S(1)}, bf16[384,256]{1,0:T(8,128)(2,1)S(1)}, u32[]{:S(2)}, u32[]{:S(2)}) collective-permute-start(bf16[384,256]{1,0:T(8,128)(2,1)S(1)} %select_bitcast_fusion.3), channel_id=1, source_target_pairs={{0,128},{16,144},{32,160},{48,176},{64,192},{80,208},{96,224},{112... | collective-permute-start | bytes 589832 | tf_op jit(solution)/shard_map/ppermute | solution.py:16
  162.1 14.0 %copy-start.3 = (bf16[2,2,256,256]{3,2,0,1:T(8,128)(2,1)S(1)}, bf16[2,2,256,256]{3,2,0,1:T(8,128)(2,1)}, u32[]{:S(2)}) copy-start(bf16[2,2,256,256]{3,2,0,1:T(8,128)(2,1)} %get-tuple-element.27) | copy-start | bytes 1572868
  162.2 22.6 %collective-permute-start.18 = (bf16[8,2,2,2,16,256]{5,4,2,3,1,0:T(8,128)(2,1)S(1)}, bf16[8,2,2,2,16,256]{5,4,2,3,1,0:T(8,128)(2,1)S(1)}, u32[]{:S(2)}, u32[]{:S(2)}) collective-permute-start(bf16[8,2,2,2,16,256]{5,4,2,3,1,0:T(8,128)(2,1)S(1)} %select_bitcast_fusion), channel_id=1, source_target_pairs={{0,1},{1,0},{2,3},{3,2},{4,5},{5,4},{6,7},{7,6},{8,9},{9,8},{10,11... | collective-permute-start | bytes 1572872 | tf_op jit(solution)/shard_map/ppermute | solution.py:72
  177.7 14.0 %collective-permute-start.13 = (bf16[2,384,256]{2,1,0:T(8,128)(2,1)}, bf16[2,384,256]{2,1,0:T(8,128)(2,1)}, u32[]{:S(2)}, u32[]{:S(2)}) collective-permute-start(bf16[2,384,256]{2,1,0:T(8,128)(2,1)} %get-tuple-element.67), channel_id=1, source_target_pairs={{0,64},{16,80},{32,96},{48,112},{64,0},{80,16},{96,32},{112,48},{1... | collective-permute-start | bytes 1179656 | tf_op jit(solution)/shard_map/ppermute | solution.py:16
  185.9 41.1 %all-to-all-start.2 = ((bf16[8,2,2,2,16,256]{5,4,2,3,1,0:T(8,128)(2,1)}), bf16[8,2,2,2,16,256]{5,4,2,3,1,0:T(8,128)(2,1)}, u32[]{:S(2)}, u32[]{:S(2)}) async-start(bf16[8,2,2,2,16,256]{5,4,2,3,1,0:T(8,128)(2,1)} %fusion.5), calls=%async_computation.2 | async-start | bytes 1048576 | tf_op jit(solution)/shard_map/all_to_all | solution.py:76
  193.9 13.0 %collective-permute-start.14 = (bf16[2,384,256]{2,1,0:T(8,128)(2,1)S(1)}, bf16[2,384,256]{2,1,0:T(8,128)(2,1)S(1)}, u32[]{:S(2)}, u32[]{:S(2)}) collective-permute-start(bf16[2,384,256]{2,1,0:T(8,128)(2,1)S(1)} %get-tuple-element.69), channel_id=1, source_target_pairs={{0,32},{16,48},{32,0},{48,16},{64,96},{80,112},{96,64},{112,80},{1... | collective-permute-start | bytes 1179656 | tf_op jit(solution)/shard_map/ppermute | solution.py:16
  198.2 13.3 %collective-permute-start.17 = (bf16[8,2,2,2,16,256]{5,4,2,3,1,0:T(8,128)(2,1)S(1)}, bf16[8,2,2,2,16,256]{5,4,2,3,1,0:T(8,128)(2,1)S(1)}, u32[]{:S(2)}, u32[]{:S(2)}) collective-permute-start(bf16[8,2,2,2,16,256]{5,4,2,3,1,0:T(8,128)(2,1)S(1)} %select_bitcast_fusion.1), channel_id=1, source_target_pairs={{0,1},{1,0},{2,3},{3,2},{4,5},{5,4},{6,7},{7,6},{8,9},{9,8},{10,11... | collective-permute-start | bytes 1572872 | tf_op jit(solution)/shard_map/ppermute | solution.py:72
  207.9 10.5 %collective-permute-start.15 = (bf16[2,384,256]{2,1,0:T(8,128)(2,1)S(1)}, bf16[2,384,256]{2,1,0:T(8,128)(2,1)S(1)}, u32[]{:S(2)}, u32[]{:S(2)}) collective-permute-start(bf16[2,384,256]{2,1,0:T(8,128)(2,1)S(1)} %get-tuple-element.71), channel_id=1, source_target_pairs={{0,16},{16,0},{32,48},{48,32},{64,80},{80,64},{96,112},{112,96},{1... | collective-permute-start | bytes 1179656 | tf_op jit(solution)/shard_map/ppermute | solution.py:16
  212.6 6.0 %copy-start.7 = (bf16[2,384,256]{1,2,0:T(8,128)(2,1)S(1)}, bf16[2,384,256]{1,2,0:T(8,128)(2,1)}, u32[]{:S(2)}) copy-start(bf16[2,384,256]{1,2,0:T(8,128)(2,1)} %copy-done.6) | copy-start | bytes 1179652
  219.8 6.1 %copy-start.27 = (pred[2]{0:T(512)(128)(4,1)S(1)}, pred[2]{0:T(512)(128)(4,1)}, u32[]{:S(2)}) copy-start(pred[2]{0:T(512)(128)(4,1)} %copy-done.26) | copy-start | bytes 10
  220.7 19.9 %collective-permute-start.16 = (bf16[8,2,2,2,16,256]{5,4,2,3,1,0:T(8,128)(2,1)}, bf16[8,2,2,2,16,256]{5,4,2,3,1,0:T(8,128)(2,1)}, u32[]{:S(2)}, u32[]{:S(2)}) collective-permute-start(bf16[8,2,2,2,16,256]{5,4,2,3,1,0:T(8,128)(2,1)} %select_bitcast_fusion.2), channel_id=1, source_target_pairs={{0,1},{1,0},{2,3},{3,2},{4,5},{5,4},{6,7},{7,6},{8,9},{9,8},{10,11... | collective-permute-start | bytes 1572872 | tf_op jit(solution)/shard_map/ppermute | solution.py:72
  227.0 24.4 %all-to-all-start.1 = ((bf16[8,2,2,2,16,256]{5,4,2,3,1,0:T(8,128)(2,1)}), bf16[8,2,2,2,16,256]{5,4,2,3,1,0:T(8,128)(2,1)S(1)}, u32[]{:S(2)}, u32[]{:S(2)}) async-start(bf16[8,2,2,2,16,256]{5,4,2,3,1,0:T(8,128)(2,1)} %fusion.6), calls=%async_computation.1 | async-start | bytes 1048576 | tf_op jit(solution)/shard_map/all_to_all | solution.py:76
  235.7 19.2 %collective-permute-start.19 = (f32[2,16,256]{2,1,0:T(8,128)S(1)}, f32[2,16,256]{2,1,0:T(8,128)S(1)}, u32[]{:S(2)}, u32[]{:S(2)}) collective-permute-start(f32[2,16,256]{2,1,0:T(8,128)S(1)} %select_bitcast_fusion.11), channel_id=1, source_target_pairs={{0,256},{16,272},{32,288},{48,304},{64,320},{80,336},{96,352},{112... | collective-permute-start | bytes 98312 | tf_op jit(solution)/shard_map/ppermute | solution.py:16
  251.3 21.4 %all-to-all-start = ((bf16[8,2,2,2,16,256]{5,4,2,3,1,0:T(8,128)(2,1)}), bf16[8,2,2,2,16,256]{5,4,2,3,1,0:T(8,128)(2,1)S(1)}, u32[]{:S(2)}, u32[]{:S(2)}) async-start(bf16[8,2,2,2,16,256]{5,4,2,3,1,0:T(8,128)(2,1)} %fusion.7), calls=%async_computation | async-start | bytes 1048576 | tf_op jit(solution)/shard_map/all_to_all | solution.py:76
  254.9 5.9 %collective-permute-start.20 = (f32[2,2,16,256]{3,2,1,0:T(8,128)S(1)}, f32[2,2,16,256]{3,2,1,0:T(8,128)S(1)}, u32[]{:S(2)}, u32[]{:S(2)}) collective-permute-start(f32[2,2,16,256]{3,2,1,0:T(8,128)S(1)} %select_bitcast_fusion.10), channel_id=1, source_target_pairs={{0,128},{16,144},{32,160},{48,176},{64,192},{80,208},{96,224},{112... | collective-permute-start | bytes 196616 | tf_op jit(solution)/shard_map/ppermute | solution.py:16
  (12 other events, 37.1 us)
Sparse Core Ops, SparseCore 0:
  16.4 44.9 all-gather.3
  70.4 38.5 all-gather.5

commit v3 on v0

v3 whole, which is shorter than its diff:
```python
import jax
import jax.numpy as jnp
import numpy as np
from jax import lax
from jax.sharding import PartitionSpec as P


SECTIONS = 6
GATHERS = ((0,), (1,), (2, 3), (4, 5))
SCATTERS = ((4, 5), (2, 3), (0, 1))


def flip(value, bit):
    mask = 1 << bit
    pairs = [(source, source ^ mask) for source in range(lax.axis_size("blk"))]
    return lax.ppermute(value, "blk", pairs)


def mine(bit):
    return (lax.axis_index("blk") >> bit) & 1


def after(value, other):
    probe = lax.squeeze(lax.slice(other, (0,) * other.ndim, (1,) * other.ndim), range(other.ndim))
    return jnp.where(probe != probe, jnp.zeros_like(value), value)


def dot(left, right):
    return jnp.einsum("...tk,...kl->...tl", left, right, preferred_element_type=jnp.float32)


def dot_back(left, right):
    return jnp.einsum("...tl,...kl->...tk", left, right, preferred_element_type=jnp.float32)


def dot_rows(left, right):
    return jnp.einsum("...tk,...tl->...kl", left, right, preferred_element_type=jnp.float32).astype(jnp.bfloat16)


def block_tables():
    weight = np.zeros((5, SECTIONS, 1), np.int32)
    for section in range(SECTIONS):
        place = {1: 0, 2: 1, 3: 2, 4: 3, 5: 4}
        if section >= 4:
            del place[4]
            place[0] = 3
        if section == 5:
            del place[5]
            place[4] = 4
        for number, bit in place.items():
            weight[bit, section, 0] = 1 << number
    local = np.array([1, 1, 1, 1, 16, 32], np.int32)[:, None]
    return weight, local


def choices(matchings):
    weight, local = block_tables()
    low, high = mine(3), mine(4)
    order = jnp.where(np.arange(SECTIONS)[:, None] < 4, low, high)
    rows = np.arange(2, dtype=np.int32)[None, :] ^ order
    owned = sum((mine(bit) * weight[bit] for bit in range(5)), rows * local)
    every = jnp.arange(matchings.shape[1], dtype=jnp.int32)
    hit = (every == owned[:, :, None]) & (matchings != every)[:, None, :]
    swapped = jnp.any(hit, axis=2)
    section = np.arange(SECTIONS)[:, None]
    turn = jnp.where(section == 4, rows ^ low, jnp.where(section == 5, rows ^ high, 0)) == 1
    return swapped ^ turn


def turned(value, yes, axis=0):
    low = lax.index_in_dim(value, 0, axis)
    high = lax.index_in_dim(value, 1, axis)
    return jnp.concatenate([jnp.where(yes, high, low), jnp.where(yes, low, high)], axis)


def core_half(terms, core):
    count, both, per_dev, size, depth, width = terms.shape
    parts = terms.reshape(count, both, per_dev, size // 2, 2, depth, width)
    half = jnp.where(core == 1, parts[:, :, :, :, 1], parts[:, :, :, :, 0])
    return jnp.moveaxis(half, 3, 0)


def scatter_sum(terms, waits):
    count, both, per_dev, depth, width = terms.shape
    size = lax.axis_size("tok")
    core = lax.axis_index("tok") & 1
    terms = terms.reshape(count, both, per_dev, size, depth // size, width)
    give = core_half(terms, 1 - core)
    if waits is not None:
        give = after(give, waits)
    came = lax.ppermute(give, "tok", [(source, source ^ 1) for source in range(size)])
    chip = (core_half(terms, core).astype(jnp.float32) + came.astype(jnp.float32)).astype(jnp.bfloat16)
    groups = [list(range(c, size, 2)) for c in range(2)]
    chip = lax.all_to_all(chip, "tok", 0, 0, axis_index_groups=groups)
    return jnp.sum(chip.astype(jnp.float32), axis=0)


def body(activations, weights, matchings, cotangent):
    width = weights.shape[4]
    bf16 = jnp.bfloat16
    low, high = mine(3) == 1, mine(4) == 1
    same = low == high
    chosen = choices(matchings)[:, None, :, None, None]

    def halves(array):
        return array[:, :width], array[:, width:]

    shards = jnp.swapaxes(weights, 1, 2)
    part = shards[4:6]
    keep = jnp.where(low, part[:, :, 1], part[:, :, 0])
    came = flip(jnp.where(low, part[:, :, 0], part[:, :, 1]), 3)
    row0, row1 = jnp.where(same, keep, came), jnp.where(same, came, keep)
    fourth = jnp.stack([row0[0], row1[0]], 1)
    fifth = jnp.stack([row0[1], flip(row1[1], 4)], 1)
    shards = [turned(shards[:4], low, 2), jnp.stack([fourth, fifth])]

    full = [None] * SECTIONS
    for group in GATHERS:
        source, base = (shards[0], 0) if group[0] < 4 else (shards[1], 4)
        begin, end = group[0] - base, group[-1] + 1 - base
        ordered = turned(source[begin:end], chosen[group[0] : group[-1] + 1], 1)
        gathered = lax.all_gather(ordered, "tok", axis=3, tiled=True)
        for place, section in enumerate(group):
            full[section] = gathered[place]

    left, right = halves(cotangent)
    came = flip(jnp.where(low, left, right), 3)
    keep = jnp.where(low, right, left)
    cotan0 = jnp.where(same, keep, came)
    cotan1 = flip(jnp.where(same, came, keep), 4)

    left, right = halves(activations)
    value = jnp.stack([jnp.where(low, right, left), jnp.where(low, left, right)])
    inputs = []
    for section in range(4):
        other = value[::-1] if section == 0 else flip(value, section - 1)
        inputs.append((value, other))
        own_w, other_w = full[section][0], full[section][1]
        if section < 3:
            value = (dot(value, own_w) + dot(other, other_w)).astype(bf16)
        else:
            send = (dot(value[1], own_w[1]) + dot(other[1], other_w[1])).astype(bf16)
            keep = (dot(value[0], own_w[0]) + dot(other[0], other_w[0])).astype(bf16)
    came = flip(send, 3)
    inputs.append((keep, came))
    own_w, other_w = full[4][0], full[4][1]
    send = (dot(keep, own_w[1]) + dot(came, other_w[1])).astype(bf16)
    keep = (dot(keep, own_w[0]) + dot(came, other_w[0])).astype(bf16)
    came = flip(send, 4)
    inputs.append((keep, came))
    own_w, other_w = full[5][0], full[5][1]

    results, grads = [], []
    for row, cotan in enumerate((cotan0, cotan1)):
        final = dot(keep, own_w[row]) + dot(came, other_w[row])
        results.append(jax.nn.gelu(final).astype(bf16))
        back_fn = jax.vjp(jax.nn.gelu, final)[1]
        grads.append(back_fn(cotan.astype(jnp.float32))[0].astype(bf16))

    terms = [None] * SECTIONS
    for section in (5, 4):
        own_w, other_w = full[section][0], full[section][1]
        sent = (dot_back(grads[0], other_w[0]) + dot_back(grads[1], other_w[1])).astype(bf16)
        back = flip(sent, section - 1)
        kept = (dot_back(grads[0], own_w[0]) + dot_back(grads[1], own_w[1])).astype(bf16)
        terms[section] = jnp.stack(
            [jnp.stack([dot_rows(part, grad) for grad in grads]) for part in inputs[section]]
        )
        grads = [kept, back]
    sums = [None] * SECTIONS
    waits = None
    for section in (3, 2, 1, 0):
        own_w, other_w = full[section][0], full[section][1]
        if section == 3:
            back = [flip(dot_back(grads[r], other_w[r]).astype(bf16), 2) for r in range(2)]
            kept = [dot_back(grads[r], own_w[r]) for r in range(2)]
            terms[section] = jnp.stack(
                [jnp.stack([dot_rows(part[r], grads[r]) for r in range(2)]) for part in inputs[section]]
            )
            grad = jnp.stack([(kept[r] + back[r].astype(jnp.float32)).astype(bf16) for r in range(2)])
        else:
            if section == 2:
                late = grad
            sent = dot_back(grad, other_w).astype(bf16)
            back = sent[::-1] if section == 0 else flip(sent, section - 1)
            terms[section] = jnp.stack([dot_rows(part, grad) for part in inputs[section]])
            grad = (dot_back(grad, own_w) + back.astype(jnp.float32)).astype(bf16)
        for group in SCATTERS:
            if section == min(group) or (section == 3 and group == (4, 5)):
                summed = scatter_sum(jnp.stack([terms[s] for s in group]), waits)
                waits = summed
                for place, s in enumerate(group):
                    sums[s] = summed[place]

    came = flip(after(results[1], late), 4)
    keep, send = jnp.where(same, results[0], came), jnp.where(same, came, results[0])
    came = flip(send, 3)
    result = jnp.concatenate([jnp.where(low, came, keep), jnp.where(low, keep, came)], axis=1)
    input_grad = jnp.concatenate([jnp.where(low, grad[1], grad[0]), jnp.where(low, grad[0], grad[1])], axis=1)

    first = turned(turned(jnp.stack(sums[:4]), chosen[:4], 1), low, 2)
    last = turned(jnp.stack(sums[4:]), chosen[4:], 1)
    row0 = last[:, :, 0]
    row1 = jnp.stack([last[0, :, 1], flip(last[1, :, 1], 4)])
    keep, send = jnp.where(same, row0, row1), jnp.where(same, row1, row0)
    came = flip(send, 3)
    last = jnp.stack([jnp.where(low, came, keep), jnp.where(low, keep, came)], 2)
    weight_grad = jnp.swapaxes(jnp.concatenate([first, last]), 1, 2)
    return result, input_grad, weight_grad


def solution(mesh):
    placed = (P("tok", "blk"), P(None, "blk", None, "tok", None), P(), P("tok", "blk"))
    return jax.shard_map(
        body,
        mesh=mesh,
        in_specs=placed,
        out_specs=(P("tok", "blk"), P("tok", "blk"), P(None, "blk", None, "tok", None)),
        check_vma=False,
    )
```

time: 316 us -> 300 us (0.949)
  starting transfers between devices: 33.8 us -> 118 us
  blocking collectives: 109 us -> 40.1 us
  waiting for transfers between devices: 118 us -> 71.9 us
  other arithmetic: 8.5 us -> 15.3 us
  between operations: 14.7 us -> 19.1 us
    ppermute x10 -> x22, starting transfers between devices: 33.8 us -> 107 us  [the longest x19 94.6 us: flip(): return lax.ppermute(value, 'blk', pairs)]
    all_gather x6 -> x2, blocking collectives: 109 us -> 40.1 us  [body(): gathered = lax.all_gather(ordered, 'tok', axis=3, tiled=True)]
    reduce_scatter x1 -> x0, waiting for transfers between devices: 55.1 us -> none  [body(): lax.psum_scatter(jnp.stack(terms).astype(jnp.bfloat16), 'tok', scatter_di...]
    ppermute x10 -> x22, waiting for transfers between devices: 62.7 us -> 28.6 us  [the longest x19 28.6 us: flip(): return lax.ppermute(value, 'blk', pairs)]
    all_to_all x0 -> x3, waiting for transfers between devices: none -> 33 us  [scatter_sum(): chip = lax.all_to_all(chip, 'tok', 0, 0, axis_index_groups=groups)]
    all_to_all x0 -> x3, starting transfers between devices: none -> 11.2 us  [scatter_sum(): chip = lax.all_to_all(chip, 'tok', 0, 0, axis_index_groups=groups)]
    all_gather x0 -> x2, waiting for transfers between devices: none -> 10.2 us  [body(): gathered = lax.all_gather(ordered, 'tok', axis=3, tiled=True)]
    unnamed x47 -> x67, local copies, waits for them, and re-layouts: 3.72 us -> 10.8 us
  transfers between devices with their start and end apart: 11 -> 27, of which waited for: 7 -> 11; matrix products, arithmetic and copies ran while one was open for 4% -> 11% of each run, Pallas kernels for 0% -> 0%
where the time goes in v3:
time: 300 us; the launch traced here: 298 us
  starting transfers between devices  118 us (39%)
  waiting for transfers between devices  71.9 us (24%)
  blocking collectives  40.1 us (13%)
  matrix products  20.7 us (7%)
  between operations  19.1 us (6%)
  other arithmetic  15.3 us (5%)
  local copies, waits for them, and re-layouts  13.4 us (4%)
    ppermute x19, starting transfers between devices, flip(): return lax.ppermute(value, 'blk', pairs)  94.6 us
    all_gather x2, blocking collectives, body(): gathered = lax.all_gather(ordered, 'tok', axis=3, tiled=True)  40.1 us
    all_to_all x3, waiting for transfers between devices, scatter_sum(): chip = lax.all_to_all(chip, 'tok', 0, 0, axis_index_groups=groups)  33 us
    ppermute x19, waiting for transfers between devices, flip(): return lax.ppermute(value, 'blk', pairs)  28.6 us
    ppermute x3, starting transfers between devices, scatter_sum(): lax.ppermute(give, 'tok', [(source, source ^ 1) for source in range(size)])  12.1 us
    all_to_all x3, starting transfers between devices, scatter_sum(): chip = lax.all_to_all(chip, 'tok', 0, 0, axis_index_groups=groups)  11.2 us
    unnamed x67, local copies, waits for them, and re-layouts  10.8 us
    all_gather x2, waiting for transfers between devices, body(): gathered = lax.all_gather(ordered, 'tok', axis=3, tiled=True)  10.2 us
  transfers between devices with their start and end apart: 27, of which 11 were waited for; matrix products, arithmetic and copies ran while one was open for 11% of the time, Pallas kernels for 0%

profile of v3, /device:TPU:1, one launch (start us, length us, event | category | flops | bytes accessed | tf_op | source)
XLA Modules:
  0.0 298.5 jit_solution(13045390823814121547)
XLA Ops:
  11.3 22.6 %all_gather.12 = bf16[1,2,2,256,256]{4,3,2,1,0:T(8,128)(2,1)S(1)} all-gather(bf16[1,2,2,16,256]{4,3,2,1,0:T(8,128)(2,1)S(1)} %pad_maximum_fusion.14), channel_id=1, replica_groups=mesh['blk'=32,'tok'=16] {'tok'}, dimensions={3}, use_global_device_ids=true | all-gather | bytes 557056 | tf_op jit(solution)/shard_map/all_gather | solution.py:122
  35.7 2.0 collective-permute-start.1
  39.6 4.9 %collective-permute-start.4 = (bf16[2,2,16,256]{3,2,1,0:T(8,128)(2,1)S(1)}, bf16[2,2,16,256]{3,2,1,0:T(8,128)(2,1)S(1)}, u32[]{:S(2)}, u32[]{:S(2)}) collective-permute-start(bf16[2,2,16,256]{3,2,1,0:T(8,128)(2,1)S(1)} %fusion.65), channel_id=1, source_target_pairs={{0,128},{16,144},{32,160},{48,176},{64,192},{80,208},{96,224},{112... | collective-permute-start | bytes 98312 | tf_op jit(solution)/shard_map/ppermute | solution.py:16
  45.2 1.9 collective-permute-start
  47.2 17.5 %all_gather.13 = bf16[1,2,2,256,256]{4,3,2,1,0:T(8,128)(2,1)S(1)} all-gather(bf16[1,2,2,16,256]{4,3,2,1,0:T(8,128)(2,1)S(1)} %pad_maximum_fusion.15), channel_id=1, replica_groups=mesh['blk'=32,'tok'=16] {'tok'}, dimensions={3}, use_global_device_ids=true | all-gather | bytes 557056 | tf_op jit(solution)/shard_map/all_gather | solution.py:122
  66.0 9.4 %collective-permute-start.5 = (bf16[2,16,256]{2,1,0:T(8,128)(2,1)S(1)}, bf16[2,16,256]{2,1,0:T(8,128)(2,1)S(1)}, u32[]{:S(2)}, u32[]{:S(2)}) collective-permute-start(bf16[2,16,256]{2,1,0:T(8,128)(2,1)S(1)} %get-tuple-element.57), channel_id=1, source_target_pairs={{0,256},{16,272},{32,288},{48,304},{64,320},{80,336},{96,352},{112... | collective-permute-start | bytes 49160 | tf_op jit(solution)/shard_map/ppermute | solution.py:16
  75.4 1.2 collective-permute-done.5
  78.1 4.5 %collective-permute-start.2 = (bf16[2,384,256]{2,1,0:T(8,128)(2,1)S(1)}, bf16[2,384,256]{2,1,0:T(8,128)(2,1)S(1)}, u32[]{:S(2)}, u32[]{:S(2)}) collective-permute-start(bf16[2,384,256]{2,1,0:T(8,128)(2,1)S(1)} %fusion.1), channel_id=1, source_target_pairs={{0,32},{16,48},{32,0},{48,16},{64,96},{80,112},{96,64},{112,80},{1... | collective-permute-start | bytes 1179656 | tf_op jit(solution)/shard_map/ppermute | solution.py:16
  82.6 1.7 broadcast_select_fusion.2
  84.3 6.3 %collective-permute-start.8 = (bf16[384,256]{1,0:T(8,128)(2,1)}, bf16[384,256]{1,0:T(8,128)(2,1)}, u32[]{:S(2)}, u32[]{:S(2)}) collective-permute-start(bf16[384,256]{1,0:T(8,128)(2,1)} %broadcast_select_fusion.2), channel_id=1, source_target_pairs={{0,256},{16,272},{32,288},{48,304},{64,320},{80,336},{96,352},{112... | collective-permute-start | bytes 589832 | tf_op jit(solution)/shard_map/ppermute | solution.py:16
  90.6 1.3 fusion.44
  92.7 2.4 collective-permute-start.3
  95.5 12.8 %collective-permute-done.3 = bf16[2,384,256]{2,1,0:T(8,128)(2,1)S(1)} collective-permute-done((bf16[2,384,256]{2,1,0:T(8,128)(2,1)S(1)}, bf16[2,384,256]{2,1,0:T(8,128)(2,1)S(1)}, u32[]{:S(2)}, u32[]{:S(2)}) %collective-permute-start.3) | collective-permute-done | bytes 393248 | tf_op jit(solution)/shard_map/ppermute | solution.py:16
  109.3 3.3 %collective-permute-start.6 = (bf16[384,256]{1,0:T(8,128)(2,1)}, bf16[384,256]{1,0:T(8,128)(2,1)S(1)}, u32[]{:S(2)}, u32[]{:S(2)}) collective-permute-start(bf16[384,256]{1,0:T(8,128)(2,1)} %fusion.6), channel_id=1, source_target_pairs={{0,128},{16,144},{32,160},{48,176},{64,192},{80,208},{96,224},{112... | collective-permute-start | bytes 589832 | tf_op jit(solution)/shard_map/ppermute | solution.py:16
  112.8 10.2 %all-gather.5.cloned.1.call-done = bf16[2,2,2,256,256]{4,3,1,2,0:T(8,128)(2,1)} async-done(((bf16[2,2,2,16,256]{4,3,1,2,0:T(8,128)(2,1)}), bf16[2,2,2,256,256]{4,3,1,2,0:T(8,128)(2,1)}) %all-gather.5.cloned.1.call-update) | async-done | bytes 1048592 | tf_op jit(solution)/shard_map/all_gather | solution.py:122
  123.0 1.2 fusion.53
  124.2 1.1 fusion.57
  125.6 7.7 %collective-permute-start.7 = (bf16[384,256]{1,0:T(8,128)(2,1)S(1)}, bf16[384,256]{1,0:T(8,128)(2,1)S(1)}, u32[]{:S(2)}, u32[]{:S(2)}) collective-permute-start(bf16[384,256]{1,0:T(8,128)(2,1)S(1)} %fusion.8), channel_id=1, source_target_pairs={{0,256},{16,272},{32,288},{48,304},{64,320},{80,336},{96,352},{112... | collective-permute-start | bytes 589832 | tf_op jit(solution)/shard_map/ppermute | solution.py:16
  133.9 5.9 %collective-permute-done.7 = bf16[384,256]{1,0:T(8,128)(2,1)S(1)} collective-permute-done((bf16[384,256]{1,0:T(8,128)(2,1)S(1)}, bf16[384,256]{1,0:T(8,128)(2,1)S(1)}, u32[]{:S(2)}, u32[]{:S(2)}) %collective-permute-start.7) | collective-permute-done | bytes 196640 | tf_op jit(solution)/shard_map/ppermute | solution.py:16
  140.1 1.2 fusion.28
  143.5 6.4 %collective-permute-start.9 = (bf16[384,256]{1,0:T(8,128)(2,1)S(1)}, bf16[384,256]{1,0:T(8,128)(2,1)S(1)}, u32[]{:S(2)}, u32[]{:S(2)}) collective-permute-start(bf16[384,256]{1,0:T(8,128)(2,1)S(1)} %fusion.10), channel_id=1, source_target_pairs={{0,256},{16,272},{32,288},{48,304},{64,320},{80,336},{96,352},{112... | collective-permute-start | bytes 589832 | tf_op jit(solution)/shard_map/ppermute | solution.py:16
  152.0 1.9 collective-permute-done.9
  154.6 8.4 %collective-permute-start.10 = (bf16[384,256]{1,0:T(8,128)(2,1)S(1)}, bf16[384,256]{1,0:T(8,128)(2,1)S(1)}, u32[]{:S(2)}, u32[]{:S(2)}) collective-permute-start(bf16[384,256]{1,0:T(8,128)(2,1)S(1)} %convolution_convert_fusion.10), channel_id=1, source_target_pairs={{0,64},{16,80},{32,96},{48,112},{64,0},{80,16},{96,32},{112,48},{1... | collective-permute-start | bytes 589832 | tf_op jit(solution)/shard_map/ppermute | solution.py:16
  163.2 4.7 %collective-permute-start.13 = (bf16[384,256]{1,0:T(8,128)(2,1)S(1)}, bf16[384,256]{1,0:T(8,128)(2,1)S(1)}, u32[]{:S(2)}, u32[]{:S(2)}) collective-permute-start(bf16[384,256]{1,0:T(8,128)(2,1)S(1)} %fusion.12), channel_id=1, source_target_pairs={{0,128},{16,144},{32,160},{48,176},{64,192},{80,208},{96,224},{112... | collective-permute-start | bytes 589832 | tf_op jit(solution)/shard_map/ppermute | solution.py:16
  168.8 3.7 %collective-permute-start.17 = (bf16[8,2,2,2,16,256]{5,4,3,2,1,0:T(8,128)(2,1)S(1)}, bf16[8,2,2,2,16,256]{5,4,3,2,1,0:T(8,128)(2,1)S(1)}, u32[]{:S(2)}, u32[]{:S(2)}) collective-permute-start(bf16[8,2,2,2,16,256]{5,4,3,2,1,0:T(8,128)(2,1)S(1)} %select_bitcast_fusion.2), channel_id=1, source_target_pairs={{0,1},{1,0},{2,3},{3,2},{4,5},{5,4},{6,7},{7,6},{8,9},{9,8},{10,11... | collective-permute-start | bytes 1572872 | tf_op jit(solution)/shard_map/ppermute | solution.py:91
  175.1 6.5 %collective-permute-start.11 = (bf16[384,256]{1,0:T(8,128)(2,1)S(1)}, bf16[384,256]{1,0:T(8,128)(2,1)S(1)}, u32[]{:S(2)}, u32[]{:S(2)}) collective-permute-start(bf16[384,256]{1,0:T(8,128)(2,1)S(1)} %fusion.46), channel_id=1, source_target_pairs={{0,256},{16,272},{32,288},{48,304},{64,320},{80,336},{96,352},{112... | collective-permute-start | bytes 589832 | tf_op jit(solution)/shard_map/ppermute | solution.py:16
  181.8 2.3 collective-permute-start.14
  184.7 2.2 collective-permute-done.11
  187.7 7.6 %collective-permute-start.12 = (bf16[384,256]{1,0:T(8,128)(2,1)}, bf16[384,256]{1,0:T(8,128)(2,1)}, u32[]{:S(2)}, u32[]{:S(2)}) collective-permute-start(bf16[384,256]{1,0:T(8,128)(2,1)} %broadcast_select_fusion.1), channel_id=1, source_target_pairs={{0,128},{16,144},{32,160},{48,176},{64,192},{80,208},{96,224},{112... | collective-permute-start | bytes 589832 | tf_op jit(solution)/shard_map/ppermute | solution.py:16
  195.7 1.0 convolution_convert_fusion.2
  196.7 4.8 %collective-permute-start.15 = (bf16[2,384,256]{2,1,0:T(8,128)(2,1)}, bf16[2,384,256]{2,1,0:T(8,128)(2,1)}, u32[]{:S(2)}, u32[]{:S(2)}) collective-permute-start(bf16[2,384,256]{2,1,0:T(8,128)(2,1)} %convolution_convert_fusion.2), channel_id=1, source_target_pairs={{0,32},{16,48},{32,0},{48,16},{64,96},{80,112},{96,64},{112,80},{1... | collective-permute-start | bytes 1179656 | tf_op jit(solution)/shard_map/ppermute | solution.py:16
  202.4 1.0 fusion.16
  203.4 4.2 %all-to-all-start = ((bf16[8,2,2,2,16,256]{5,4,3,2,1,0:T(8,128)(2,1)}), bf16[8,2,2,2,16,256]{5,4,3,2,1,0:T(8,128)(2,1)}, u32[]{:S(2)}, u32[]{:S(2)}) async-start(bf16[8,2,2,2,16,256]{5,4,3,2,1,0:T(8,128)(2,1)} %fusion.16), calls=%async_computation | async-start | bytes 1048576 | tf_op jit(solution)/shard_map/all_to_all | solution.py:94
  208.6 1.1 broadcast_select_fusion.4
  210.9 1.4 add_convert_fusion
  212.6 2.2 collective-permute-start.16
  214.8 7.5 %all-to-all-done = bf16[8,2,2,2,16,256]{5,4,3,2,1,0:T(8,128)(2,1)} async-done(((bf16[8,2,2,2,16,256]{5,4,3,2,1,0:T(8,128)(2,1)}), bf16[8,2,2,2,16,256]{5,4,3,2,1,0:T(8,128)(2,1)}, u32[]{:S(2)}, u32[]{:S(2)}) %all-to-all-start) | async-done | bytes 524320 | tf_op jit(solution)/shard_map/all_to_all | solution.py:94
  222.3 1.1 convert_reduce_fusion.2
  225.3 6.1 %collective-permute-start.18 = (bf16[8,2,2,2,16,256]{5,4,3,2,1,0:T(8,128)(2,1)S(1)}, bf16[8,2,2,2,16,256]{5,4,3,2,1,0:T(8,128)(2,1)S(1)}, u32[]{:S(2)}, u32[]{:S(2)}) collective-permute-start(bf16[8,2,2,2,16,256]{5,4,3,2,1,0:T(8,128)(2,1)S(1)} %select_bitcast_fusion.1), channel_id=1, source_target_pairs={{0,1},{1,0},{2,3},{3,2},{4,5},{5,4},{6,7},{7,6},{8,9},{9,8},{10,11... | collective-permute-start | bytes 1572872 | tf_op jit(solution)/shard_map/ppermute | solution.py:91
  232.2 1.3 fusion.3
  234.5 3.5 %all-to-all-start.1 = ((bf16[8,2,2,2,16,256]{5,4,3,2,1,0:T(8,128)(2,1)}), bf16[8,2,2,2,16,256]{5,4,3,2,1,0:T(8,128)(2,1)S(1)}, u32[]{:S(2)}, u32[]{:S(2)}) async-start(bf16[8,2,2,2,16,256]{5,4,3,2,1,0:T(8,128)(2,1)} %fusion.18), calls=%async_computation.1 | async-start | bytes 1048576 | tf_op jit(solution)/shard_map/all_to_all | solution.py:94
  241.0 15.1 %all-to-all-done.1 = bf16[8,2,2,2,16,256]{5,4,3,2,1,0:T(8,128)(2,1)S(1)} async-done(((bf16[8,2,2,2,16,256]{5,4,3,2,1,0:T(8,128)(2,1)}), bf16[8,2,2,2,16,256]{5,4,3,2,1,0:T(8,128)(2,1)S(1)}, u32[]{:S(2)}, u32[]{:S(2)}) %all-to-all-start.1) | async-done | bytes 524320 | tf_op jit(solution)/shard_map/all_to_all | solution.py:94
  258.0 2.3 collective-permute-start.19
  260.7 7.4 %collective-permute-start.20 = (f32[2,16,256]{2,1,0:T(8,128)S(1)}, f32[2,16,256]{2,1,0:T(8,128)S(1)}, u32[]{:S(2)}, u32[]{:S(2)}) collective-permute-start(f32[2,16,256]{2,1,0:T(8,128)S(1)} %get-tuple-element.48), channel_id=1, source_target_pairs={{0,256},{16,272},{32,288},{48,304},{64,320},{80,336},{96,352},{112... | collective-permute-start | bytes 98312 | tf_op jit(solution)/shard_map/ppermute | solution.py:16
  269.2 3.5 %all-to-all-start.2 = ((bf16[8,2,2,2,16,256]{5,4,3,2,1,0:T(8,128)(2,1)}), bf16[8,2,2,2,16,256]{5,4,3,2,1,0:T(8,128)(2,1)S(1)}, u32[]{:S(2)}, u32[]{:S(2)}) async-start(bf16[8,2,2,2,16,256]{5,4,3,2,1,0:T(8,128)(2,1)} %fusion.20), calls=%async_computation.2 | async-start | bytes 1048576 | tf_op jit(solution)/shard_map/all_to_all | solution.py:94
  272.7 1.9 collective-permute-start.21
  275.7 4.4 %collective-permute-done.21 = f32[2,2,16,256]{3,2,1,0:T(8,128)S(1)} collective-permute-done((f32[2,2,16,256]{3,2,1,0:T(8,128)S(1)}, f32[2,2,16,256]{3,2,1,0:T(8,128)S(1)}, u32[]{:S(2)}, u32[]{:S(2)}) %collective-permute-start.21) | collective-permute-done | bytes 65568 | tf_op jit(solution)/shard_map/ppermute | solution.py:16
  280.1 10.5 %all-to-all-done.2 = bf16[8,2,2,2,16,256]{5,4,3,2,1,0:T(8,128)(2,1)S(1)} async-done(((bf16[8,2,2,2,16,256]{5,4,3,2,1,0:T(8,128)(2,1)}), bf16[8,2,2,2,16,256]{5,4,3,2,1,0:T(8,128)(2,1)S(1)}, u32[]{:S(2)}, u32[]{:S(2)}) %all-to-all-start.2) | async-done | bytes 524320 | tf_op jit(solution)/shard_map/all_to_all | solution.py:94
  (198 shorter events, 36.1 us)
Async XLA Ops:
  7.2 83.4 %all-gather.3.cloned.1.call-start = ((), (), s32[]{:S(2)}) async-start(), calls=%async_computation.3 | async-start | bytes 1114112 | tf_op jit(solution)/shard_map/all_gather | solution.py:122
  11.2 22.7 %copy-start.20 = (bf16[384,512]{1,0:T(8,128)(2,1)S(1)}, bf16[384,512]{1,0:T(8,128)(2,1)}, u32[]{:S(2)}) copy-start(bf16[384,512]{1,0:T(8,128)(2,1)} %param.14) | copy-start | bytes 1179652
  33.9 0.8 copy-start.8
  35.7 29.1 %copy-start.3 = (bf16[2,384,256]{2,1,0:T(8,128)(2,1)}, bf16[2,384,256]{2,1,0:T(8,128)(2,1)S(1)}, u32[]{:S(2)}) copy-start(bf16[2,384,256]{2,1,0:T(8,128)(2,1)S(1)} %fusion) | copy-start | bytes 1179652
  35.7 8.8 %copy-start.12 = (bf16[384,512]{1,0:T(8,128)(2,1)S(1)}, bf16[384,512]{1,0:T(8,128)(2,1)}, u32[]{:S(2)}) copy-start(bf16[384,512]{1,0:T(8,128)(2,1)} %param.17) | copy-start | bytes 1179652
  35.7 41.7 %collective-permute-start.1 = (bf16[2,384,256]{2,1,0:T(8,128)(2,1)S(1)}, bf16[2,384,256]{2,1,0:T(8,128)(2,1)S(1)}, u32[]{:S(2)}, u32[]{:S(2)}) collective-permute-start(bf16[2,384,256]{2,1,0:T(8,128)(2,1)S(1)} %fusion), channel_id=1, source_target_pairs={{0,16},{16,0},{32,48},{48,32},{64,80},{80,64},{96,112},{112,96},{1... | collective-permute-start | bytes 1179656 | tf_op jit(solution)/shard_map/ppermute | solution.py:16
  38.8 84.2 %all-gather.5.cloned.1.call-start = ((), (), s32[]{:S(2)}) async-start(), calls=%async_computation.4 | async-start | bytes 1114112 | tf_op jit(solution)/shard_map/all_gather | solution.py:122
  39.6 25.7 %collective-permute-start.4 = (bf16[2,2,16,256]{3,2,1,0:T(8,128)(2,1)S(1)}, bf16[2,2,16,256]{3,2,1,0:T(8,128)(2,1)S(1)}, u32[]{:S(2)}, u32[]{:S(2)}) collective-permute-start(bf16[2,2,16,256]{3,2,1,0:T(8,128)(2,1)S(1)} %fusion.65), channel_id=1, source_target_pairs={{0,128},{16,144},{32,160},{48,176},{64,192},{80,208},{96,224},{112... | collective-permute-start | bytes 98312 | tf_op jit(solution)/shard_map/ppermute | solution.py:16
  45.2 37.4 %collective-permute-start = (bf16[384,256]{1,0:T(8,128)(2,1)}, bf16[384,256]{1,0:T(8,128)(2,1)}, u32[]{:S(2)}, u32[]{:S(2)}) collective-permute-start(bf16[384,256]{1,0:T(8,128)(2,1)} %broadcast_select_fusion.5), channel_id=1, source_target_pairs={{0,128},{16,144},{32,160},{48,176},{64,192},{80,208},{96,224},{112... | collective-permute-start | bytes 589832 | tf_op jit(solution)/shard_map/ppermute | solution.py:16
  66.0 10.6 %collective-permute-start.5 = (bf16[2,16,256]{2,1,0:T(8,128)(2,1)S(1)}, bf16[2,16,256]{2,1,0:T(8,128)(2,1)S(1)}, u32[]{:S(2)}, u32[]{:S(2)}) collective-permute-start(bf16[2,16,256]{2,1,0:T(8,128)(2,1)S(1)} %get-tuple-element.57), channel_id=1, source_target_pairs={{0,256},{16,272},{32,288},{48,304},{64,320},{80,336},{96,352},{112... | collective-permute-start | bytes 49160 | tf_op jit(solution)/shard_map/ppermute | solution.py:16
  78.1 13.8 %collective-permute-start.2 = (bf16[2,384,256]{2,1,0:T(8,128)(2,1)S(1)}, bf16[2,384,256]{2,1,0:T(8,128)(2,1)S(1)}, u32[]{:S(2)}, u32[]{:S(2)}) collective-permute-start(bf16[2,384,256]{2,1,0:T(8,128)(2,1)S(1)} %fusion.1), channel_id=1, source_target_pairs={{0,32},{16,48},{32,0},{48,16},{64,96},{80,112},{96,64},{112,80},{1... | collective-permute-start | bytes 1179656 | tf_op jit(solution)/shard_map/ppermute | solution.py:16
  84.3 55.8 %collective-permute-start.8 = (bf16[384,256]{1,0:T(8,128)(2,1)}, bf16[384,256]{1,0:T(8,128)(2,1)}, u32[]{:S(2)}, u32[]{:S(2)}) collective-permute-start(bf16[384,256]{1,0:T(8,128)(2,1)} %broadcast_select_fusion.2), channel_id=1, source_target_pairs={{0,256},{16,272},{32,288},{48,304},{64,320},{80,336},{96,352},{112... | collective-permute-start | bytes 589832 | tf_op jit(solution)/shard_map/ppermute | solution.py:16
  90.6 1.3 copy-start.5
  92.7 15.7 %collective-permute-start.3 = (bf16[2,384,256]{2,1,0:T(8,128)(2,1)S(1)}, bf16[2,384,256]{2,1,0:T(8,128)(2,1)S(1)}, u32[]{:S(2)}, u32[]{:S(2)}) collective-permute-start(bf16[2,384,256]{2,1,0:T(8,128)(2,1)S(1)} %fusion.2), channel_id=1, source_target_pairs={{0,64},{16,80},{32,96},{48,112},{64,0},{80,16},{96,32},{112,48},{1... | collective-permute-start | bytes 1179656 | tf_op jit(solution)/shard_map/ppermute | solution.py:16
  108.4 4.2 %copy-start.18 = (bf16[2,384,256]{2,1,0:T(8,128)(2,1)}, bf16[2,384,256]{2,1,0:T(8,128)(2,1)S(1)}, u32[]{:S(2)}) copy-start(bf16[2,384,256]{2,1,0:T(8,128)(2,1)S(1)} %collective-permute-done.3) | copy-start | bytes 1179652
  109.3 16.0 %collective-permute-start.6 = (bf16[384,256]{1,0:T(8,128)(2,1)}, bf16[384,256]{1,0:T(8,128)(2,1)S(1)}, u32[]{:S(2)}, u32[]{:S(2)}) collective-permute-start(bf16[384,256]{1,0:T(8,128)(2,1)} %fusion.6), channel_id=1, source_target_pairs={{0,128},{16,144},{32,160},{48,176},{64,192},{80,208},{96,224},{112... | collective-permute-start | bytes 589832 | tf_op jit(solution)/shard_map/ppermute | solution.py:16
  123.0 2.3 copy-start
  125.6 14.3 %collective-permute-start.7 = (bf16[384,256]{1,0:T(8,128)(2,1)S(1)}, bf16[384,256]{1,0:T(8,128)(2,1)S(1)}, u32[]{:S(2)}, u32[]{:S(2)}) collective-permute-start(bf16[384,256]{1,0:T(8,128)(2,1)S(1)} %fusion.8), channel_id=1, source_target_pairs={{0,256},{16,272},{32,288},{48,304},{64,320},{80,336},{96,352},{112... | collective-permute-start | bytes 589832 | tf_op jit(solution)/shard_map/ppermute | solution.py:16
  141.3 1.0 copy-start.13
  142.8 44.1 %copy-start.14 = (f32[384,256]{1,0:T(8,128)}, f32[384,256]{1,0:T(8,128)S(1)}, u32[]{:S(2)}) copy-start(f32[384,256]{1,0:T(8,128)S(1)} %get-tuple-element.61) | copy-start | bytes 1179652
  143.5 10.3 %collective-permute-start.9 = (bf16[384,256]{1,0:T(8,128)(2,1)S(1)}, bf16[384,256]{1,0:T(8,128)(2,1)S(1)}, u32[]{:S(2)}, u32[]{:S(2)}) collective-permute-start(bf16[384,256]{1,0:T(8,128)(2,1)S(1)} %fusion.10), channel_id=1, source_target_pairs={{0,256},{16,272},{32,288},{48,304},{64,320},{80,336},{96,352},{112... | collective-permute-start | bytes 589832 | tf_op jit(solution)/shard_map/ppermute | solution.py:16
  154.6 18.2 %collective-permute-start.10 = (bf16[384,256]{1,0:T(8,128)(2,1)S(1)}, bf16[384,256]{1,0:T(8,128)(2,1)S(1)}, u32[]{:S(2)}, u32[]{:S(2)}) collective-permute-start(bf16[384,256]{1,0:T(8,128)(2,1)S(1)} %convolution_convert_fusion.10), channel_id=1, source_target_pairs={{0,64},{16,80},{32,96},{48,112},{64,0},{80,16},{96,32},{112,48},{1... | collective-permute-start | bytes 589832 | tf_op jit(solution)/shard_map/ppermute | solution.py:16
  163.2 18.3 %collective-permute-start.13 = (bf16[384,256]{1,0:T(8,128)(2,1)S(1)}, bf16[384,256]{1,0:T(8,128)(2,1)S(1)}, u32[]{:S(2)}, u32[]{:S(2)}) collective-permute-start(bf16[384,256]{1,0:T(8,128)(2,1)S(1)} %fusion.12), channel_id=1, source_target_pairs={{0,128},{16,144},{32,160},{48,176},{64,192},{80,208},{96,224},{112... | collective-permute-start | bytes 589832 | tf_op jit(solution)/shard_map/ppermute | solution.py:16
  168.8 3.8 %copy-start.19 = (bf16[2,384,256]{2,1,0:T(8,128)(2,1)S(1)}, bf16[2,384,256]{2,1,0:T(8,128)(2,1)}, u32[]{:S(2)}) copy-start(bf16[2,384,256]{2,1,0:T(8,128)(2,1)} %copy-done.18) | copy-start | bytes 1179652
  168.8 33.6 %collective-permute-start.17 = (bf16[8,2,2,2,16,256]{5,4,3,2,1,0:T(8,128)(2,1)S(1)}, bf16[8,2,2,2,16,256]{5,4,3,2,1,0:T(8,128)(2,1)S(1)}, u32[]{:S(2)}, u32[]{:S(2)}) collective-permute-start(bf16[8,2,2,2,16,256]{5,4,3,2,1,0:T(8,128)(2,1)S(1)} %select_bitcast_fusion.2), channel_id=1, source_target_pairs={{0,1},{1,0},{2,3},{3,2},{4,5},{5,4},{6,7},{7,6},{8,9},{9,8},{10,11... | collective-permute-start | bytes 1572872 | tf_op jit(solution)/shard_map/ppermute | solution.py:91
  173.1 28.8 %copy-start.21 = (bf16[1,384,256]{2,1,0:T(8,128)(2,1)}, bf16[1,384,256]{2,1,0:T(8,128)(2,1)S(1)}, u32[]{:S(2)}) copy-start(bf16[1,384,256]{2,1,0:T(8,128)(2,1)S(1)} %fusion.45) | copy-start | bytes 589828
  175.1 11.8 %collective-permute-start.11 = (bf16[384,256]{1,0:T(8,128)(2,1)S(1)}, bf16[384,256]{1,0:T(8,128)(2,1)S(1)}, u32[]{:S(2)}, u32[]{:S(2)}) collective-permute-start(bf16[384,256]{1,0:T(8,128)(2,1)S(1)} %fusion.46), channel_id=1, source_target_pairs={{0,256},{16,272},{32,288},{48,304},{64,320},{80,336},{96,352},{112... | collective-permute-start | bytes 589832 | tf_op jit(solution)/shard_map/ppermute | solution.py:16
  181.8 13.6 %collective-permute-start.14 = (bf16[384,256]{1,0:T(8,128)(2,1)S(1)}, bf16[384,256]{1,0:T(8,128)(2,1)S(1)}, u32[]{:S(2)}, u32[]{:S(2)}) collective-permute-start(bf16[384,256]{1,0:T(8,128)(2,1)S(1)} %convolution_convert_fusion.9), channel_id=1, source_target_pairs={{0,64},{16,80},{32,96},{48,112},{64,0},{80,16},{96,32},{112,48},{1... | collective-permute-start | bytes 589832 | tf_op jit(solution)/shard_map/ppermute | solution.py:16
  187.7 20.1 %collective-permute-start.12 = (bf16[384,256]{1,0:T(8,128)(2,1)}, bf16[384,256]{1,0:T(8,128)(2,1)}, u32[]{:S(2)}, u32[]{:S(2)}) collective-permute-start(bf16[384,256]{1,0:T(8,128)(2,1)} %broadcast_select_fusion.1), channel_id=1, source_target_pairs={{0,128},{16,144},{32,160},{48,176},{64,192},{80,208},{96,224},{112... | collective-permute-start | bytes 589832 | tf_op jit(solution)/shard_map/ppermute | solution.py:16
  195.6 6.3 %copy-start.23 = (bf16[1,384,256]{2,1,0:T(8,128)(2,1)}, bf16[1,384,256]{2,1,0:T(8,128)(2,1)S(1)}, u32[]{:S(2)}) copy-start(bf16[1,384,256]{2,1,0:T(8,128)(2,1)S(1)} %fusion.14) | copy-start | bytes 589828
  196.7 5.2 %copy-start.17 = (bf16[2,384,256]{2,1,0:T(8,128)(2,1)S(1)}, bf16[2,384,256]{2,1,0:T(8,128)(2,1)}, u32[]{:S(2)}) copy-start(bf16[2,384,256]{2,1,0:T(8,128)(2,1)} %copy-done.16) | copy-start | bytes 1179652
  196.7 13.9 %collective-permute-start.15 = (bf16[2,384,256]{2,1,0:T(8,128)(2,1)}, bf16[2,384,256]{2,1,0:T(8,128)(2,1)}, u32[]{:S(2)}, u32[]{:S(2)}) collective-permute-start(bf16[2,384,256]{2,1,0:T(8,128)(2,1)} %convolution_convert_fusion.2), channel_id=1, source_target_pairs={{0,32},{16,48},{32,0},{48,16},{64,96},{80,112},{96,64},{112,80},{1... | collective-permute-start | bytes 1179656 | tf_op jit(solution)/shard_map/ppermute | solution.py:16
  203.4 18.9 %all-to-all-start = ((bf16[8,2,2,2,16,256]{5,4,3,2,1,0:T(8,128)(2,1)}), bf16[8,2,2,2,16,256]{5,4,3,2,1,0:T(8,128)(2,1)}, u32[]{:S(2)}, u32[]{:S(2)}) async-start(bf16[8,2,2,2,16,256]{5,4,3,2,1,0:T(8,128)(2,1)} %fusion.16), calls=%async_computation | async-start | bytes 1048576 | tf_op jit(solution)/shard_map/all_to_all | solution.py:94
  207.6 1.0 copy-start.15
  209.8 1.0 copy-start.22
  209.8 1.2 copy-start.24
  212.6 19.6 %collective-permute-start.16 = (bf16[2,384,256]{2,1,0:T(8,128)(2,1)S(1)}, bf16[2,384,256]{2,1,0:T(8,128)(2,1)}, u32[]{:S(2)}, u32[]{:S(2)}) collective-permute-start(bf16[2,384,256]{2,1,0:T(8,128)(2,1)S(1)} %convolution_convert_fusion.1), channel_id=1, source_target_pairs={{0,16},{16,0},{32,48},{48,32},{64,80},{80,64},{96,112},{112,96},{1... | collective-permute-start | bytes 1179656 | tf_op jit(solution)/shard_map/ppermute | solution.py:16
  225.3 6.2 %copy-start.4 = (bf16[2,384,256]{2,1,0:T(8,128)(2,1)S(1)}, bf16[2,384,256]{2,1,0:T(8,128)(2,1)}, u32[]{:S(2)}) copy-start(bf16[2,384,256]{2,1,0:T(8,128)(2,1)} %copy-done.3) | copy-start | bytes 1179652
  225.3 6.5 %copy-start.11 = (bf16[2,384,256]{2,1,0:T(8,128)(2,1)S(1)}, bf16[2,384,256]{2,1,0:T(8,128)(2,1)}, u32[]{:S(2)}) copy-start(bf16[2,384,256]{2,1,0:T(8,128)(2,1)} %copy-done.10) | copy-start | bytes 1179652
  225.3 8.2 %collective-permute-start.18 = (bf16[8,2,2,2,16,256]{5,4,3,2,1,0:T(8,128)(2,1)S(1)}, bf16[8,2,2,2,16,256]{5,4,3,2,1,0:T(8,128)(2,1)S(1)}, u32[]{:S(2)}, u32[]{:S(2)}) collective-permute-start(bf16[8,2,2,2,16,256]{5,4,3,2,1,0:T(8,128)(2,1)S(1)} %select_bitcast_fusion.1), channel_id=1, source_target_pairs={{0,1},{1,0},{2,3},{3,2},{4,5},{5,4},{6,7},{7,6},{8,9},{9,8},{10,11... | collective-permute-start | bytes 1572872 | tf_op jit(solution)/shard_map/ppermute | solution.py:91
  234.5 21.5 %all-to-all-start.1 = ((bf16[8,2,2,2,16,256]{5,4,3,2,1,0:T(8,128)(2,1)}), bf16[8,2,2,2,16,256]{5,4,3,2,1,0:T(8,128)(2,1)S(1)}, u32[]{:S(2)}, u32[]{:S(2)}) async-start(bf16[8,2,2,2,16,256]{5,4,3,2,1,0:T(8,128)(2,1)} %fusion.18), calls=%async_computation.1 | async-start | bytes 1048576 | tf_op jit(solution)/shard_map/all_to_all | solution.py:94
  238.4 0.9 copy-start.7
  238.4 1.0 copy-start.9
  239.4 1.0 copy-start.2
  258.0 10.2 %collective-permute-start.19 = (bf16[8,2,2,2,16,256]{5,4,3,2,1,0:T(8,128)(2,1)S(1)}, bf16[8,2,2,2,16,256]{5,4,3,2,1,0:T(8,128)(2,1)S(1)}, u32[]{:S(2)}, u32[]{:S(2)}) collective-permute-start(bf16[8,2,2,2,16,256]{5,4,3,2,1,0:T(8,128)(2,1)S(1)} %select_bitcast_fusion), channel_id=1, source_target_pairs={{0,1},{1,0},{2,3},{3,2},{4,5},{5,4},{6,7},{7,6},{8,9},{9,8},{10,11... | collective-permute-start | bytes 1572872 | tf_op jit(solution)/shard_map/ppermute | solution.py:91
  260.7 12.0 %collective-permute-start.20 = (f32[2,16,256]{2,1,0:T(8,128)S(1)}, f32[2,16,256]{2,1,0:T(8,128)S(1)}, u32[]{:S(2)}, u32[]{:S(2)}) collective-permute-start(f32[2,16,256]{2,1,0:T(8,128)S(1)} %get-tuple-element.48), channel_id=1, source_target_pairs={{0,256},{16,272},{32,288},{48,304},{64,320},{80,336},{96,352},{112... | collective-permute-start | bytes 98312 | tf_op jit(solution)/shard_map/ppermute | solution.py:16
  269.2 21.4 %all-to-all-start.2 = ((bf16[8,2,2,2,16,256]{5,4,3,2,1,0:T(8,128)(2,1)}), bf16[8,2,2,2,16,256]{5,4,3,2,1,0:T(8,128)(2,1)S(1)}, u32[]{:S(2)}, u32[]{:S(2)}) async-start(bf16[8,2,2,2,16,256]{5,4,3,2,1,0:T(8,128)(2,1)} %fusion.20), calls=%async_computation.2 | async-start | bytes 1048576 | tf_op jit(solution)/shard_map/all_to_all | solution.py:94
  272.7 7.3 %collective-permute-start.21 = (f32[2,2,16,256]{3,2,1,0:T(8,128)S(1)}, f32[2,2,16,256]{3,2,1,0:T(8,128)S(1)}, u32[]{:S(2)}, u32[]{:S(2)}) collective-permute-start(f32[2,2,16,256]{3,2,1,0:T(8,128)S(1)} %fusion.64), channel_id=1, source_target_pairs={{0,128},{16,144},{32,160},{48,176},{64,192},{80,208},{96,224},{112... | collective-permute-start | bytes 196616 | tf_op jit(solution)/shard_map/ppermute | solution.py:16
  (11 other events, 7.6 us)
Sparse Core Ops, SparseCore 0:
  38.9 41.7 all-gather.2
  82.9 40.0 all-gather.4

commit v4 on v3

--- a/solution.py
+++ b/solution.py
@@ -6,8 +6,6 @@
 
 
 SECTIONS = 6
-GATHERS = ((0,), (1,), (2, 3), (4, 5))
-SCATTERS = ((4, 5), (2, 3), (0, 1))
 
 
 def flip(value, bit):
@@ -35,6 +33,15 @@
 
 def dot_rows(left, right):
     return jnp.einsum("...tk,...tl->...kl", left, right, preferred_element_type=jnp.float32).astype(jnp.bfloat16)
+
+
+def pack(small, large):
+    return jnp.concatenate([small.reshape(-1, small.shape[-1]), large])
+
+
+def unpack(packed, like):
+    rows = like.size // like.shape[-1]
+    return packed[:rows].reshape(like.shape), packed[rows:]
 
 
 def block_tables():
@@ -80,7 +87,7 @@
     return jnp.moveaxis(half, 3, 0)
 
 
-def scatter_sum(terms, waits):
+def chip_sum(terms, waits):
     count, both, per_dev, depth, width = terms.shape
     size = lax.axis_size("tok")
     core = lax.axis_index("tok") & 1
@@ -89,7 +96,11 @@
     if waits is not None:
         give = after(give, waits)
     came = lax.ppermute(give, "tok", [(source, source ^ 1) for source in range(size)])
-    chip = (core_half(terms, core).astype(jnp.float32) + came.astype(jnp.float32)).astype(jnp.bfloat16)
+    return (core_half(terms, core).astype(jnp.float32) + came.astype(jnp.float32)).astype(jnp.bfloat16)
+
+
+def all_sum(chip):
+    size = lax.axis_size("tok")
     groups = [list(range(c, size, 2)) for c in range(2)]
     chip = lax.all_to_all(chip, "tok", 0, 0, axis_index_groups=groups)
     return jnp.sum(chip.astype(jnp.float32), axis=0)
@@ -107,33 +118,33 @@
 
     shards = jnp.swapaxes(weights, 1, 2)
     part = shards[4:6]
+    left, right = halves(cotangent)
     keep = jnp.where(low, part[:, :, 1], part[:, :, 0])
-    came = flip(jnp.where(low, part[:, :, 0], part[:, :, 1]), 3)
+    cot_keep = jnp.where(low, right, left)
+    send = jnp.where(low, part[:, :, 0], part[:, :, 1])
+    came, cot_came = unpack(flip(pack(send, jnp.where(low, left, right)), 3), send)
     row0, row1 = jnp.where(same, keep, came), jnp.where(same, came, keep)
+    cotan0 = jnp.where(same, cot_keep, cot_came)
+    cot_send = jnp.where(same, cot_came, cot_keep)
     fourth = jnp.stack([row0[0], row1[0]], 1)
-    fifth = jnp.stack([row0[1], flip(row1[1], 4)], 1)
-    shards = [turned(shards[:4], low, 2), jnp.stack([fourth, fifth])]
-
-    full = [None] * SECTIONS
-    for group in GATHERS:
-        source, base = (shards[0], 0) if group[0] < 4 else (shards[1], 4)
-        begin, end = group[0] - base, group[-1] + 1 - base
-        ordered = turned(source[begin:end], chosen[group[0] : group[-1] + 1], 1)
-        gathered = lax.all_gather(ordered, "tok", axis=3, tiled=True)
-        for place, section in enumerate(group):
-            full[section] = gathered[place]
-
-    left, right = halves(cotangent)
-    came = flip(jnp.where(low, left, right), 3)
-    keep = jnp.where(low, right, left)
-    cotan0 = jnp.where(same, keep, came)
-    cotan1 = flip(jnp.where(same, came, keep), 4)
+
+    early = turned(turned(shards[:4], low, 2), chosen[:4], 1)
+    full = list(lax.all_gather(early[:1], "tok", axis=3, tiled=True))
+    full += list(lax.all_gather(early[1:], "tok", axis=3, tiled=True))
 
     left, right = halves(activations)
     value = jnp.stack([jnp.where(low, right, left), jnp.where(low, left, right)])
-    inputs = []
-    for section in range(4):
-        other = value[::-1] if section == 0 else flip(value, section - 1)
+    other = value[::-1]
+    inputs = [(value, other)]
+    value = (dot(value, full[0][0]) + dot(other, full[0][1])).astype(bf16)
+
+    came, cotan1 = unpack(flip(pack(after(row1[1], value), cot_send), 4), row1[1])
+    fifth = jnp.stack([row0[1], came], 1)
+    late = turned(jnp.stack([fourth, fifth]), chosen[4:], 1)
+    full += list(lax.all_gather(late, "tok", axis=3, tiled=True))
+
+    for section in range(1, 4):
+        other = flip(value, section - 1)
         inputs.append((value, other))
         own_w, other_w = full[section][0], full[section][1]
         if section < 3:
@@ -167,44 +178,34 @@
             [jnp.stack([dot_rows(part, grad) for grad in grads]) for part in inputs[section]]
         )
         grads = [kept, back]
-    sums = [None] * SECTIONS
-    waits = None
+    chip = chip_sum(jnp.stack(terms[4:]), None)
+    grad = after(jnp.stack(grads), chip)
+    sums45 = all_sum(chip)
     for section in (3, 2, 1, 0):
         own_w, other_w = full[section][0], full[section][1]
-        if section == 3:
-            back = [flip(dot_back(grads[r], other_w[r]).astype(bf16), 2) for r in range(2)]
-            kept = [dot_back(grads[r], own_w[r]) for r in range(2)]
-            terms[section] = jnp.stack(
-                [jnp.stack([dot_rows(part[r], grads[r]) for r in range(2)]) for part in inputs[section]]
-            )
-            grad = jnp.stack([(kept[r] + back[r].astype(jnp.float32)).astype(bf16) for r in range(2)])
-        else:
-            if section == 2:
-                late = grad
-            sent = dot_back(grad, other_w).astype(bf16)
-            back = sent[::-1] if section == 0 else flip(sent, section - 1)
-            terms[section] = jnp.stack([dot_rows(part, grad) for part in inputs[section]])
-            grad = (dot_back(grad, own_w) + back.astype(jnp.float32)).astype(bf16)
-        for group in SCATTERS:
-            if section == min(group) or (section == 3 and group == (4, 5)):
-                summed = scatter_sum(jnp.stack([terms[s] for s in group]), waits)
-                waits = summed
-                for place, s in enumerate(group):
-                    sums[s] = summed[place]
-
-    came = flip(after(results[1], late), 4)
-    keep, send = jnp.where(same, results[0], came), jnp.where(same, came, results[0])
-    came = flip(send, 3)
-    result = jnp.concatenate([jnp.where(low, came, keep), jnp.where(low, keep, came)], axis=1)
+        sent = dot_back(grad, other_w).astype(bf16)
+        back = sent[::-1] if section == 0 else flip(sent, section - 1)
+        terms[section] = jnp.stack([dot_rows(part, grad) for part in inputs[section]])
+        grad = (dot_back(grad, own_w) + back.astype(jnp.float32)).astype(bf16)
+        if section == 2:
+            chip = chip_sum(jnp.stack(terms[2:4]), None)
+            grad = after(after(grad, chip), sums45)
+            sums23 = all_sum(chip)
+        if section == 1:
+            near_end = grad
+    sums01 = all_sum(chip_sum(jnp.stack(terms[:2]), sums23))
     input_grad = jnp.concatenate([jnp.where(low, grad[1], grad[0]), jnp.where(low, grad[0], grad[1])], axis=1)
 
-    first = turned(turned(jnp.stack(sums[:4]), chosen[:4], 1), low, 2)
-    last = turned(jnp.stack(sums[4:]), chosen[4:], 1)
+    first = turned(turned(jnp.concatenate([sums01, sums23]), chosen[:4], 1), low, 2)
+    last = turned(sums45, chosen[4:], 1).astype(bf16)
+    came, out_came = unpack(flip(pack(after(last[1, :, 1], near_end), results[1]), 4), last[1, :, 1])
     row0 = last[:, :, 0]
-    row1 = jnp.stack([last[0, :, 1], flip(last[1, :, 1], 4)])
+    row1 = jnp.stack([last[0, :, 1], came])
     keep, send = jnp.where(same, row0, row1), jnp.where(same, row1, row0)
-    came = flip(send, 3)
-    last = jnp.stack([jnp.where(low, came, keep), jnp.where(low, keep, came)], 2)
+    out_keep, out_send = jnp.where(same, results[0], out_came), jnp.where(same, out_came, results[0])
+    came, out_came = unpack(flip(pack(send, out_send), 3), send)
+    last = jnp.stack([jnp.where(low, came, keep), jnp.where(low, keep, came)], 2).astype(jnp.float32)
+    result = jnp.concatenate([jnp.where(low, out_came, out_keep), jnp.where(low, out_keep, out_came)], axis=1)
     weight_grad = jnp.swapaxes(jnp.concatenate([first, last]), 1, 2)
     return result, input_grad, weight_grad
 

time: 300 us -> 277 us (0.923)
  blocking collectives: 40.1 us -> 20.1 us
  matrix products: 20.7 us -> 34 us
  starting transfers between devices: 118 us -> 106 us
  local copies, waits for them, and re-layouts: 13.4 us -> 8.79 us
  waiting for transfers between devices: 71.9 us -> 67.9 us
  between operations: 19.1 us -> 22.9 us
    ppermute x19 -> x14, starting transfers between devices: 94.6 us -> 69 us  [flip(): return lax.ppermute(value, 'blk', pairs)]
    all_to_all x3, waiting for transfers between devices: 33 us -> 11.3 us  [all_sum(): chip = lax.all_to_all(chip, 'tok', 0, 0, axis_index_groups=groups)]
    ppermute x19 -> x14, waiting for transfers between devices: 28.6 us -> 48.8 us  [flip(): return lax.ppermute(value, 'blk', pairs)]
    all_gather x2 -> x1, blocking collectives: 40.1 us -> 20.1 us  [body(): full = list(lax.all_gather(early[:1], 'tok', axis=3, tiled=True))]
    ppermute x3, starting transfers between devices: 12.1 us -> 22.4 us  [chip_sum(): lax.ppermute(give, 'tok', [(source, source ^ 1) for source in range(size)])]
    unnamed x67 -> x53, local copies, waits for them, and re-layouts: 10.8 us -> 3.55 us
    dot_general x18, matrix products: 7.97 us -> 13.6 us  [dot(): jnp.einsum('...tk,...kl->...tl', left, right, preferred_element_type=jnp....]
    dot_general x18 -> x16, matrix products: 5.22 us -> 10.6 us  [dot_rows(): jnp.einsum('...tk,...tl->...kl', left, right, preferred_element_type=jnp....]
  transfers between devices with their start and end apart: 27 -> 22, of which waited for: 11 -> 14; matrix products, arithmetic and copies ran while one was open for 11% -> 15% of each run, Pallas kernels for 0% -> 0%
where the time goes in v4:
time: 277 us; the launch traced here: 276 us
  starting transfers between devices  106 us (38%)
  waiting for transfers between devices  67.9 us (25%)
  matrix products  34 us (12%)
  between operations  22.9 us (8%)
  blocking collectives  20.1 us (7%)
  other arithmetic  15.6 us (6%)
  local copies, waits for them, and re-layouts  8.79 us (3%)
    ppermute x14, starting transfers between devices, flip(): return lax.ppermute(value, 'blk', pairs)  69 us
    ppermute x14, waiting for transfers between devices, flip(): return lax.ppermute(value, 'blk', pairs)  48.8 us
    ppermute x3, starting transfers between devices, chip_sum(): lax.ppermute(give, 'tok', [(source, source ^ 1) for source in range(size)])  22.4 us
    all_gather x1, blocking collectives, body(): full = list(lax.all_gather(early[:1], 'tok', axis=3, tiled=True))  20.1 us
    all_to_all x3, starting transfers between devices, all_sum(): chip = lax.all_to_all(chip, 'tok', 0, 0, axis_index_groups=groups)  15 us
    dot_general x18, matrix products, dot(): jnp.einsum('...tk,...kl->...tl', left, right, preferred_element_type=jnp....  13.6 us
    all_to_all x3, waiting for transfers between devices, all_sum(): chip = lax.all_to_all(chip, 'tok', 0, 0, axis_index_groups=groups)  11.3 us
    dot_general x16, matrix products, dot_rows(): jnp.einsum('...tk,...tl->...kl', left, right, preferred_element_type=jnp....  10.6 us
  transfers between devices with their start and end apart: 22, of which 14 were waited for; matrix products, arithmetic and copies ran while one was open for 15% of the time, Pallas kernels for 0%

profile of v4, /device:TPU:1, one launch (start us, length us, event | category | flops | bytes accessed | tf_op | source)
XLA Modules:
  0.0 275.6 jit_solution(7660779623488372473)
XLA Ops:
  13.6 6.6 %collective-permute-start.3 = (bf16[448,256]{1,0:T(8,128)(2,1)S(1)}, bf16[448,256]{1,0:T(8,128)(2,1)S(1)}, u32[]{:S(2)}, u32[]{:S(2)}) collective-permute-start(bf16[448,256]{1,0:T(8,128)(2,1)S(1)} %pad_maximum_fusion.3), channel_id=1, source_target_pairs={{0,128},{16,144},{32,160},{48,176},{64,192},{80,208},{96,224},{112... | collective-permute-start | bytes 688136 | tf_op jit(solution)/shard_map/ppermute | solution.py:14
  20.4 20.1 %all_gather.9 = bf16[1,2,2,256,256]{4,3,2,1,0:T(8,128)(2,1)S(1)} all-gather(bf16[1,2,2,16,256]{4,3,2,1,0:T(8,128)(2,1)S(1)} %pad_maximum_fusion.14), channel_id=1, replica_groups=mesh['blk'=32,'tok'=16] {'tok'}, dimensions={3}, use_global_device_ids=true | all-gather | bytes 557056 | tf_op jit(solution)/shard_map/all_gather | solution.py:132
  41.0 3.3 %collective-permute-start = (bf16[2,384,256]{2,1,0:T(8,128)(2,1)S(1)}, bf16[2,384,256]{2,1,0:T(8,128)(2,1)}, u32[]{:S(2)}, u32[]{:S(2)}) collective-permute-start(bf16[2,384,256]{2,1,0:T(8,128)(2,1)S(1)} %fusion), channel_id=1, source_target_pairs={{0,16},{16,0},{32,48},{48,32},{64,80},{80,64},{96,112},{112,96},{1... | collective-permute-start | bytes 1179656 | tf_op jit(solution)/shard_map/ppermute | solution.py:14
  47.2 8.9 %collective-permute-start.4 = (bf16[416,256]{1,0:T(8,128)(2,1)S(1)}, bf16[416,256]{1,0:T(8,128)(2,1)S(1)}, u32[]{:S(2)}, u32[]{:S(2)}) collective-permute-start(bf16[416,256]{1,0:T(8,128)(2,1)S(1)} %pad_maximum_fusion.5), channel_id=1, source_target_pairs={{0,256},{16,272},{32,288},{48,304},{64,320},{80,336},{96,352},{112... | collective-permute-start | bytes 638984 | tf_op jit(solution)/shard_map/ppermute | solution.py:14
  56.2 7.2 %collective-permute-done.4 = bf16[416,256]{1,0:T(8,128)(2,1)S(1)} collective-permute-done((bf16[416,256]{1,0:T(8,128)(2,1)S(1)}, bf16[416,256]{1,0:T(8,128)(2,1)S(1)}, u32[]{:S(2)}, u32[]{:S(2)}) %collective-permute-start.4) | collective-permute-done | bytes 213024 | tf_op jit(solution)/shard_map/ppermute | solution.py:14
  64.1 1.3 fusion.45
  65.5 1.3 fusion.1
  66.8 4.4 %collective-permute-start.1 = (bf16[2,384,256]{2,1,0:T(8,128)(2,1)S(1)}, bf16[2,384,256]{2,1,0:T(8,128)(2,1)}, u32[]{:S(2)}, u32[]{:S(2)}) collective-permute-start(bf16[2,384,256]{2,1,0:T(8,128)(2,1)S(1)} %fusion.1), channel_id=1, source_target_pairs={{0,32},{16,48},{32,0},{48,16},{64,96},{80,112},{96,64},{112,80},{1... | collective-permute-start | bytes 1179656 | tf_op jit(solution)/shard_map/ppermute | solution.py:14
  71.5 8.3 %collective-permute-done.1 = bf16[2,384,256]{2,1,0:T(8,128)(2,1)} collective-permute-done((bf16[2,384,256]{2,1,0:T(8,128)(2,1)S(1)}, bf16[2,384,256]{2,1,0:T(8,128)(2,1)}, u32[]{:S(2)}, u32[]{:S(2)}) %collective-permute-start.1) | collective-permute-done | bytes 393248 | tf_op jit(solution)/shard_map/ppermute | solution.py:14
  79.8 1.3 fusion.2
  81.1 6.3 %collective-permute-start.2 = (bf16[2,384,256]{2,1,0:T(8,128)(2,1)S(1)}, bf16[2,384,256]{2,1,0:T(8,128)(2,1)S(1)}, u32[]{:S(2)}, u32[]{:S(2)}) collective-permute-start(bf16[2,384,256]{2,1,0:T(8,128)(2,1)S(1)} %fusion.2), channel_id=1, source_target_pairs={{0,64},{16,80},{32,96},{48,112},{64,0},{80,16},{96,32},{112,48},{1... | collective-permute-start | bytes 1179656 | tf_op jit(solution)/shard_map/ppermute | solution.py:14
  87.8 7.5 %collective-permute-done.2 = bf16[2,384,256]{2,1,0:T(8,128)(2,1)S(1)} collective-permute-done((bf16[2,384,256]{2,1,0:T(8,128)(2,1)S(1)}, bf16[2,384,256]{2,1,0:T(8,128)(2,1)S(1)}, u32[]{:S(2)}, u32[]{:S(2)}) %collective-permute-start.2) | collective-permute-done | bytes 393248 | tf_op jit(solution)/shard_map/ppermute | solution.py:14
  96.2 1.9 collective-permute-start.5
  98.3 7.8 %all-gather.5.cloned.1.call-done = bf16[2,2,2,256,256]{4,3,1,2,0:T(8,128)(2,1)} async-done(((bf16[2,2,2,16,256]{4,3,1,2,0:T(8,128)(2,1)}), bf16[2,2,2,256,256]{4,3,1,2,0:T(8,128)(2,1)}) %all-gather.5.cloned.1.call-update) | async-done | bytes 1048592 | tf_op jit(solution)/shard_map/all_gather | solution.py:144
  106.1 1.2 fusion.52
  109.3 1.2 fusion.11
  110.5 7.5 %collective-permute-start.6 = (bf16[384,256]{1,0:T(8,128)(2,1)S(1)}, bf16[384,256]{1,0:T(8,128)(2,1)S(1)}, u32[]{:S(2)}, u32[]{:S(2)}) collective-permute-start(bf16[384,256]{1,0:T(8,128)(2,1)S(1)} %fusion.11), channel_id=1, source_target_pairs={{0,256},{16,272},{32,288},{48,304},{64,320},{80,336},{96,352},{112... | collective-permute-start | bytes 589832 | tf_op jit(solution)/shard_map/ppermute | solution.py:14
  119.7 2.1 collective-permute-done.6
  121.8 1.2 fusion.25
  125.2 7.1 %collective-permute-start.7 = (bf16[384,256]{1,0:T(8,128)(2,1)S(1)}, bf16[384,256]{1,0:T(8,128)(2,1)S(1)}, u32[]{:S(2)}, u32[]{:S(2)}) collective-permute-start(bf16[384,256]{1,0:T(8,128)(2,1)S(1)} %fusion.13), channel_id=1, source_target_pairs={{0,256},{16,272},{32,288},{48,304},{64,320},{80,336},{96,352},{112... | collective-permute-start | bytes 589832 | tf_op jit(solution)/shard_map/ppermute | solution.py:14
  137.3 12.5 %collective-permute-start.8 = (bf16[8,2,2,2,16,256]{5,4,3,2,1,0:T(8,128)(2,1)S(1)}, bf16[8,2,2,2,16,256]{5,4,3,2,1,0:T(8,128)(2,1)S(1)}, u32[]{:S(2)}, u32[]{:S(2)}) collective-permute-start(bf16[8,2,2,2,16,256]{5,4,3,2,1,0:T(8,128)(2,1)S(1)} %select_bitcast_fusion.2), channel_id=1, source_target_pairs={{0,1},{1,0},{2,3},{3,2},{4,5},{5,4},{6,7},{7,6},{8,9},{9,8},{10,11... | collective-permute-start | bytes 1572872 | tf_op jit(solution)/shard_map/ppermute | solution.py:98
  151.0 2.2 collective-permute-start.9
  155.0 5.5 %all-to-all-start = ((bf16[8,2,2,2,16,256]{5,4,3,2,1,0:T(8,128)(2,1)}), bf16[8,2,2,2,16,256]{5,4,3,2,1,0:T(8,128)(2,1)}, u32[]{:S(2)}, u32[]{:S(2)}) async-start(bf16[8,2,2,2,16,256]{5,4,3,2,1,0:T(8,128)(2,1)} %copy-done.4), calls=%async_computation | async-start | bytes 1048576 | tf_op jit(solution)/shard_map/all_to_all | solution.py:105
  161.8 2.3 collective-permute-done.9
  164.0 1.3 convolution_convert_fusion.3
  165.3 1.9 collective-permute-start.10
  167.3 1.3 convolution_convert_fusion.9
  168.6 1.3 convolution_convert_fusion.8
  169.9 7.7 %collective-permute-done.10 = bf16[2,384,256]{2,1,0:T(8,128)(2,1)S(1)} collective-permute-done((bf16[2,384,256]{2,1,0:T(8,128)(2,1)S(1)}, bf16[2,384,256]{2,1,0:T(8,128)(2,1)S(1)}, u32[]{:S(2)}, u32[]{:S(2)}) %collective-permute-start.10) | collective-permute-done | bytes 393248 | tf_op jit(solution)/shard_map/ppermute | solution.py:14
  177.6 1.2 fusion.3
  179.2 1.3 convolution_convert_fusion.10
  180.8 3.1 %collective-permute-start.11 = (bf16[8,2,2,2,16,256]{5,4,3,2,1,0:T(8,128)(2,1)S(1)}, bf16[8,2,2,2,16,256]{5,4,3,2,1,0:T(8,128)(2,1)S(1)}, u32[]{:S(2)}, u32[]{:S(2)}) collective-permute-start(bf16[8,2,2,2,16,256]{5,4,3,2,1,0:T(8,128)(2,1)S(1)} %select_bitcast_fusion.1), channel_id=1, source_target_pairs={{0,1},{1,0},{2,3},{3,2},{4,5},{5,4},{6,7},{7,6},{8,9},{9,8},{10,11... | collective-permute-start | bytes 1572872 | tf_op jit(solution)/shard_map/ppermute | solution.py:98
  184.2 4.7 %collective-permute-start.12 = (bf16[2,384,256]{2,1,0:T(8,128)(2,1)S(1)}, bf16[2,384,256]{2,1,0:T(8,128)(2,1)S(1)}, u32[]{:S(2)}, u32[]{:S(2)}) collective-permute-start(bf16[2,384,256]{2,1,0:T(8,128)(2,1)S(1)} %convolution_convert_fusion.2), channel_id=1, source_target_pairs={{0,32},{16,48},{32,0},{48,16},{64,96},{80,112},{96,64},{112,80},{1... | collective-permute-start | bytes 1179656 | tf_op jit(solution)/shard_map/ppermute | solution.py:14
  195.4 3.1 %collective-permute-done.12 = bf16[2,384,256]{2,1,0:T(8,128)(2,1)S(1)} collective-permute-done((bf16[2,384,256]{2,1,0:T(8,128)(2,1)S(1)}, bf16[2,384,256]{2,1,0:T(8,128)(2,1)S(1)}, u32[]{:S(2)}, u32[]{:S(2)}) %collective-permute-start.12) | collective-permute-done | bytes 393248 | tf_op jit(solution)/shard_map/ppermute | solution.py:14
  198.5 1.3 fusion.7
  200.1 1.2 convolution_convert_fusion.1
  201.4 3.0 %collective-permute-start.13 = (bf16[2,384,256]{2,1,0:T(8,128)(2,1)S(1)}, bf16[2,384,256]{2,1,0:T(8,128)(2,1)S(1)}, u32[]{:S(2)}, u32[]{:S(2)}) collective-permute-start(bf16[2,384,256]{2,1,0:T(8,128)(2,1)S(1)} %convolution_convert_fusion.1), channel_id=1, source_target_pairs={{0,16},{16,0},{32,48},{48,32},{64,80},{80,64},{96,112},{112,96},{1... | collective-permute-start | bytes 1179656 | tf_op jit(solution)/shard_map/ppermute | solution.py:14
  204.5 4.5 %all-to-all-start.1 = ((bf16[8,2,2,2,16,256]{5,4,3,2,1,0:T(8,128)(2,1)}), bf16[8,2,2,2,16,256]{5,4,3,2,1,0:T(8,128)(2,1)S(1)}, u32[]{:S(2)}, u32[]{:S(2)}) async-start(bf16[8,2,2,2,16,256]{5,4,3,2,1,0:T(8,128)(2,1)} %fusion.20), calls=%async_computation.1 | async-start | bytes 1048576 | tf_op jit(solution)/shard_map/all_to_all | solution.py:105
  209.6 1.3 convolution_convert_fusion.4
  210.9 2.2 collective-permute-done.13
  213.1 1.2 add_convert_fusion
  217.6 6.9 %collective-permute-start.14 = (bf16[416,256]{1,0:T(8,128)(2,1)}, bf16[416,256]{1,0:T(8,128)(2,1)}, u32[]{:S(2)}, u32[]{:S(2)}) collective-permute-start(bf16[416,256]{1,0:T(8,128)(2,1)} %pad_maximum_fusion.6), channel_id=1, source_target_pairs={{0,256},{16,272},{32,288},{48,304},{64,320},{80,336},{96,352},{112... | collective-permute-start | bytes 638984 | tf_op jit(solution)/shard_map/ppermute | solution.py:14
  225.5 3.3 %collective-permute-done.14 = bf16[416,256]{1,0:T(8,128)(2,1)} collective-permute-done((bf16[416,256]{1,0:T(8,128)(2,1)}, bf16[416,256]{1,0:T(8,128)(2,1)}, u32[]{:S(2)}, u32[]{:S(2)}) %collective-permute-start.14) | collective-permute-done | bytes 213024 | tf_op jit(solution)/shard_map/ppermute | solution.py:14
  231.4 6.8 %collective-permute-start.16 = (bf16[8,2,2,2,16,256]{5,4,3,2,1,0:T(8,128)(2,1)S(1)}, bf16[8,2,2,2,16,256]{5,4,3,2,1,0:T(8,128)(2,1)S(1)}, u32[]{:S(2)}, u32[]{:S(2)}) collective-permute-start(bf16[8,2,2,2,16,256]{5,4,3,2,1,0:T(8,128)(2,1)S(1)} %select_bitcast_fusion), channel_id=1, source_target_pairs={{0,1},{1,0},{2,3},{3,2},{4,5},{5,4},{6,7},{7,6},{8,9},{9,8},{10,11... | collective-permute-start | bytes 1572872 | tf_op jit(solution)/shard_map/ppermute | solution.py:98
  239.4 4.4 %collective-permute-start.15 = (bf16[448,256]{1,0:T(8,128)(2,1)S(1)}, bf16[448,256]{1,0:T(8,128)(2,1)S(1)}, u32[]{:S(2)}, u32[]{:S(2)}) collective-permute-start(bf16[448,256]{1,0:T(8,128)(2,1)S(1)} %pad_maximum_fusion.4), channel_id=1, source_target_pairs={{0,128},{16,144},{32,160},{48,176},{64,192},{80,208},{96,224},{112... | collective-permute-start | bytes 688136 | tf_op jit(solution)/shard_map/ppermute | solution.py:14
  244.8 5.0 %all-to-all-start.2 = ((bf16[8,2,2,2,16,256]{5,4,3,2,1,0:T(8,128)(2,1)}), bf16[8,2,2,2,16,256]{5,4,3,2,1,0:T(8,128)(2,1)S(1)}, u32[]{:S(2)}, u32[]{:S(2)}) async-start(bf16[8,2,2,2,16,256]{5,4,3,2,1,0:T(8,128)(2,1)} %fusion.18), calls=%async_computation.2 | async-start | bytes 1048576 | tf_op jit(solution)/shard_map/all_to_all | solution.py:105
  250.9 3.7 %collective-permute-done.15 = bf16[448,256]{1,0:T(8,128)(2,1)S(1)} collective-permute-done((bf16[448,256]{1,0:T(8,128)(2,1)S(1)}, bf16[448,256]{1,0:T(8,128)(2,1)S(1)}, u32[]{:S(2)}, u32[]{:S(2)}) %collective-permute-start.15) | collective-permute-done | bytes 229408 | tf_op jit(solution)/shard_map/ppermute | solution.py:14
  256.5 11.3 %all-to-all-done.2 = bf16[8,2,2,2,16,256]{5,4,3,2,1,0:T(8,128)(2,1)S(1)} async-done(((bf16[8,2,2,2,16,256]{5,4,3,2,1,0:T(8,128)(2,1)}), bf16[8,2,2,2,16,256]{5,4,3,2,1,0:T(8,128)(2,1)S(1)}, u32[]{:S(2)}, u32[]{:S(2)}) %all-to-all-start.2) | async-done | bytes 524320 | tf_op jit(solution)/shard_map/all_to_all | solution.py:105
  (172 shorter events, 40.9 us)
Async XLA Ops:
  7.2 6.4 %copy-start.11 = (bf16[384,512]{1,0:T(8,128)(2,1)S(1)}, bf16[384,512]{1,0:T(8,128)(2,1)}, u32[]{:S(2)}) copy-start(bf16[384,512]{1,0:T(8,128)(2,1)} %param.17) | copy-start | bytes 1179652
  7.2 13.1 %copy-start.16 = (bf16[384,512]{1,0:T(8,128)(2,1)S(1)}, bf16[384,512]{1,0:T(8,128)(2,1)}, u32[]{:S(2)}) copy-start(bf16[384,512]{1,0:T(8,128)(2,1)} %param.14) | copy-start | bytes 1179652
  7.2 56.9 %all-gather.3.cloned.1.call-start = ((), (), s32[]{:S(2)}) async-start(), calls=%async_computation.3 | async-start | bytes 1671168 | tf_op jit(solution)/shard_map/all_gather | solution.py:133
  11.0 9.3 %copy-start.21 = (pred[4,2]{1,0:T(4,128)(4,1)}, pred[4,2]{1,0:T(4,128)(4,1)S(1)}, u32[]{:S(2)}) copy-start(pred[4,2]{1,0:T(4,128)(4,1)S(1)} %copy.83) | copy-start | bytes 28
  12.7 93.3 %all-gather.5.cloned.1.call-start = ((), (), s32[]{:S(2)}) async-start(), calls=%async_computation.4 | async-start | bytes 1114112 | tf_op jit(solution)/shard_map/all_gather | solution.py:144
  13.6 32.7 %collective-permute-start.3 = (bf16[448,256]{1,0:T(8,128)(2,1)S(1)}, bf16[448,256]{1,0:T(8,128)(2,1)S(1)}, u32[]{:S(2)}, u32[]{:S(2)}) collective-permute-start(bf16[448,256]{1,0:T(8,128)(2,1)S(1)} %pad_maximum_fusion.3), channel_id=1, source_target_pairs={{0,128},{16,144},{32,160},{48,176},{64,192},{80,208},{96,224},{112... | collective-permute-start | bytes 688136 | tf_op jit(solution)/shard_map/ppermute | solution.py:14
  20.3 20.2 %copy-start.5 = (bf16[1,384,256]{2,1,0:T(8,128)(2,1)}, bf16[1,384,256]{2,1,0:T(8,128)(2,1)S(1)}, u32[]{:S(2)}) copy-start(bf16[1,384,256]{2,1,0:T(8,128)(2,1)S(1)} %get-tuple-element.26) | copy-start | bytes 589828
  20.3 20.2 %copy-start.7 = (bf16[1,384,256]{2,1,0:T(8,128)(2,1)}, bf16[1,384,256]{2,1,0:T(8,128)(2,1)S(1)}, u32[]{:S(2)}) copy-start(bf16[1,384,256]{2,1,0:T(8,128)(2,1)S(1)} %get-tuple-element.27) | copy-start | bytes 589828
  41.0 24.4 %collective-permute-start = (bf16[2,384,256]{2,1,0:T(8,128)(2,1)S(1)}, bf16[2,384,256]{2,1,0:T(8,128)(2,1)}, u32[]{:S(2)}, u32[]{:S(2)}) collective-permute-start(bf16[2,384,256]{2,1,0:T(8,128)(2,1)S(1)} %fusion), channel_id=1, source_target_pairs={{0,16},{16,0},{32,48},{48,32},{64,80},{80,64},{96,112},{112,96},{1... | collective-permute-start | bytes 1179656 | tf_op jit(solution)/shard_map/ppermute | solution.py:14
  46.3 17.8 %copy-start.18 = (bf16[448,256]{1,0:T(8,128)(2,1)}, bf16[448,256]{1,0:T(8,128)(2,1)S(1)}, u32[]{:S(2)}) copy-start(bf16[448,256]{1,0:T(8,128)(2,1)S(1)} %collective-permute-done.3) | copy-start | bytes 688132
  47.2 16.1 %collective-permute-start.4 = (bf16[416,256]{1,0:T(8,128)(2,1)S(1)}, bf16[416,256]{1,0:T(8,128)(2,1)S(1)}, u32[]{:S(2)}, u32[]{:S(2)}) collective-permute-start(bf16[416,256]{1,0:T(8,128)(2,1)S(1)} %pad_maximum_fusion.5), channel_id=1, source_target_pairs={{0,256},{16,272},{32,288},{48,304},{64,320},{80,336},{96,352},{112... | collective-permute-start | bytes 638984 | tf_op jit(solution)/shard_map/ppermute | solution.py:14
  63.3 0.8 copy-start.23
  64.1 7.1 %copy-start = (bf16[3,2,2,256,256]{4,3,2,1,0:T(8,128)(2,1)S(1)}, bf16[3,2,2,256,256]{4,3,2,1,0:T(8,128)(2,1)}, u32[]{:S(2)}) copy-start(bf16[3,2,2,256,256]{4,3,2,1,0:T(8,128)(2,1)} %all-gather.3.cloned.1.call-done) | copy-start | bytes 4718596
  66.8 13.0 %collective-permute-start.1 = (bf16[2,384,256]{2,1,0:T(8,128)(2,1)S(1)}, bf16[2,384,256]{2,1,0:T(8,128)(2,1)}, u32[]{:S(2)}, u32[]{:S(2)}) collective-permute-start(bf16[2,384,256]{2,1,0:T(8,128)(2,1)S(1)} %fusion.1), channel_id=1, source_target_pairs={{0,32},{16,48},{32,0},{48,16},{64,96},{80,112},{96,64},{112,80},{1... | collective-permute-start | bytes 1179656 | tf_op jit(solution)/shard_map/ppermute | solution.py:14
  81.1 15.1 %copy-start.9 = (bf16[2,384,256]{2,1,0:T(8,128)(2,1)}, bf16[2,384,256]{2,1,0:T(8,128)(2,1)S(1)}, u32[]{:S(2)}) copy-start(bf16[2,384,256]{2,1,0:T(8,128)(2,1)S(1)} %fusion.2) | copy-start | bytes 1179652
  81.1 14.2 %collective-permute-start.2 = (bf16[2,384,256]{2,1,0:T(8,128)(2,1)S(1)}, bf16[2,384,256]{2,1,0:T(8,128)(2,1)S(1)}, u32[]{:S(2)}, u32[]{:S(2)}) collective-permute-start(bf16[2,384,256]{2,1,0:T(8,128)(2,1)S(1)} %fusion.2), channel_id=1, source_target_pairs={{0,64},{16,80},{32,96},{48,112},{64,0},{80,16},{96,32},{112,48},{1... | collective-permute-start | bytes 1179656 | tf_op jit(solution)/shard_map/ppermute | solution.py:14
  95.3 2.8 %copy-start.14 = (bf16[2,384,256]{2,1,0:T(8,128)(2,1)}, bf16[2,384,256]{2,1,0:T(8,128)(2,1)S(1)}, u32[]{:S(2)}) copy-start(bf16[2,384,256]{2,1,0:T(8,128)(2,1)S(1)} %collective-permute-done.2) | copy-start | bytes 1179652
  96.2 13.2 %collective-permute-start.5 = (bf16[384,256]{1,0:T(8,128)(2,1)}, bf16[384,256]{1,0:T(8,128)(2,1)}, u32[]{:S(2)}, u32[]{:S(2)}) collective-permute-start(bf16[384,256]{1,0:T(8,128)(2,1)} %fusion.9), channel_id=1, source_target_pairs={{0,128},{16,144},{32,160},{48,176},{64,192},{80,208},{96,224},{112... | collective-permute-start | bytes 589832 | tf_op jit(solution)/shard_map/ppermute | solution.py:14
  106.1 12.0 %copy-start.3 = (bf16[2,2,2,256,256]{4,3,1,2,0:T(8,128)(2,1)S(1)}, bf16[2,2,2,256,256]{4,3,1,2,0:T(8,128)(2,1)}, u32[]{:S(2)}) copy-start(bf16[2,2,2,256,256]{4,3,1,2,0:T(8,128)(2,1)} %all-gather.5.cloned.1.call-done) | copy-start | bytes 3145732
  108.4 13.4 %copy-start.12 = (bf16[384,512]{1,0:T(8,128)(2,1)S(1)}, bf16[384,512]{1,0:T(8,128)(2,1)}, u32[]{:S(2)}) copy-start(bf16[384,512]{1,0:T(8,128)(2,1)} %param.17) | copy-start | bytes 1179652
  108.4 13.4 %copy-start.19 = (bf16[448,256]{1,0:T(8,128)(2,1)S(1)}, bf16[448,256]{1,0:T(8,128)(2,1)}, u32[]{:S(2)}) copy-start(bf16[448,256]{1,0:T(8,128)(2,1)} %copy-done.18) | copy-start | bytes 688132
  110.5 11.3 %collective-permute-start.6 = (bf16[384,256]{1,0:T(8,128)(2,1)S(1)}, bf16[384,256]{1,0:T(8,128)(2,1)S(1)}, u32[]{:S(2)}, u32[]{:S(2)}) collective-permute-start(bf16[384,256]{1,0:T(8,128)(2,1)S(1)} %fusion.11), channel_id=1, source_target_pairs={{0,256},{16,272},{32,288},{48,304},{64,320},{80,336},{96,352},{112... | collective-permute-start | bytes 589832 | tf_op jit(solution)/shard_map/ppermute | solution.py:14
  119.7 3.6 %copy-start.24 = (bf16[416,256]{1,0:T(8,128)(2,1)S(1)}, bf16[416,256]{1,0:T(8,128)(2,1)}, u32[]{:S(2)}) copy-start(bf16[416,256]{1,0:T(8,128)(2,1)} %copy-done.23) | copy-start | bytes 638980
  125.2 10.3 %collective-permute-start.7 = (bf16[384,256]{1,0:T(8,128)(2,1)S(1)}, bf16[384,256]{1,0:T(8,128)(2,1)S(1)}, u32[]{:S(2)}, u32[]{:S(2)}) collective-permute-start(bf16[384,256]{1,0:T(8,128)(2,1)S(1)} %fusion.13), channel_id=1, source_target_pairs={{0,256},{16,272},{32,288},{48,304},{64,320},{80,336},{96,352},{112... | collective-permute-start | bytes 589832 | tf_op jit(solution)/shard_map/ppermute | solution.py:14
  137.3 16.1 %collective-permute-start.8 = (bf16[8,2,2,2,16,256]{5,4,3,2,1,0:T(8,128)(2,1)S(1)}, bf16[8,2,2,2,16,256]{5,4,3,2,1,0:T(8,128)(2,1)S(1)}, u32[]{:S(2)}, u32[]{:S(2)}) collective-permute-start(bf16[8,2,2,2,16,256]{5,4,3,2,1,0:T(8,128)(2,1)S(1)} %select_bitcast_fusion.2), channel_id=1, source_target_pairs={{0,1},{1,0},{2,3},{3,2},{4,5},{5,4},{6,7},{7,6},{8,9},{9,8},{10,11... | collective-permute-start | bytes 1572872 | tf_op jit(solution)/shard_map/ppermute | solution.py:98
  151.0 13.0 %collective-permute-start.9 = (bf16[384,256]{1,0:T(8,128)(2,1)}, bf16[384,256]{1,0:T(8,128)(2,1)}, u32[]{:S(2)}, u32[]{:S(2)}) collective-permute-start(bf16[384,256]{1,0:T(8,128)(2,1)} %fusion.15), channel_id=1, source_target_pairs={{0,128},{16,144},{32,160},{48,176},{64,192},{80,208},{96,224},{112... | collective-permute-start | bytes 589832 | tf_op jit(solution)/shard_map/ppermute | solution.py:14
  153.7 0.8 copy-start.4
  155.0 37.4 %all-to-all-start = ((bf16[8,2,2,2,16,256]{5,4,3,2,1,0:T(8,128)(2,1)}), bf16[8,2,2,2,16,256]{5,4,3,2,1,0:T(8,128)(2,1)}, u32[]{:S(2)}, u32[]{:S(2)}) async-start(bf16[8,2,2,2,16,256]{5,4,3,2,1,0:T(8,128)(2,1)} %copy-done.4), calls=%async_computation | async-start | bytes 1048576 | tf_op jit(solution)/shard_map/all_to_all | solution.py:105
  160.5 6.8 %copy-start.10 = (bf16[2,384,256]{2,1,0:T(8,128)(2,1)S(1)}, bf16[2,384,256]{2,1,0:T(8,128)(2,1)}, u32[]{:S(2)}) copy-start(bf16[2,384,256]{2,1,0:T(8,128)(2,1)} %copy-done.9) | copy-start | bytes 1179652
  164.0 4.5 %copy-start.15 = (bf16[2,384,256]{2,1,0:T(8,128)(2,1)S(1)}, bf16[2,384,256]{2,1,0:T(8,128)(2,1)}, u32[]{:S(2)}) copy-start(bf16[2,384,256]{2,1,0:T(8,128)(2,1)} %copy-done.14) | copy-start | bytes 1179652
  165.3 12.3 %collective-permute-start.10 = (bf16[2,384,256]{2,1,0:T(8,128)(2,1)S(1)}, bf16[2,384,256]{2,1,0:T(8,128)(2,1)S(1)}, u32[]{:S(2)}, u32[]{:S(2)}) collective-permute-start(bf16[2,384,256]{2,1,0:T(8,128)(2,1)S(1)} %convolution_convert_fusion.3), channel_id=1, source_target_pairs={{0,64},{16,80},{32,96},{48,112},{64,0},{80,16},{96,32},{112,48},{1... | collective-permute-start | bytes 1179656 | tf_op jit(solution)/shard_map/ppermute | solution.py:14
  178.8 5.1 %copy-start.1 = (bf16[2,384,256]{2,1,0:T(8,128)(2,1)}, bf16[2,384,256]{2,1,0:T(8,128)(2,1)S(1)}, u32[]{:S(2)}) copy-start(bf16[2,384,256]{2,1,0:T(8,128)(2,1)S(1)} %fusion.3) | copy-start | bytes 1179652
  180.8 8.1 %collective-permute-start.11 = (bf16[8,2,2,2,16,256]{5,4,3,2,1,0:T(8,128)(2,1)S(1)}, bf16[8,2,2,2,16,256]{5,4,3,2,1,0:T(8,128)(2,1)S(1)}, u32[]{:S(2)}, u32[]{:S(2)}) collective-permute-start(bf16[8,2,2,2,16,256]{5,4,3,2,1,0:T(8,128)(2,1)S(1)} %select_bitcast_fusion.1), channel_id=1, source_target_pairs={{0,1},{1,0},{2,3},{3,2},{4,5},{5,4},{6,7},{7,6},{8,9},{9,8},{10,11... | collective-permute-start | bytes 1572872 | tf_op jit(solution)/shard_map/ppermute | solution.py:98
  184.2 14.3 %copy-start.2 = (bf16[2,384,256]{2,1,0:T(8,128)(2,1)S(1)}, bf16[2,384,256]{2,1,0:T(8,128)(2,1)}, u32[]{:S(2)}) copy-start(bf16[2,384,256]{2,1,0:T(8,128)(2,1)} %copy-done.1) | copy-start | bytes 1179652
  184.2 14.3 %collective-permute-start.12 = (bf16[2,384,256]{2,1,0:T(8,128)(2,1)S(1)}, bf16[2,384,256]{2,1,0:T(8,128)(2,1)S(1)}, u32[]{:S(2)}, u32[]{:S(2)}) collective-permute-start(bf16[2,384,256]{2,1,0:T(8,128)(2,1)S(1)} %convolution_convert_fusion.2), channel_id=1, source_target_pairs={{0,32},{16,48},{32,0},{48,16},{64,96},{80,112},{96,64},{112,80},{1... | collective-permute-start | bytes 1179656 | tf_op jit(solution)/shard_map/ppermute | solution.py:14
  201.4 11.7 %collective-permute-start.13 = (bf16[2,384,256]{2,1,0:T(8,128)(2,1)S(1)}, bf16[2,384,256]{2,1,0:T(8,128)(2,1)S(1)}, u32[]{:S(2)}, u32[]{:S(2)}) collective-permute-start(bf16[2,384,256]{2,1,0:T(8,128)(2,1)S(1)} %convolution_convert_fusion.1), channel_id=1, source_target_pairs={{0,16},{16,0},{32,48},{48,32},{64,80},{80,64},{96,112},{112,96},{1... | collective-permute-start | bytes 1179656 | tf_op jit(solution)/shard_map/ppermute | solution.py:14
  204.5 25.0 %all-to-all-start.1 = ((bf16[8,2,2,2,16,256]{5,4,3,2,1,0:T(8,128)(2,1)}), bf16[8,2,2,2,16,256]{5,4,3,2,1,0:T(8,128)(2,1)S(1)}, u32[]{:S(2)}, u32[]{:S(2)}) async-start(bf16[8,2,2,2,16,256]{5,4,3,2,1,0:T(8,128)(2,1)} %fusion.20), calls=%async_computation.1 | async-start | bytes 1048576 | tf_op jit(solution)/shard_map/all_to_all | solution.py:105
  210.9 6.0 %copy-start.20 = (bf16[384,256]{1,0:T(8,128)(2,1)S(1)}, bf16[384,256]{1,0:T(8,128)(2,1)}, u32[]{:S(2)}) copy-start(bf16[384,256]{1,0:T(8,128)(2,1)} %get-tuple-element.25) | copy-start | bytes 589828
  214.9 9.6 %copy-start.6 = (bf16[1,384,256]{2,1,0:T(8,128)(2,1)S(1)}, bf16[1,384,256]{2,1,0:T(8,128)(2,1)}, u32[]{:S(2)}) copy-start(bf16[1,384,256]{2,1,0:T(8,128)(2,1)} %copy-done.5) | copy-start | bytes 589828
  214.9 9.7 %copy-start.8 = (bf16[1,384,256]{2,1,0:T(8,128)(2,1)S(1)}, bf16[1,384,256]{2,1,0:T(8,128)(2,1)}, u32[]{:S(2)}) copy-start(bf16[1,384,256]{2,1,0:T(8,128)(2,1)} %copy-done.7) | copy-start | bytes 589828
  217.6 11.2 %collective-permute-start.14 = (bf16[416,256]{1,0:T(8,128)(2,1)}, bf16[416,256]{1,0:T(8,128)(2,1)}, u32[]{:S(2)}, u32[]{:S(2)}) collective-permute-start(bf16[416,256]{1,0:T(8,128)(2,1)} %pad_maximum_fusion.6), channel_id=1, source_target_pairs={{0,256},{16,272},{32,288},{48,304},{64,320},{80,336},{96,352},{112... | collective-permute-start | bytes 638984 | tf_op jit(solution)/shard_map/ppermute | solution.py:14
  225.1 13.1 %copy-start.17 = (bf16[2,2,1,16,256]{4,3,1,2,0:T(8,128)(2,1)S(1)}, bf16[2,2,1,16,256]{4,3,1,2,0:T(8,128)(2,1)}, u32[]{:S(2)}) copy-start(bf16[2,2,1,16,256]{4,3,1,2,0:T(8,128)(2,1)} %pad_maximum_fusion.12) | copy-start | bytes 98308
  225.4 12.8 %copy-start.13 = (f32[384,256]{1,0:T(8,128)S(1)}, f32[384,256]{1,0:T(8,128)}, u32[]{:S(2)}) copy-start(f32[384,256]{1,0:T(8,128)} %get-tuple-element.49) | copy-start | bytes 1179652
  231.4 12.3 %collective-permute-start.16 = (bf16[8,2,2,2,16,256]{5,4,3,2,1,0:T(8,128)(2,1)S(1)}, bf16[8,2,2,2,16,256]{5,4,3,2,1,0:T(8,128)(2,1)S(1)}, u32[]{:S(2)}, u32[]{:S(2)}) collective-permute-start(bf16[8,2,2,2,16,256]{5,4,3,2,1,0:T(8,128)(2,1)S(1)} %select_bitcast_fusion), channel_id=1, source_target_pairs={{0,1},{1,0},{2,3},{3,2},{4,5},{5,4},{6,7},{7,6},{8,9},{9,8},{10,11... | collective-permute-start | bytes 1572872 | tf_op jit(solution)/shard_map/ppermute | solution.py:98
  239.4 15.2 %collective-permute-start.15 = (bf16[448,256]{1,0:T(8,128)(2,1)S(1)}, bf16[448,256]{1,0:T(8,128)(2,1)S(1)}, u32[]{:S(2)}, u32[]{:S(2)}) collective-permute-start(bf16[448,256]{1,0:T(8,128)(2,1)S(1)} %pad_maximum_fusion.4), channel_id=1, source_target_pairs={{0,128},{16,144},{32,160},{48,176},{64,192},{80,208},{96,224},{112... | collective-permute-start | bytes 688136 | tf_op jit(solution)/shard_map/ppermute | solution.py:14
  244.8 23.0 %all-to-all-start.2 = ((bf16[8,2,2,2,16,256]{5,4,3,2,1,0:T(8,128)(2,1)}), bf16[8,2,2,2,16,256]{5,4,3,2,1,0:T(8,128)(2,1)S(1)}, u32[]{:S(2)}, u32[]{:S(2)}) async-start(bf16[8,2,2,2,16,256]{5,4,3,2,1,0:T(8,128)(2,1)} %fusion.18), calls=%async_computation.2 | async-start | bytes 1048576 | tf_op jit(solution)/shard_map/all_to_all | solution.py:105
  250.9 17.0 %copy-start.22 = (pred[4,2]{1,0:T(4,128)(4,1)S(1)}, pred[4,2]{1,0:T(4,128)(4,1)}, u32[]{:S(2)}) copy-start(pred[4,2]{1,0:T(4,128)(4,1)} %copy-done.21) | copy-start | bytes 28
Sparse Core Ops, SparseCore 0:
  12.9 47.3 all-gather.2
  64.2 41.8 all-gather.4

commit v5 on v4

v5 whole, which is shorter than its diff:
```python
import math

import jax
import jax.numpy as jnp
from jax import lax
from jax.experimental import pallas as pl
from jax.experimental.pallas import tpu as pltpu
from jax.sharding import PartitionSpec as P


SECTIONS = 6


def flip(value, bit):
    mask = 1 << bit
    pairs = [(source, source ^ mask) for source in range(lax.axis_size("blk"))]
    return lax.ppermute(value, "blk", pairs)


def after(value, other):
    start = (0,) * other.ndim
    probe = lax.slice(other, start, (1,) * (other.ndim - 1) + other.shape[-1:]).reshape(other.shape[-1])
    return jnp.where(probe != probe, jnp.zeros_like(value), value)


def dot(left, right):
    return jnp.einsum("...tk,...kl->...tl", left, right, preferred_element_type=jnp.float32)


def dot_back(left, right):
    return jnp.einsum("...tl,...kl->...tk", left, right, preferred_element_type=jnp.float32)


def dot_rows(left, right):
    return jnp.einsum("...tk,...tl->...kl", left, right, preferred_element_type=jnp.float32).astype(jnp.bfloat16)


def unpack(packed, shape):
    rows = math.prod(shape[:-1])
    return packed[:rows].reshape(shape), packed[rows:]


def bits():
    index = lax.axis_index("blk")
    return index, (index >> 3) & 1, (index >> 4) & 1


def choice(matchings, section, row):
    index, low, high = bits()
    if section < 4:
        block = (row ^ low) + 2 * index
        turn = 0
    elif section == 4:
        block = low + 2 * (index & 7) + 16 * (row ^ high) + 32 * high
        turn = row ^ high ^ low
    else:
        block = low + 2 * (index & 7) + 16 * high + 32 * (row ^ high)
        turn = row
    return (matchings[section, block] != block).astype(jnp.int32) ^ turn


def prepare(matchings, weights, cotangent, first, rest, keep, packed):
    _, low, _ = bits()
    width = weights.shape[-1]
    depth = weights.shape[-2]
    for section in range(4):
        for row in range(2):
            at = choice(matchings, section, row)
            out = first.at[0] if section == 0 else rest.at[section - 1]
            out[0, row] = weights[section, row ^ low, at]
            out[1, row] = weights[section, row ^ low, 1 - at]
    for place in range(2):
        for both in range(2):
            keep[place, both] = weights[4 + place, low, both]
            packed[pl.ds((2 * place + both) * depth, depth)] = weights[4 + place, 1 - low, both]
    packed[4 * depth :] = jnp.where(low == 1, cotangent[:, :width], cotangent[:, width:])


def between(matchings, keep, came, cotangent, fourth, fifth, packed, cotan):
    _, low, high = bits()
    width = keep.shape[-1]
    depth = keep.shape[-2]
    same = low == high

    def came_at(place, both):
        return came[pl.ds(pl.multiple_of((2 * place + both) * depth, depth), depth)]

    for row in range(2):
        at = choice(matchings, 4, row)
        own = same if row == 0 else jnp.logical_not(same)
        for slot, both in enumerate((at, 1 - at)):
            fourth[slot, row] = jnp.where(own, keep[0, both], came_at(0, both))
    for both in range(2):
        mine5, yours5 = keep[1, both], came_at(1, both)
        fifth[both] = jnp.where(same, mine5, yours5)
        packed[pl.ds(both * depth, depth)] = jnp.where(same, yours5, mine5)
    cot_keep = jnp.where(low == 1, cotangent[:, width:], cotangent[:, :width])
    cot_came = came[4 * depth :]
    cotan[...] = jnp.where(same, cot_keep, cot_came)
    packed[2 * depth :] = jnp.where(same, cot_came, cot_keep)


def gather_late(matchings, fourth, fifth, came, late):
    depth = fourth.shape[-2]
    late[0] = fourth[...]
    for row in range(2):
        at = choice(matchings, 5, row)
        for slot, both in enumerate((at, 1 - at)):
            if row == 0:
                late[1, slot, row] = fifth[both]
            else:
                late[1, slot, row] = came[pl.ds(pl.multiple_of(both * depth, depth), depth)]


def total(parts, place, slot, row):
    parts = [parts[chip, place, slot, row].astype(jnp.float32) for chip in range(parts.shape[0])]
    while len(parts) > 1:
        parts = [a + b for a, b in zip(parts[::2], parts[1::2])]
    return parts[0]


def unorder_late(matchings, parts, rows):
    for place in range(2):
        for row in range(2):
            at = choice(matchings, 4 + place, row)
            for slot, both in enumerate((at, 1 - at)):
                rows[row, place, both] = total(parts, 1 + place, slot, row).astype(rows.dtype)


def finish(matchings, parts_low, parts_high, keep, came, out):
    _, low, _ = bits()
    depth = out.shape[-2]
    for section in range(4):
        parts = parts_low if section < 3 else parts_high
        for row in range(2):
            at = choice(matchings, section, row)
            for slot, both in enumerate((at, 1 - at)):
                out[section, row ^ low, both] = total(parts, section % 3, slot, row)
    for place in range(2):
        for both in range(2):
            out[4 + place, low, both] = keep[place, both].astype(jnp.float32)
            given = came[pl.ds((2 * place + both) * depth, depth)]
            out[4 + place, 1 - low, both] = given.astype(jnp.float32)


def local(kernel, matchings, *arrays, outs):
    whole = pl.BlockSpec(memory_space=pltpu.VMEM)
    moved = sum(math.prod(x.shape) * x.dtype.itemsize for x in (*arrays, *outs))
    result = pl.pallas_call(
        kernel,
        out_shape=outs,
        in_specs=[pl.BlockSpec(memory_space=pltpu.SMEM)] + [whole] * len(arrays),
        out_specs=[whole] * len(outs),
        cost_estimate=pl.CostEstimate(flops=0, bytes_accessed=moved, transcendentals=0),
        compiler_params=pltpu.CompilerParams(vmem_limit_bytes=16 * 2**20),
    )(matchings, *arrays)
    return result[0] if len(outs) == 1 else result


def core_half(terms, core):
    count, both, per_dev, size, depth, width = terms.shape
    parts = terms.reshape(count, both, per_dev, size // 2, 2, depth, width)
    half = jnp.where(core == 1, parts[:, :, :, :, 1], parts[:, :, :, :, 0])
    return jnp.moveaxis(half, 3, 0)


def chip_sum(terms, waits):
    count, both, per_dev, depth, width = terms.shape
    size = lax.axis_size("tok")
    core = lax.axis_index("tok") & 1
    terms = terms.reshape(count, both, per_dev, size, depth // size, width)
    give = core_half(terms, 1 - core)
    if waits is not None:
        give = after(give, waits)
    came = lax.ppermute(give, "tok", [(source, source ^ 1) for source in range(size)])
    return (core_half(terms, core).astype(jnp.float32) + came.astype(jnp.float32)).astype(jnp.bfloat16)


def all_parts(chip):
    size = lax.axis_size("tok")
    groups = [list(range(c, size, 2)) for c in range(2)]
    return lax.all_to_all(chip, "tok", 0, 0, axis_index_groups=groups)


def body(activations, weights, matchings, cotangent):
    depth, width = weights.shape[3:]
    tokens = activations.shape[0]
    bf16 = jnp.bfloat16
    _, low, high = bits()
    low, same = low == 1, low == high

    def shape(*dims, dtype=bf16):
        return jax.ShapeDtypeStruct((*dims, width), dtype)

    first, rest, keep, packed = local(
        prepare,
        matchings,
        weights,
        cotangent,
        outs=[shape(1, 2, 2, depth), shape(3, 2, 2, depth), shape(2, 2, depth), shape(4 * depth + tokens)],
    )
    came = flip(packed, 3)
    full = list(lax.all_gather(first, "tok", axis=3, tiled=True))
    full += list(lax.all_gather(rest, "tok", axis=3, tiled=True))

    left, right = activations[:, :width], activations[:, width:]
    value = jnp.stack([jnp.where(low, right, left), jnp.where(low, left, right)])
    other = value[::-1]
    inputs = [(value, other)]
    value = (dot(value, full[0][0]) + dot(other, full[0][1])).astype(bf16)

    fourth, fifth, packed, cotan0 = local(
        between,
        matchings,
        keep,
        came,
        cotangent,
        outs=[shape(2, 2, depth), shape(2, depth), shape(2 * depth + tokens), shape(tokens)],
    )
    came = flip(packed, 4)
    cotan1 = came[2 * depth :]
    late = local(gather_late, matchings, fourth, fifth, came, outs=[shape(2, 2, 2, depth)])
    full += list(lax.all_gather(late, "tok", axis=3, tiled=True))

    for section in range(1, 4):
        other = flip(value, section - 1)
        inputs.append((value, other))
        own_w, other_w = full[section][0], full[section][1]
        if section < 3:
            value = (dot(value, own_w) + dot(other, other_w)).astype(bf16)
        else:
            send = (dot(value[1], own_w[1]) + dot(other[1], other_w[1])).astype(bf16)
            keep = (dot(value[0], own_w[0]) + dot(other[0], other_w[0])).astype(bf16)
    came = flip(send, 3)
    inputs.append((keep, came))
    own_w, other_w = full[4][0], full[4][1]
    send = (dot(keep, own_w[1]) + dot(came, other_w[1])).astype(bf16)
    keep = (dot(keep, own_w[0]) + dot(came, other_w[0])).astype(bf16)
    came = flip(send, 4)
    inputs.append((keep, came))
    own_w, other_w = full[5][0], full[5][1]

    results, grads = [], []
    for row, cotan in enumerate((cotan0, cotan1)):
        final = dot(keep, own_w[row]) + dot(came, other_w[row])
        results.append(jax.nn.gelu(final).astype(bf16))
        back_fn = jax.vjp(jax.nn.gelu, final)[1]
        grads.append(back_fn(cotan.astype(jnp.float32))[0].astype(bf16))

    terms = [None] * SECTIONS
    for section in (5, 4):
        own_w, other_w = full[section][0], full[section][1]
        sent = (dot_back(grads[0], other_w[0]) + dot_back(grads[1], other_w[1])).astype(bf16)
        back = flip(sent, section - 1)
        kept = (dot_back(grads[0], own_w[0]) + dot_back(grads[1], own_w[1])).astype(bf16)
        terms[section] = jnp.stack(
            [jnp.stack([dot_rows(part, grad) for grad in grads]) for part in inputs[section]]
        )
        grads = [kept, back]
    grad = jnp.stack(grads)
    for section in (3, 2, 1, 0):
        own_w, other_w = full[section][0], full[section][1]
        sent = dot_back(grad, other_w).astype(bf16)
        back = sent[::-1] if section == 0 else flip(sent, section - 1)
        terms[section] = jnp.stack([dot_rows(part, grad) for part in inputs[section]])
        if section == 3:
            chip = chip_sum(jnp.stack(terms[3:]), None)
            parts_high = all_parts(chip)
        grad = (dot_back(grad, own_w) + back.astype(jnp.float32)).astype(bf16)
        if section == 2:
            grad = after(grad, chip)
    chip = chip_sum(jnp.stack(terms[:3]), parts_high)
    parts_low = all_parts(chip)
    input_grad = jnp.concatenate([jnp.where(low, grad[1], grad[0]), jnp.where(low, grad[0], grad[1])], axis=1)

    rows = local(unorder_late, matchings, parts_high, outs=[shape(2, 2, 2, depth)])
    packed = jnp.concatenate([rows[1, 1].reshape(-1, width), after(results[1], chip)])
    came, out_came = unpack(flip(packed, 4), (2, depth, width))
    row0, row1 = rows[0], jnp.stack([rows[1, 0], came])
    keep, send = jnp.where(same, row0, row1), jnp.where(same, row1, row0)
    out_keep, out_send = jnp.where(same, results[0], out_came), jnp.where(same, out_came, results[0])
    packed = flip(jnp.concatenate([send.reshape(-1, width), out_send]), 3)
    out_came = packed[4 * depth :]
    result = jnp.concatenate([jnp.where(low, out_came, out_keep), jnp.where(low, out_keep, out_came)], axis=1)
    weight_grad = local(
        finish, matchings, parts_low, parts_high, keep, packed, outs=[shape(6, 2, 2, depth, dtype=jnp.float32)]
    )
    return result, input_grad, weight_grad


def solution(mesh):
    placed = (P("tok", "blk"), P(None, "blk", None, "tok", None), P(), P("tok", "blk"))
    return jax.shard_map(
        body,
        mesh=mesh,
        in_specs=placed,
        out_specs=(P("tok", "blk"), P("tok", "blk"), P(None, "blk", None, "tok", None)),
        check_vma=False,
    )
```

time: 277 us -> 255 us (0.921)
  starting transfers between devices: 106 us -> 88.6 us
  waiting for transfers between devices: 67.9 us -> 78.2 us
  between operations: 22.9 us -> 14.9 us
  other arithmetic: 15.6 us -> 8.73 us
  Pallas kernels: 0 us -> 5.36 us
  matrix products: 34 us -> 30.7 us
    ppermute x14, waiting for transfers between devices: 48.8 us -> 65.4 us  [flip(): return lax.ppermute(value, 'blk', pairs)]
    ppermute x3 -> x2, starting transfers between devices: 22.4 us -> 12 us  [chip_sum(): lax.ppermute(give, 'tok', [(source, source ^ 1) for source in range(size)])]
    ppermute x14, starting transfers between devices: 69 us -> 59.5 us  [flip(): return lax.ppermute(value, 'blk', pairs)]
    all_to_all x3 -> x2, waiting for transfers between devices: 11.3 us -> 5.48 us  [all_parts(): return lax.all_to_all(chip, 'tok', 0, 0, axis_index_groups=groups)]
    pallas_call x0 -> x5, Pallas kernels: none -> 5.36 us  [local(): pl.pallas_call(kernel, out_shape=outs, in_specs=[pl.BlockSpec(memory_spac...]
    slice x13 -> x2, local copies, waits for them, and re-layouts: 4.83 us -> 0.01 us  [the longest x1 0.01 us: body(): row0, row1 = (rows[0], jnp.stack([rows[1, 0], came]))]
    dot_general x16, matrix products: 10.6 us -> 6.34 us  [dot_rows(): jnp.einsum('...tk,...tl->...kl', left, right, preferred_element_type=jnp....]
    all_to_all x3 -> x2, starting transfers between devices: 15 us -> 17 us  [all_parts(): return lax.all_to_all(chip, 'tok', 0, 0, axis_index_groups=groups)]
  transfers between devices with their start and end apart: 22 -> 20, of which waited for: 14 -> 14; matrix products, arithmetic and copies ran while one was open for 15% -> 13% of each run, Pallas kernels for 0% -> 1%
where the time goes in v5:
time: 255 us; the launch traced here: 254 us
  starting transfers between devices  88.6 us (35%)
  waiting for transfers between devices  78.2 us (31%)
  matrix products  30.7 us (12%)
  blocking collectives  20.1 us (8%)
  between operations  14.9 us (6%)
  other arithmetic  8.73 us (3%)
  local copies, waits for them, and re-layouts  7.17 us (3%)
  Pallas kernels  5.36 us (2%)
    ppermute x14, waiting for transfers between devices, flip(): return lax.ppermute(value, 'blk', pairs)  65.4 us
    ppermute x14, starting transfers between devices, flip(): return lax.ppermute(value, 'blk', pairs)  59.5 us
    all_gather x1, blocking collectives, body(): full = list(lax.all_gather(first, 'tok', axis=3, tiled=True))  20.1 us
    all_to_all x2, starting transfers between devices, all_parts(): return lax.all_to_all(chip, 'tok', 0, 0, axis_index_groups=groups)  17 us
    dot_general x18, matrix products, dot(): jnp.einsum('...tk,...kl->...tl', left, right, preferred_element_type=jnp....  14.5 us
    ppermute x2, starting transfers between devices, chip_sum(): lax.ppermute(give, 'tok', [(source, source ^ 1) for source in range(size)])  12 us
    dot_general x16, matrix products, dot_back(): jnp.einsum('...tl,...kl->...tk', left, right, preferred_element_type=jnp....  9.87 us
    dot_general x16, matrix products, dot_rows(): jnp.einsum('...tk,...tl->...kl', left, right, preferred_element_type=jnp....  6.34 us
  transfers between devices with their start and end apart: 20, of which 14 were waited for; matrix products, arithmetic and copies ran while one was open for 13% of the time, Pallas kernels for 1%

profile of v5, /device:TPU:1, one launch (start us, length us, event | category | flops | bytes accessed | tf_op | source)
XLA Modules:
  0.0 253.7 jit_solution(7582320957493072434)
XLA Ops:
  9.8 1.3 shard_map.67
  11.2 6.6 %collective-permute-start.2 = (bf16[448,256]{1,0:T(8,128)(2,1)S(1)}, bf16[448,256]{1,0:T(8,128)(2,1)S(1)}, u32[]{:S(2)}, u32[]{:S(2)}) collective-permute-start(bf16[448,256]{1,0:T(8,128)(2,1)S(1)} %get-tuple-element.14), channel_id=1, source_target_pairs={{0,128},{16,144},{32,160},{48,176},{64,192},{80,208},{96,224},{112... | collective-permute-start | bytes 688136 | tf_op jit(solution)/shard_map/ppermute | solution.py:17
  19.0 20.1 %all_gather.9 = bf16[1,2,2,256,256]{4,3,2,1,0:T(8,128)(2,1)S(1)} all-gather(bf16[1,2,2,16,256]{4,3,2,1,0:T(8,128)(2,1)S(1)} %get-tuple-element.11), channel_id=1, replica_groups=mesh['blk'=32,'tok'=16] {'tok'}, dimensions={3}, use_global_device_ids=true | all-gather | bytes 557056 | tf_op jit(solution)/shard_map/all_gather | solution.py:203
  40.0 9.1 %collective-permute-start.4 = (bf16[416,256]{1,0:T(8,128)(2,1)S(1)}, bf16[416,256]{1,0:T(8,128)(2,1)S(1)}, u32[]{:S(2)}, u32[]{:S(2)}) collective-permute-start(bf16[416,256]{1,0:T(8,128)(2,1)S(1)} %get-tuple-element.18), channel_id=1, source_target_pairs={{0,256},{16,272},{32,288},{48,304},{64,320},{80,336},{96,352},{112... | collective-permute-start | bytes 638984 | tf_op jit(solution)/shard_map/ppermute | solution.py:17
  49.5 3.1 %collective-permute-start = (bf16[2,384,256]{2,1,0:T(8,128)(2,1)S(1)}, bf16[2,384,256]{2,1,0:T(8,128)(2,1)S(1)}, u32[]{:S(2)}, u32[]{:S(2)}) collective-permute-start(bf16[2,384,256]{2,1,0:T(8,128)(2,1)S(1)} %fusion.4), channel_id=1, source_target_pairs={{0,16},{16,0},{32,48},{48,32},{64,80},{80,64},{96,112},{112,96},{1... | collective-permute-start | bytes 1179656 | tf_op jit(solution)/shard_map/ppermute | solution.py:17
  52.6 4.0 %collective-permute-done.4.came = bf16[416,256]{1,0:T(8,128)(2,1)S(1)} collective-permute-done((bf16[416,256]{1,0:T(8,128)(2,1)S(1)}, bf16[416,256]{1,0:T(8,128)(2,1)S(1)}, u32[]{:S(2)}, u32[]{:S(2)}) %collective-permute-start.4) | collective-permute-done | bytes 213024 | tf_op jit(solution)/shard_map/ppermute | solution.py:17
  56.6 1.3 shard_map.69
  58.8 1.2 fusion.42
  60.0 1.6 collective-permute-done
  62.4 1.2 fusion.5
  63.6 4.6 %collective-permute-start.1 = (bf16[2,384,256]{2,1,0:T(8,128)(2,1)S(1)}, bf16[2,384,256]{2,1,0:T(8,128)(2,1)S(1)}, u32[]{:S(2)}, u32[]{:S(2)}) collective-permute-start(bf16[2,384,256]{2,1,0:T(8,128)(2,1)S(1)} %fusion.5), channel_id=1, source_target_pairs={{0,32},{16,48},{32,0},{48,16},{64,96},{80,112},{96,64},{112,80},{1... | collective-permute-start | bytes 1179656 | tf_op jit(solution)/shard_map/ppermute | solution.py:17
  68.3 1.2 fusion.43
  69.5 6.9 %collective-permute-done.1 = bf16[2,384,256]{2,1,0:T(8,128)(2,1)S(1)} collective-permute-done((bf16[2,384,256]{2,1,0:T(8,128)(2,1)S(1)}, bf16[2,384,256]{2,1,0:T(8,128)(2,1)S(1)}, u32[]{:S(2)}, u32[]{:S(2)}) %collective-permute-start.1) | collective-permute-done | bytes 393248 | tf_op jit(solution)/shard_map/ppermute | solution.py:17
  76.3 1.4 fusion.6
  77.7 3.2 %collective-permute-start.3 = (bf16[2,384,256]{2,1,0:T(8,128)(2,1)S(1)}, bf16[2,384,256]{2,1,0:T(8,128)(2,1)S(1)}, u32[]{:S(2)}, u32[]{:S(2)}) collective-permute-start(bf16[2,384,256]{2,1,0:T(8,128)(2,1)S(1)} %fusion.6), channel_id=1, source_target_pairs={{0,64},{16,80},{32,96},{48,112},{64,0},{80,16},{96,32},{112,48},{1... | collective-permute-start | bytes 1179656 | tf_op jit(solution)/shard_map/ppermute | solution.py:17
  81.0 1.1 fusion.44
  83.2 4.9 %collective-permute-done.3 = bf16[2,384,256]{2,1,0:T(8,128)(2,1)S(1)} collective-permute-done((bf16[2,384,256]{2,1,0:T(8,128)(2,1)S(1)}, bf16[2,384,256]{2,1,0:T(8,128)(2,1)S(1)}, u32[]{:S(2)}, u32[]{:S(2)}) %collective-permute-start.3) | collective-permute-done | bytes 393248 | tf_op jit(solution)/shard_map/ppermute | solution.py:17
  88.1 1.2 fusion.13
  89.3 4.0 %collective-permute-start.5 = (bf16[384,256]{1,0:T(8,128)(2,1)S(1)}, bf16[384,256]{1,0:T(8,128)(2,1)S(1)}, u32[]{:S(2)}, u32[]{:S(2)}) collective-permute-start(bf16[384,256]{1,0:T(8,128)(2,1)S(1)} %fusion.13), channel_id=1, source_target_pairs={{0,128},{16,144},{32,160},{48,176},{64,192},{80,208},{96,224},{112... | collective-permute-start | bytes 589832 | tf_op jit(solution)/shard_map/ppermute | solution.py:17
  94.4 6.3 %all-gather.5.cloned.1.call-done = bf16[2,2,2,256,256]{4,3,2,1,0:T(8,128)(2,1)} async-done(((bf16[2,2,2,16,256]{4,3,2,1,0:T(8,128)(2,1)}), bf16[2,2,2,256,256]{4,3,2,1,0:T(8,128)(2,1)}) %all-gather.5.cloned.1.call-update) | async-done | bytes 1048592 | tf_op jit(solution)/shard_map/all_gather | solution.py:223
  104.0 8.8 %collective-permute-start.6 = (bf16[384,256]{1,0:T(8,128)(2,1)S(1)}, bf16[384,256]{1,0:T(8,128)(2,1)S(1)}, u32[]{:S(2)}, u32[]{:S(2)}) collective-permute-start(bf16[384,256]{1,0:T(8,128)(2,1)S(1)} %fusion.14), channel_id=1, source_target_pairs={{0,256},{16,272},{32,288},{48,304},{64,320},{80,336},{96,352},{112... | collective-permute-start | bytes 589832 | tf_op jit(solution)/shard_map/ppermute | solution.py:17
  113.3 6.2 %collective-permute-done.6 = bf16[384,256]{1,0:T(8,128)(2,1)S(1)} collective-permute-done((bf16[384,256]{1,0:T(8,128)(2,1)S(1)}, bf16[384,256]{1,0:T(8,128)(2,1)S(1)}, u32[]{:S(2)}, u32[]{:S(2)}) %collective-permute-start.6) | collective-permute-done | bytes 196640 | tf_op jit(solution)/shard_map/ppermute | solution.py:17
  120.7 1.2 fusion.28
  123.4 4.1 %collective-permute-start.7 = (bf16[384,256]{1,0:T(8,128)(2,1)S(1)}, bf16[384,256]{1,0:T(8,128)(2,1)S(1)}, u32[]{:S(2)}, u32[]{:S(2)}) collective-permute-start(bf16[384,256]{1,0:T(8,128)(2,1)S(1)} %fusion.17), channel_id=1, source_target_pairs={{0,256},{16,272},{32,288},{48,304},{64,320},{80,336},{96,352},{112... | collective-permute-start | bytes 589832 | tf_op jit(solution)/shard_map/ppermute | solution.py:17
  128.3 7.5 %collective-permute-done.7 = bf16[384,256]{1,0:T(8,128)(2,1)S(1)} collective-permute-done((bf16[384,256]{1,0:T(8,128)(2,1)S(1)}, bf16[384,256]{1,0:T(8,128)(2,1)S(1)}, u32[]{:S(2)}, u32[]{:S(2)}) %collective-permute-start.7) | collective-permute-done | bytes 196640 | tf_op jit(solution)/shard_map/ppermute | solution.py:17
  136.3 2.1 collective-permute-start.8
  139.5 6.1 %collective-permute-done.8 = bf16[384,256]{1,0:T(8,128)(2,1)S(1)} collective-permute-done((bf16[384,256]{1,0:T(8,128)(2,1)S(1)}, bf16[384,256]{1,0:T(8,128)(2,1)S(1)}, u32[]{:S(2)}, u32[]{:S(2)}) %collective-permute-start.8) | collective-permute-done | bytes 196640 | tf_op jit(solution)/shard_map/ppermute | solution.py:17
  146.2 1.9 collective-permute-start.10
  149.1 7.0 %collective-permute-start.9 = (bf16[8,3,2,2,16,256]{5,4,3,2,1,0:T(8,128)(2,1)S(1)}, bf16[8,3,2,2,16,256]{5,4,3,2,1,0:T(8,128)(2,1)S(1)}, u32[]{:S(2)}, u32[]{:S(2)}) collective-permute-start(bf16[8,3,2,2,16,256]{5,4,3,2,1,0:T(8,128)(2,1)S(1)} %select_bitcast_fusion), channel_id=1, source_target_pairs={{0,1},{1,0},{2,3},{3,2},{4,5},{5,4},{6,7},{7,6},{8,9},{9,8},{10,11... | collective-permute-start | bytes 2359304 | tf_op jit(solution)/shard_map/ppermute | solution.py:175
  157.5 3.7 %collective-permute-start.11 = (bf16[2,384,256]{2,1,0:T(8,128)(2,1)}, bf16[2,384,256]{2,1,0:T(8,128)(2,1)}, u32[]{:S(2)}, u32[]{:S(2)}) collective-permute-start(bf16[2,384,256]{2,1,0:T(8,128)(2,1)} %convolution_convert_fusion.2), channel_id=1, source_target_pairs={{0,32},{16,48},{32,0},{48,16},{64,96},{80,112},{96,64},{112,80},{1... | collective-permute-start | bytes 1179656 | tf_op jit(solution)/shard_map/ppermute | solution.py:17
  163.4 1.3 fusion.3
  164.6 13.5 %all-to-all-start = ((bf16[8,3,2,2,16,256]{5,4,3,2,1,0:T(8,128)(2,1)}), bf16[8,3,2,2,16,256]{5,4,3,2,1,0:T(8,128)(2,1)S(1)}, u32[]{:S(2)}, u32[]{:S(2)}) async-start(bf16[8,3,2,2,16,256]{5,4,3,2,1,0:T(8,128)(2,1)} %fusion.3), calls=%async_computation | async-start | bytes 1572864 | tf_op jit(solution)/shard_map/all_to_all | solution.py:182
  178.9 1.4 fusion.8
  180.3 1.2 convolution_convert_fusion.1
  181.5 2.0 collective-permute-start.12
  184.3 7.2 %collective-permute-done.12 = bf16[2,384,256]{2,1,0:T(8,128)(2,1)S(1)} collective-permute-done((bf16[2,384,256]{2,1,0:T(8,128)(2,1)S(1)}, bf16[2,384,256]{2,1,0:T(8,128)(2,1)S(1)}, u32[]{:S(2)}, u32[]{:S(2)}) %collective-permute-start.12) | collective-permute-done | bytes 393248 | tf_op jit(solution)/shard_map/ppermute | solution.py:17
  191.5 1.2 fusion.9
  193.8 5.5 %all-to-all-done.parts.parts_high = bf16[8,3,2,2,16,256]{5,4,3,2,1,0:T(8,128)(2,1)S(1)} async-done(((bf16[8,3,2,2,16,256]{5,4,3,2,1,0:T(8,128)(2,1)}), bf16[8,3,2,2,16,256]{5,4,3,2,1,0:T(8,128)(2,1)S(1)}, u32[]{:S(2)}, u32[]{:S(2)}) %all-to-all-start) | async-done | bytes 786464 | tf_op jit(solution)/shard_map/all_to_all | solution.py:182
  200.4 5.0 %collective-permute-start.13 = (bf16[8,3,2,2,16,256]{5,4,3,2,1,0:T(8,128)(2,1)}, bf16[8,3,2,2,16,256]{5,4,3,2,1,0:T(8,128)(2,1)}, u32[]{:S(2)}, u32[]{:S(2)}) collective-permute-start(bf16[8,3,2,2,16,256]{5,4,3,2,1,0:T(8,128)(2,1)} %fusion.20), channel_id=1, source_target_pairs={{0,1},{1,0},{2,3},{3,2},{4,5},{5,4},{6,7},{7,6},{8,9},{9,8},{10,11... | collective-permute-start | bytes 2359304 | tf_op jit(solution)/shard_map/ppermute | solution.py:175
  205.4 2.1 convolution_convert_fusion
  207.5 1.8 rev.7
  210.5 1.6 fusion.1
  213.1 4.3 %collective-permute-start.14 = (bf16[416,256]{1,0:T(8,128)(2,1)}, bf16[416,256]{1,0:T(8,128)(2,1)S(1)}, u32[]{:S(2)}, u32[]{:S(2)}) collective-permute-start(bf16[416,256]{1,0:T(8,128)(2,1)} %pad_maximum_fusion.5), channel_id=1, source_target_pairs={{0,256},{16,272},{32,288},{48,304},{64,320},{80,336},{96,352},{112... | collective-permute-start | bytes 638984 | tf_op jit(solution)/shard_map/ppermute | solution.py:17
  217.8 3.6 %all-to-all-start.1 = ((bf16[8,3,2,2,16,256]{5,4,3,2,1,0:T(8,128)(2,1)}), bf16[8,3,2,2,16,256]{5,4,3,2,1,0:T(8,128)(2,1)S(1)}, u32[]{:S(2)}, u32[]{:S(2)}) async-start(bf16[8,3,2,2,16,256]{5,4,3,2,1,0:T(8,128)(2,1)} %copy-done.8), calls=%async_computation.1 | async-start | bytes 1572864 | tf_op jit(solution)/shard_map/all_to_all | solution.py:182
  221.3 9.6 %collective-permute-done.14 = bf16[416,256]{1,0:T(8,128)(2,1)S(1)} collective-permute-done((bf16[416,256]{1,0:T(8,128)(2,1)}, bf16[416,256]{1,0:T(8,128)(2,1)S(1)}, u32[]{:S(2)}, u32[]{:S(2)}) %collective-permute-start.14) | collective-permute-done | bytes 213024 | tf_op jit(solution)/shard_map/ppermute | solution.py:17
  231.1 1.9 collective-permute-start.15
  234.1 10.3 %collective-permute-done.15.came = bf16[448,256]{1,0:T(8,128)(2,1)S(1)} collective-permute-done((bf16[448,256]{1,0:T(8,128)(2,1)S(1)}, bf16[448,256]{1,0:T(8,128)(2,1)S(1)}, u32[]{:S(2)}, u32[]{:S(2)}) %collective-permute-start.15) | collective-permute-done | bytes 229408 | tf_op jit(solution)/shard_map/ppermute | solution.py:17
  245.4 1.5 shard_map.71
  (134 shorter events, 31.0 us)
Async XLA Ops:
  7.2 51.6 %all-gather.3.cloned.1.call-start = ((), (), s32[]{:S(2)}) async-start(), calls=%async_computation.2 | async-start | bytes 1671168 | tf_op jit(solution)/shard_map/all_gather | solution.py:204
  7.2 1.0 copy-start
  8.2 0.9 copy-start.2
  9.1 0.7 copy-start.3
  11.1 89.6 %all-gather.5.cloned.1.call-start = ((), (), s32[]{:S(2)}) async-start(), calls=%async_computation.3 | async-start | bytes 1114112 | tf_op jit(solution)/shard_map/all_gather | solution.py:223
  11.2 28.2 %collective-permute-start.2 = (bf16[448,256]{1,0:T(8,128)(2,1)S(1)}, bf16[448,256]{1,0:T(8,128)(2,1)S(1)}, u32[]{:S(2)}, u32[]{:S(2)}) collective-permute-start(bf16[448,256]{1,0:T(8,128)(2,1)S(1)} %get-tuple-element.14), channel_id=1, source_target_pairs={{0,128},{16,144},{32,160},{48,176},{64,192},{80,208},{96,224},{112... | collective-permute-start | bytes 688136 | tf_op jit(solution)/shard_map/ppermute | solution.py:17
  18.9 20.4 %copy-start.10 = (bf16[1,384,256]{2,1,0:T(8,128)(2,1)}, bf16[1,384,256]{2,1,0:T(8,128)(2,1)S(1)}, u32[]{:S(2)}) copy-start(bf16[1,384,256]{2,1,0:T(8,128)(2,1)S(1)} %get-tuple-element.34) | copy-start | bytes 589828
  19.0 20.4 %copy-start.1 = (bf16[384,512]{1,0:T(8,128)(2,1)S(1)}, bf16[384,512]{1,0:T(8,128)(2,1)}, u32[]{:S(2)}) copy-start(bf16[384,512]{1,0:T(8,128)(2,1)} %cotangent.3) | copy-start | bytes 1179652
  19.0 20.4 %copy-start.4 = (s32[6,64]{1,0:T(8,128)S(1)}, s32[6,64]{1,0:T(8,128)}, u32[]{:S(2)}) copy-start(s32[6,64]{1,0:T(8,128)} %matchings.9) | copy-start | bytes 4612
  40.0 16.5 %collective-permute-start.4 = (bf16[416,256]{1,0:T(8,128)(2,1)S(1)}, bf16[416,256]{1,0:T(8,128)(2,1)S(1)}, u32[]{:S(2)}, u32[]{:S(2)}) collective-permute-start(bf16[416,256]{1,0:T(8,128)(2,1)S(1)} %get-tuple-element.18), channel_id=1, source_target_pairs={{0,256},{16,272},{32,288},{48,304},{64,320},{80,336},{96,352},{112... | collective-permute-start | bytes 638984 | tf_op jit(solution)/shard_map/ppermute | solution.py:17
  49.5 14.1 %copy-start.12 = (bf16[2,384,256]{2,1,0:T(8,128)(2,1)}, bf16[2,384,256]{2,1,0:T(8,128)(2,1)S(1)}, u32[]{:S(2)}) copy-start(bf16[2,384,256]{2,1,0:T(8,128)(2,1)S(1)} %fusion.4) | copy-start | bytes 1179652
  49.5 12.1 %collective-permute-start = (bf16[2,384,256]{2,1,0:T(8,128)(2,1)S(1)}, bf16[2,384,256]{2,1,0:T(8,128)(2,1)S(1)}, u32[]{:S(2)}, u32[]{:S(2)}) collective-permute-start(bf16[2,384,256]{2,1,0:T(8,128)(2,1)S(1)} %fusion.4), channel_id=1, source_target_pairs={{0,16},{16,0},{32,48},{48,32},{64,80},{80,64},{96,112},{112,96},{1... | collective-permute-start | bytes 1179656 | tf_op jit(solution)/shard_map/ppermute | solution.py:17
  61.6 0.8 copy-start.21
  63.6 12.7 %collective-permute-start.1 = (bf16[2,384,256]{2,1,0:T(8,128)(2,1)S(1)}, bf16[2,384,256]{2,1,0:T(8,128)(2,1)S(1)}, u32[]{:S(2)}, u32[]{:S(2)}) collective-permute-start(bf16[2,384,256]{2,1,0:T(8,128)(2,1)S(1)} %fusion.5), channel_id=1, source_target_pairs={{0,32},{16,48},{32,0},{48,16},{64,96},{80,112},{96,64},{112,80},{1... | collective-permute-start | bytes 1179656 | tf_op jit(solution)/shard_map/ppermute | solution.py:17
  76.3 6.9 %copy-start.14 = (bf16[2,384,256]{2,1,0:T(8,128)(2,1)}, bf16[2,384,256]{2,1,0:T(8,128)(2,1)S(1)}, u32[]{:S(2)}) copy-start(bf16[2,384,256]{2,1,0:T(8,128)(2,1)S(1)} %collective-permute-done.1) | copy-start | bytes 1179652
  77.7 10.4 %copy-start.16 = (bf16[2,384,256]{2,1,0:T(8,128)(2,1)}, bf16[2,384,256]{2,1,0:T(8,128)(2,1)S(1)}, u32[]{:S(2)}) copy-start(bf16[2,384,256]{2,1,0:T(8,128)(2,1)S(1)} %fusion.6) | copy-start | bytes 1179652
  77.7 10.4 %collective-permute-start.3 = (bf16[2,384,256]{2,1,0:T(8,128)(2,1)S(1)}, bf16[2,384,256]{2,1,0:T(8,128)(2,1)S(1)}, u32[]{:S(2)}, u32[]{:S(2)}) collective-permute-start(bf16[2,384,256]{2,1,0:T(8,128)(2,1)S(1)} %fusion.6), channel_id=1, source_target_pairs={{0,64},{16,80},{32,96},{48,112},{64,0},{80,16},{96,32},{112,48},{1... | collective-permute-start | bytes 1179656 | tf_op jit(solution)/shard_map/ppermute | solution.py:17
  88.1 5.2 %copy-start.23 = (bf16[2,384,256]{2,1,0:T(8,128)(2,1)}, bf16[2,384,256]{2,1,0:T(8,128)(2,1)S(1)}, u32[]{:S(2)}) copy-start(bf16[2,384,256]{2,1,0:T(8,128)(2,1)S(1)} %collective-permute-done.3) | copy-start | bytes 1179652
  89.3 12.5 %collective-permute-start.5 = (bf16[384,256]{1,0:T(8,128)(2,1)S(1)}, bf16[384,256]{1,0:T(8,128)(2,1)S(1)}, u32[]{:S(2)}, u32[]{:S(2)}) collective-permute-start(bf16[384,256]{1,0:T(8,128)(2,1)S(1)} %fusion.13), channel_id=1, source_target_pairs={{0,128},{16,144},{32,160},{48,176},{64,192},{80,208},{96,224},{112... | collective-permute-start | bytes 589832 | tf_op jit(solution)/shard_map/ppermute | solution.py:17
  100.8 12.1 %copy-start.5 = (bf16[2,2,2,256,256]{4,3,2,1,0:T(8,128)(2,1)S(1)}, bf16[2,2,2,256,256]{4,3,2,1,0:T(8,128)(2,1)}, u32[]{:S(2)}) copy-start(bf16[2,2,2,256,256]{4,3,2,1,0:T(8,128)(2,1)} %all-gather.5.cloned.1.call-done) | copy-start | bytes 3145732
  104.0 15.5 %collective-permute-start.6 = (bf16[384,256]{1,0:T(8,128)(2,1)S(1)}, bf16[384,256]{1,0:T(8,128)(2,1)S(1)}, u32[]{:S(2)}, u32[]{:S(2)}) collective-permute-start(bf16[384,256]{1,0:T(8,128)(2,1)S(1)} %fusion.14), channel_id=1, source_target_pairs={{0,256},{16,272},{32,288},{48,304},{64,320},{80,336},{96,352},{112... | collective-permute-start | bytes 589832 | tf_op jit(solution)/shard_map/ppermute | solution.py:17
  123.4 12.4 %collective-permute-start.7 = (bf16[384,256]{1,0:T(8,128)(2,1)S(1)}, bf16[384,256]{1,0:T(8,128)(2,1)S(1)}, u32[]{:S(2)}, u32[]{:S(2)}) collective-permute-start(bf16[384,256]{1,0:T(8,128)(2,1)S(1)} %fusion.17), channel_id=1, source_target_pairs={{0,256},{16,272},{32,288},{48,304},{64,320},{80,336},{96,352},{112... | collective-permute-start | bytes 589832 | tf_op jit(solution)/shard_map/ppermute | solution.py:17
  136.3 9.2 %copy-start.17 = (bf16[2,384,256]{2,1,0:T(8,128)(2,1)S(1)}, bf16[2,384,256]{2,1,0:T(8,128)(2,1)}, u32[]{:S(2)}) copy-start(bf16[2,384,256]{2,1,0:T(8,128)(2,1)} %copy-done.16) | copy-start | bytes 1179652
  136.3 9.2 %collective-permute-start.8 = (bf16[384,256]{1,0:T(8,128)(2,1)S(1)}, bf16[384,256]{1,0:T(8,128)(2,1)S(1)}, u32[]{:S(2)}, u32[]{:S(2)}) collective-permute-start(bf16[384,256]{1,0:T(8,128)(2,1)S(1)} %fusion.18), channel_id=1, source_target_pairs={{0,128},{16,144},{32,160},{48,176},{64,192},{80,208},{96,224},{112... | collective-permute-start | bytes 589832 | tf_op jit(solution)/shard_map/ppermute | solution.py:17
  138.7 7.3 %copy-start.9 = (bf16[3,2,2,256,256]{4,3,2,1,0:T(8,128)(2,1)S(1)}, bf16[3,2,2,256,256]{4,3,2,1,0:T(8,128)(2,1)}, u32[]{:S(2)}) copy-start(bf16[3,2,2,256,256]{4,3,2,1,0:T(8,128)(2,1)} %all-gather.3.cloned.1.call-done) | copy-start | bytes 4718596
  139.2 9.0 %copy-start.24 = (bf16[2,384,256]{2,1,0:T(8,128)(2,1)S(1)}, bf16[2,384,256]{2,1,0:T(8,128)(2,1)}, u32[]{:S(2)}) copy-start(bf16[2,384,256]{2,1,0:T(8,128)(2,1)} %copy-done.23) | copy-start | bytes 1179652
  146.2 9.9 %collective-permute-start.10 = (bf16[2,384,256]{2,1,0:T(8,128)(2,1)S(1)}, bf16[2,384,256]{2,1,0:T(8,128)(2,1)S(1)}, u32[]{:S(2)}, u32[]{:S(2)}) collective-permute-start(bf16[2,384,256]{2,1,0:T(8,128)(2,1)S(1)} %convolution_convert_fusion.3), channel_id=1, source_target_pairs={{0,64},{16,80},{32,96},{48,112},{64,0},{80,16},{96,32},{112,48},{1... | collective-permute-start | bytes 1179656 | tf_op jit(solution)/shard_map/ppermute | solution.py:17
  149.1 13.2 %copy-start.15 = (bf16[2,384,256]{2,1,0:T(8,128)(2,1)S(1)}, bf16[2,384,256]{2,1,0:T(8,128)(2,1)}, u32[]{:S(2)}) copy-start(bf16[2,384,256]{2,1,0:T(8,128)(2,1)} %copy-done.14) | copy-start | bytes 1179652
  149.1 14.3 %collective-permute-start.9 = (bf16[8,3,2,2,16,256]{5,4,3,2,1,0:T(8,128)(2,1)S(1)}, bf16[8,3,2,2,16,256]{5,4,3,2,1,0:T(8,128)(2,1)S(1)}, u32[]{:S(2)}, u32[]{:S(2)}) collective-permute-start(bf16[8,3,2,2,16,256]{5,4,3,2,1,0:T(8,128)(2,1)S(1)} %select_bitcast_fusion), channel_id=1, source_target_pairs={{0,1},{1,0},{2,3},{3,2},{4,5},{5,4},{6,7},{7,6},{8,9},{9,8},{10,11... | collective-permute-start | bytes 2359304 | tf_op jit(solution)/shard_map/ppermute | solution.py:175
  157.5 21.3 %collective-permute-start.11 = (bf16[2,384,256]{2,1,0:T(8,128)(2,1)}, bf16[2,384,256]{2,1,0:T(8,128)(2,1)}, u32[]{:S(2)}, u32[]{:S(2)}) collective-permute-start(bf16[2,384,256]{2,1,0:T(8,128)(2,1)} %convolution_convert_fusion.2), channel_id=1, source_target_pairs={{0,32},{16,48},{32,0},{48,16},{64,96},{80,112},{96,64},{112,80},{1... | collective-permute-start | bytes 1179656 | tf_op jit(solution)/shard_map/ppermute | solution.py:17
  164.6 34.7 %all-to-all-start = ((bf16[8,3,2,2,16,256]{5,4,3,2,1,0:T(8,128)(2,1)}), bf16[8,3,2,2,16,256]{5,4,3,2,1,0:T(8,128)(2,1)S(1)}, u32[]{:S(2)}, u32[]{:S(2)}) async-start(bf16[8,3,2,2,16,256]{5,4,3,2,1,0:T(8,128)(2,1)} %fusion.3), calls=%async_computation | async-start | bytes 1572864 | tf_op jit(solution)/shard_map/all_to_all | solution.py:182
  178.1 5.4 %copy-start.13 = (bf16[2,384,256]{2,1,0:T(8,128)(2,1)S(1)}, bf16[2,384,256]{2,1,0:T(8,128)(2,1)}, u32[]{:S(2)}) copy-start(bf16[2,384,256]{2,1,0:T(8,128)(2,1)} %copy-done.12) | copy-start | bytes 1179652
  178.8 5.0 %copy-start.22 = (bf16[2,384,256]{2,1,0:T(8,128)(2,1)S(1)}, bf16[2,384,256]{2,1,0:T(8,128)(2,1)}, u32[]{:S(2)}) copy-start(bf16[2,384,256]{2,1,0:T(8,128)(2,1)} %copy-done.21) | copy-start | bytes 1179652
  181.5 10.0 %collective-permute-start.12 = (bf16[2,384,256]{2,1,0:T(8,128)(2,1)S(1)}, bf16[2,384,256]{2,1,0:T(8,128)(2,1)S(1)}, u32[]{:S(2)}, u32[]{:S(2)}) collective-permute-start(bf16[2,384,256]{2,1,0:T(8,128)(2,1)S(1)} %convolution_convert_fusion.1), channel_id=1, source_target_pairs={{0,16},{16,0},{32,48},{48,32},{64,80},{80,64},{96,112},{112,96},{1... | collective-permute-start | bytes 1179656 | tf_op jit(solution)/shard_map/ppermute | solution.py:17
  183.9 8.9 %copy-start.11 = (bf16[1,384,256]{2,1,0:T(8,128)(2,1)S(1)}, bf16[1,384,256]{2,1,0:T(8,128)(2,1)}, u32[]{:S(2)}) copy-start(bf16[1,384,256]{2,1,0:T(8,128)(2,1)} %copy-done.10) | copy-start | bytes 589828
  184.3 9.3 %copy-start.19 = (bf16[2,256,256]{2,1,0:T(8,128)(2,1)S(1)}, bf16[2,256,256]{2,1,0:T(8,128)(2,1)}, u32[]{:S(2)}) copy-start(bf16[2,256,256]{2,1,0:T(8,128)(2,1)} %convolution_convert_fusion.5) | copy-start | bytes 786436
  184.3 9.3 %copy-start.20 = (bf16[2,256,256]{2,1,0:T(8,128)(2,1)S(1)}, bf16[2,256,256]{2,1,0:T(8,128)(2,1)}, u32[]{:S(2)}) copy-start(bf16[2,256,256]{2,1,0:T(8,128)(2,1)} %convolution_convert_fusion.4) | copy-start | bytes 786436
  192.8 0.7 copy-start.6
  200.4 10.1 %collective-permute-start.13 = (bf16[8,3,2,2,16,256]{5,4,3,2,1,0:T(8,128)(2,1)}, bf16[8,3,2,2,16,256]{5,4,3,2,1,0:T(8,128)(2,1)}, u32[]{:S(2)}, u32[]{:S(2)}) collective-permute-start(bf16[8,3,2,2,16,256]{5,4,3,2,1,0:T(8,128)(2,1)} %fusion.20), channel_id=1, source_target_pairs={{0,1},{1,0},{2,3},{3,2},{4,5},{5,4},{6,7},{7,6},{8,9},{9,8},{10,11... | collective-permute-start | bytes 2359304 | tf_op jit(solution)/shard_map/ppermute | solution.py:175
  210.5 1.6 copy-start.25
  210.5 6.9 %copy-start.7 = (bf16[2,384,256]{2,1,0:T(8,128)(2,1)S(1)}, bf16[2,384,256]{2,1,0:T(8,128)(2,1)}, u32[]{:S(2)}) copy-start(bf16[2,384,256]{2,1,0:T(8,128)(2,1)} %copy-done.6) | copy-start | bytes 1179652
  210.5 6.9 %copy-start.18 = (bf16[2,384,256]{1,2,0:T(8,128)(2,1)S(1)}, bf16[2,384,256]{1,2,0:T(8,128)(2,1)}, u32[]{:S(2)}) copy-start(bf16[2,384,256]{1,2,0:T(8,128)(2,1)} %rev.7) | copy-start | bytes 1179652
  212.1 5.6 %copy-start.8 = (bf16[8,3,2,2,16,256]{5,4,3,2,1,0:T(8,128)(2,1)}, bf16[8,3,2,2,16,256]{5,4,3,2,1,0:T(8,128)(2,1)S(1)}, u32[]{:S(2)}) copy-start(bf16[8,3,2,2,16,256]{5,4,3,2,1,0:T(8,128)(2,1)S(1)} %fusion.1) | copy-start | bytes 2359300
  213.1 17.8 %copy-start.26 = (bf16[1,2,16,256]{3,2,1,0:T(8,128)(2,1)S(1)}, bf16[1,2,16,256]{3,2,1,0:T(8,128)(2,1)}, u32[]{:S(2)}) copy-start(bf16[1,2,16,256]{3,2,1,0:T(8,128)(2,1)} %get-tuple-element.35) | copy-start | bytes 49156
  213.1 17.8 %collective-permute-start.14 = (bf16[416,256]{1,0:T(8,128)(2,1)}, bf16[416,256]{1,0:T(8,128)(2,1)S(1)}, u32[]{:S(2)}, u32[]{:S(2)}) collective-permute-start(bf16[416,256]{1,0:T(8,128)(2,1)} %pad_maximum_fusion.5), channel_id=1, source_target_pairs={{0,256},{16,272},{32,288},{48,304},{64,320},{80,336},{96,352},{112... | collective-permute-start | bytes 638984 | tf_op jit(solution)/shard_map/ppermute | solution.py:17
  217.8 27.6 %all-to-all-start.1 = ((bf16[8,3,2,2,16,256]{5,4,3,2,1,0:T(8,128)(2,1)}), bf16[8,3,2,2,16,256]{5,4,3,2,1,0:T(8,128)(2,1)S(1)}, u32[]{:S(2)}, u32[]{:S(2)}) async-start(bf16[8,3,2,2,16,256]{5,4,3,2,1,0:T(8,128)(2,1)} %copy-done.8), calls=%async_computation.1 | async-start | bytes 1572864 | tf_op jit(solution)/shard_map/all_to_all | solution.py:182
  231.1 13.3 %collective-permute-start.15 = (bf16[448,256]{1,0:T(8,128)(2,1)S(1)}, bf16[448,256]{1,0:T(8,128)(2,1)S(1)}, u32[]{:S(2)}, u32[]{:S(2)}) collective-permute-start(bf16[448,256]{1,0:T(8,128)(2,1)S(1)} %pad_maximum_fusion.4), channel_id=1, source_target_pairs={{0,128},{16,144},{32,160},{48,176},{64,192},{80,208},{96,224},{112... | collective-permute-start | bytes 688136 | tf_op jit(solution)/shard_map/ppermute | solution.py:17
Sparse Core Ops, SparseCore 0:
  11.3 47.4 all-gather.2
  60.9 39.7 all-gather.4

commit v6 on v5

--- a/solution.py
+++ b/solution.py
@@ -33,11 +33,6 @@
 
 def dot_rows(left, right):
     return jnp.einsum("...tk,...tl->...kl", left, right, preferred_element_type=jnp.float32).astype(jnp.bfloat16)
-
-
-def unpack(packed, shape):
-    rows = math.prod(shape[:-1])
-    return packed[:rows].reshape(shape), packed[rows:]
 
 
 def bits():
@@ -59,16 +54,20 @@
     return (matchings[section, block] != block).astype(jnp.int32) ^ turn
 
 
-def prepare(matchings, weights, cotangent, first, rest, keep, packed):
+def order_early(matchings, weights, first, rest):
     _, low, _ = bits()
-    width = weights.shape[-1]
-    depth = weights.shape[-2]
     for section in range(4):
         for row in range(2):
             at = choice(matchings, section, row)
             out = first.at[0] if section == 0 else rest.at[section - 1]
             out[0, row] = weights[section, row ^ low, at]
             out[1, row] = weights[section, row ^ low, 1 - at]
+
+
+def pack_late(matchings, weights, cotangent, keep, packed):
+    _, low, _ = bits()
+    width = weights.shape[-1]
+    depth = weights.shape[-2]
     for place in range(2):
         for both in range(2):
             keep[place, both] = weights[4 + place, low, both]
@@ -164,15 +163,12 @@
     return jnp.moveaxis(half, 3, 0)
 
 
-def chip_sum(terms, waits):
+def chip_sum(terms):
     count, both, per_dev, depth, width = terms.shape
     size = lax.axis_size("tok")
     core = lax.axis_index("tok") & 1
     terms = terms.reshape(count, both, per_dev, size, depth // size, width)
-    give = core_half(terms, 1 - core)
-    if waits is not None:
-        give = after(give, waits)
-    came = lax.ppermute(give, "tok", [(source, source ^ 1) for source in range(size)])
+    came = lax.ppermute(core_half(terms, 1 - core), "tok", [(source, source ^ 1) for source in range(size)])
     return (core_half(terms, core).astype(jnp.float32) + came.astype(jnp.float32)).astype(jnp.bfloat16)
 
 
@@ -192,12 +188,9 @@
     def shape(*dims, dtype=bf16):
         return jax.ShapeDtypeStruct((*dims, width), dtype)
 
-    first, rest, keep, packed = local(
-        prepare,
-        matchings,
-        weights,
-        cotangent,
-        outs=[shape(1, 2, 2, depth), shape(3, 2, 2, depth), shape(2, 2, depth), shape(4 * depth + tokens)],
+    first, rest = local(order_early, matchings, weights, outs=[shape(1, 2, 2, depth), shape(3, 2, 2, depth)])
+    keep, packed = local(
+        pack_late, matchings, weights, cotangent, outs=[shape(2, 2, depth), shape(4 * depth + tokens)]
     )
     came = flip(packed, 3)
     full = list(lax.all_gather(first, "tok", axis=3, tiled=True))
@@ -225,6 +218,7 @@
     for section in range(1, 4):
         other = flip(value, section - 1)
         inputs.append((value, other))
+        full[section] = after(full[section], value)
         own_w, other_w = full[section][0], full[section][1]
         if section < 3:
             value = (dot(value, own_w) + dot(other, other_w)).astype(bf16)
@@ -233,11 +227,13 @@
             keep = (dot(value[0], own_w[0]) + dot(other[0], other_w[0])).astype(bf16)
     came = flip(send, 3)
     inputs.append((keep, came))
+    full[4] = after(full[4], send)
     own_w, other_w = full[4][0], full[4][1]
     send = (dot(keep, own_w[1]) + dot(came, other_w[1])).astype(bf16)
     keep = (dot(keep, own_w[0]) + dot(came, other_w[0])).astype(bf16)
     came = flip(send, 4)
     inputs.append((keep, came))
+    full[5] = after(full[5], send)
     own_w, other_w = full[5][0], full[5][1]
 
     results, grads = [], []
@@ -258,33 +254,40 @@
         )
         grads = [kept, back]
     grad = jnp.stack(grads)
-    for section in (3, 2, 1, 0):
+    for section in (3, 2, 1):
         own_w, other_w = full[section][0], full[section][1]
         sent = dot_back(grad, other_w).astype(bf16)
-        back = sent[::-1] if section == 0 else flip(sent, section - 1)
+        back = flip(sent, section - 1)
         terms[section] = jnp.stack([dot_rows(part, grad) for part in inputs[section]])
         if section == 3:
-            chip = chip_sum(jnp.stack(terms[3:]), None)
+            chip = chip_sum(jnp.stack(terms[3:]))
             parts_high = all_parts(chip)
         grad = (dot_back(grad, own_w) + back.astype(jnp.float32)).astype(bf16)
         if section == 2:
             grad = after(grad, chip)
-    chip = chip_sum(jnp.stack(terms[:3]), parts_high)
+    terms[0] = jnp.stack([dot_rows(part, grad) for part in inputs[0]])
+    chip = after(chip_sum(jnp.stack(terms[:3])), parts_high)
     parts_low = all_parts(chip)
-    input_grad = jnp.concatenate([jnp.where(low, grad[1], grad[0]), jnp.where(low, grad[0], grad[1])], axis=1)
+
+    out_came = flip(after(results[1], sent), 4)
+    out_keep, out_send = jnp.where(same, results[0], out_came), jnp.where(same, out_came, results[0])
+    out_came = flip(after(out_send, chip), 3)
+    result = jnp.concatenate([jnp.where(low, out_came, out_keep), jnp.where(low, out_keep, out_came)], axis=1)
 
     rows = local(unorder_late, matchings, parts_high, outs=[shape(2, 2, 2, depth)])
-    packed = jnp.concatenate([rows[1, 1].reshape(-1, width), after(results[1], chip)])
-    came, out_came = unpack(flip(packed, 4), (2, depth, width))
-    row0, row1 = rows[0], jnp.stack([rows[1, 0], came])
+    row0, row1 = rows[0], jnp.stack([rows[1, 0], flip(rows[1, 1], 4)])
     keep, send = jnp.where(same, row0, row1), jnp.where(same, row1, row0)
-    out_keep, out_send = jnp.where(same, results[0], out_came), jnp.where(same, out_came, results[0])
-    packed = flip(jnp.concatenate([send.reshape(-1, width), out_send]), 3)
-    out_came = packed[4 * depth :]
-    result = jnp.concatenate([jnp.where(low, out_came, out_keep), jnp.where(low, out_keep, out_came)], axis=1)
+    came = flip(send, 3).reshape(4 * depth, width)
     weight_grad = local(
-        finish, matchings, parts_low, parts_high, keep, packed, outs=[shape(6, 2, 2, depth, dtype=jnp.float32)]
+        finish, matchings, parts_low, parts_high, keep, came, outs=[shape(6, 2, 2, depth, dtype=jnp.float32)]
     )
+
+    grad = after(grad, chip)
+    own_w, other_w = full[0][0], full[0][1]
+    first, second = [
+        (dot_back(grad[r], own_w[r]) + dot_back(grad[1 - r], other_w[1 - r])).astype(bf16) for r in range(2)
+    ]
+    input_grad = jnp.concatenate([jnp.where(low, second, first), jnp.where(low, first, second)], axis=1)
     return result, input_grad, weight_grad
 
 

time: 255 us -> 245 us (0.961)
  waiting for transfers between devices: 78.2 us -> 66.7 us
  matrix products: 30.7 us -> 20 us
  starting transfers between devices: 88.6 us -> 96.5 us
  other arithmetic: 8.73 us -> 13.4 us
    ppermute x14 -> x16, starting transfers between devices: 59.5 us -> 76.8 us  [flip(): return lax.ppermute(value, 'blk', pairs)]
    ppermute x14 -> x16, waiting for transfers between devices: 65.4 us -> 56.5 us  [flip(): return lax.ppermute(value, 'blk', pairs)]
    dot_general x18, matrix products: 14.5 us -> 6.17 us  [dot(): jnp.einsum('...tk,...kl->...tl', left, right, preferred_element_type=jnp....]
    all_to_all x2, starting transfers between devices: 17 us -> 10.9 us  [all_parts(): return lax.all_to_all(chip, 'tok', 0, 0, axis_index_groups=groups)]
    all_to_all x2, waiting for transfers between devices: 5.48 us -> 0.17 us  [all_parts(): return lax.all_to_all(chip, 'tok', 0, 0, axis_index_groups=groups)]
    select_n x2 -> x9, other arithmetic: 1.22 us -> 5.94 us  [after(): return jnp.where(probe != probe, jnp.zeros_like(value), value)]
    all_gather x1, waiting for transfers between devices: 6.33 us -> 9.94 us  [body(): full += list(lax.all_gather(late, 'tok', axis=3, tiled=True))]
    dot_general x16 -> x18, matrix products: 9.87 us -> 6.44 us  [dot_back(): jnp.einsum('...tl,...kl->...tk', left, right, preferred_element_type=jnp....]
  transfers between devices with their start and end apart: 20 -> 22, of which waited for: 14 -> 11; matrix products, arithmetic and copies ran while one was open for 13% -> 12% of each run, Pallas kernels for 1% -> 1%
where the time goes in v6:
time: 245 us; the launch traced here: 243 us
  starting transfers between devices  96.5 us (39%)
  waiting for transfers between devices  66.7 us (27%)
  blocking collectives  20.2 us (8%)
  matrix products  20 us (8%)
  between operations  15 us (6%)
  other arithmetic  13.4 us (5%)
  Pallas kernels  5.96 us (2%)
  local copies, waits for them, and re-layouts  5.63 us (2%)
    ppermute x16, starting transfers between devices, flip(): return lax.ppermute(value, 'blk', pairs)  76.8 us
    ppermute x16, waiting for transfers between devices, flip(): return lax.ppermute(value, 'blk', pairs)  56.5 us
    all_gather x1, blocking collectives, body(): full = list(lax.all_gather(first, 'tok', axis=3, tiled=True))  20.2 us
    all_to_all x2, starting transfers between devices, all_parts(): return lax.all_to_all(chip, 'tok', 0, 0, axis_index_groups=groups)  10.9 us
    all_gather x1, waiting for transfers between devices, body(): full += list(lax.all_gather(late, 'tok', axis=3, tiled=True))  9.94 us
    ppermute x2, starting transfers between devices, chip_sum(): lax.ppermute(core_half(terms, 1 - core), 'tok', [(source, source ^ 1) for...  8.67 us
    dot_general x16, matrix products, dot_rows(): jnp.einsum('...tk,...tl->...kl', left, right, preferred_element_type=jnp....  7.34 us
    dot_general x18, matrix products, dot_back(): jnp.einsum('...tl,...kl->...tk', left, right, preferred_element_type=jnp....  6.44 us
  transfers between devices with their start and end apart: 22, of which 11 were waited for; matrix products, arithmetic and copies ran while one was open for 12% of the time, Pallas kernels for 1%

profile of v6, /device:TPU:1, one launch (start us, length us, event | category | flops | bytes accessed | tf_op | source)
XLA Modules:
  0.0 243.3 jit_solution(3674141731803966817)
XLA Ops:
  8.8 1.3 shard_map.67
  10.2 1.0 copy-done
  13.4 6.6 %collective-permute-start.2 = (bf16[448,256]{1,0:T(8,128)(2,1)S(1)}, bf16[448,256]{1,0:T(8,128)(2,1)S(1)}, u32[]{:S(2)}, u32[]{:S(2)}) collective-permute-start(bf16[448,256]{1,0:T(8,128)(2,1)S(1)} %get-tuple-element.14), channel_id=1, source_target_pairs={{0,128},{16,144},{32,160},{48,176},{64,192},{80,208},{96,224},{112... | collective-permute-start | bytes 688136 | tf_op jit(solution)/shard_map/ppermute | solution.py:17
  20.1 1.1 select_bitcast_fusion.3
  21.3 20.2 %all_gather.9 = bf16[1,2,2,256,256]{4,3,2,1,0:T(8,128)(2,1)S(1)} all-gather(bf16[1,2,2,16,256]{4,3,2,1,0:T(8,128)(2,1)S(1)} %get-tuple-element.11), channel_id=1, replica_groups=mesh['blk'=32,'tok'=16] {'tok'}, dimensions={3}, use_global_device_ids=true | all-gather | bytes 557056 | tf_op jit(solution)/shard_map/all_gather | solution.py:196
  42.4 10.2 %collective-permute-start.4 = (bf16[416,256]{1,0:T(8,128)(2,1)S(1)}, bf16[416,256]{1,0:T(8,128)(2,1)S(1)}, u32[]{:S(2)}, u32[]{:S(2)}) collective-permute-start(bf16[416,256]{1,0:T(8,128)(2,1)S(1)} %get-tuple-element.18), channel_id=1, source_target_pairs={{0,256},{16,272},{32,288},{48,304},{64,320},{80,336},{96,352},{112... | collective-permute-start | bytes 638984 | tf_op jit(solution)/shard_map/ppermute | solution.py:17
  52.9 3.1 %collective-permute-start = (bf16[2,384,256]{2,1,0:T(8,128)(2,1)S(1)}, bf16[2,384,256]{2,1,0:T(8,128)(2,1)}, u32[]{:S(2)}, u32[]{:S(2)}) collective-permute-start(bf16[2,384,256]{2,1,0:T(8,128)(2,1)S(1)} %fusion.4), channel_id=1, source_target_pairs={{0,16},{16,0},{32,48},{48,32},{64,80},{80,64},{96,112},{112,96},{1... | collective-permute-start | bytes 1179656 | tf_op jit(solution)/shard_map/ppermute | solution.py:17
  56.0 6.6 %collective-permute-done.4.came = bf16[416,256]{1,0:T(8,128)(2,1)S(1)} collective-permute-done((bf16[416,256]{1,0:T(8,128)(2,1)S(1)}, bf16[416,256]{1,0:T(8,128)(2,1)S(1)}, u32[]{:S(2)}, u32[]{:S(2)}) %collective-permute-start.4) | collective-permute-done | bytes 213024 | tf_op jit(solution)/shard_map/ppermute | solution.py:17
  62.6 1.2 shard_map.70
  63.9 1.1 fusion.26
  65.3 1.4 fusion.5
  66.7 4.3 %collective-permute-start.1 = (bf16[2,384,256]{2,1,0:T(8,128)(2,1)S(1)}, bf16[2,384,256]{2,1,0:T(8,128)(2,1)S(1)}, u32[]{:S(2)}, u32[]{:S(2)}) collective-permute-start(bf16[2,384,256]{2,1,0:T(8,128)(2,1)S(1)} %fusion.5), channel_id=1, source_target_pairs={{0,32},{16,48},{32,0},{48,16},{64,96},{80,112},{96,64},{112,80},{1... | collective-permute-start | bytes 1179656 | tf_op jit(solution)/shard_map/ppermute | solution.py:17
  71.4 8.4 %collective-permute-done.1 = bf16[2,384,256]{2,1,0:T(8,128)(2,1)S(1)} collective-permute-done((bf16[2,384,256]{2,1,0:T(8,128)(2,1)S(1)}, bf16[2,384,256]{2,1,0:T(8,128)(2,1)S(1)}, u32[]{:S(2)}, u32[]{:S(2)}) %collective-permute-start.1) | collective-permute-done | bytes 393248 | tf_op jit(solution)/shard_map/ppermute | solution.py:17
  80.1 2.5 %collective-permute-start.3 = (bf16[2,384,256]{2,1,0:T(8,128)(2,1)S(1)}, bf16[2,384,256]{2,1,0:T(8,128)(2,1)S(1)}, u32[]{:S(2)}, u32[]{:S(2)}) collective-permute-start(bf16[2,384,256]{2,1,0:T(8,128)(2,1)S(1)} %fusion.6), channel_id=1, source_target_pairs={{0,64},{16,80},{32,96},{48,112},{64,0},{80,16},{96,32},{112,48},{1... | collective-permute-start | bytes 1179656 | tf_op jit(solution)/shard_map/ppermute | solution.py:17
  83.0 7.7 %collective-permute-done.3 = bf16[2,384,256]{2,1,0:T(8,128)(2,1)S(1)} collective-permute-done((bf16[2,384,256]{2,1,0:T(8,128)(2,1)S(1)}, bf16[2,384,256]{2,1,0:T(8,128)(2,1)S(1)}, u32[]{:S(2)}, u32[]{:S(2)}) %collective-permute-start.3) | collective-permute-done | bytes 393248 | tf_op jit(solution)/shard_map/ppermute | solution.py:17
  91.0 1.9 collective-permute-start.5
  93.2 9.9 %all-gather.5.cloned.1.call-done = bf16[2,2,2,256,256]{4,3,2,1,0:T(8,128)(2,1)} async-done(((bf16[2,2,2,16,256]{4,3,2,1,0:T(8,128)(2,1)}), bf16[2,2,2,256,256]{4,3,2,1,0:T(8,128)(2,1)}) %all-gather.5.cloned.1.call-update) | async-done | bytes 1048592 | tf_op jit(solution)/shard_map/all_gather | solution.py:216
  103.1 1.2 fusion.23
  104.9 7.8 %collective-permute-start.6 = (bf16[384,256]{1,0:T(8,128)(2,1)S(1)}, bf16[384,256]{1,0:T(8,128)(2,1)S(1)}, u32[]{:S(2)}, u32[]{:S(2)}) collective-permute-start(bf16[384,256]{1,0:T(8,128)(2,1)S(1)} %fusion.13), channel_id=1, source_target_pairs={{0,256},{16,272},{32,288},{48,304},{64,320},{80,336},{96,352},{112... | collective-permute-start | bytes 589832 | tf_op jit(solution)/shard_map/ppermute | solution.py:17
  113.4 5.8 %collective-permute-done.6 = bf16[384,256]{1,0:T(8,128)(2,1)S(1)} collective-permute-done((bf16[384,256]{1,0:T(8,128)(2,1)S(1)}, bf16[384,256]{1,0:T(8,128)(2,1)S(1)}, u32[]{:S(2)}, u32[]{:S(2)}) %collective-permute-start.6) | collective-permute-done | bytes 196640 | tf_op jit(solution)/shard_map/ppermute | solution.py:17
  120.5 1.2 fusion.34
  123.2 5.5 %collective-permute-start.7 = (bf16[384,256]{1,0:T(8,128)(2,1)S(1)}, bf16[384,256]{1,0:T(8,128)(2,1)S(1)}, u32[]{:S(2)}, u32[]{:S(2)}) collective-permute-start(bf16[384,256]{1,0:T(8,128)(2,1)S(1)} %fusion.15), channel_id=1, source_target_pairs={{0,256},{16,272},{32,288},{48,304},{64,320},{80,336},{96,352},{112... | collective-permute-start | bytes 589832 | tf_op jit(solution)/shard_map/ppermute | solution.py:17
  129.6 4.0 %collective-permute-done.7 = bf16[384,256]{1,0:T(8,128)(2,1)S(1)} collective-permute-done((bf16[384,256]{1,0:T(8,128)(2,1)S(1)}, bf16[384,256]{1,0:T(8,128)(2,1)S(1)}, u32[]{:S(2)}, u32[]{:S(2)}) %collective-permute-start.7) | collective-permute-done | bytes 196640 | tf_op jit(solution)/shard_map/ppermute | solution.py:17
  133.8 10.4 %collective-permute-start.8 = (bf16[384,256]{1,0:T(8,128)(2,1)S(1)}, bf16[384,256]{1,0:T(8,128)(2,1)S(1)}, u32[]{:S(2)}, u32[]{:S(2)}) collective-permute-start(bf16[384,256]{1,0:T(8,128)(2,1)S(1)} %fusion.17), channel_id=1, source_target_pairs={{0,128},{16,144},{32,160},{48,176},{64,192},{80,208},{96,224},{112... | collective-permute-start | bytes 589832 | tf_op jit(solution)/shard_map/ppermute | solution.py:17
  145.1 7.0 %collective-permute-done.8 = bf16[384,256]{1,0:T(8,128)(2,1)S(1)} collective-permute-done((bf16[384,256]{1,0:T(8,128)(2,1)S(1)}, bf16[384,256]{1,0:T(8,128)(2,1)S(1)}, u32[]{:S(2)}, u32[]{:S(2)}) %collective-permute-start.8) | collective-permute-done | bytes 196640 | tf_op jit(solution)/shard_map/ppermute | solution.py:17
  152.7 1.9 collective-permute-start.10
  155.6 3.2 %collective-permute-start.9 = (bf16[8,3,2,2,16,256]{5,4,3,2,1,0:T(8,128)(2,1)S(1)}, bf16[8,3,2,2,16,256]{5,4,3,2,1,0:T(8,128)(2,1)S(1)}, u32[]{:S(2)}, u32[]{:S(2)}) collective-permute-start(bf16[8,3,2,2,16,256]{5,4,3,2,1,0:T(8,128)(2,1)S(1)} %select_bitcast_fusion.1), channel_id=1, source_target_pairs={{0,1},{1,0},{2,3},{3,2},{4,5},{5,4},{6,7},{7,6},{8,9},{9,8},{10,11... | collective-permute-start | bytes 2359304 | tf_op jit(solution)/shard_map/ppermute | solution.py:171
  158.7 5.3 %collective-permute-done.10 = bf16[2,384,256]{2,1,0:T(8,128)(2,1)S(1)} collective-permute-done((bf16[2,384,256]{2,1,0:T(8,128)(2,1)S(1)}, bf16[2,384,256]{2,1,0:T(8,128)(2,1)S(1)}, u32[]{:S(2)}, u32[]{:S(2)}) %collective-permute-start.10) | collective-permute-done | bytes 393248 | tf_op jit(solution)/shard_map/ppermute | solution.py:17
  164.4 1.0 convolution_convert_fusion.1
  165.4 4.6 %collective-permute-start.11 = (bf16[2,384,256]{2,1,0:T(8,128)(2,1)}, bf16[2,384,256]{2,1,0:T(8,128)(2,1)}, u32[]{:S(2)}, u32[]{:S(2)}) collective-permute-start(bf16[2,384,256]{2,1,0:T(8,128)(2,1)} %convolution_convert_fusion.1), channel_id=1, source_target_pairs={{0,32},{16,48},{32,0},{48,16},{64,96},{80,112},{96,64},{112,80},{1... | collective-permute-start | bytes 1179656 | tf_op jit(solution)/shard_map/ppermute | solution.py:17
  170.1 1.0 convolution_convert_fusion.4
  171.1 1.1 convolution_convert_fusion.3
  172.2 1.2 fusion.3
  173.4 3.8 %all-to-all-start = ((bf16[8,3,2,2,16,256]{5,4,3,2,1,0:T(8,128)(2,1)}), bf16[8,3,2,2,16,256]{5,4,3,2,1,0:T(8,128)(2,1)S(1)}, u32[]{:S(2)}, u32[]{:S(2)}) async-start(bf16[8,3,2,2,16,256]{5,4,3,2,1,0:T(8,128)(2,1)} %fusion.3), calls=%async_computation | async-start | bytes 1572864 | tf_op jit(solution)/shard_map/all_to_all | solution.py:178
  178.0 1.3 fusion.8
  179.6 2.9 %collective-permute-start.12 = (bf16[2,384,256]{2,1,0:T(8,128)(2,1)S(1)}, bf16[2,384,256]{2,1,0:T(8,128)(2,1)S(1)}, u32[]{:S(2)}, u32[]{:S(2)}) collective-permute-start(bf16[2,384,256]{2,1,0:T(8,128)(2,1)S(1)} %convolution_convert_fusion), channel_id=1, source_target_pairs={{0,16},{16,0},{32,48},{48,32},{64,80},{80,64},{96,112},{112,96},{1... | collective-permute-start | bytes 1179656 | tf_op jit(solution)/shard_map/ppermute | solution.py:17
  182.9 1.4 convolution_convert_fusion.5
  184.4 5.1 %collective-permute-done.12 = bf16[2,384,256]{2,1,0:T(8,128)(2,1)S(1)} collective-permute-done((bf16[2,384,256]{2,1,0:T(8,128)(2,1)S(1)}, bf16[2,384,256]{2,1,0:T(8,128)(2,1)S(1)}, u32[]{:S(2)}, u32[]{:S(2)}) %collective-permute-start.12) | collective-permute-done | bytes 393248 | tf_op jit(solution)/shard_map/ppermute | solution.py:17
  191.8 5.5 %collective-permute-start.13 = (bf16[8,3,2,2,16,256]{5,4,3,2,1,0:T(8,128)(2,1)}, bf16[8,3,2,2,16,256]{5,4,3,2,1,0:T(8,128)(2,1)}, u32[]{:S(2)}, u32[]{:S(2)}) collective-permute-start(bf16[8,3,2,2,16,256]{5,4,3,2,1,0:T(8,128)(2,1)} %select_bitcast_fusion), channel_id=1, source_target_pairs={{0,1},{1,0},{2,3},{3,2},{4,5},{5,4},{6,7},{7,6},{8,9},{9,8},{10,11... | collective-permute-start | bytes 2359304 | tf_op jit(solution)/shard_map/ppermute | solution.py:171
  198.1 1.8 fusion.56
  199.9 1.9 collective-permute-start.14
  201.8 1.5 fusion.21
  204.3 7.1 %all-to-all-start.1 = ((bf16[8,3,2,2,16,256]{5,4,3,2,1,0:T(8,128)(2,1)}), bf16[8,3,2,2,16,256]{5,4,3,2,1,0:T(8,128)(2,1)S(1)}, u32[]{:S(2)}, u32[]{:S(2)}) async-start(bf16[8,3,2,2,16,256]{5,4,3,2,1,0:T(8,128)(2,1)} %copy-done.13), calls=%async_computation.1 | async-start | bytes 1572864 | tf_op jit(solution)/shard_map/all_to_all | solution.py:178
  212.1 7.0 %collective-permute-start.16 = (bf16[2,16,256]{2,1,0:T(8,128)(2,1)S(1)}, bf16[2,16,256]{2,1,0:T(8,128)(2,1)S(1)}, u32[]{:S(2)}, u32[]{:S(2)}) collective-permute-start(bf16[2,16,256]{2,1,0:T(8,128)(2,1)S(1)} %get-tuple-element.32), channel_id=1, source_target_pairs={{0,256},{16,272},{32,288},{48,304},{64,320},{80,336},{96,352},{112... | collective-permute-start | bytes 49160 | tf_op jit(solution)/shard_map/ppermute | solution.py:17
  219.3 1.9 collective-permute-start.15
  223.0 4.3 %collective-permute-start.17 = (bf16[2,2,16,256]{3,2,1,0:T(8,128)(2,1)S(1)}, bf16[2,2,16,256]{3,2,1,0:T(8,128)(2,1)S(1)}, u32[]{:S(2)}, u32[]{:S(2)}) collective-permute-start(bf16[2,2,16,256]{3,2,1,0:T(8,128)(2,1)S(1)} %get-tuple-element.29), channel_id=1, source_target_pairs={{0,128},{16,144},{32,160},{48,176},{64,192},{80,208},{96,224},{112... | collective-permute-start | bytes 98312 | tf_op jit(solution)/shard_map/ppermute | solution.py:17
  227.3 6.5 %collective-permute-done.15 = bf16[384,256]{1,0:T(8,128)(2,1)S(1)} collective-permute-done((bf16[384,256]{1,0:T(8,128)(2,1)S(1)}, bf16[384,256]{1,0:T(8,128)(2,1)S(1)}, u32[]{:S(2)}, u32[]{:S(2)}) %collective-permute-start.15) | collective-permute-done | bytes 196640 | tf_op jit(solution)/shard_map/ppermute | solution.py:17
  235.0 1.5 shard_map.72
  (153 shorter events, 23.9 us)
Async XLA Ops:
  7.2 56.7 %all-gather.3.cloned.1.call-start = ((), (), s32[]{:S(2)}) async-start(), calls=%async_computation.2 | async-start | bytes 1671168 | tf_op jit(solution)/shard_map/all_gather | solution.py:197
  7.2 0.9 copy-start.2
  10.1 93.0 %all-gather.5.cloned.1.call-start = ((), (), s32[]{:S(2)}) async-start(), calls=%async_computation.3 | async-start | bytes 1114112 | tf_op jit(solution)/shard_map/all_gather | solution.py:216
  10.2 1.0 copy-start
  13.4 28.3 %collective-permute-start.2 = (bf16[448,256]{1,0:T(8,128)(2,1)S(1)}, bf16[448,256]{1,0:T(8,128)(2,1)S(1)}, u32[]{:S(2)}, u32[]{:S(2)}) collective-permute-start(bf16[448,256]{1,0:T(8,128)(2,1)S(1)} %get-tuple-element.14), channel_id=1, source_target_pairs={{0,128},{16,144},{32,160},{48,176},{64,192},{80,208},{96,224},{112... | collective-permute-start | bytes 688136 | tf_op jit(solution)/shard_map/ppermute | solution.py:17
  21.2 20.6 %copy-start.1 = (bf16[384,512]{1,0:T(8,128)(2,1)S(1)}, bf16[384,512]{1,0:T(8,128)(2,1)}, u32[]{:S(2)}) copy-start(bf16[384,512]{1,0:T(8,128)(2,1)} %cotangent.3) | copy-start | bytes 1179652
  21.2 20.5 %copy-start.6 = (s32[6,64]{1,0:T(8,128)S(1)}, s32[6,64]{1,0:T(8,128)}, u32[]{:S(2)}) copy-start(s32[6,64]{1,0:T(8,128)} %matchings.11) | copy-start | bytes 4612
  21.3 31.6 %copy-start.9 = (bf16[2,384,256]{2,1,0:T(8,128)(2,1)}, bf16[2,384,256]{2,1,0:T(8,128)(2,1)S(1)}, u32[]{:S(2)}) copy-start(bf16[2,384,256]{2,1,0:T(8,128)(2,1)S(1)} %rev.3) | copy-start | bytes 1179652
  42.4 20.2 %collective-permute-start.4 = (bf16[416,256]{1,0:T(8,128)(2,1)S(1)}, bf16[416,256]{1,0:T(8,128)(2,1)S(1)}, u32[]{:S(2)}, u32[]{:S(2)}) collective-permute-start(bf16[416,256]{1,0:T(8,128)(2,1)S(1)} %get-tuple-element.18), channel_id=1, source_target_pairs={{0,256},{16,272},{32,288},{48,304},{64,320},{80,336},{96,352},{112... | collective-permute-start | bytes 638984 | tf_op jit(solution)/shard_map/ppermute | solution.py:17
  52.9 13.8 %copy-start.16 = (bf16[2,384,256]{2,1,0:T(8,128)(2,1)}, bf16[2,384,256]{2,1,0:T(8,128)(2,1)S(1)}, u32[]{:S(2)}) copy-start(bf16[2,384,256]{2,1,0:T(8,128)(2,1)S(1)} %fusion.4) | copy-start | bytes 1179652
  52.9 12.4 %collective-permute-start = (bf16[2,384,256]{2,1,0:T(8,128)(2,1)S(1)}, bf16[2,384,256]{2,1,0:T(8,128)(2,1)}, u32[]{:S(2)}, u32[]{:S(2)}) collective-permute-start(bf16[2,384,256]{2,1,0:T(8,128)(2,1)S(1)} %fusion.4), channel_id=1, source_target_pairs={{0,16},{16,0},{32,48},{48,32},{64,80},{80,64},{96,112},{112,96},{1... | collective-permute-start | bytes 1179656 | tf_op jit(solution)/shard_map/ppermute | solution.py:17
  65.0 6.0 %copy-start.22 = (bf16[3,2,2,256,256]{4,3,2,1,0:T(8,128)(2,1)S(1)}, bf16[3,2,2,256,256]{4,3,2,1,0:T(8,128)(2,1)}, u32[]{:S(2)}) copy-start(bf16[3,2,2,256,256]{4,3,2,1,0:T(8,128)(2,1)} %all-gather.3.cloned.1.call-done) | copy-start | bytes 4718596
  66.7 13.3 %copy-start.11 = (bf16[2,384,256]{2,1,0:T(8,128)(2,1)}, bf16[2,384,256]{2,1,0:T(8,128)(2,1)S(1)}, u32[]{:S(2)}) copy-start(bf16[2,384,256]{2,1,0:T(8,128)(2,1)S(1)} %fusion.5) | copy-start | bytes 1179652
  66.7 13.0 %collective-permute-start.1 = (bf16[2,384,256]{2,1,0:T(8,128)(2,1)S(1)}, bf16[2,384,256]{2,1,0:T(8,128)(2,1)S(1)}, u32[]{:S(2)}, u32[]{:S(2)}) collective-permute-start(bf16[2,384,256]{2,1,0:T(8,128)(2,1)S(1)} %fusion.5), channel_id=1, source_target_pairs={{0,32},{16,48},{32,0},{48,16},{64,96},{80,112},{96,64},{112,80},{1... | collective-permute-start | bytes 1179656 | tf_op jit(solution)/shard_map/ppermute | solution.py:17
  71.1 9.0 %copy-start.7 = (bf16[2,2,256,256]{3,2,1,0:T(8,128)(2,1)}, bf16[2,2,256,256]{3,2,1,0:T(8,128)(2,1)S(1)}, u32[]{:S(2)}) copy-start(bf16[2,2,256,256]{3,2,1,0:T(8,128)(2,1)S(1)} %fusion.25) | copy-start | bytes 1572868
  79.8 3.0 %copy-start.18 = (bf16[2,384,256]{2,1,0:T(8,128)(2,1)}, bf16[2,384,256]{2,1,0:T(8,128)(2,1)S(1)}, u32[]{:S(2)}) copy-start(bf16[2,384,256]{2,1,0:T(8,128)(2,1)S(1)} %collective-permute-done.1) | copy-start | bytes 1179652
  80.0 10.9 %copy-start.20 = (bf16[2,384,256]{2,1,0:T(8,128)(2,1)}, bf16[2,384,256]{2,1,0:T(8,128)(2,1)S(1)}, u32[]{:S(2)}) copy-start(bf16[2,384,256]{2,1,0:T(8,128)(2,1)S(1)} %fusion.6) | copy-start | bytes 1179652
  80.1 10.7 %collective-permute-start.3 = (bf16[2,384,256]{2,1,0:T(8,128)(2,1)S(1)}, bf16[2,384,256]{2,1,0:T(8,128)(2,1)S(1)}, u32[]{:S(2)}, u32[]{:S(2)}) collective-permute-start(bf16[2,384,256]{2,1,0:T(8,128)(2,1)S(1)} %fusion.6), channel_id=1, source_target_pairs={{0,64},{16,80},{32,96},{48,112},{64,0},{80,16},{96,32},{112,48},{1... | collective-permute-start | bytes 1179656 | tf_op jit(solution)/shard_map/ppermute | solution.py:17
  82.6 69.8 %copy-start.14 = (bf16[2,2,256,256]{3,2,1,0:T(8,128)(2,1)}, bf16[2,2,256,256]{3,2,1,0:T(8,128)(2,1)S(1)}, u32[]{:S(2)}) copy-start(bf16[2,2,256,256]{3,2,1,0:T(8,128)(2,1)S(1)} %fusion.24) | copy-start | bytes 1572868
  90.8 2.2 copy-start.28
  91.0 13.7 %collective-permute-start.5 = (bf16[384,256]{1,0:T(8,128)(2,1)S(1)}, bf16[384,256]{1,0:T(8,128)(2,1)S(1)}, u32[]{:S(2)}, u32[]{:S(2)}) collective-permute-start(bf16[384,256]{1,0:T(8,128)(2,1)S(1)} %fusion.11), channel_id=1, source_target_pairs={{0,128},{16,144},{32,160},{48,176},{64,192},{80,208},{96,224},{112... | collective-permute-start | bytes 589832 | tf_op jit(solution)/shard_map/ppermute | solution.py:17
  103.1 9.6 %copy-start.27 = (bf16[2,2,2,256,256]{4,3,2,1,0:T(8,128)(2,1)S(1)}, bf16[2,2,2,256,256]{4,3,2,1,0:T(8,128)(2,1)}, u32[]{:S(2)}) copy-start(bf16[2,2,2,256,256]{4,3,2,1,0:T(8,128)(2,1)} %all-gather.5.cloned.1.call-done) | copy-start | bytes 3145732
  104.9 14.3 %collective-permute-start.6 = (bf16[384,256]{1,0:T(8,128)(2,1)S(1)}, bf16[384,256]{1,0:T(8,128)(2,1)S(1)}, u32[]{:S(2)}, u32[]{:S(2)}) collective-permute-start(bf16[384,256]{1,0:T(8,128)(2,1)S(1)} %fusion.13), channel_id=1, source_target_pairs={{0,256},{16,272},{32,288},{48,304},{64,320},{80,336},{96,352},{112... | collective-permute-start | bytes 589832 | tf_op jit(solution)/shard_map/ppermute | solution.py:17
  123.2 10.3 %collective-permute-start.7 = (bf16[384,256]{1,0:T(8,128)(2,1)S(1)}, bf16[384,256]{1,0:T(8,128)(2,1)S(1)}, u32[]{:S(2)}, u32[]{:S(2)}) collective-permute-start(bf16[384,256]{1,0:T(8,128)(2,1)S(1)} %fusion.15), channel_id=1, source_target_pairs={{0,256},{16,272},{32,288},{48,304},{64,320},{80,336},{96,352},{112... | collective-permute-start | bytes 589832 | tf_op jit(solution)/shard_map/ppermute | solution.py:17
  129.6 22.4 %copy-start.21 = (bf16[2,384,256]{2,1,0:T(8,128)(2,1)S(1)}, bf16[2,384,256]{2,1,0:T(8,128)(2,1)}, u32[]{:S(2)}) copy-start(bf16[2,384,256]{2,1,0:T(8,128)(2,1)} %copy-done.20) | copy-start | bytes 1179652
  133.8 18.2 %collective-permute-start.8 = (bf16[384,256]{1,0:T(8,128)(2,1)S(1)}, bf16[384,256]{1,0:T(8,128)(2,1)S(1)}, u32[]{:S(2)}, u32[]{:S(2)}) collective-permute-start(bf16[384,256]{1,0:T(8,128)(2,1)S(1)} %fusion.17), channel_id=1, source_target_pairs={{0,128},{16,144},{32,160},{48,176},{64,192},{80,208},{96,224},{112... | collective-permute-start | bytes 589832 | tf_op jit(solution)/shard_map/ppermute | solution.py:17
  144.8 9.8 %copy-start.29 = (bf16[2,384,256]{2,1,0:T(8,128)(2,1)S(1)}, bf16[2,384,256]{2,1,0:T(8,128)(2,1)}, u32[]{:S(2)}) copy-start(bf16[2,384,256]{2,1,0:T(8,128)(2,1)} %copy-done.28) | copy-start | bytes 1179652
  152.7 11.4 %collective-permute-start.10 = (bf16[2,384,256]{2,1,0:T(8,128)(2,1)S(1)}, bf16[2,384,256]{2,1,0:T(8,128)(2,1)S(1)}, u32[]{:S(2)}, u32[]{:S(2)}) collective-permute-start(bf16[2,384,256]{2,1,0:T(8,128)(2,1)S(1)} %convolution_convert_fusion.2), channel_id=1, source_target_pairs={{0,64},{16,80},{32,96},{48,112},{64,0},{80,16},{96,32},{112,48},{1... | collective-permute-start | bytes 1179656 | tf_op jit(solution)/shard_map/ppermute | solution.py:17
  155.4 8.6 %copy-start.15 = (bf16[2,2,256,256]{3,2,1,0:T(8,128)(2,1)S(1)}, bf16[2,2,256,256]{3,2,1,0:T(8,128)(2,1)}, u32[]{:S(2)}) copy-start(bf16[2,2,256,256]{3,2,1,0:T(8,128)(2,1)} %copy-done.14) | copy-start | bytes 1572868
  155.4 8.9 %copy-start.8 = (bf16[2,2,256,256]{3,2,1,0:T(8,128)(2,1)S(1)}, bf16[2,2,256,256]{3,2,1,0:T(8,128)(2,1)}, u32[]{:S(2)}) copy-start(bf16[2,2,256,256]{3,2,1,0:T(8,128)(2,1)} %copy-done.7) | copy-start | bytes 1572868
  155.5 14.5 %copy-start.12 = (bf16[2,384,256]{2,1,0:T(8,128)(2,1)S(1)}, bf16[2,384,256]{2,1,0:T(8,128)(2,1)}, u32[]{:S(2)}) copy-start(bf16[2,384,256]{2,1,0:T(8,128)(2,1)} %copy-done.11) | copy-start | bytes 1179652
  155.6 15.6 %copy-start.19 = (bf16[2,384,256]{2,1,0:T(8,128)(2,1)S(1)}, bf16[2,384,256]{2,1,0:T(8,128)(2,1)}, u32[]{:S(2)}) copy-start(bf16[2,384,256]{2,1,0:T(8,128)(2,1)} %copy-done.18) | copy-start | bytes 1179652
  155.6 16.6 %collective-permute-start.9 = (bf16[8,3,2,2,16,256]{5,4,3,2,1,0:T(8,128)(2,1)S(1)}, bf16[8,3,2,2,16,256]{5,4,3,2,1,0:T(8,128)(2,1)S(1)}, u32[]{:S(2)}, u32[]{:S(2)}) collective-permute-start(bf16[8,3,2,2,16,256]{5,4,3,2,1,0:T(8,128)(2,1)S(1)} %select_bitcast_fusion.1), channel_id=1, source_target_pairs={{0,1},{1,0},{2,3},{3,2},{4,5},{5,4},{6,7},{7,6},{8,9},{9,8},{10,11... | collective-permute-start | bytes 2359304 | tf_op jit(solution)/shard_map/ppermute | solution.py:171
  165.4 12.6 %collective-permute-start.11 = (bf16[2,384,256]{2,1,0:T(8,128)(2,1)}, bf16[2,384,256]{2,1,0:T(8,128)(2,1)}, u32[]{:S(2)}, u32[]{:S(2)}) collective-permute-start(bf16[2,384,256]{2,1,0:T(8,128)(2,1)} %convolution_convert_fusion.1), channel_id=1, source_target_pairs={{0,32},{16,48},{32,0},{48,16},{64,96},{80,112},{96,64},{112,80},{1... | collective-permute-start | bytes 1179656 | tf_op jit(solution)/shard_map/ppermute | solution.py:17
  173.4 28.4 %all-to-all-start = ((bf16[8,3,2,2,16,256]{5,4,3,2,1,0:T(8,128)(2,1)}), bf16[8,3,2,2,16,256]{5,4,3,2,1,0:T(8,128)(2,1)S(1)}, u32[]{:S(2)}, u32[]{:S(2)}) async-start(bf16[8,3,2,2,16,256]{5,4,3,2,1,0:T(8,128)(2,1)} %fusion.3), calls=%async_computation | async-start | bytes 1572864 | tf_op jit(solution)/shard_map/all_to_all | solution.py:178
  177.3 5.3 %copy-start.17 = (bf16[2,384,256]{2,1,0:T(8,128)(2,1)S(1)}, bf16[2,384,256]{2,1,0:T(8,128)(2,1)}, u32[]{:S(2)}) copy-start(bf16[2,384,256]{2,1,0:T(8,128)(2,1)} %copy-done.16) | copy-start | bytes 1179652
  179.6 4.7 %copy-start.30 = (bf16[2,384,256]{2,1,0:T(8,128)(2,1)}, bf16[2,384,256]{2,1,0:T(8,128)(2,1)S(1)}, u32[]{:S(2)}) copy-start(bf16[2,384,256]{2,1,0:T(8,128)(2,1)S(1)} %convolution_convert_fusion) | copy-start | bytes 1179652
  179.6 9.8 %collective-permute-start.12 = (bf16[2,384,256]{2,1,0:T(8,128)(2,1)S(1)}, bf16[2,384,256]{2,1,0:T(8,128)(2,1)S(1)}, u32[]{:S(2)}, u32[]{:S(2)}) collective-permute-start(bf16[2,384,256]{2,1,0:T(8,128)(2,1)S(1)} %convolution_convert_fusion), channel_id=1, source_target_pairs={{0,16},{16,0},{32,48},{48,32},{64,80},{80,64},{96,112},{112,96},{1... | collective-permute-start | bytes 1179656 | tf_op jit(solution)/shard_map/ppermute | solution.py:17
  182.9 6.8 %copy-start.10 = (bf16[2,384,256]{2,1,0:T(8,128)(2,1)S(1)}, bf16[2,384,256]{2,1,0:T(8,128)(2,1)}, u32[]{:S(2)}) copy-start(bf16[2,384,256]{2,1,0:T(8,128)(2,1)} %copy-done.9) | copy-start | bytes 1179652
  184.4 6.2 %copy-start.25 = (bf16[2,256,256]{2,1,0:T(8,128)(2,1)S(1)}, bf16[2,256,256]{2,1,0:T(8,128)(2,1)}, u32[]{:S(2)}) copy-start(bf16[2,256,256]{2,1,0:T(8,128)(2,1)} %convolution_convert_fusion.4) | copy-start | bytes 786436
  184.4 6.2 %copy-start.26 = (bf16[2,256,256]{2,1,0:T(8,128)(2,1)S(1)}, bf16[2,256,256]{2,1,0:T(8,128)(2,1)}, u32[]{:S(2)}) copy-start(bf16[2,256,256]{2,1,0:T(8,128)(2,1)} %convolution_convert_fusion.3) | copy-start | bytes 786436
  191.8 10.0 %collective-permute-start.13 = (bf16[8,3,2,2,16,256]{5,4,3,2,1,0:T(8,128)(2,1)}, bf16[8,3,2,2,16,256]{5,4,3,2,1,0:T(8,128)(2,1)}, u32[]{:S(2)}, u32[]{:S(2)}) collective-permute-start(bf16[8,3,2,2,16,256]{5,4,3,2,1,0:T(8,128)(2,1)} %select_bitcast_fusion), channel_id=1, source_target_pairs={{0,1},{1,0},{2,3},{3,2},{4,5},{5,4},{6,7},{7,6},{8,9},{9,8},{10,11... | collective-permute-start | bytes 2359304 | tf_op jit(solution)/shard_map/ppermute | solution.py:171
  199.9 19.2 %collective-permute-start.14 = (bf16[384,256]{1,0:T(8,128)(2,1)}, bf16[384,256]{1,0:T(8,128)(2,1)S(1)}, u32[]{:S(2)}, u32[]{:S(2)}) collective-permute-start(bf16[384,256]{1,0:T(8,128)(2,1)} %fusion.56), channel_id=1, source_target_pairs={{0,256},{16,272},{32,288},{48,304},{64,320},{80,336},{96,352},{112... | collective-permute-start | bytes 589832 | tf_op jit(solution)/shard_map/ppermute | solution.py:17
  204.3 14.8 %copy-start.24 = (bf16[2,384,256]{2,1,0:T(8,128)(2,1)S(1)}, bf16[2,384,256]{2,1,0:T(8,128)(2,1)}, u32[]{:S(2)}) copy-start(bf16[2,384,256]{2,1,0:T(8,128)(2,1)} %copy-done.23) | copy-start | bytes 1179652
  204.3 30.7 %all-to-all-start.1 = ((bf16[8,3,2,2,16,256]{5,4,3,2,1,0:T(8,128)(2,1)}), bf16[8,3,2,2,16,256]{5,4,3,2,1,0:T(8,128)(2,1)S(1)}, u32[]{:S(2)}, u32[]{:S(2)}) async-start(bf16[8,3,2,2,16,256]{5,4,3,2,1,0:T(8,128)(2,1)} %copy-done.13), calls=%async_computation.1 | async-start | bytes 1572864 | tf_op jit(solution)/shard_map/all_to_all | solution.py:178
  212.1 10.9 %collective-permute-start.16 = (bf16[2,16,256]{2,1,0:T(8,128)(2,1)S(1)}, bf16[2,16,256]{2,1,0:T(8,128)(2,1)S(1)}, u32[]{:S(2)}, u32[]{:S(2)}) collective-permute-start(bf16[2,16,256]{2,1,0:T(8,128)(2,1)S(1)} %get-tuple-element.32), channel_id=1, source_target_pairs={{0,256},{16,272},{32,288},{48,304},{64,320},{80,336},{96,352},{112... | collective-permute-start | bytes 49160 | tf_op jit(solution)/shard_map/ppermute | solution.py:17
  219.3 14.5 %collective-permute-start.15 = (bf16[384,256]{1,0:T(8,128)(2,1)S(1)}, bf16[384,256]{1,0:T(8,128)(2,1)S(1)}, u32[]{:S(2)}, u32[]{:S(2)}) collective-permute-start(bf16[384,256]{1,0:T(8,128)(2,1)S(1)} %select_select_fusion), channel_id=1, source_target_pairs={{0,128},{16,144},{32,160},{48,176},{64,192},{80,208},{96,224},{112... | collective-permute-start | bytes 589832 | tf_op jit(solution)/shard_map/ppermute | solution.py:17
  223.0 11.8 %collective-permute-start.17 = (bf16[2,2,16,256]{3,2,1,0:T(8,128)(2,1)S(1)}, bf16[2,2,16,256]{3,2,1,0:T(8,128)(2,1)S(1)}, u32[]{:S(2)}, u32[]{:S(2)}) collective-permute-start(bf16[2,2,16,256]{3,2,1,0:T(8,128)(2,1)S(1)} %get-tuple-element.29), channel_id=1, source_target_pairs={{0,128},{16,144},{32,160},{48,176},{64,192},{80,208},{96,224},{112... | collective-permute-start | bytes 98312 | tf_op jit(solution)/shard_map/ppermute | solution.py:17
  (5 other events, 4.0 us)
Sparse Core Ops, SparseCore 0:
  10.7 47.2 all-gather.2
  64.0 39.0 all-gather.4

commit v7 on v6

--- a/solution.py
+++ b/solution.py
@@ -60,8 +60,8 @@
         for row in range(2):
             at = choice(matchings, section, row)
             out = first.at[0] if section == 0 else rest.at[section - 1]
-            out[0, row] = weights[section, row ^ low, at]
-            out[1, row] = weights[section, row ^ low, 1 - at]
+            out[row, 0] = weights[section, row ^ low, at]
+            out[row, 1] = weights[section, row ^ low, 1 - at]
 
 
 def pack_late(matchings, weights, cotangent, keep, packed):
@@ -88,7 +88,7 @@
         at = choice(matchings, 4, row)
         own = same if row == 0 else jnp.logical_not(same)
         for slot, both in enumerate((at, 1 - at)):
-            fourth[slot, row] = jnp.where(own, keep[0, both], came_at(0, both))
+            fourth[row, slot] = jnp.where(own, keep[0, both], came_at(0, both))
     for both in range(2):
         mine5, yours5 = keep[1, both], came_at(1, both)
         fifth[both] = jnp.where(same, mine5, yours5)
@@ -106,9 +106,9 @@
         at = choice(matchings, 5, row)
         for slot, both in enumerate((at, 1 - at)):
             if row == 0:
-                late[1, slot, row] = fifth[both]
+                late[1, row, slot] = fifth[both]
             else:
-                late[1, slot, row] = came[pl.ds(pl.multiple_of(both * depth, depth), depth)]
+                late[1, row, slot] = came[pl.ds(pl.multiple_of(both * depth, depth), depth)]
 
 
 def total(parts, place, slot, row):
@@ -156,6 +156,10 @@
     return result[0] if len(outs) == 1 else result
 
 
+def row_terms(parts, grads):
+    return jnp.stack([jnp.stack([dot_rows(part[r], grads[r]) for r in range(2)]) for part in parts])
+
+
 def core_half(terms, core):
     count, both, per_dev, size, depth, width = terms.shape
     parts = terms.reshape(count, both, per_dev, size // 2, 2, depth, width)
@@ -197,10 +201,9 @@
     full += list(lax.all_gather(rest, "tok", axis=3, tiled=True))
 
     left, right = activations[:, :width], activations[:, width:]
-    value = jnp.stack([jnp.where(low, right, left), jnp.where(low, left, right)])
-    other = value[::-1]
-    inputs = [(value, other)]
-    value = (dot(value, full[0][0]) + dot(other, full[0][1])).astype(bf16)
+    rows = [jnp.where(low, right, left), jnp.where(low, left, right)]
+    inputs = [(rows, rows[::-1])]
+    rows = [(dot(rows[r], full[0][r, 0]) + dot(rows[1 - r], full[0][r, 1])).astype(bf16) for r in range(2)]
 
     fourth, fifth, packed, cotan0 = local(
         between,
@@ -216,60 +219,64 @@
     full += list(lax.all_gather(late, "tok", axis=3, tiled=True))
 
     for section in range(1, 4):
-        other = flip(value, section - 1)
-        inputs.append((value, other))
-        full[section] = after(full[section], value)
-        own_w, other_w = full[section][0], full[section][1]
-        if section < 3:
-            value = (dot(value, own_w) + dot(other, other_w)).astype(bf16)
-        else:
-            send = (dot(value[1], own_w[1]) + dot(other[1], other_w[1])).astype(bf16)
-            keep = (dot(value[0], own_w[0]) + dot(other[0], other_w[0])).astype(bf16)
+        second = flip(rows[1], section - 1)
+        others = [flip(rows[0], section - 1), second]
+        inputs.append((rows, others))
+        second_w = after(full[section][1], rows[0])
+        second = (dot(rows[1], second_w[0]) + dot(others[1], second_w[1])).astype(bf16)
+        first_w = after(full[section][0], second)
+        first = (dot(rows[0], first_w[0]) + dot(others[0], first_w[1])).astype(bf16)
+        full[section] = [first_w, second_w]
+        rows = [first, second]
+    keep, send = rows
     came = flip(send, 3)
     inputs.append((keep, came))
     full[4] = after(full[4], send)
-    own_w, other_w = full[4][0], full[4][1]
-    send = (dot(keep, own_w[1]) + dot(came, other_w[1])).astype(bf16)
-    keep = (dot(keep, own_w[0]) + dot(came, other_w[0])).astype(bf16)
+    send = (dot(keep, full[4][1, 0]) + dot(came, full[4][1, 1])).astype(bf16)
+    keep = (dot(keep, full[4][0, 0]) + dot(came, full[4][0, 1])).astype(bf16)
     came = flip(send, 4)
     inputs.append((keep, came))
     full[5] = after(full[5], send)
-    own_w, other_w = full[5][0], full[5][1]
 
     results, grads = [], []
     for row, cotan in enumerate((cotan0, cotan1)):
-        final = dot(keep, own_w[row]) + dot(came, other_w[row])
+        final = dot(keep, full[5][row, 0]) + dot(came, full[5][row, 1])
         results.append(jax.nn.gelu(final).astype(bf16))
         back_fn = jax.vjp(jax.nn.gelu, final)[1]
         grads.append(back_fn(cotan.astype(jnp.float32))[0].astype(bf16))
 
     terms = [None] * SECTIONS
     for section in (5, 4):
-        own_w, other_w = full[section][0], full[section][1]
-        sent = (dot_back(grads[0], other_w[0]) + dot_back(grads[1], other_w[1])).astype(bf16)
+        both = full[section]
+        sent = (dot_back(grads[0], both[0, 1]) + dot_back(grads[1], both[1, 1])).astype(bf16)
         back = flip(sent, section - 1)
-        kept = (dot_back(grads[0], own_w[0]) + dot_back(grads[1], own_w[1])).astype(bf16)
+        kept = (dot_back(grads[0], both[0, 0]) + dot_back(grads[1], both[1, 0])).astype(bf16)
         terms[section] = jnp.stack(
             [jnp.stack([dot_rows(part, grad) for grad in grads]) for part in inputs[section]]
         )
         grads = [kept, back]
-    grad = jnp.stack(grads)
+    before = sent
     for section in (3, 2, 1):
-        own_w, other_w = full[section][0], full[section][1]
-        sent = dot_back(grad, other_w).astype(bf16)
-        back = flip(sent, section - 1)
-        terms[section] = jnp.stack([dot_rows(part, grad) for part in inputs[section]])
+        both = full[section]
+        sent = [dot_back(grads[r], both[r][1]).astype(bf16) for r in range(2)]
+        sent[0] = after(sent[0], before)
+        back = [flip(part, section - 1) for part in sent]
+        terms[section] = row_terms(inputs[section], grads)
         if section == 3:
             chip = chip_sum(jnp.stack(terms[3:]))
             parts_high = all_parts(chip)
-        grad = (dot_back(grad, own_w) + back.astype(jnp.float32)).astype(bf16)
+        grads = [
+            (dot_back(grads[r], both[r][0]) + back[r].astype(jnp.float32)).astype(bf16) for r in range(2)
+        ]
+        before = sent[1]
         if section == 2:
-            grad = after(grad, chip)
-    terms[0] = jnp.stack([dot_rows(part, grad) for part in inputs[0]])
+            grads[0] = after(grads[0], chip)
+    grads = [after(grads[r], sent[1 - r]) for r in range(2)]
+    terms[0] = row_terms(inputs[0], grads)
     chip = after(chip_sum(jnp.stack(terms[:3])), parts_high)
     parts_low = all_parts(chip)
 
-    out_came = flip(after(results[1], sent), 4)
+    out_came = flip(after(results[1], sent[1]), 4)
     out_keep, out_send = jnp.where(same, results[0], out_came), jnp.where(same, out_came, results[0])
     out_came = flip(after(out_send, chip), 3)
     result = jnp.concatenate([jnp.where(low, out_came, out_keep), jnp.where(low, out_keep, out_came)], axis=1)
@@ -282,10 +289,10 @@
         finish, matchings, parts_low, parts_high, keep, came, outs=[shape(6, 2, 2, depth, dtype=jnp.float32)]
     )
 
-    grad = after(grad, chip)
-    own_w, other_w = full[0][0], full[0][1]
+    grads = [after(grad, chip) for grad in grads]
     first, second = [
-        (dot_back(grad[r], own_w[r]) + dot_back(grad[1 - r], other_w[1 - r])).astype(bf16) for r in range(2)
+        (dot_back(grads[r], full[0][r, 0]) + dot_back(grads[1 - r], full[0][1 - r, 1])).astype(bf16)
+        for r in range(2)
     ]
     input_grad = jnp.concatenate([jnp.where(low, second, first), jnp.where(low, first, second)], axis=1)
     return result, input_grad, weight_grad

time: 245 us -> 259 us (1.057)
  starting transfers between devices: 96.5 us -> 106 us
  matrix products: 20 us -> 25.5 us
  waiting for transfers between devices: 66.7 us -> 61.2 us
  other arithmetic: 13.4 us -> 16.1 us
    ppermute x16 -> x22, waiting for transfers between devices: 56.5 us -> 38.5 us  [flip(): return lax.ppermute(value, 'blk', pairs)]
    ppermute x16 -> x22, starting transfers between devices: 76.8 us -> 91.6 us  [flip(): return lax.ppermute(value, 'blk', pairs)]
    all_gather x1, waiting for transfers between devices: 9.94 us -> 17.7 us  [body(): full += list(lax.all_gather(late, 'tok', axis=3, tiled=True))]
    all_to_all x2, waiting for transfers between devices: 0.17 us -> 5.03 us  [all_parts(): return lax.all_to_all(chip, 'tok', 0, 0, axis_index_groups=groups)]
    all_to_all x2, starting transfers between devices: 10.9 us -> 7.61 us  [all_parts(): return lax.all_to_all(chip, 'tok', 0, 0, axis_index_groups=groups)]
    dot_general x16 -> x24, matrix products: 7.34 us -> 10.4 us  [dot_rows(): jnp.einsum('...tk,...tl->...kl', left, right, preferred_element_type=jnp....]
    select_n x9 -> x11, other arithmetic: 5.94 us -> 7.66 us  [after(): return jnp.where(probe != probe, jnp.zeros_like(value), value)]
    dot_general x18 -> x24, matrix products: 6.44 us -> 8.13 us  [dot_back(): jnp.einsum('...tl,...kl->...tk', left, right, preferred_element_type=jnp....]
  transfers between devices with their start and end apart: 22 -> 28, of which waited for: 11 -> 13; matrix products, arithmetic and copies ran while one was open for 12% -> 15% of each run, Pallas kernels for 1% -> 1%
where the time goes in v7:
time: 259 us; the launch traced here: 258 us
  starting transfers between devices  106 us (41%)
  waiting for transfers between devices  61.2 us (24%)
  matrix products  25.5 us (10%)
  blocking collectives  20.1 us (8%)
  other arithmetic  16.1 us (6%)
  between operations  15.4 us (6%)
  local copies, waits for them, and re-layouts  7.07 us (3%)
  Pallas kernels  5.97 us (2%)
    ppermute x22, starting transfers between devices, flip(): return lax.ppermute(value, 'blk', pairs)  91.6 us
    ppermute x22, waiting for transfers between devices, flip(): return lax.ppermute(value, 'blk', pairs)  38.5 us
    all_gather x1, blocking collectives, body(): full = list(lax.all_gather(first, 'tok', axis=3, tiled=True))  20.1 us
    all_gather x1, waiting for transfers between devices, body(): full += list(lax.all_gather(late, 'tok', axis=3, tiled=True))  17.7 us
    dot_general x24, matrix products, dot_rows(): jnp.einsum('...tk,...tl->...kl', left, right, preferred_element_type=jnp....  10.4 us
    dot_general x24, matrix products, dot_back(): jnp.einsum('...tl,...kl->...tk', left, right, preferred_element_type=jnp....  8.13 us
    select_n x11, other arithmetic, after(): return jnp.where(probe != probe, jnp.zeros_like(value), value)  7.66 us
    all_to_all x2, starting transfers between devices, all_parts(): return lax.all_to_all(chip, 'tok', 0, 0, axis_index_groups=groups)  7.61 us
  transfers between devices with their start and end apart: 28, of which 13 were waited for; matrix products, arithmetic and copies ran while one was open for 15% of the time, Pallas kernels for 1%

profile of v7, /device:TPU:1, one launch (start us, length us, event | category | flops | bytes accessed | tf_op | source)
XLA Modules:
  0.0 257.6 jit_solution(13382480047073381741)
XLA Ops:
  8.8 1.3 shard_map.67
  13.4 6.6 %collective-permute-start.4 = (bf16[448,256]{1,0:T(8,128)(2,1)S(1)}, bf16[448,256]{1,0:T(8,128)(2,1)S(1)}, u32[]{:S(2)}, u32[]{:S(2)}) collective-permute-start(bf16[448,256]{1,0:T(8,128)(2,1)S(1)} %get-tuple-element.14), channel_id=1, source_target_pairs={{0,128},{16,144},{32,160},{48,176},{64,192},{80,208},{96,224},{112... | collective-permute-start | bytes 688136 | tf_op jit(solution)/shard_map/ppermute | solution.py:17
  21.2 20.1 %all_gather.9 = bf16[1,2,2,256,256]{4,3,2,1,0:T(8,128)(2,1)S(1)} all-gather(bf16[1,2,2,16,256]{4,3,2,1,0:T(8,128)(2,1)S(1)} %get-tuple-element.11), channel_id=1, replica_groups=mesh['blk'=32,'tok'=16] {'tok'}, dimensions={3}, use_global_device_ids=true | all-gather | bytes 557056 | tf_op jit(solution)/shard_map/all_gather | solution.py:200
  41.7 3.1 %collective-permute-start = (bf16[384,256]{1,0:T(8,128)(2,1)S(1)}, bf16[384,256]{1,0:T(8,128)(2,1)S(1)}, u32[]{:S(2)}, u32[]{:S(2)}) collective-permute-start(bf16[384,256]{1,0:T(8,128)(2,1)S(1)} %fusion.5), channel_id=1, source_target_pairs={{0,16},{16,0},{32,48},{48,32},{64,80},{80,64},{96,112},{112,96},{1... | collective-permute-start | bytes 589832 | tf_op jit(solution)/shard_map/ppermute | solution.py:17
  45.8 10.3 %collective-permute-start.7 = (bf16[416,256]{1,0:T(8,128)(2,1)S(1)}, bf16[416,256]{1,0:T(8,128)(2,1)S(1)}, u32[]{:S(2)}, u32[]{:S(2)}) collective-permute-start(bf16[416,256]{1,0:T(8,128)(2,1)S(1)} %get-tuple-element.18), channel_id=1, source_target_pairs={{0,256},{16,272},{32,288},{48,304},{64,320},{80,336},{96,352},{112... | collective-permute-start | bytes 638984 | tf_op jit(solution)/shard_map/ppermute | solution.py:17
  56.3 2.2 collective-permute-start.1
  58.5 7.3 %collective-permute-done.7.came = bf16[416,256]{1,0:T(8,128)(2,1)S(1)} collective-permute-done((bf16[416,256]{1,0:T(8,128)(2,1)S(1)}, bf16[416,256]{1,0:T(8,128)(2,1)S(1)}, u32[]{:S(2)}, u32[]{:S(2)}) %collective-permute-start.7) | collective-permute-done | bytes 213024 | tf_op jit(solution)/shard_map/ppermute | solution.py:17
  65.9 1.2 shard_map.70
  69.2 4.3 %collective-permute-start.2 = (bf16[384,256]{1,0:T(8,128)(2,1)S(1)}, bf16[384,256]{1,0:T(8,128)(2,1)S(1)}, u32[]{:S(2)}, u32[]{:S(2)}) collective-permute-start(bf16[384,256]{1,0:T(8,128)(2,1)S(1)} %fusion.6), channel_id=1, source_target_pairs={{0,32},{16,48},{32,0},{48,16},{64,96},{80,112},{96,64},{112,80},{1... | collective-permute-start | bytes 589832 | tf_op jit(solution)/shard_map/ppermute | solution.py:17
  74.5 2.5 collective-permute-start.3
  78.2 2.4 collective-permute-start.5
  80.9 2.1 collective-permute-done.3
  83.2 2.4 collective-permute-start.6
  86.8 1.9 collective-permute-start.8
  88.8 17.7 %all-gather.5.cloned.1.call-done = bf16[2,2,2,256,256]{4,3,2,1,0:T(8,128)(2,1)} async-done(((bf16[2,2,2,16,256]{4,3,2,1,0:T(8,128)(2,1)}), bf16[2,2,2,256,256]{4,3,2,1,0:T(8,128)(2,1)}) %all-gather.5.cloned.1.call-update) | async-done | bytes 1048592 | tf_op jit(solution)/shard_map/all_gather | solution.py:219
  107.8 1.2 fusion.11
  109.7 7.6 %collective-permute-start.9 = (bf16[384,256]{1,0:T(8,128)(2,1)S(1)}, bf16[384,256]{1,0:T(8,128)(2,1)S(1)}, u32[]{:S(2)}, u32[]{:S(2)}) collective-permute-start(bf16[384,256]{1,0:T(8,128)(2,1)S(1)} %fusion.13), channel_id=1, source_target_pairs={{0,256},{16,272},{32,288},{48,304},{64,320},{80,336},{96,352},{112... | collective-permute-start | bytes 589832 | tf_op jit(solution)/shard_map/ppermute | solution.py:17
  118.0 5.9 %collective-permute-done.9 = bf16[384,256]{1,0:T(8,128)(2,1)S(1)} collective-permute-done((bf16[384,256]{1,0:T(8,128)(2,1)S(1)}, bf16[384,256]{1,0:T(8,128)(2,1)S(1)}, u32[]{:S(2)}, u32[]{:S(2)}) %collective-permute-start.9) | collective-permute-done | bytes 196640 | tf_op jit(solution)/shard_map/ppermute | solution.py:17
  125.1 1.2 fusion.38
  127.8 5.5 %collective-permute-start.10 = (bf16[384,256]{1,0:T(8,128)(2,1)S(1)}, bf16[384,256]{1,0:T(8,128)(2,1)S(1)}, u32[]{:S(2)}, u32[]{:S(2)}) collective-permute-start(bf16[384,256]{1,0:T(8,128)(2,1)S(1)} %fusion.15), channel_id=1, source_target_pairs={{0,256},{16,272},{32,288},{48,304},{64,320},{80,336},{96,352},{112... | collective-permute-start | bytes 589832 | tf_op jit(solution)/shard_map/ppermute | solution.py:17
  134.2 4.0 %collective-permute-done.10 = bf16[384,256]{1,0:T(8,128)(2,1)S(1)} collective-permute-done((bf16[384,256]{1,0:T(8,128)(2,1)S(1)}, bf16[384,256]{1,0:T(8,128)(2,1)S(1)}, u32[]{:S(2)}, u32[]{:S(2)}) %collective-permute-start.10) | collective-permute-done | bytes 196640 | tf_op jit(solution)/shard_map/ppermute | solution.py:17
  138.4 10.6 %collective-permute-start.11 = (bf16[384,256]{1,0:T(8,128)(2,1)S(1)}, bf16[384,256]{1,0:T(8,128)(2,1)S(1)}, u32[]{:S(2)}, u32[]{:S(2)}) collective-permute-start(bf16[384,256]{1,0:T(8,128)(2,1)S(1)} %fusion.17), channel_id=1, source_target_pairs={{0,128},{16,144},{32,160},{48,176},{64,192},{80,208},{96,224},{112... | collective-permute-start | bytes 589832 | tf_op jit(solution)/shard_map/ppermute | solution.py:17
  149.9 2.1 collective-permute-start.15
  152.5 1.2 convolution_convert_fusion.27
  153.7 2.7 %collective-permute-done.11 = bf16[384,256]{1,0:T(8,128)(2,1)S(1)} collective-permute-done((bf16[384,256]{1,0:T(8,128)(2,1)S(1)}, bf16[384,256]{1,0:T(8,128)(2,1)S(1)}, u32[]{:S(2)}, u32[]{:S(2)}) %collective-permute-start.11) | collective-permute-done | bytes 196640 | tf_op jit(solution)/shard_map/ppermute | solution.py:17
  156.6 1.9 collective-permute-start.13
  158.6 2.7 %collective-permute-done.15 = bf16[384,256]{1,0:T(8,128)(2,1)S(1)} collective-permute-done((bf16[384,256]{1,0:T(8,128)(2,1)S(1)}, bf16[384,256]{1,0:T(8,128)(2,1)S(1)}, u32[]{:S(2)}, u32[]{:S(2)}) %collective-permute-start.15) | collective-permute-done | bytes 196640 | tf_op jit(solution)/shard_map/ppermute | solution.py:17
  164.5 5.2 %collective-permute-start.16 = (bf16[384,256]{1,0:T(8,128)(2,1)S(1)}, bf16[384,256]{1,0:T(8,128)(2,1)S(1)}, u32[]{:S(2)}, u32[]{:S(2)}) collective-permute-start(bf16[384,256]{1,0:T(8,128)(2,1)S(1)} %broadcast_select_fusion.3), channel_id=1, source_target_pairs={{0,32},{16,48},{32,0},{48,16},{64,96},{80,112},{96,64},{112,80},{1... | collective-permute-start | bytes 589832 | tf_op jit(solution)/shard_map/ppermute | solution.py:17
  169.7 2.8 %collective-permute-start.12 = (bf16[8,3,2,2,16,256]{5,4,3,2,1,0:T(8,128)(2,1)S(1)}, bf16[8,3,2,2,16,256]{5,4,3,2,1,0:T(8,128)(2,1)S(1)}, u32[]{:S(2)}, u32[]{:S(2)}) collective-permute-start(bf16[8,3,2,2,16,256]{5,4,3,2,1,0:T(8,128)(2,1)S(1)} %select_bitcast_fusion.1), channel_id=1, source_target_pairs={{0,1},{1,0},{2,3},{3,2},{4,5},{5,4},{6,7},{7,6},{8,9},{9,8},{10,11... | collective-permute-start | bytes 2359304 | tf_op jit(solution)/shard_map/ppermute | solution.py:175
  174.0 2.0 collective-permute-start.14
  178.8 5.2 %collective-permute-done.14 = bf16[384,256]{1,0:T(8,128)(2,1)S(1)} collective-permute-done((bf16[384,256]{1,0:T(8,128)(2,1)S(1)}, bf16[384,256]{1,0:T(8,128)(2,1)S(1)}, u32[]{:S(2)}, u32[]{:S(2)}) %collective-permute-start.14) | collective-permute-done | bytes 196640 | tf_op jit(solution)/shard_map/ppermute | solution.py:17
  185.3 2.2 collective-permute-start.18
  189.4 1.3 fusion.3
  191.4 4.1 %all-to-all-start = ((bf16[8,3,2,2,16,256]{5,4,3,2,1,0:T(8,128)(2,1)}), bf16[8,3,2,2,16,256]{5,4,3,2,1,0:T(8,128)(2,1)S(1)}, u32[]{:S(2)}, u32[]{:S(2)}) async-start(bf16[8,3,2,2,16,256]{5,4,3,2,1,0:T(8,128)(2,1)} %fusion.3), calls=%async_computation | async-start | bytes 1572864 | tf_op jit(solution)/shard_map/all_to_all | solution.py:182
  195.8 3.1 %collective-permute-start.17 = (bf16[384,256]{1,0:T(8,128)(2,1)S(1)}, bf16[384,256]{1,0:T(8,128)(2,1)S(1)}, u32[]{:S(2)}, u32[]{:S(2)}) collective-permute-start(bf16[384,256]{1,0:T(8,128)(2,1)S(1)} %fusion.25), channel_id=1, source_target_pairs={{0,16},{16,0},{32,48},{48,32},{64,80},{80,64},{96,112},{112,96},{1... | collective-permute-start | bytes 589832 | tf_op jit(solution)/shard_map/ppermute | solution.py:17
  201.2 1.5 collective-permute-done.17
  205.1 4.2 %collective-permute-start.19 = (bf16[8,3,2,2,16,256]{5,4,3,2,1,0:T(8,128)(2,1)}, bf16[8,3,2,2,16,256]{5,4,3,2,1,0:T(8,128)(2,1)}, u32[]{:S(2)}, u32[]{:S(2)}) collective-permute-start(bf16[8,3,2,2,16,256]{5,4,3,2,1,0:T(8,128)(2,1)} %select_bitcast_fusion), channel_id=1, source_target_pairs={{0,1},{1,0},{2,3},{3,2},{4,5},{5,4},{6,7},{7,6},{8,9},{9,8},{10,11... | collective-permute-start | bytes 2359304 | tf_op jit(solution)/shard_map/ppermute | solution.py:175
  209.2 1.8 fusion.57
  211.1 4.7 %collective-permute-start.20 = (bf16[384,256]{1,0:T(8,128)(2,1)}, bf16[384,256]{1,0:T(8,128)(2,1)}, u32[]{:S(2)}, u32[]{:S(2)}) collective-permute-start(bf16[384,256]{1,0:T(8,128)(2,1)} %fusion.57), channel_id=1, source_target_pairs={{0,256},{16,272},{32,288},{48,304},{64,320},{80,336},{96,352},{112... | collective-permute-start | bytes 589832 | tf_op jit(solution)/shard_map/ppermute | solution.py:17
  215.8 3.3 %all-to-all-done.parts.parts_high = bf16[8,3,2,2,16,256]{5,4,3,2,1,0:T(8,128)(2,1)S(1)} async-done(((bf16[8,3,2,2,16,256]{5,4,3,2,1,0:T(8,128)(2,1)}), bf16[8,3,2,2,16,256]{5,4,3,2,1,0:T(8,128)(2,1)S(1)}, u32[]{:S(2)}, u32[]{:S(2)}) %all-to-all-start) | async-done | bytes 786464 | tf_op jit(solution)/shard_map/all_to_all | solution.py:182
  219.1 2.4 fusion.28
  222.2 3.6 %all-to-all-start.1 = ((bf16[8,3,2,2,16,256]{5,4,3,2,1,0:T(8,128)(2,1)}), bf16[8,3,2,2,16,256]{5,4,3,2,1,0:T(8,128)(2,1)S(1)}, u32[]{:S(2)}, u32[]{:S(2)}) async-start(bf16[8,3,2,2,16,256]{5,4,3,2,1,0:T(8,128)(2,1)} %fusion.28), calls=%async_computation.1 | async-start | bytes 1572864 | tf_op jit(solution)/shard_map/all_to_all | solution.py:182
  226.5 4.8 %collective-permute-start.22 = (bf16[2,16,256]{2,1,0:T(8,128)(2,1)S(1)}, bf16[2,16,256]{2,1,0:T(8,128)(2,1)S(1)}, u32[]{:S(2)}, u32[]{:S(2)}) collective-permute-start(bf16[2,16,256]{2,1,0:T(8,128)(2,1)S(1)} %get-tuple-element.32), channel_id=1, source_target_pairs={{0,256},{16,272},{32,288},{48,304},{64,320},{80,336},{96,352},{112... | collective-permute-start | bytes 49160 | tf_op jit(solution)/shard_map/ppermute | solution.py:17
  232.6 2.2 collective-permute-start.21
  236.3 4.0 %collective-permute-start.23 = (bf16[2,2,16,256]{3,2,1,0:T(8,128)(2,1)S(1)}, bf16[2,2,16,256]{3,2,1,0:T(8,128)(2,1)S(1)}, u32[]{:S(2)}, u32[]{:S(2)}) collective-permute-start(bf16[2,2,16,256]{3,2,1,0:T(8,128)(2,1)S(1)} %get-tuple-element.29), channel_id=1, source_target_pairs={{0,128},{16,144},{32,160},{48,176},{64,192},{80,208},{96,224},{112... | collective-permute-start | bytes 98312 | tf_op jit(solution)/shard_map/ppermute | solution.py:17
  240.3 6.2 %collective-permute-done.21 = bf16[384,256]{1,0:T(8,128)(2,1)S(1)} collective-permute-done((bf16[384,256]{1,0:T(8,128)(2,1)S(1)}, bf16[384,256]{1,0:T(8,128)(2,1)S(1)}, u32[]{:S(2)}, u32[]{:S(2)}) %collective-permute-start.21) | collective-permute-done | bytes 196640 | tf_op jit(solution)/shard_map/ppermute | solution.py:17
  247.5 1.8 all-to-all-done.1.parts_low
  249.3 1.5 shard_map.72
  (231 shorter events, 42.6 us)
Async XLA Ops:
  7.2 60.0 %all-gather.3.cloned.1.call-start = ((), (), s32[]{:S(2)}) async-start(), calls=%async_computation.2 | async-start | bytes 1671168 | tf_op jit(solution)/shard_map/all_gather | solution.py:201
  10.1 96.3 %all-gather.5.cloned.1.call-start = ((), (), s32[]{:S(2)}) async-start(), calls=%async_computation.3 | async-start | bytes 1114112 | tf_op jit(solution)/shard_map/all_gather | solution.py:219
  13.4 31.6 %collective-permute-start.4 = (bf16[448,256]{1,0:T(8,128)(2,1)S(1)}, bf16[448,256]{1,0:T(8,128)(2,1)S(1)}, u32[]{:S(2)}, u32[]{:S(2)}) collective-permute-start(bf16[448,256]{1,0:T(8,128)(2,1)S(1)} %get-tuple-element.14), channel_id=1, source_target_pairs={{0,128},{16,144},{32,160},{48,176},{64,192},{80,208},{96,224},{112... | collective-permute-start | bytes 688136 | tf_op jit(solution)/shard_map/ppermute | solution.py:17
  21.1 23.9 %copy-start.1 = (bf16[384,512]{1,0:T(8,128)(2,1)S(1)}, bf16[384,512]{1,0:T(8,128)(2,1)}, u32[]{:S(2)}) copy-start(bf16[384,512]{1,0:T(8,128)(2,1)} %cotangent.3) | copy-start | bytes 1179652
  21.2 23.9 %copy-start.6 = (s32[6,64]{1,0:T(8,128)S(1)}, s32[6,64]{1,0:T(8,128)}, u32[]{:S(2)}) copy-start(s32[6,64]{1,0:T(8,128)} %matchings.11) | copy-start | bytes 4612
  41.7 26.6 %copy-start.11 = (bf16[384,256]{1,0:T(8,128)(2,1)}, bf16[384,256]{1,0:T(8,128)(2,1)S(1)}, u32[]{:S(2)}) copy-start(bf16[384,256]{1,0:T(8,128)(2,1)S(1)} %fusion.5) | copy-start | bytes 589828
  41.7 26.8 %collective-permute-start = (bf16[384,256]{1,0:T(8,128)(2,1)S(1)}, bf16[384,256]{1,0:T(8,128)(2,1)S(1)}, u32[]{:S(2)}, u32[]{:S(2)}) collective-permute-start(bf16[384,256]{1,0:T(8,128)(2,1)S(1)} %fusion.5), channel_id=1, source_target_pairs={{0,16},{16,0},{32,48},{48,32},{64,80},{80,64},{96,112},{112,96},{1... | collective-permute-start | bytes 589832 | tf_op jit(solution)/shard_map/ppermute | solution.py:17
  45.8 20.1 %collective-permute-start.7 = (bf16[416,256]{1,0:T(8,128)(2,1)S(1)}, bf16[416,256]{1,0:T(8,128)(2,1)S(1)}, u32[]{:S(2)}, u32[]{:S(2)}) collective-permute-start(bf16[416,256]{1,0:T(8,128)(2,1)S(1)} %get-tuple-element.18), channel_id=1, source_target_pairs={{0,256},{16,272},{32,288},{48,304},{64,320},{80,336},{96,352},{112... | collective-permute-start | bytes 638984 | tf_op jit(solution)/shard_map/ppermute | solution.py:17
  56.3 17.5 %copy-start.32 = (bf16[384,256]{1,0:T(8,128)(2,1)}, bf16[384,256]{1,0:T(8,128)(2,1)S(1)}, u32[]{:S(2)}) copy-start(bf16[384,256]{1,0:T(8,128)(2,1)S(1)} %fusion.4) | copy-start | bytes 589828
  56.3 17.5 %collective-permute-start.1 = (bf16[384,256]{1,0:T(8,128)(2,1)S(1)}, bf16[384,256]{1,0:T(8,128)(2,1)S(1)}, u32[]{:S(2)}, u32[]{:S(2)}) collective-permute-start(bf16[384,256]{1,0:T(8,128)(2,1)S(1)} %fusion.4), channel_id=1, source_target_pairs={{0,16},{16,0},{32,48},{48,32},{64,80},{80,64},{96,112},{112,96},{1... | collective-permute-start | bytes 589832 | tf_op jit(solution)/shard_map/ppermute | solution.py:17
  68.8 8.4 %copy-start.13 = (bf16[384,256]{1,0:T(8,128)(2,1)}, bf16[384,256]{1,0:T(8,128)(2,1)S(1)}, u32[]{:S(2)}) copy-start(bf16[384,256]{1,0:T(8,128)(2,1)S(1)} %fusion.6) | copy-start | bytes 589828
  69.2 8.8 %collective-permute-start.2 = (bf16[384,256]{1,0:T(8,128)(2,1)S(1)}, bf16[384,256]{1,0:T(8,128)(2,1)S(1)}, u32[]{:S(2)}, u32[]{:S(2)}) collective-permute-start(bf16[384,256]{1,0:T(8,128)(2,1)S(1)} %fusion.6), channel_id=1, source_target_pairs={{0,32},{16,48},{32,0},{48,16},{64,96},{80,112},{96,64},{112,80},{1... | collective-permute-start | bytes 589832 | tf_op jit(solution)/shard_map/ppermute | solution.py:17
  74.5 8.5 %collective-permute-start.3 = (bf16[384,256]{1,0:T(8,128)(2,1)S(1)}, bf16[384,256]{1,0:T(8,128)(2,1)S(1)}, u32[]{:S(2)}, u32[]{:S(2)}) collective-permute-start(bf16[384,256]{1,0:T(8,128)(2,1)S(1)} %fusion.7), channel_id=1, source_target_pairs={{0,32},{16,48},{32,0},{48,16},{64,96},{80,112},{96,64},{112,80},{1... | collective-permute-start | bytes 589832 | tf_op jit(solution)/shard_map/ppermute | solution.py:17
  78.2 7.6 %collective-permute-start.5 = (bf16[384,256]{1,0:T(8,128)(2,1)S(1)}, bf16[384,256]{1,0:T(8,128)(2,1)S(1)}, u32[]{:S(2)}, u32[]{:S(2)}) collective-permute-start(bf16[384,256]{1,0:T(8,128)(2,1)S(1)} %fusion.8), channel_id=1, source_target_pairs={{0,64},{16,80},{32,96},{48,112},{64,0},{80,16},{96,32},{112,48},{1... | collective-permute-start | bytes 589832 | tf_op jit(solution)/shard_map/ppermute | solution.py:17
  83.2 24.3 %copy-start.19 = (bf16[384,256]{1,0:T(8,128)(2,1)}, bf16[384,256]{1,0:T(8,128)(2,1)S(1)}, u32[]{:S(2)}) copy-start(bf16[384,256]{1,0:T(8,128)(2,1)S(1)} %fusion.9) | copy-start | bytes 589828
  83.2 24.6 %collective-permute-start.6 = (bf16[384,256]{1,0:T(8,128)(2,1)S(1)}, bf16[384,256]{1,0:T(8,128)(2,1)}, u32[]{:S(2)}, u32[]{:S(2)}) collective-permute-start(bf16[384,256]{1,0:T(8,128)(2,1)S(1)} %fusion.9), channel_id=1, source_target_pairs={{0,64},{16,80},{32,96},{48,112},{64,0},{80,16},{96,32},{112,48},{1... | collective-permute-start | bytes 589832 | tf_op jit(solution)/shard_map/ppermute | solution.py:17
  85.6 21.9 %copy-start.9 = (bf16[2,256,256]{2,1,0:T(8,128)(2,1)}, bf16[2,256,256]{2,1,0:T(8,128)(2,1)S(1)}, u32[]{:S(2)}) copy-start(bf16[2,256,256]{2,1,0:T(8,128)(2,1)S(1)} %fusion.52) | copy-start | bytes 786436
  86.8 22.6 %collective-permute-start.8 = (bf16[384,256]{1,0:T(8,128)(2,1)S(1)}, bf16[384,256]{1,0:T(8,128)(2,1)S(1)}, u32[]{:S(2)}, u32[]{:S(2)}) collective-permute-start(bf16[384,256]{1,0:T(8,128)(2,1)S(1)} %fusion.10), channel_id=1, source_target_pairs={{0,128},{16,144},{32,160},{48,176},{64,192},{80,208},{96,224},{112... | collective-permute-start | bytes 589832 | tf_op jit(solution)/shard_map/ppermute | solution.py:17
  88.8 20.4 %copy-start.26 = (bf16[2,256,256]{2,1,0:T(8,128)(2,1)}, bf16[2,256,256]{2,1,0:T(8,128)(2,1)S(1)}, u32[]{:S(2)}) copy-start(bf16[2,256,256]{2,1,0:T(8,128)(2,1)S(1)} %fusion.51) | copy-start | bytes 786436
  107.7 9.6 %copy-start.31 = (bf16[2,2,2,256,256]{4,3,2,1,0:T(8,128)(2,1)S(1)}, bf16[2,2,2,256,256]{4,3,2,1,0:T(8,128)(2,1)}, u32[]{:S(2)}) copy-start(bf16[2,2,2,256,256]{4,3,2,1,0:T(8,128)(2,1)} %all-gather.5.cloned.1.call-done) | copy-start | bytes 3145732
  109.7 14.2 %collective-permute-start.9 = (bf16[384,256]{1,0:T(8,128)(2,1)S(1)}, bf16[384,256]{1,0:T(8,128)(2,1)S(1)}, u32[]{:S(2)}, u32[]{:S(2)}) collective-permute-start(bf16[384,256]{1,0:T(8,128)(2,1)S(1)} %fusion.13), channel_id=1, source_target_pairs={{0,256},{16,272},{32,288},{48,304},{64,320},{80,336},{96,352},{112... | collective-permute-start | bytes 589832 | tf_op jit(solution)/shard_map/ppermute | solution.py:17
  127.8 10.3 %collective-permute-start.10 = (bf16[384,256]{1,0:T(8,128)(2,1)S(1)}, bf16[384,256]{1,0:T(8,128)(2,1)S(1)}, u32[]{:S(2)}, u32[]{:S(2)}) collective-permute-start(bf16[384,256]{1,0:T(8,128)(2,1)S(1)} %fusion.15), channel_id=1, source_target_pairs={{0,256},{16,272},{32,288},{48,304},{64,320},{80,336},{96,352},{112... | collective-permute-start | bytes 589832 | tf_op jit(solution)/shard_map/ppermute | solution.py:17
  133.6 15.7 %copy-start.20 = (bf16[384,256]{1,0:T(8,128)(2,1)S(1)}, bf16[384,256]{1,0:T(8,128)(2,1)}, u32[]{:S(2)}) copy-start(bf16[384,256]{1,0:T(8,128)(2,1)} %copy-done.19) | copy-start | bytes 589828
  133.9 15.7 %copy-start.27 = (bf16[2,256,256]{2,1,0:T(8,128)(2,1)S(1)}, bf16[2,256,256]{2,1,0:T(8,128)(2,1)}, u32[]{:S(2)}) copy-start(bf16[2,256,256]{2,1,0:T(8,128)(2,1)} %copy-done.26) | copy-start | bytes 786436
  138.4 18.0 %copy-start.10 = (bf16[2,256,256]{2,1,0:T(8,128)(2,1)S(1)}, bf16[2,256,256]{2,1,0:T(8,128)(2,1)}, u32[]{:S(2)}) copy-start(bf16[2,256,256]{2,1,0:T(8,128)(2,1)} %copy-done.9) | copy-start | bytes 786436
  138.4 17.9 %collective-permute-start.11 = (bf16[384,256]{1,0:T(8,128)(2,1)S(1)}, bf16[384,256]{1,0:T(8,128)(2,1)S(1)}, u32[]{:S(2)}, u32[]{:S(2)}) collective-permute-start(bf16[384,256]{1,0:T(8,128)(2,1)S(1)} %fusion.17), channel_id=1, source_target_pairs={{0,128},{16,144},{32,160},{48,176},{64,192},{80,208},{96,224},{112... | collective-permute-start | bytes 589832 | tf_op jit(solution)/shard_map/ppermute | solution.py:17
  149.6 11.9 %copy-start.16 = (bf16[384,256]{1,0:T(8,128)(2,1)S(1)}, bf16[384,256]{1,0:T(8,128)(2,1)}, u32[]{:S(2)}) copy-start(bf16[384,256]{1,0:T(8,128)(2,1)} %copy-done.15) | copy-start | bytes 589828
  149.9 12.6 %copy-start.41 = (bf16[384,256]{1,0:T(8,128)(2,1)S(1)}, bf16[384,256]{1,0:T(8,128)(2,1)}, u32[]{:S(2)}) copy-start(bf16[384,256]{1,0:T(8,128)(2,1)} %copy-done.40) | copy-start | bytes 589828
  149.9 11.4 %collective-permute-start.15 = (bf16[384,256]{1,0:T(8,128)(2,1)S(1)}, bf16[384,256]{1,0:T(8,128)(2,1)S(1)}, u32[]{:S(2)}, u32[]{:S(2)}) collective-permute-start(bf16[384,256]{1,0:T(8,128)(2,1)S(1)} %broadcast_select_fusion.4), channel_id=1, source_target_pairs={{0,64},{16,80},{32,96},{48,112},{64,0},{80,16},{96,32},{112,48},{1... | collective-permute-start | bytes 589832 | tf_op jit(solution)/shard_map/ppermute | solution.py:17
  152.2 10.5 %copy-start.18 = (bf16[384,256]{1,0:T(8,128)(2,1)S(1)}, bf16[384,256]{1,0:T(8,128)(2,1)}, u32[]{:S(2)}) copy-start(bf16[384,256]{1,0:T(8,128)(2,1)} %copy-done.17) | copy-start | bytes 589828
  156.6 16.9 %collective-permute-start.13 = (bf16[384,256]{1,0:T(8,128)(2,1)S(1)}, bf16[384,256]{1,0:T(8,128)(2,1)S(1)}, u32[]{:S(2)}, u32[]{:S(2)}) collective-permute-start(bf16[384,256]{1,0:T(8,128)(2,1)S(1)} %convolution_convert_fusion.5), channel_id=1, source_target_pairs={{0,64},{16,80},{32,96},{48,112},{64,0},{80,16},{96,32},{112,48},{1... | collective-permute-start | bytes 589832 | tf_op jit(solution)/shard_map/ppermute | solution.py:17
  164.5 12.5 %collective-permute-start.16 = (bf16[384,256]{1,0:T(8,128)(2,1)S(1)}, bf16[384,256]{1,0:T(8,128)(2,1)S(1)}, u32[]{:S(2)}, u32[]{:S(2)}) collective-permute-start(bf16[384,256]{1,0:T(8,128)(2,1)S(1)} %broadcast_select_fusion.3), channel_id=1, source_target_pairs={{0,32},{16,48},{32,0},{48,16},{64,96},{80,112},{96,64},{112,80},{1... | collective-permute-start | bytes 589832 | tf_op jit(solution)/shard_map/ppermute | solution.py:17
  169.7 19.6 %collective-permute-start.12 = (bf16[8,3,2,2,16,256]{5,4,3,2,1,0:T(8,128)(2,1)S(1)}, bf16[8,3,2,2,16,256]{5,4,3,2,1,0:T(8,128)(2,1)S(1)}, u32[]{:S(2)}, u32[]{:S(2)}) collective-permute-start(bf16[8,3,2,2,16,256]{5,4,3,2,1,0:T(8,128)(2,1)S(1)} %select_bitcast_fusion.1), channel_id=1, source_target_pairs={{0,1},{1,0},{2,3},{3,2},{4,5},{5,4},{6,7},{7,6},{8,9},{9,8},{10,11... | collective-permute-start | bytes 2359304 | tf_op jit(solution)/shard_map/ppermute | solution.py:175
  173.7 10.6 %copy-start.22 = (bf16[2,256,256]{2,1,0:T(8,128)(2,1)S(1)}, bf16[2,256,256]{2,1,0:T(8,128)(2,1)}, u32[]{:S(2)}) copy-start(bf16[2,256,256]{2,1,0:T(8,128)(2,1)} %copy-done.21) | copy-start | bytes 786436
  174.0 14.2 %copy-start.12 = (bf16[384,256]{1,0:T(8,128)(2,1)S(1)}, bf16[384,256]{1,0:T(8,128)(2,1)}, u32[]{:S(2)}) copy-start(bf16[384,256]{1,0:T(8,128)(2,1)} %copy-done.11) | copy-start | bytes 589828
  174.0 10.1 %collective-permute-start.14 = (bf16[384,256]{1,0:T(8,128)(2,1)S(1)}, bf16[384,256]{1,0:T(8,128)(2,1)S(1)}, u32[]{:S(2)}, u32[]{:S(2)}) collective-permute-start(bf16[384,256]{1,0:T(8,128)(2,1)S(1)} %convolution_convert_fusion.4), channel_id=1, source_target_pairs={{0,32},{16,48},{32,0},{48,16},{64,96},{80,112},{96,64},{112,80},{1... | collective-permute-start | bytes 589832 | tf_op jit(solution)/shard_map/ppermute | solution.py:17
  177.0 11.5 %copy-start.35 = (bf16[384,256]{1,0:T(8,128)(2,1)S(1)}, bf16[384,256]{1,0:T(8,128)(2,1)}, u32[]{:S(2)}) copy-start(bf16[384,256]{1,0:T(8,128)(2,1)} %copy-done.34) | copy-start | bytes 589828
  185.3 13.9 %collective-permute-start.18 = (bf16[384,256]{1,0:T(8,128)(2,1)}, bf16[384,256]{1,0:T(8,128)(2,1)}, u32[]{:S(2)}, u32[]{:S(2)}) collective-permute-start(bf16[384,256]{1,0:T(8,128)(2,1)} %convolution_convert_fusion.3), channel_id=1, source_target_pairs={{0,16},{16,0},{32,48},{48,32},{64,80},{80,64},{96,112},{112,96},{1... | collective-permute-start | bytes 589832 | tf_op jit(solution)/shard_map/ppermute | solution.py:17
  190.6 8.5 %copy-start.23 = (bf16[2,256,256]{2,1,0:T(8,128)(2,1)S(1)}, bf16[2,256,256]{2,1,0:T(8,128)(2,1)}, u32[]{:S(2)}) copy-start(bf16[2,256,256]{2,1,0:T(8,128)(2,1)} %copy-done.21) | copy-start | bytes 786436
  191.4 27.6 %all-to-all-start = ((bf16[8,3,2,2,16,256]{5,4,3,2,1,0:T(8,128)(2,1)}), bf16[8,3,2,2,16,256]{5,4,3,2,1,0:T(8,128)(2,1)S(1)}, u32[]{:S(2)}, u32[]{:S(2)}) async-start(bf16[8,3,2,2,16,256]{5,4,3,2,1,0:T(8,128)(2,1)} %fusion.3), calls=%async_computation | async-start | bytes 1572864 | tf_op jit(solution)/shard_map/all_to_all | solution.py:182
  195.8 7.0 %collective-permute-start.17 = (bf16[384,256]{1,0:T(8,128)(2,1)S(1)}, bf16[384,256]{1,0:T(8,128)(2,1)S(1)}, u32[]{:S(2)}, u32[]{:S(2)}) collective-permute-start(bf16[384,256]{1,0:T(8,128)(2,1)S(1)} %fusion.25), channel_id=1, source_target_pairs={{0,16},{16,0},{32,48},{48,32},{64,80},{80,64},{96,112},{112,96},{1... | collective-permute-start | bytes 589832 | tf_op jit(solution)/shard_map/ppermute | solution.py:17
  205.1 14.0 %collective-permute-start.19 = (bf16[8,3,2,2,16,256]{5,4,3,2,1,0:T(8,128)(2,1)}, bf16[8,3,2,2,16,256]{5,4,3,2,1,0:T(8,128)(2,1)}, u32[]{:S(2)}, u32[]{:S(2)}) collective-permute-start(bf16[8,3,2,2,16,256]{5,4,3,2,1,0:T(8,128)(2,1)} %select_bitcast_fusion), channel_id=1, source_target_pairs={{0,1},{1,0},{2,3},{3,2},{4,5},{5,4},{6,7},{7,6},{8,9},{9,8},{10,11... | collective-permute-start | bytes 2359304 | tf_op jit(solution)/shard_map/ppermute | solution.py:175
  211.1 20.4 %collective-permute-start.20 = (bf16[384,256]{1,0:T(8,128)(2,1)}, bf16[384,256]{1,0:T(8,128)(2,1)}, u32[]{:S(2)}, u32[]{:S(2)}) collective-permute-start(bf16[384,256]{1,0:T(8,128)(2,1)} %fusion.57), channel_id=1, source_target_pairs={{0,256},{16,272},{32,288},{48,304},{64,320},{80,336},{96,352},{112... | collective-permute-start | bytes 589832 | tf_op jit(solution)/shard_map/ppermute | solution.py:17
  221.5 9.7 %copy-start.8 = (bf16[384,256]{1,0:T(8,128)(2,1)S(1)}, bf16[384,256]{1,0:T(8,128)(2,1)}, u32[]{:S(2)}) copy-start(bf16[384,256]{1,0:T(8,128)(2,1)} %copy-done.7) | copy-start | bytes 589828
  222.2 27.1 %all-to-all-start.1 = ((bf16[8,3,2,2,16,256]{5,4,3,2,1,0:T(8,128)(2,1)}), bf16[8,3,2,2,16,256]{5,4,3,2,1,0:T(8,128)(2,1)S(1)}, u32[]{:S(2)}, u32[]{:S(2)}) async-start(bf16[8,3,2,2,16,256]{5,4,3,2,1,0:T(8,128)(2,1)} %fusion.28), calls=%async_computation.1 | async-start | bytes 1572864 | tf_op jit(solution)/shard_map/all_to_all | solution.py:182
  226.5 9.8 %collective-permute-start.22 = (bf16[2,16,256]{2,1,0:T(8,128)(2,1)S(1)}, bf16[2,16,256]{2,1,0:T(8,128)(2,1)S(1)}, u32[]{:S(2)}, u32[]{:S(2)}) collective-permute-start(bf16[2,16,256]{2,1,0:T(8,128)(2,1)S(1)} %get-tuple-element.32), channel_id=1, source_target_pairs={{0,256},{16,272},{32,288},{48,304},{64,320},{80,336},{96,352},{112... | collective-permute-start | bytes 49160 | tf_op jit(solution)/shard_map/ppermute | solution.py:17
  232.6 13.9 %collective-permute-start.21 = (bf16[384,256]{1,0:T(8,128)(2,1)S(1)}, bf16[384,256]{1,0:T(8,128)(2,1)S(1)}, u32[]{:S(2)}, u32[]{:S(2)}) collective-permute-start(bf16[384,256]{1,0:T(8,128)(2,1)S(1)} %select_select_fusion), channel_id=1, source_target_pairs={{0,128},{16,144},{32,160},{48,176},{64,192},{80,208},{96,224},{112... | collective-permute-start | bytes 589832 | tf_op jit(solution)/shard_map/ppermute | solution.py:17
  236.3 11.2 %collective-permute-start.23 = (bf16[2,2,16,256]{3,2,1,0:T(8,128)(2,1)S(1)}, bf16[2,2,16,256]{3,2,1,0:T(8,128)(2,1)S(1)}, u32[]{:S(2)}, u32[]{:S(2)}) collective-permute-start(bf16[2,2,16,256]{3,2,1,0:T(8,128)(2,1)S(1)} %get-tuple-element.29), channel_id=1, source_target_pairs={{0,128},{16,144},{32,160},{48,176},{64,192},{80,208},{96,224},{112... | collective-permute-start | bytes 98312 | tf_op jit(solution)/shard_map/ppermute | solution.py:17
  (31 other events, 120.9 us)
Sparse Core Ops, SparseCore 0:
  10.7 47.2 all-gather.2
  67.3 39.1 all-gather.4

commit v8 on v6

--- a/solution.py
+++ b/solution.py
@@ -156,6 +156,17 @@
     return result[0] if len(outs) == 1 else result
 
 
+def row_terms(parts, grads):
+    return jnp.stack([jnp.stack([dot_rows(part[r], grads[r]) for r in range(2)]) for part in parts])
+
+
+def spread(shards):
+    size = lax.axis_size("tok")
+    every = lax.all_to_all(jnp.broadcast_to(shards, (size, *shards.shape)), "tok", 0, 0)
+    every = jnp.moveaxis(every, 0, 3)
+    return list(every.reshape(*shards.shape[:3], size * shards.shape[3], shards.shape[4]))
+
+
 def core_half(terms, core):
     count, both, per_dev, size, depth, width = terms.shape
     parts = terms.reshape(count, both, per_dev, size // 2, 2, depth, width)
@@ -210,21 +221,27 @@
         cotangent,
         outs=[shape(2, 2, depth), shape(2, depth), shape(2 * depth + tokens), shape(tokens)],
     )
-    came = flip(packed, 4)
-    cotan1 = came[2 * depth :]
-    late = local(gather_late, matchings, fourth, fifth, came, outs=[shape(2, 2, 2, depth)])
-    full += list(lax.all_gather(late, "tok", axis=3, tiled=True))
-
+    late = flip(packed, 4)
+    cotan1 = late[2 * depth :]
+
+    other = flip(value, 0)
+    rows, others = [value[0], value[1]], [other[0], other[1]]
     for section in range(1, 4):
-        other = flip(value, section - 1)
-        inputs.append((value, other))
-        full[section] = after(full[section], value)
-        own_w, other_w = full[section][0], full[section][1]
-        if section < 3:
-            value = (dot(value, own_w) + dot(other, other_w)).astype(bf16)
-        else:
-            send = (dot(value[1], own_w[1]) + dot(other[1], other_w[1])).astype(bf16)
-            keep = (dot(value[0], own_w[0]) + dot(other[0], other_w[0])).astype(bf16)
+        if section > 1:
+            second = flip(rows[1], section - 1)
+            others = [flip(rows[0], section - 1), second]
+        inputs.append((rows, others))
+        weight = after(full[section], rows[0])
+        first, second = [
+            (dot(rows[r], weight[0, r]) + dot(others[r], weight[1, r])).astype(bf16) for r in range(2)
+        ]
+        full[section] = weight
+        if section == 1:
+            late = after(late, second)
+            late = local(gather_late, matchings, fourth, fifth, late, outs=[shape(2, 2, 2, depth)])
+            full += spread(late)
+        rows = [first, second]
+    keep, send = rows
     came = flip(send, 3)
     inputs.append((keep, came))
     full[4] = after(full[4], send)
@@ -258,7 +275,7 @@
         own_w, other_w = full[section][0], full[section][1]
         sent = dot_back(grad, other_w).astype(bf16)
         back = flip(sent, section - 1)
-        terms[section] = jnp.stack([dot_rows(part, grad) for part in inputs[section]])
+        terms[section] = row_terms(inputs[section], grad)
         if section == 3:
             chip = chip_sum(jnp.stack(terms[3:]))
             parts_high = all_parts(chip)

time: 245 us -> 259 us (1.057)
  matrix products: 20 us -> 27.1 us
  starting transfers between devices: 96.5 us -> 103 us
  waiting for transfers between devices: 66.7 us -> 61.7 us
  other arithmetic: 13.4 us -> 17.5 us
    ppermute x16 -> x18, waiting for transfers between devices: 56.5 us -> 44.6 us  [flip(): return lax.ppermute(value, 'blk', pairs)]
    all_to_all x0 -> x1, waiting for transfers between devices: none -> 10.2 us  [spread(): lax.all_to_all(jnp.broadcast_to(shards, (size, *shards.shape)), 'tok', 0, 0)]
    all_gather x1 -> x0, waiting for transfers between devices: 9.94 us -> none  [body(): full += list(lax.all_gather(late, 'tok', axis=3, tiled=True))]
    all_to_all x0 -> x1, starting transfers between devices: none -> 5.5 us  [spread(): lax.all_to_all(jnp.broadcast_to(shards, (size, *shards.shape)), 'tok', 0, 0)]
    all_to_all x2, waiting for transfers between devices: 0.17 us -> 4.92 us  [all_parts(): return lax.all_to_all(chip, 'tok', 0, 0, axis_index_groups=groups)]
    dot_general x18 -> x22, matrix products: 6.17 us -> 10.6 us  [dot(): jnp.einsum('...tk,...kl->...tl', left, right, preferred_element_type=jnp....]
    ppermute x16 -> x18, starting transfers between devices: 76.8 us -> 79.9 us  [flip(): return lax.ppermute(value, 'blk', pairs)]
    dot_general x16 -> x22, matrix products: 7.34 us -> 9.99 us  [dot_rows(): jnp.einsum('...tk,...tl->...kl', left, right, preferred_element_type=jnp....]
  transfers between devices with their start and end apart: 22 -> 24, of which waited for: 11 -> 11; matrix products, arithmetic and copies ran while one was open for 12% -> 16% of each run, Pallas kernels for 1% -> 1%
where the time goes in v8:
time: 259 us; the launch traced here: 257 us
  starting transfers between devices  103 us (40%)
  waiting for transfers between devices  61.7 us (24%)
  matrix products  27.1 us (10%)
  blocking collectives  20 us (8%)
  other arithmetic  17.5 us (7%)
  between operations  15.2 us (6%)
  local copies, waits for them, and re-layouts  6.7 us (3%)
  Pallas kernels  5.35 us (2%)
    ppermute x18, starting transfers between devices, flip(): return lax.ppermute(value, 'blk', pairs)  79.9 us
    ppermute x18, waiting for transfers between devices, flip(): return lax.ppermute(value, 'blk', pairs)  44.6 us
    all_gather x1, blocking collectives, body(): full = list(lax.all_gather(first, 'tok', axis=3, tiled=True))  20 us
    dot_general x22, matrix products, dot(): jnp.einsum('...tk,...kl->...tl', left, right, preferred_element_type=jnp....  10.6 us
    all_to_all x2, starting transfers between devices, all_parts(): return lax.all_to_all(chip, 'tok', 0, 0, axis_index_groups=groups)  10.2 us
    all_to_all x1, waiting for transfers between devices, spread(): lax.all_to_all(jnp.broadcast_to(shards, (size, *shards.shape)), 'tok', 0, 0)  10.2 us
    dot_general x22, matrix products, dot_rows(): jnp.einsum('...tk,...tl->...kl', left, right, preferred_element_type=jnp....  9.99 us
    select_n x10, other arithmetic, after(): return jnp.where(probe != probe, jnp.zeros_like(value), value)  7.81 us
  transfers between devices with their start and end apart: 24, of which 11 were waited for; matrix products, arithmetic and copies ran while one was open for 16% of the time, Pallas kernels for 1%

profile of v8, /device:TPU:1, one launch (start us, length us, event | category | flops | bytes accessed | tf_op | source)
XLA Modules:
  0.0 257.0 jit_solution(6352165160746170794)
XLA Ops:
  8.8 1.3 shard_map.67
  13.4 6.6 %collective-permute-start.2 = (bf16[448,256]{1,0:T(8,128)(2,1)S(1)}, bf16[448,256]{1,0:T(8,128)(2,1)S(1)}, u32[]{:S(2)}, u32[]{:S(2)}) collective-permute-start(bf16[448,256]{1,0:T(8,128)(2,1)S(1)} %get-tuple-element.14), channel_id=1, source_target_pairs={{0,128},{16,144},{32,160},{48,176},{64,192},{80,208},{96,224},{112... | collective-permute-start | bytes 688136 | tf_op jit(solution)/shard_map/ppermute | solution.py:17
  21.2 20.0 %all_gather.6 = bf16[1,2,2,256,256]{4,3,2,1,0:T(8,128)(2,1)S(1)} all-gather(bf16[1,2,2,16,256]{4,3,2,1,0:T(8,128)(2,1)S(1)} %get-tuple-element.11), channel_id=1, replica_groups=mesh['blk'=32,'tok'=16] {'tok'}, dimensions={3}, use_global_device_ids=true | all-gather | bytes 557056 | tf_op jit(solution)/shard_map/all_gather | solution.py:207
  41.8 3.1 %collective-permute-start = (bf16[2,384,256]{2,1,0:T(8,128)(2,1)S(1)}, bf16[2,384,256]{2,1,0:T(8,128)(2,1)S(1)}, u32[]{:S(2)}, u32[]{:S(2)}) collective-permute-start(bf16[2,384,256]{2,1,0:T(8,128)(2,1)S(1)} %fusion.4), channel_id=1, source_target_pairs={{0,16},{16,0},{32,48},{48,32},{64,80},{80,64},{96,112},{112,96},{1... | collective-permute-start | bytes 1179656 | tf_op jit(solution)/shard_map/ppermute | solution.py:17
  45.6 10.4 %collective-permute-start.6 = (bf16[416,256]{1,0:T(8,128)(2,1)S(1)}, bf16[416,256]{1,0:T(8,128)(2,1)S(1)}, u32[]{:S(2)}, u32[]{:S(2)}) collective-permute-start(bf16[416,256]{1,0:T(8,128)(2,1)S(1)} %get-tuple-element.18), channel_id=1, source_target_pairs={{0,256},{16,272},{32,288},{48,304},{64,320},{80,336},{96,352},{112... | collective-permute-start | bytes 638984 | tf_op jit(solution)/shard_map/ppermute | solution.py:17
  56.1 1.9 all-gather.2.cloned.1.call-done
  59.6 4.6 %collective-permute-start.4 = (bf16[384,256]{1,0:T(8,128)(2,1)S(1)}, bf16[384,256]{1,0:T(8,128)(2,1)}, u32[]{:S(2)}, u32[]{:S(2)}) collective-permute-start(bf16[384,256]{1,0:T(8,128)(2,1)S(1)} %fusion.11), channel_id=1, source_target_pairs={{0,32},{16,48},{32,0},{48,16},{64,96},{80,112},{96,64},{112,80},{1... | collective-permute-start | bytes 589832 | tf_op jit(solution)/shard_map/ppermute | solution.py:17
  66.0 2.2 collective-permute-start.1
  70.9 1.1 broadcast_in_dim.53
  72.0 5.5 %all-to-all-start = ((bf16[16,2,2,2,16,256]{5,4,3,2,1,0:T(8,128)(2,1)}), bf16[16,2,2,2,16,256]{5,4,3,2,1,0:T(8,128)(2,1)S(1)}, u32[]{:S(2)}, u32[]{:S(2)}) async-start(bf16[16,2,2,2,16,256]{5,4,3,2,1,0:T(8,128)(2,1)} %broadcast_in_dim.53), calls=%async_computation | async-start | bytes 2097152 | tf_op jit(solution)/shard_map/all_to_all | solution.py:165
  77.5 1.1 fusion.55
  78.7 1.1 fusion.12
  79.8 3.3 %collective-permute-start.5 = (bf16[384,256]{1,0:T(8,128)(2,1)S(1)}, bf16[384,256]{1,0:T(8,128)(2,1)S(1)}, u32[]{:S(2)}, u32[]{:S(2)}) collective-permute-start(bf16[384,256]{1,0:T(8,128)(2,1)S(1)} %fusion.12), channel_id=1, source_target_pairs={{0,64},{16,80},{32,96},{48,112},{64,0},{80,16},{96,32},{112,48},{1... | collective-permute-start | bytes 589832 | tf_op jit(solution)/shard_map/ppermute | solution.py:17
  83.1 1.1 fusion.9
  84.3 2.0 collective-permute-start.3
  89.1 4.5 %collective-permute-start.7 = (bf16[384,256]{1,0:T(8,128)(2,1)}, bf16[384,256]{1,0:T(8,128)(2,1)S(1)}, u32[]{:S(2)}, u32[]{:S(2)}) collective-permute-start(bf16[384,256]{1,0:T(8,128)(2,1)} %fusion.13), channel_id=1, source_target_pairs={{0,128},{16,144},{32,160},{48,176},{64,192},{80,208},{96,224},{112... | collective-permute-start | bytes 589832 | tf_op jit(solution)/shard_map/ppermute | solution.py:17
  95.2 10.2 %all-to-all-done = bf16[16,2,2,2,16,256]{5,4,3,2,1,0:T(8,128)(2,1)S(1)} async-done(((bf16[16,2,2,2,16,256]{5,4,3,2,1,0:T(8,128)(2,1)}), bf16[16,2,2,2,16,256]{5,4,3,2,1,0:T(8,128)(2,1)S(1)}, u32[]{:S(2)}, u32[]{:S(2)}) %all-to-all-start) | async-done | bytes 1048608 | tf_op jit(solution)/shard_map/all_to_all | solution.py:165
  106.1 8.2 %collective-permute-start.8 = (bf16[384,256]{1,0:T(8,128)(2,1)S(1)}, bf16[384,256]{1,0:T(8,128)(2,1)S(1)}, u32[]{:S(2)}, u32[]{:S(2)}) collective-permute-start(bf16[384,256]{1,0:T(8,128)(2,1)S(1)} %fusion.15), channel_id=1, source_target_pairs={{0,256},{16,272},{32,288},{48,304},{64,320},{80,336},{96,352},{112... | collective-permute-start | bytes 589832 | tf_op jit(solution)/shard_map/ppermute | solution.py:17
  115.3 7.0 %collective-permute-done.8 = bf16[384,256]{1,0:T(8,128)(2,1)S(1)} collective-permute-done((bf16[384,256]{1,0:T(8,128)(2,1)S(1)}, bf16[384,256]{1,0:T(8,128)(2,1)S(1)}, u32[]{:S(2)}, u32[]{:S(2)}) %collective-permute-start.8) | collective-permute-done | bytes 196640 | tf_op jit(solution)/shard_map/ppermute | solution.py:17
  123.6 1.2 fusion.33
  126.3 7.8 %collective-permute-start.9 = (bf16[384,256]{1,0:T(8,128)(2,1)S(1)}, bf16[384,256]{1,0:T(8,128)(2,1)S(1)}, u32[]{:S(2)}, u32[]{:S(2)}) collective-permute-start(bf16[384,256]{1,0:T(8,128)(2,1)S(1)} %fusion.17), channel_id=1, source_target_pairs={{0,256},{16,272},{32,288},{48,304},{64,320},{80,336},{96,352},{112... | collective-permute-start | bytes 589832 | tf_op jit(solution)/shard_map/ppermute | solution.py:17
  134.9 6.7 %collective-permute-done.9 = bf16[384,256]{1,0:T(8,128)(2,1)S(1)} collective-permute-done((bf16[384,256]{1,0:T(8,128)(2,1)S(1)}, bf16[384,256]{1,0:T(8,128)(2,1)S(1)}, u32[]{:S(2)}, u32[]{:S(2)}) %collective-permute-start.9) | collective-permute-done | bytes 196640 | tf_op jit(solution)/shard_map/ppermute | solution.py:17
  142.4 4.5 %collective-permute-start.10 = (bf16[384,256]{1,0:T(8,128)(2,1)S(1)}, bf16[384,256]{1,0:T(8,128)(2,1)S(1)}, u32[]{:S(2)}, u32[]{:S(2)}) collective-permute-start(bf16[384,256]{1,0:T(8,128)(2,1)S(1)} %fusion.19), channel_id=1, source_target_pairs={{0,128},{16,144},{32,160},{48,176},{64,192},{80,208},{96,224},{112... | collective-permute-start | bytes 589832 | tf_op jit(solution)/shard_map/ppermute | solution.py:17
  147.7 7.7 %collective-permute-done.10 = bf16[384,256]{1,0:T(8,128)(2,1)S(1)} collective-permute-done((bf16[384,256]{1,0:T(8,128)(2,1)S(1)}, bf16[384,256]{1,0:T(8,128)(2,1)S(1)}, u32[]{:S(2)}, u32[]{:S(2)}) %collective-permute-start.10) | collective-permute-done | bytes 196640 | tf_op jit(solution)/shard_map/ppermute | solution.py:17
  155.7 1.9 collective-permute-start.12
  158.8 2.5 collective-permute-start.11
  161.3 6.5 %collective-permute-done.12 = bf16[2,384,256]{2,1,0:T(8,128)(2,1)S(1)} collective-permute-done((bf16[2,384,256]{2,1,0:T(8,128)(2,1)S(1)}, bf16[2,384,256]{2,1,0:T(8,128)(2,1)S(1)}, u32[]{:S(2)}, u32[]{:S(2)}) %collective-permute-start.12) | collective-permute-done | bytes 393248 | tf_op jit(solution)/shard_map/ppermute | solution.py:17
  169.4 4.0 %collective-permute-start.13 = (bf16[2,384,256]{2,1,0:T(8,128)(2,1)}, bf16[2,384,256]{2,1,0:T(8,128)(2,1)}, u32[]{:S(2)}, u32[]{:S(2)}) collective-permute-start(bf16[2,384,256]{2,1,0:T(8,128)(2,1)} %convolution_convert_fusion.1), channel_id=1, source_target_pairs={{0,32},{16,48},{32,0},{48,16},{64,96},{80,112},{96,64},{112,80},{1... | collective-permute-start | bytes 1179656 | tf_op jit(solution)/shard_map/ppermute | solution.py:17
  173.5 1.2 convolution_convert_fusion.8
  174.7 1.8 convolution_convert_fusion.5
  176.5 1.9 convolution_convert_fusion.6
  178.3 1.2 fusion.3
  179.6 3.7 %all-to-all-start.1 = ((bf16[8,3,2,2,16,256]{5,4,3,2,1,0:T(8,128)(2,1)}), bf16[8,3,2,2,16,256]{5,4,3,2,1,0:T(8,128)(2,1)S(1)}, u32[]{:S(2)}, u32[]{:S(2)}) async-start(bf16[8,3,2,2,16,256]{5,4,3,2,1,0:T(8,128)(2,1)} %fusion.3), calls=%async_computation.1 | async-start | bytes 1572864 | tf_op jit(solution)/shard_map/all_to_all | solution.py:189
  184.0 1.4 broadcast_select_fusion.3
  186.3 2.4 collective-permute-start.14
  189.4 7.1 %collective-permute-done.14 = bf16[2,384,256]{2,1,0:T(8,128)(2,1)S(1)} collective-permute-done((bf16[2,384,256]{2,1,0:T(8,128)(2,1)S(1)}, bf16[2,384,256]{2,1,0:T(8,128)(2,1)S(1)}, u32[]{:S(2)}, u32[]{:S(2)}) %collective-permute-start.14) | collective-permute-done | bytes 393248 | tf_op jit(solution)/shard_map/ppermute | solution.py:17
  198.9 5.2 %collective-permute-start.15 = (bf16[8,3,2,2,16,256]{5,4,3,2,1,0:T(8,128)(2,1)}, bf16[8,3,2,2,16,256]{5,4,3,2,1,0:T(8,128)(2,1)}, u32[]{:S(2)}, u32[]{:S(2)}) collective-permute-start(bf16[8,3,2,2,16,256]{5,4,3,2,1,0:T(8,128)(2,1)} %select_bitcast_fusion), channel_id=1, source_target_pairs={{0,1},{1,0},{2,3},{3,2},{4,5},{5,4},{6,7},{7,6},{8,9},{9,8},{10,11... | collective-permute-start | bytes 2359304 | tf_op jit(solution)/shard_map/ppermute | solution.py:182
  204.8 1.8 fusion.47
  206.7 8.6 %collective-permute-start.16 = (bf16[384,256]{1,0:T(8,128)(2,1)}, bf16[384,256]{1,0:T(8,128)(2,1)S(1)}, u32[]{:S(2)}, u32[]{:S(2)}) collective-permute-start(bf16[384,256]{1,0:T(8,128)(2,1)} %fusion.47), channel_id=1, source_target_pairs={{0,256},{16,272},{32,288},{48,304},{64,320},{80,336},{96,352},{112... | collective-permute-start | bytes 589832 | tf_op jit(solution)/shard_map/ppermute | solution.py:17
  215.3 2.4 fusion.22
  218.5 6.6 %all-to-all-start.2 = ((bf16[8,3,2,2,16,256]{5,4,3,2,1,0:T(8,128)(2,1)}), bf16[8,3,2,2,16,256]{5,4,3,2,1,0:T(8,128)(2,1)S(1)}, u32[]{:S(2)}, u32[]{:S(2)}) async-start(bf16[8,3,2,2,16,256]{5,4,3,2,1,0:T(8,128)(2,1)} %fusion.22), calls=%async_computation.2 | async-start | bytes 1572864 | tf_op jit(solution)/shard_map/all_to_all | solution.py:189
  225.8 1.9 collective-permute-start.18
  227.9 1.9 collective-permute-start.17
  231.6 2.5 collective-permute-done.18
  234.2 1.9 collective-permute-start.19
  236.1 6.7 %collective-permute-done.17 = bf16[384,256]{1,0:T(8,128)(2,1)S(1)} collective-permute-done((bf16[384,256]{1,0:T(8,128)(2,1)S(1)}, bf16[384,256]{1,0:T(8,128)(2,1)S(1)}, u32[]{:S(2)}, u32[]{:S(2)}) %collective-permute-start.17) | collective-permute-done | bytes 196640 | tf_op jit(solution)/shard_map/ppermute | solution.py:17
  243.7 4.9 %all-to-all-done.2.parts_low = bf16[8,3,2,2,16,256]{5,4,3,2,1,0:T(8,128)(2,1)S(1)} async-done(((bf16[8,3,2,2,16,256]{5,4,3,2,1,0:T(8,128)(2,1)}), bf16[8,3,2,2,16,256]{5,4,3,2,1,0:T(8,128)(2,1)S(1)}, u32[]{:S(2)}, u32[]{:S(2)}) %all-to-all-start.2) | async-done | bytes 786464 | tf_op jit(solution)/shard_map/all_to_all | solution.py:189
  248.7 1.5 shard_map.72
  (186 shorter events, 36.8 us)
Async XLA Ops:
  7.2 50.8 %all-gather.2.cloned.1.call-start = ((), (), s32[]{:S(2)}) async-start(), calls=%async_computation.3 | async-start | bytes 1671168 | tf_op jit(solution)/shard_map/all_gather | solution.py:208
  13.4 31.6 %collective-permute-start.2 = (bf16[448,256]{1,0:T(8,128)(2,1)S(1)}, bf16[448,256]{1,0:T(8,128)(2,1)S(1)}, u32[]{:S(2)}, u32[]{:S(2)}) collective-permute-start(bf16[448,256]{1,0:T(8,128)(2,1)S(1)} %get-tuple-element.14), channel_id=1, source_target_pairs={{0,128},{16,144},{32,160},{48,176},{64,192},{80,208},{96,224},{112... | collective-permute-start | bytes 688136 | tf_op jit(solution)/shard_map/ppermute | solution.py:17
  21.1 20.4 %copy-start.17 = (bf16[1,384,256]{2,1,0:T(8,128)(2,1)}, bf16[1,384,256]{2,1,0:T(8,128)(2,1)S(1)}, u32[]{:S(2)}) copy-start(bf16[1,384,256]{2,1,0:T(8,128)(2,1)S(1)} %get-tuple-element.29) | copy-start | bytes 589828
  21.1 20.4 %copy-start.19 = (bf16[1,384,256]{2,1,0:T(8,128)(2,1)}, bf16[1,384,256]{2,1,0:T(8,128)(2,1)S(1)}, u32[]{:S(2)}) copy-start(bf16[1,384,256]{2,1,0:T(8,128)(2,1)S(1)} %get-tuple-element.30) | copy-start | bytes 589828
  41.8 22.4 %copy-start.21 = (bf16[2,384,256]{2,1,0:T(8,128)(2,1)}, bf16[2,384,256]{2,1,0:T(8,128)(2,1)S(1)}, u32[]{:S(2)}) copy-start(bf16[2,384,256]{2,1,0:T(8,128)(2,1)S(1)} %fusion.4) | copy-start | bytes 1179652
  41.8 17.5 %collective-permute-start = (bf16[2,384,256]{2,1,0:T(8,128)(2,1)S(1)}, bf16[2,384,256]{2,1,0:T(8,128)(2,1)S(1)}, u32[]{:S(2)}, u32[]{:S(2)}) collective-permute-start(bf16[2,384,256]{2,1,0:T(8,128)(2,1)S(1)} %fusion.4), channel_id=1, source_target_pairs={{0,16},{16,0},{32,48},{48,32},{64,80},{80,64},{96,112},{112,96},{1... | collective-permute-start | bytes 1179656 | tf_op jit(solution)/shard_map/ppermute | solution.py:17
  45.6 24.6 %collective-permute-start.6 = (bf16[416,256]{1,0:T(8,128)(2,1)S(1)}, bf16[416,256]{1,0:T(8,128)(2,1)S(1)}, u32[]{:S(2)}, u32[]{:S(2)}) collective-permute-start(bf16[416,256]{1,0:T(8,128)(2,1)S(1)} %get-tuple-element.18), channel_id=1, source_target_pairs={{0,256},{16,272},{32,288},{48,304},{64,320},{80,336},{96,352},{112... | collective-permute-start | bytes 638984 | tf_op jit(solution)/shard_map/ppermute | solution.py:17
  59.1 6.2 %copy-start.7 = (bf16[2,2,256,256]{3,2,1,0:T(8,128)(2,1)}, bf16[2,2,256,256]{3,2,1,0:T(8,128)(2,1)S(1)}, u32[]{:S(2)}) copy-start(bf16[2,2,256,256]{3,2,1,0:T(8,128)(2,1)S(1)} %fusion.25) | copy-start | bytes 1572868
  59.3 10.0 %copy-start.30 = (bf16[2,384,256]{2,1,0:T(8,128)(2,1)}, bf16[2,384,256]{2,1,0:T(8,128)(2,1)S(1)}, u32[]{:S(2)}) copy-start(bf16[2,384,256]{2,1,0:T(8,128)(2,1)S(1)} %collective-permute-done) | copy-start | bytes 1179652
  59.5 10.7 %copy-start.24 = (bf16[384,256]{1,0:T(8,128)(2,1)}, bf16[384,256]{1,0:T(8,128)(2,1)S(1)}, u32[]{:S(2)}) copy-start(bf16[384,256]{1,0:T(8,128)(2,1)S(1)} %fusion.11) | copy-start | bytes 589828
  59.6 19.1 %collective-permute-start.4 = (bf16[384,256]{1,0:T(8,128)(2,1)S(1)}, bf16[384,256]{1,0:T(8,128)(2,1)}, u32[]{:S(2)}, u32[]{:S(2)}) collective-permute-start(bf16[384,256]{1,0:T(8,128)(2,1)S(1)} %fusion.11), channel_id=1, source_target_pairs={{0,32},{16,48},{32,0},{48,16},{64,96},{80,112},{96,64},{112,80},{1... | collective-permute-start | bytes 589832 | tf_op jit(solution)/shard_map/ppermute | solution.py:17
  66.0 17.1 %collective-permute-start.1 = (bf16[384,256]{1,0:T(8,128)(2,1)}, bf16[384,256]{1,0:T(8,128)(2,1)}, u32[]{:S(2)}, u32[]{:S(2)}) collective-permute-start(bf16[384,256]{1,0:T(8,128)(2,1)} %fusion.8), channel_id=1, source_target_pairs={{0,32},{16,48},{32,0},{48,16},{64,96},{80,112},{96,64},{112,80},{1... | collective-permute-start | bytes 589832 | tf_op jit(solution)/shard_map/ppermute | solution.py:17
  72.0 6.6 %copy-start.23 = (f32[384,256]{1,0:T(8,128)S(1)}, f32[384,256]{1,0:T(8,128)}, u32[]{:S(2)}) copy-start(f32[384,256]{1,0:T(8,128)} %fusion.53) | copy-start | bytes 1179652
  72.0 33.4 %all-to-all-start = ((bf16[16,2,2,2,16,256]{5,4,3,2,1,0:T(8,128)(2,1)}), bf16[16,2,2,2,16,256]{5,4,3,2,1,0:T(8,128)(2,1)S(1)}, u32[]{:S(2)}, u32[]{:S(2)}) async-start(bf16[16,2,2,2,16,256]{5,4,3,2,1,0:T(8,128)(2,1)} %broadcast_in_dim.53), calls=%async_computation | async-start | bytes 2097152 | tf_op jit(solution)/shard_map/all_to_all | solution.py:165
  79.8 8.0 %copy-start.13 = (bf16[384,256]{1,0:T(8,128)(2,1)}, bf16[384,256]{1,0:T(8,128)(2,1)S(1)}, u32[]{:S(2)}) copy-start(bf16[384,256]{1,0:T(8,128)(2,1)S(1)} %fusion.12) | copy-start | bytes 589828
  79.8 8.4 %collective-permute-start.5 = (bf16[384,256]{1,0:T(8,128)(2,1)S(1)}, bf16[384,256]{1,0:T(8,128)(2,1)S(1)}, u32[]{:S(2)}, u32[]{:S(2)}) collective-permute-start(bf16[384,256]{1,0:T(8,128)(2,1)S(1)} %fusion.12), channel_id=1, source_target_pairs={{0,64},{16,80},{32,96},{48,112},{64,0},{80,16},{96,32},{112,48},{1... | collective-permute-start | bytes 589832 | tf_op jit(solution)/shard_map/ppermute | solution.py:17
  84.3 4.8 %copy-start.15 = (bf16[384,256]{1,0:T(8,128)(2,1)}, bf16[384,256]{1,0:T(8,128)(2,1)S(1)}, u32[]{:S(2)}) copy-start(bf16[384,256]{1,0:T(8,128)(2,1)S(1)} %fusion.9) | copy-start | bytes 589828
  84.3 10.0 %collective-permute-start.3 = (bf16[384,256]{1,0:T(8,128)(2,1)S(1)}, bf16[384,256]{1,0:T(8,128)(2,1)S(1)}, u32[]{:S(2)}, u32[]{:S(2)}) collective-permute-start(bf16[384,256]{1,0:T(8,128)(2,1)S(1)} %fusion.9), channel_id=1, source_target_pairs={{0,64},{16,80},{32,96},{48,112},{64,0},{80,16},{96,32},{112,48},{1... | collective-permute-start | bytes 589832 | tf_op jit(solution)/shard_map/ppermute | solution.py:17
  87.4 6.9 %copy-start.11 = (bf16[2,2,256,256]{3,2,1,0:T(8,128)(2,1)}, bf16[2,2,256,256]{3,2,1,0:T(8,128)(2,1)S(1)}, u32[]{:S(2)}) copy-start(bf16[2,2,256,256]{3,2,1,0:T(8,128)(2,1)S(1)} %fusion.23) | copy-start | bytes 1572868
  88.2 17.4 %copy-start.26 = (bf16[384,256]{1,0:T(8,128)(2,1)}, bf16[384,256]{1,0:T(8,128)(2,1)S(1)}, u32[]{:S(2)}) copy-start(bf16[384,256]{1,0:T(8,128)(2,1)S(1)} %collective-permute-done.5) | copy-start | bytes 589828
  89.1 16.8 %collective-permute-start.7 = (bf16[384,256]{1,0:T(8,128)(2,1)}, bf16[384,256]{1,0:T(8,128)(2,1)S(1)}, u32[]{:S(2)}, u32[]{:S(2)}) collective-permute-start(bf16[384,256]{1,0:T(8,128)(2,1)} %fusion.13), channel_id=1, source_target_pairs={{0,128},{16,144},{32,160},{48,176},{64,192},{80,208},{96,224},{112... | collective-permute-start | bytes 589832 | tf_op jit(solution)/shard_map/ppermute | solution.py:17
  106.1 16.2 %collective-permute-start.8 = (bf16[384,256]{1,0:T(8,128)(2,1)S(1)}, bf16[384,256]{1,0:T(8,128)(2,1)S(1)}, u32[]{:S(2)}, u32[]{:S(2)}) collective-permute-start(bf16[384,256]{1,0:T(8,128)(2,1)S(1)} %fusion.15), channel_id=1, source_target_pairs={{0,256},{16,272},{32,288},{48,304},{64,320},{80,336},{96,352},{112... | collective-permute-start | bytes 589832 | tf_op jit(solution)/shard_map/ppermute | solution.py:17
  126.0 15.8 %copy-start.16 = (bf16[384,256]{1,0:T(8,128)(2,1)S(1)}, bf16[384,256]{1,0:T(8,128)(2,1)}, u32[]{:S(2)}) copy-start(bf16[384,256]{1,0:T(8,128)(2,1)} %copy-done.15) | copy-start | bytes 589828
  126.3 15.3 %collective-permute-start.9 = (bf16[384,256]{1,0:T(8,128)(2,1)S(1)}, bf16[384,256]{1,0:T(8,128)(2,1)S(1)}, u32[]{:S(2)}, u32[]{:S(2)}) collective-permute-start(bf16[384,256]{1,0:T(8,128)(2,1)S(1)} %fusion.17), channel_id=1, source_target_pairs={{0,256},{16,272},{32,288},{48,304},{64,320},{80,336},{96,352},{112... | collective-permute-start | bytes 589832 | tf_op jit(solution)/shard_map/ppermute | solution.py:17
  134.9 12.5 %copy-start.29 = (bf16[384,256]{1,0:T(8,128)(2,1)S(1)}, bf16[384,256]{1,0:T(8,128)(2,1)}, u32[]{:S(2)}) copy-start(bf16[384,256]{1,0:T(8,128)(2,1)} %copy-done.28) | copy-start | bytes 589828
  141.8 13.6 %copy-start.12 = (bf16[2,2,256,256]{3,2,1,0:T(8,128)(2,1)S(1)}, bf16[2,2,256,256]{3,2,1,0:T(8,128)(2,1)}, u32[]{:S(2)}) copy-start(bf16[2,2,256,256]{3,2,1,0:T(8,128)(2,1)} %copy-done.11) | copy-start | bytes 1572868
  142.4 15.3 %copy-start.27 = (bf16[384,256]{1,0:T(8,128)(2,1)S(1)}, bf16[384,256]{1,0:T(8,128)(2,1)}, u32[]{:S(2)}) copy-start(bf16[384,256]{1,0:T(8,128)(2,1)} %copy-done.26) | copy-start | bytes 589828
  142.4 15.5 %copy-start.14 = (bf16[384,256]{1,0:T(8,128)(2,1)S(1)}, bf16[384,256]{1,0:T(8,128)(2,1)}, u32[]{:S(2)}) copy-start(bf16[384,256]{1,0:T(8,128)(2,1)} %copy-done.13) | copy-start | bytes 589828
  142.4 13.0 %collective-permute-start.10 = (bf16[384,256]{1,0:T(8,128)(2,1)S(1)}, bf16[384,256]{1,0:T(8,128)(2,1)S(1)}, u32[]{:S(2)}, u32[]{:S(2)}) collective-permute-start(bf16[384,256]{1,0:T(8,128)(2,1)S(1)} %fusion.19), channel_id=1, source_target_pairs={{0,128},{16,144},{32,160},{48,176},{64,192},{80,208},{96,224},{112... | collective-permute-start | bytes 589832 | tf_op jit(solution)/shard_map/ppermute | solution.py:17
  155.7 12.1 %collective-permute-start.12 = (bf16[2,384,256]{2,1,0:T(8,128)(2,1)S(1)}, bf16[2,384,256]{2,1,0:T(8,128)(2,1)S(1)}, u32[]{:S(2)}, u32[]{:S(2)}) collective-permute-start(bf16[2,384,256]{2,1,0:T(8,128)(2,1)S(1)} %convolution_convert_fusion.2), channel_id=1, source_target_pairs={{0,64},{16,80},{32,96},{48,112},{64,0},{80,16},{96,32},{112,48},{1... | collective-permute-start | bytes 1179656 | tf_op jit(solution)/shard_map/ppermute | solution.py:17
  158.7 10.4 %copy-start.25 = (bf16[384,256]{1,0:T(8,128)(2,1)S(1)}, bf16[384,256]{1,0:T(8,128)(2,1)}, u32[]{:S(2)}) copy-start(bf16[384,256]{1,0:T(8,128)(2,1)} %copy-done.24) | copy-start | bytes 589828
  158.8 19.6 %collective-permute-start.11 = (bf16[8,3,2,2,16,256]{5,4,3,2,1,0:T(8,128)(2,1)S(1)}, bf16[8,3,2,2,16,256]{5,4,3,2,1,0:T(8,128)(2,1)S(1)}, u32[]{:S(2)}, u32[]{:S(2)}) collective-permute-start(bf16[8,3,2,2,16,256]{5,4,3,2,1,0:T(8,128)(2,1)S(1)} %select_bitcast_fusion.1), channel_id=1, source_target_pairs={{0,1},{1,0},{2,3},{3,2},{4,5},{5,4},{6,7},{7,6},{8,9},{9,8},{10,11... | collective-permute-start | bytes 2359304 | tf_op jit(solution)/shard_map/ppermute | solution.py:182
  168.1 10.2 %copy-start.33 = (bf16[2,384,256]{2,1,0:T(8,128)(2,1)}, bf16[2,384,256]{2,1,0:T(8,128)(2,1)S(1)}, u32[]{:S(2)}) copy-start(bf16[2,384,256]{2,1,0:T(8,128)(2,1)S(1)} %fusion.5) | copy-start | bytes 1179652
  169.4 14.6 %collective-permute-start.13 = (bf16[2,384,256]{2,1,0:T(8,128)(2,1)}, bf16[2,384,256]{2,1,0:T(8,128)(2,1)}, u32[]{:S(2)}, u32[]{:S(2)}) collective-permute-start(bf16[2,384,256]{2,1,0:T(8,128)(2,1)} %convolution_convert_fusion.1), channel_id=1, source_target_pairs={{0,32},{16,48},{32,0},{48,16},{64,96},{80,112},{96,64},{112,80},{1... | collective-permute-start | bytes 1179656 | tf_op jit(solution)/shard_map/ppermute | solution.py:17
  179.6 5.9 %copy-start.22 = (bf16[2,384,256]{2,1,0:T(8,128)(2,1)S(1)}, bf16[2,384,256]{2,1,0:T(8,128)(2,1)}, u32[]{:S(2)}) copy-start(bf16[2,384,256]{2,1,0:T(8,128)(2,1)} %copy-done.21) | copy-start | bytes 1179652
  179.6 35.7 %all-to-all-start.1 = ((bf16[8,3,2,2,16,256]{5,4,3,2,1,0:T(8,128)(2,1)}), bf16[8,3,2,2,16,256]{5,4,3,2,1,0:T(8,128)(2,1)S(1)}, u32[]{:S(2)}, u32[]{:S(2)}) async-start(bf16[8,3,2,2,16,256]{5,4,3,2,1,0:T(8,128)(2,1)} %fusion.3), calls=%async_computation.1 | async-start | bytes 1572864 | tf_op jit(solution)/shard_map/all_to_all | solution.py:189
  186.3 10.1 %collective-permute-start.14 = (bf16[2,384,256]{2,1,0:T(8,128)(2,1)S(1)}, bf16[2,384,256]{2,1,0:T(8,128)(2,1)S(1)}, u32[]{:S(2)}, u32[]{:S(2)}) collective-permute-start(bf16[2,384,256]{2,1,0:T(8,128)(2,1)S(1)} %convolution_convert_fusion), channel_id=1, source_target_pairs={{0,16},{16,0},{32,48},{48,32},{64,80},{80,64},{96,112},{112,96},{1... | collective-permute-start | bytes 1179656 | tf_op jit(solution)/shard_map/ppermute | solution.py:17
  189.0 8.1 %copy-start.18 = (bf16[1,384,256]{2,1,0:T(8,128)(2,1)S(1)}, bf16[1,384,256]{2,1,0:T(8,128)(2,1)}, u32[]{:S(2)}) copy-start(bf16[1,384,256]{2,1,0:T(8,128)(2,1)} %copy-done.17) | copy-start | bytes 589828
  189.0 8.1 %copy-start.20 = (bf16[1,384,256]{2,1,0:T(8,128)(2,1)S(1)}, bf16[1,384,256]{2,1,0:T(8,128)(2,1)}, u32[]{:S(2)}) copy-start(bf16[1,384,256]{2,1,0:T(8,128)(2,1)} %copy-done.19) | copy-start | bytes 589828
  189.3 8.2 %copy-start.36 = (bf16[256,256]{1,0:T(8,128)(2,1)S(1)}, bf16[256,256]{1,0:T(8,128)(2,1)}, u32[]{:S(2)}) copy-start(bf16[256,256]{1,0:T(8,128)(2,1)} %convolution_convert_fusion.5) | copy-start | bytes 393220
  189.3 8.2 %copy-start.37 = (bf16[256,256]{1,0:T(8,128)(2,1)S(1)}, bf16[256,256]{1,0:T(8,128)(2,1)}, u32[]{:S(2)}) copy-start(bf16[256,256]{1,0:T(8,128)(2,1)} %convolution_convert_fusion.6) | copy-start | bytes 393220
  198.9 16.4 %collective-permute-start.15 = (bf16[8,3,2,2,16,256]{5,4,3,2,1,0:T(8,128)(2,1)}, bf16[8,3,2,2,16,256]{5,4,3,2,1,0:T(8,128)(2,1)}, u32[]{:S(2)}, u32[]{:S(2)}) collective-permute-start(bf16[8,3,2,2,16,256]{5,4,3,2,1,0:T(8,128)(2,1)} %select_bitcast_fusion), channel_id=1, source_target_pairs={{0,1},{1,0},{2,3},{3,2},{4,5},{5,4},{6,7},{7,6},{8,9},{9,8},{10,11... | collective-permute-start | bytes 2359304 | tf_op jit(solution)/shard_map/ppermute | solution.py:182
  206.7 21.1 %collective-permute-start.16 = (bf16[384,256]{1,0:T(8,128)(2,1)}, bf16[384,256]{1,0:T(8,128)(2,1)S(1)}, u32[]{:S(2)}, u32[]{:S(2)}) collective-permute-start(bf16[384,256]{1,0:T(8,128)(2,1)} %fusion.47), channel_id=1, source_target_pairs={{0,256},{16,272},{32,288},{48,304},{64,320},{80,336},{96,352},{112... | collective-permute-start | bytes 589832 | tf_op jit(solution)/shard_map/ppermute | solution.py:17
  217.8 9.9 %copy-start.10 = (bf16[2,384,256]{2,1,0:T(8,128)(2,1)S(1)}, bf16[2,384,256]{2,1,0:T(8,128)(2,1)}, u32[]{:S(2)}) copy-start(bf16[2,384,256]{2,1,0:T(8,128)(2,1)} %copy-done.9) | copy-start | bytes 1179652
  218.5 30.1 %all-to-all-start.2 = ((bf16[8,3,2,2,16,256]{5,4,3,2,1,0:T(8,128)(2,1)}), bf16[8,3,2,2,16,256]{5,4,3,2,1,0:T(8,128)(2,1)S(1)}, u32[]{:S(2)}, u32[]{:S(2)}) async-start(bf16[8,3,2,2,16,256]{5,4,3,2,1,0:T(8,128)(2,1)} %fusion.22), calls=%async_computation.2 | async-start | bytes 1572864 | tf_op jit(solution)/shard_map/all_to_all | solution.py:189
  225.8 8.4 %collective-permute-start.18 = (bf16[2,16,256]{2,1,0:T(8,128)(2,1)S(1)}, bf16[2,16,256]{2,1,0:T(8,128)(2,1)S(1)}, u32[]{:S(2)}, u32[]{:S(2)}) collective-permute-start(bf16[2,16,256]{2,1,0:T(8,128)(2,1)S(1)} %get-tuple-element.34), channel_id=1, source_target_pairs={{0,256},{16,272},{32,288},{48,304},{64,320},{80,336},{96,352},{112... | collective-permute-start | bytes 49160 | tf_op jit(solution)/shard_map/ppermute | solution.py:17
  227.9 14.8 %collective-permute-start.17 = (bf16[384,256]{1,0:T(8,128)(2,1)S(1)}, bf16[384,256]{1,0:T(8,128)(2,1)S(1)}, u32[]{:S(2)}, u32[]{:S(2)}) collective-permute-start(bf16[384,256]{1,0:T(8,128)(2,1)S(1)} %select_select_fusion), channel_id=1, source_target_pairs={{0,128},{16,144},{32,160},{48,176},{64,192},{80,208},{96,224},{112... | collective-permute-start | bytes 589832 | tf_op jit(solution)/shard_map/ppermute | solution.py:17
  234.2 9.6 %collective-permute-start.19 = (bf16[2,2,16,256]{3,2,1,0:T(8,128)(2,1)S(1)}, bf16[2,2,16,256]{3,2,1,0:T(8,128)(2,1)S(1)}, u32[]{:S(2)}, u32[]{:S(2)}) collective-permute-start(bf16[2,2,16,256]{3,2,1,0:T(8,128)(2,1)S(1)} %get-tuple-element.31), channel_id=1, source_target_pairs={{0,128},{16,144},{32,160},{48,176},{64,192},{80,208},{96,224},{112... | collective-permute-start | bytes 98312 | tf_op jit(solution)/shard_map/ppermute | solution.py:17
  (14 other events, 25.0 us)
Sparse Core Ops, SparseCore 0:
  10.7 47.2 all-gather.1

commit v9 on v6

--- a/solution.py
+++ b/solution.py
@@ -248,6 +248,8 @@
         own_w, other_w = full[section][0], full[section][1]
         sent = (dot_back(grads[0], other_w[0]) + dot_back(grads[1], other_w[1])).astype(bf16)
         back = flip(sent, section - 1)
+        if section == 5:
+            grads = [after(grad, sent) for grad in grads]
         kept = (dot_back(grads[0], own_w[0]) + dot_back(grads[1], own_w[1])).astype(bf16)
         terms[section] = jnp.stack(
             [jnp.stack([dot_rows(part, grad) for grad in grads]) for part in inputs[section]]
@@ -269,7 +271,7 @@
     chip = after(chip_sum(jnp.stack(terms[:3])), parts_high)
     parts_low = all_parts(chip)
 
-    out_came = flip(after(results[1], sent), 4)
+    out_came = flip(results[1], 4)
     out_keep, out_send = jnp.where(same, results[0], out_came), jnp.where(same, out_came, results[0])
     out_came = flip(after(out_send, chip), 3)
     result = jnp.concatenate([jnp.where(low, out_came, out_keep), jnp.where(low, out_keep, out_came)], axis=1)

time: 245 us -> 241 us (0.984)
  waiting for transfers between devices: 66.7 us -> 62.6 us
  starting transfers between devices: 96.5 us -> 100 us
  other arithmetic: 13.4 us -> 10.9 us
    ppermute x16, starting transfers between devices: 76.8 us -> 81.2 us  [flip(): return lax.ppermute(value, 'blk', pairs)]
    ppermute x16, waiting for transfers between devices: 56.5 us -> 52.2 us  [flip(): return lax.ppermute(value, 'blk', pairs)]
    select_n x9 -> x8, other arithmetic: 5.94 us -> 4.13 us  [after(): return jnp.where(probe != probe, jnp.zeros_like(value), value)]
    unnamed x62 -> x60, local copies, waits for them, and re-layouts: 5.24 us -> 5.24 us
  transfers between devices with their start and end apart: 22 -> 22, of which waited for: 11 -> 12; matrix products, arithmetic and copies ran while one was open for 12% -> 11% of each run, Pallas kernels for 1% -> 1%
where the time goes in v9:
time: 241 us; the launch traced here: 240 us
  starting transfers between devices  100 us (41%)
  waiting for transfers between devices  62.6 us (26%)
  blocking collectives  20.2 us (8%)
  matrix products  19.9 us (8%)
  between operations  15 us (6%)
  other arithmetic  10.9 us (5%)
  Pallas kernels  5.98 us (2%)
  local copies, waits for them, and re-layouts  5.63 us (2%)
    ppermute x16, starting transfers between devices, flip(): return lax.ppermute(value, 'blk', pairs)  81.2 us
    ppermute x16, waiting for transfers between devices, flip(): return lax.ppermute(value, 'blk', pairs)  52.2 us
    all_gather x1, blocking collectives, body(): full = list(lax.all_gather(first, 'tok', axis=3, tiled=True))  20.2 us
    all_to_all x2, starting transfers between devices, all_parts(): return lax.all_to_all(chip, 'tok', 0, 0, axis_index_groups=groups)  10.6 us
    all_gather x1, waiting for transfers between devices, body(): full += list(lax.all_gather(late, 'tok', axis=3, tiled=True))  9.91 us
    ppermute x2, starting transfers between devices, chip_sum(): lax.ppermute(core_half(terms, 1 - core), 'tok', [(source, source ^ 1) for...  8.16 us
    dot_general x16, matrix products, dot_rows(): jnp.einsum('...tk,...tl->...kl', left, right, preferred_element_type=jnp....  7.36 us
    dot_general x18, matrix products, dot_back(): jnp.einsum('...tl,...kl->...tk', left, right, preferred_element_type=jnp....  6.42 us
  transfers between devices with their start and end apart: 22, of which 12 were waited for; matrix products, arithmetic and copies ran while one was open for 11% of the time, Pallas kernels for 1%

profile of v9, /device:TPU:1, one launch (start us, length us, event | category | flops | bytes accessed | tf_op | source)
XLA Modules:
  0.0 240.3 jit_solution(15410224564682252949)
XLA Ops:
  8.8 1.3 shard_map.67
  10.2 1.0 copy-done
  13.4 6.6 %collective-permute-start.2 = (bf16[448,256]{1,0:T(8,128)(2,1)S(1)}, bf16[448,256]{1,0:T(8,128)(2,1)S(1)}, u32[]{:S(2)}, u32[]{:S(2)}) collective-permute-start(bf16[448,256]{1,0:T(8,128)(2,1)S(1)} %get-tuple-element.14), channel_id=1, source_target_pairs={{0,128},{16,144},{32,160},{48,176},{64,192},{80,208},{96,224},{112... | collective-permute-start | bytes 688136 | tf_op jit(solution)/shard_map/ppermute | solution.py:17
  20.1 1.1 select_bitcast_fusion.3
  21.3 20.2 %all_gather.9 = bf16[1,2,2,256,256]{4,3,2,1,0:T(8,128)(2,1)S(1)} all-gather(bf16[1,2,2,16,256]{4,3,2,1,0:T(8,128)(2,1)S(1)} %get-tuple-element.11), channel_id=1, replica_groups=mesh['blk'=32,'tok'=16] {'tok'}, dimensions={3}, use_global_device_ids=true | all-gather | bytes 557056 | tf_op jit(solution)/shard_map/all_gather | solution.py:196
  42.4 10.2 %collective-permute-start.4 = (bf16[416,256]{1,0:T(8,128)(2,1)S(1)}, bf16[416,256]{1,0:T(8,128)(2,1)S(1)}, u32[]{:S(2)}, u32[]{:S(2)}) collective-permute-start(bf16[416,256]{1,0:T(8,128)(2,1)S(1)} %get-tuple-element.18), channel_id=1, source_target_pairs={{0,256},{16,272},{32,288},{48,304},{64,320},{80,336},{96,352},{112... | collective-permute-start | bytes 638984 | tf_op jit(solution)/shard_map/ppermute | solution.py:17
  52.9 3.1 %collective-permute-start = (bf16[2,384,256]{2,1,0:T(8,128)(2,1)S(1)}, bf16[2,384,256]{2,1,0:T(8,128)(2,1)}, u32[]{:S(2)}, u32[]{:S(2)}) collective-permute-start(bf16[2,384,256]{2,1,0:T(8,128)(2,1)S(1)} %fusion.4), channel_id=1, source_target_pairs={{0,16},{16,0},{32,48},{48,32},{64,80},{80,64},{96,112},{112,96},{1... | collective-permute-start | bytes 1179656 | tf_op jit(solution)/shard_map/ppermute | solution.py:17
  56.0 6.6 %collective-permute-done.4.came = bf16[416,256]{1,0:T(8,128)(2,1)S(1)} collective-permute-done((bf16[416,256]{1,0:T(8,128)(2,1)S(1)}, bf16[416,256]{1,0:T(8,128)(2,1)S(1)}, u32[]{:S(2)}, u32[]{:S(2)}) %collective-permute-start.4) | collective-permute-done | bytes 213024 | tf_op jit(solution)/shard_map/ppermute | solution.py:17
  62.6 1.3 shard_map.70
  63.9 1.1 fusion.26
  65.3 1.4 fusion.5
  66.8 4.2 %collective-permute-start.1 = (bf16[2,384,256]{2,1,0:T(8,128)(2,1)S(1)}, bf16[2,384,256]{2,1,0:T(8,128)(2,1)S(1)}, u32[]{:S(2)}, u32[]{:S(2)}) collective-permute-start(bf16[2,384,256]{2,1,0:T(8,128)(2,1)S(1)} %fusion.5), channel_id=1, source_target_pairs={{0,32},{16,48},{32,0},{48,16},{64,96},{80,112},{96,64},{112,80},{1... | collective-permute-start | bytes 1179656 | tf_op jit(solution)/shard_map/ppermute | solution.py:17
  71.3 8.4 %collective-permute-done.1 = bf16[2,384,256]{2,1,0:T(8,128)(2,1)S(1)} collective-permute-done((bf16[2,384,256]{2,1,0:T(8,128)(2,1)S(1)}, bf16[2,384,256]{2,1,0:T(8,128)(2,1)S(1)}, u32[]{:S(2)}, u32[]{:S(2)}) %collective-permute-start.1) | collective-permute-done | bytes 393248 | tf_op jit(solution)/shard_map/ppermute | solution.py:17
  80.1 2.4 %collective-permute-start.3 = (bf16[2,384,256]{2,1,0:T(8,128)(2,1)S(1)}, bf16[2,384,256]{2,1,0:T(8,128)(2,1)S(1)}, u32[]{:S(2)}, u32[]{:S(2)}) collective-permute-start(bf16[2,384,256]{2,1,0:T(8,128)(2,1)S(1)} %fusion.6), channel_id=1, source_target_pairs={{0,64},{16,80},{32,96},{48,112},{64,0},{80,16},{96,32},{112,48},{1... | collective-permute-start | bytes 1179656 | tf_op jit(solution)/shard_map/ppermute | solution.py:17
  83.1 7.8 %collective-permute-done.3 = bf16[2,384,256]{2,1,0:T(8,128)(2,1)S(1)} collective-permute-done((bf16[2,384,256]{2,1,0:T(8,128)(2,1)S(1)}, bf16[2,384,256]{2,1,0:T(8,128)(2,1)S(1)}, u32[]{:S(2)}, u32[]{:S(2)}) %collective-permute-start.3) | collective-permute-done | bytes 393248 | tf_op jit(solution)/shard_map/ppermute | solution.py:17
  91.0 1.9 collective-permute-start.5
  93.2 9.9 %all-gather.5.cloned.1.call-done = bf16[2,2,2,256,256]{4,3,2,1,0:T(8,128)(2,1)} async-done(((bf16[2,2,2,16,256]{4,3,2,1,0:T(8,128)(2,1)}), bf16[2,2,2,256,256]{4,3,2,1,0:T(8,128)(2,1)}) %all-gather.5.cloned.1.call-update) | async-done | bytes 1048592 | tf_op jit(solution)/shard_map/all_gather | solution.py:216
  103.1 1.2 fusion.23
  105.0 7.8 %collective-permute-start.6 = (bf16[384,256]{1,0:T(8,128)(2,1)S(1)}, bf16[384,256]{1,0:T(8,128)(2,1)S(1)}, u32[]{:S(2)}, u32[]{:S(2)}) collective-permute-start(bf16[384,256]{1,0:T(8,128)(2,1)S(1)} %fusion.13), channel_id=1, source_target_pairs={{0,256},{16,272},{32,288},{48,304},{64,320},{80,336},{96,352},{112... | collective-permute-start | bytes 589832 | tf_op jit(solution)/shard_map/ppermute | solution.py:17
  113.5 4.3 %collective-permute-done.6 = bf16[384,256]{1,0:T(8,128)(2,1)S(1)} collective-permute-done((bf16[384,256]{1,0:T(8,128)(2,1)S(1)}, bf16[384,256]{1,0:T(8,128)(2,1)S(1)}, u32[]{:S(2)}, u32[]{:S(2)}) %collective-permute-start.6) | collective-permute-done | bytes 196640 | tf_op jit(solution)/shard_map/ppermute | solution.py:17
  118.5 1.2 fusion.34
  120.7 7.1 %collective-permute-start.7 = (bf16[384,256]{1,0:T(8,128)(2,1)S(1)}, bf16[384,256]{1,0:T(8,128)(2,1)S(1)}, u32[]{:S(2)}, u32[]{:S(2)}) collective-permute-start(bf16[384,256]{1,0:T(8,128)(2,1)S(1)} %fusion.14), channel_id=1, source_target_pairs={{0,256},{16,272},{32,288},{48,304},{64,320},{80,336},{96,352},{112... | collective-permute-start | bytes 589832 | tf_op jit(solution)/shard_map/ppermute | solution.py:17
  129.6 1.4 collective-permute-done.7
  131.3 12.0 %collective-permute-start.8 = (bf16[384,256]{1,0:T(8,128)(2,1)S(1)}, bf16[384,256]{1,0:T(8,128)(2,1)S(1)}, u32[]{:S(2)}, u32[]{:S(2)}) collective-permute-start(bf16[384,256]{1,0:T(8,128)(2,1)S(1)} %fusion.17), channel_id=1, source_target_pairs={{0,128},{16,144},{32,160},{48,176},{64,192},{80,208},{96,224},{112... | collective-permute-start | bytes 589832 | tf_op jit(solution)/shard_map/ppermute | solution.py:17
  144.1 6.9 %collective-permute-done.8 = bf16[384,256]{1,0:T(8,128)(2,1)S(1)} collective-permute-done((bf16[384,256]{1,0:T(8,128)(2,1)S(1)}, bf16[384,256]{1,0:T(8,128)(2,1)S(1)}, u32[]{:S(2)}, u32[]{:S(2)}) %collective-permute-start.8) | collective-permute-done | bytes 196640 | tf_op jit(solution)/shard_map/ppermute | solution.py:17
  151.7 1.9 collective-permute-start.10
  154.6 3.2 %collective-permute-start.9 = (bf16[8,3,2,2,16,256]{5,4,3,2,1,0:T(8,128)(2,1)S(1)}, bf16[8,3,2,2,16,256]{5,4,3,2,1,0:T(8,128)(2,1)S(1)}, u32[]{:S(2)}, u32[]{:S(2)}) collective-permute-start(bf16[8,3,2,2,16,256]{5,4,3,2,1,0:T(8,128)(2,1)S(1)} %select_bitcast_fusion.1), channel_id=1, source_target_pairs={{0,1},{1,0},{2,3},{3,2},{4,5},{5,4},{6,7},{7,6},{8,9},{9,8},{10,11... | collective-permute-start | bytes 2359304 | tf_op jit(solution)/shard_map/ppermute | solution.py:171
  157.7 5.3 %collective-permute-done.10 = bf16[2,384,256]{2,1,0:T(8,128)(2,1)S(1)} collective-permute-done((bf16[2,384,256]{2,1,0:T(8,128)(2,1)S(1)}, bf16[2,384,256]{2,1,0:T(8,128)(2,1)S(1)}, u32[]{:S(2)}, u32[]{:S(2)}) %collective-permute-start.10) | collective-permute-done | bytes 393248 | tf_op jit(solution)/shard_map/ppermute | solution.py:17
  163.4 1.0 convolution_convert_fusion.1
  164.4 4.7 %collective-permute-start.11 = (bf16[2,384,256]{2,1,0:T(8,128)(2,1)}, bf16[2,384,256]{2,1,0:T(8,128)(2,1)}, u32[]{:S(2)}, u32[]{:S(2)}) collective-permute-start(bf16[2,384,256]{2,1,0:T(8,128)(2,1)} %convolution_convert_fusion.1), channel_id=1, source_target_pairs={{0,32},{16,48},{32,0},{48,16},{64,96},{80,112},{96,64},{112,80},{1... | collective-permute-start | bytes 1179656 | tf_op jit(solution)/shard_map/ppermute | solution.py:17
  169.1 1.0 convolution_convert_fusion.4
  170.2 1.1 convolution_convert_fusion.3
  171.2 1.2 fusion.3
  172.5 3.8 %all-to-all-start = ((bf16[8,3,2,2,16,256]{5,4,3,2,1,0:T(8,128)(2,1)}), bf16[8,3,2,2,16,256]{5,4,3,2,1,0:T(8,128)(2,1)S(1)}, u32[]{:S(2)}, u32[]{:S(2)}) async-start(bf16[8,3,2,2,16,256]{5,4,3,2,1,0:T(8,128)(2,1)} %fusion.3), calls=%async_computation | async-start | bytes 1572864 | tf_op jit(solution)/shard_map/all_to_all | solution.py:178
  177.0 1.3 fusion.8
  178.6 4.1 %collective-permute-start.12 = (bf16[2,384,256]{2,1,0:T(8,128)(2,1)S(1)}, bf16[2,384,256]{2,1,0:T(8,128)(2,1)S(1)}, u32[]{:S(2)}, u32[]{:S(2)}) collective-permute-start(bf16[2,384,256]{2,1,0:T(8,128)(2,1)S(1)} %convolution_convert_fusion), channel_id=1, source_target_pairs={{0,16},{16,0},{32,48},{48,32},{64,80},{80,64},{96,112},{112,96},{1... | collective-permute-start | bytes 1179656 | tf_op jit(solution)/shard_map/ppermute | solution.py:17
  183.1 1.4 convolution_convert_fusion.5
  184.5 5.0 %collective-permute-done.12 = bf16[2,384,256]{2,1,0:T(8,128)(2,1)S(1)} collective-permute-done((bf16[2,384,256]{2,1,0:T(8,128)(2,1)S(1)}, bf16[2,384,256]{2,1,0:T(8,128)(2,1)S(1)}, u32[]{:S(2)}, u32[]{:S(2)}) %collective-permute-start.12) | collective-permute-done | bytes 393248 | tf_op jit(solution)/shard_map/ppermute | solution.py:17
  190.9 1.0 select_bitcast_fusion
  191.9 5.0 %collective-permute-start.13 = (bf16[8,3,2,2,16,256]{5,4,3,2,1,0:T(8,128)(2,1)}, bf16[8,3,2,2,16,256]{5,4,3,2,1,0:T(8,128)(2,1)}, u32[]{:S(2)}, u32[]{:S(2)}) collective-permute-start(bf16[8,3,2,2,16,256]{5,4,3,2,1,0:T(8,128)(2,1)} %select_bitcast_fusion), channel_id=1, source_target_pairs={{0,1},{1,0},{2,3},{3,2},{4,5},{5,4},{6,7},{7,6},{8,9},{9,8},{10,11... | collective-permute-start | bytes 2359304 | tf_op jit(solution)/shard_map/ppermute | solution.py:171
  196.9 1.9 collective-permute-start.14
  199.1 1.5 fusion.21
  201.6 6.8 %all-to-all-start.1 = ((bf16[8,3,2,2,16,256]{5,4,3,2,1,0:T(8,128)(2,1)}), bf16[8,3,2,2,16,256]{5,4,3,2,1,0:T(8,128)(2,1)S(1)}, u32[]{:S(2)}, u32[]{:S(2)}) async-start(bf16[8,3,2,2,16,256]{5,4,3,2,1,0:T(8,128)(2,1)} %copy-done.13), calls=%async_computation.1 | async-start | bytes 1572864 | tf_op jit(solution)/shard_map/all_to_all | solution.py:178
  209.1 7.0 %collective-permute-start.16 = (bf16[2,16,256]{2,1,0:T(8,128)(2,1)S(1)}, bf16[2,16,256]{2,1,0:T(8,128)(2,1)S(1)}, u32[]{:S(2)}, u32[]{:S(2)}) collective-permute-start(bf16[2,16,256]{2,1,0:T(8,128)(2,1)S(1)} %get-tuple-element.34), channel_id=1, source_target_pairs={{0,256},{16,272},{32,288},{48,304},{64,320},{80,336},{96,352},{112... | collective-permute-start | bytes 49160 | tf_op jit(solution)/shard_map/ppermute | solution.py:17
  216.3 1.9 collective-permute-start.15
  220.0 4.3 %collective-permute-start.17 = (bf16[2,2,16,256]{3,2,1,0:T(8,128)(2,1)S(1)}, bf16[2,2,16,256]{3,2,1,0:T(8,128)(2,1)S(1)}, u32[]{:S(2)}, u32[]{:S(2)}) collective-permute-start(bf16[2,2,16,256]{3,2,1,0:T(8,128)(2,1)S(1)} %get-tuple-element.31), channel_id=1, source_target_pairs={{0,128},{16,144},{32,160},{48,176},{64,192},{80,208},{96,224},{112... | collective-permute-start | bytes 98312 | tf_op jit(solution)/shard_map/ppermute | solution.py:17
  224.3 6.5 %collective-permute-done.15 = bf16[384,256]{1,0:T(8,128)(2,1)S(1)} collective-permute-done((bf16[384,256]{1,0:T(8,128)(2,1)S(1)}, bf16[384,256]{1,0:T(8,128)(2,1)S(1)}, u32[]{:S(2)}, u32[]{:S(2)}) %collective-permute-start.15) | collective-permute-done | bytes 196640 | tf_op jit(solution)/shard_map/ppermute | solution.py:17
  231.9 1.5 shard_map.72
  (150 shorter events, 22.5 us)
Async XLA Ops:
  7.2 56.8 %all-gather.3.cloned.1.call-start = ((), (), s32[]{:S(2)}) async-start(), calls=%async_computation.2 | async-start | bytes 1671168 | tf_op jit(solution)/shard_map/all_gather | solution.py:197
  7.2 0.9 copy-start.2
  10.1 93.0 %all-gather.5.cloned.1.call-start = ((), (), s32[]{:S(2)}) async-start(), calls=%async_computation.3 | async-start | bytes 1114112 | tf_op jit(solution)/shard_map/all_gather | solution.py:216
  10.2 1.0 copy-start
  11.2 0.9 copy-start.3
  13.4 28.3 %collective-permute-start.2 = (bf16[448,256]{1,0:T(8,128)(2,1)S(1)}, bf16[448,256]{1,0:T(8,128)(2,1)S(1)}, u32[]{:S(2)}, u32[]{:S(2)}) collective-permute-start(bf16[448,256]{1,0:T(8,128)(2,1)S(1)} %get-tuple-element.14), channel_id=1, source_target_pairs={{0,128},{16,144},{32,160},{48,176},{64,192},{80,208},{96,224},{112... | collective-permute-start | bytes 688136 | tf_op jit(solution)/shard_map/ppermute | solution.py:17
  21.2 20.6 %copy-start.1 = (bf16[384,512]{1,0:T(8,128)(2,1)S(1)}, bf16[384,512]{1,0:T(8,128)(2,1)}, u32[]{:S(2)}) copy-start(bf16[384,512]{1,0:T(8,128)(2,1)} %cotangent.3) | copy-start | bytes 1179652
  21.2 20.5 %copy-start.6 = (s32[6,64]{1,0:T(8,128)S(1)}, s32[6,64]{1,0:T(8,128)}, u32[]{:S(2)}) copy-start(s32[6,64]{1,0:T(8,128)} %matchings.11) | copy-start | bytes 4612
  21.3 31.6 %copy-start.9 = (bf16[2,384,256]{2,1,0:T(8,128)(2,1)}, bf16[2,384,256]{2,1,0:T(8,128)(2,1)S(1)}, u32[]{:S(2)}) copy-start(bf16[2,384,256]{2,1,0:T(8,128)(2,1)S(1)} %rev.3) | copy-start | bytes 1179652
  42.4 20.2 %collective-permute-start.4 = (bf16[416,256]{1,0:T(8,128)(2,1)S(1)}, bf16[416,256]{1,0:T(8,128)(2,1)S(1)}, u32[]{:S(2)}, u32[]{:S(2)}) collective-permute-start(bf16[416,256]{1,0:T(8,128)(2,1)S(1)} %get-tuple-element.18), channel_id=1, source_target_pairs={{0,256},{16,272},{32,288},{48,304},{64,320},{80,336},{96,352},{112... | collective-permute-start | bytes 638984 | tf_op jit(solution)/shard_map/ppermute | solution.py:17
  52.9 13.8 %copy-start.16 = (bf16[2,384,256]{2,1,0:T(8,128)(2,1)}, bf16[2,384,256]{2,1,0:T(8,128)(2,1)S(1)}, u32[]{:S(2)}) copy-start(bf16[2,384,256]{2,1,0:T(8,128)(2,1)S(1)} %fusion.4) | copy-start | bytes 1179652
  52.9 12.4 %collective-permute-start = (bf16[2,384,256]{2,1,0:T(8,128)(2,1)S(1)}, bf16[2,384,256]{2,1,0:T(8,128)(2,1)}, u32[]{:S(2)}, u32[]{:S(2)}) collective-permute-start(bf16[2,384,256]{2,1,0:T(8,128)(2,1)S(1)} %fusion.4), channel_id=1, source_target_pairs={{0,16},{16,0},{32,48},{48,32},{64,80},{80,64},{96,112},{112,96},{1... | collective-permute-start | bytes 1179656 | tf_op jit(solution)/shard_map/ppermute | solution.py:17
  65.0 6.0 %copy-start.22 = (bf16[3,2,2,256,256]{4,3,2,1,0:T(8,128)(2,1)S(1)}, bf16[3,2,2,256,256]{4,3,2,1,0:T(8,128)(2,1)}, u32[]{:S(2)}) copy-start(bf16[3,2,2,256,256]{4,3,2,1,0:T(8,128)(2,1)} %all-gather.3.cloned.1.call-done) | copy-start | bytes 4718596
  66.7 13.3 %copy-start.11 = (bf16[2,384,256]{2,1,0:T(8,128)(2,1)}, bf16[2,384,256]{2,1,0:T(8,128)(2,1)S(1)}, u32[]{:S(2)}) copy-start(bf16[2,384,256]{2,1,0:T(8,128)(2,1)S(1)} %fusion.5) | copy-start | bytes 1179652
  66.8 13.0 %collective-permute-start.1 = (bf16[2,384,256]{2,1,0:T(8,128)(2,1)S(1)}, bf16[2,384,256]{2,1,0:T(8,128)(2,1)S(1)}, u32[]{:S(2)}, u32[]{:S(2)}) collective-permute-start(bf16[2,384,256]{2,1,0:T(8,128)(2,1)S(1)} %fusion.5), channel_id=1, source_target_pairs={{0,32},{16,48},{32,0},{48,16},{64,96},{80,112},{96,64},{112,80},{1... | collective-permute-start | bytes 1179656 | tf_op jit(solution)/shard_map/ppermute | solution.py:17
  71.1 9.0 %copy-start.7 = (bf16[2,2,256,256]{3,2,1,0:T(8,128)(2,1)}, bf16[2,2,256,256]{3,2,1,0:T(8,128)(2,1)S(1)}, u32[]{:S(2)}) copy-start(bf16[2,2,256,256]{3,2,1,0:T(8,128)(2,1)S(1)} %fusion.25) | copy-start | bytes 1572868
  79.8 3.0 %copy-start.18 = (bf16[2,384,256]{2,1,0:T(8,128)(2,1)}, bf16[2,384,256]{2,1,0:T(8,128)(2,1)S(1)}, u32[]{:S(2)}) copy-start(bf16[2,384,256]{2,1,0:T(8,128)(2,1)S(1)} %collective-permute-done.1) | copy-start | bytes 1179652
  80.1 10.9 %copy-start.20 = (bf16[2,384,256]{2,1,0:T(8,128)(2,1)}, bf16[2,384,256]{2,1,0:T(8,128)(2,1)S(1)}, u32[]{:S(2)}) copy-start(bf16[2,384,256]{2,1,0:T(8,128)(2,1)S(1)} %fusion.6) | copy-start | bytes 1179652
  80.1 10.7 %collective-permute-start.3 = (bf16[2,384,256]{2,1,0:T(8,128)(2,1)S(1)}, bf16[2,384,256]{2,1,0:T(8,128)(2,1)S(1)}, u32[]{:S(2)}, u32[]{:S(2)}) collective-permute-start(bf16[2,384,256]{2,1,0:T(8,128)(2,1)S(1)} %fusion.6), channel_id=1, source_target_pairs={{0,64},{16,80},{32,96},{48,112},{64,0},{80,16},{96,32},{112,48},{1... | collective-permute-start | bytes 1179656 | tf_op jit(solution)/shard_map/ppermute | solution.py:17
  82.6 68.7 %copy-start.14 = (bf16[2,2,256,256]{3,2,1,0:T(8,128)(2,1)}, bf16[2,2,256,256]{3,2,1,0:T(8,128)(2,1)S(1)}, u32[]{:S(2)}) copy-start(bf16[2,2,256,256]{3,2,1,0:T(8,128)(2,1)S(1)} %fusion.24) | copy-start | bytes 1572868
  90.8 2.2 copy-start.28
  91.0 13.7 %collective-permute-start.5 = (bf16[384,256]{1,0:T(8,128)(2,1)S(1)}, bf16[384,256]{1,0:T(8,128)(2,1)S(1)}, u32[]{:S(2)}, u32[]{:S(2)}) collective-permute-start(bf16[384,256]{1,0:T(8,128)(2,1)S(1)} %fusion.11), channel_id=1, source_target_pairs={{0,128},{16,144},{32,160},{48,176},{64,192},{80,208},{96,224},{112... | collective-permute-start | bytes 589832 | tf_op jit(solution)/shard_map/ppermute | solution.py:17
  103.1 9.6 %copy-start.27 = (bf16[2,2,2,256,256]{4,3,2,1,0:T(8,128)(2,1)S(1)}, bf16[2,2,2,256,256]{4,3,2,1,0:T(8,128)(2,1)}, u32[]{:S(2)}) copy-start(bf16[2,2,2,256,256]{4,3,2,1,0:T(8,128)(2,1)} %all-gather.5.cloned.1.call-done) | copy-start | bytes 3145732
  105.0 12.8 %collective-permute-start.6 = (bf16[384,256]{1,0:T(8,128)(2,1)S(1)}, bf16[384,256]{1,0:T(8,128)(2,1)S(1)}, u32[]{:S(2)}, u32[]{:S(2)}) collective-permute-start(bf16[384,256]{1,0:T(8,128)(2,1)S(1)} %fusion.13), channel_id=1, source_target_pairs={{0,256},{16,272},{32,288},{48,304},{64,320},{80,336},{96,352},{112... | collective-permute-start | bytes 589832 | tf_op jit(solution)/shard_map/ppermute | solution.py:17
  120.7 10.3 %collective-permute-start.7 = (bf16[384,256]{1,0:T(8,128)(2,1)S(1)}, bf16[384,256]{1,0:T(8,128)(2,1)S(1)}, u32[]{:S(2)}, u32[]{:S(2)}) collective-permute-start(bf16[384,256]{1,0:T(8,128)(2,1)S(1)} %fusion.14), channel_id=1, source_target_pairs={{0,256},{16,272},{32,288},{48,304},{64,320},{80,336},{96,352},{112... | collective-permute-start | bytes 589832 | tf_op jit(solution)/shard_map/ppermute | solution.py:17
  129.6 21.4 %copy-start.21 = (bf16[2,384,256]{2,1,0:T(8,128)(2,1)S(1)}, bf16[2,384,256]{2,1,0:T(8,128)(2,1)}, u32[]{:S(2)}) copy-start(bf16[2,384,256]{2,1,0:T(8,128)(2,1)} %copy-done.20) | copy-start | bytes 1179652
  131.3 19.7 %collective-permute-start.8 = (bf16[384,256]{1,0:T(8,128)(2,1)S(1)}, bf16[384,256]{1,0:T(8,128)(2,1)S(1)}, u32[]{:S(2)}, u32[]{:S(2)}) collective-permute-start(bf16[384,256]{1,0:T(8,128)(2,1)S(1)} %fusion.17), channel_id=1, source_target_pairs={{0,128},{16,144},{32,160},{48,176},{64,192},{80,208},{96,224},{112... | collective-permute-start | bytes 589832 | tf_op jit(solution)/shard_map/ppermute | solution.py:17
  143.8 9.8 %copy-start.29 = (bf16[2,384,256]{2,1,0:T(8,128)(2,1)S(1)}, bf16[2,384,256]{2,1,0:T(8,128)(2,1)}, u32[]{:S(2)}) copy-start(bf16[2,384,256]{2,1,0:T(8,128)(2,1)} %copy-done.28) | copy-start | bytes 1179652
  151.7 11.4 %collective-permute-start.10 = (bf16[2,384,256]{2,1,0:T(8,128)(2,1)S(1)}, bf16[2,384,256]{2,1,0:T(8,128)(2,1)S(1)}, u32[]{:S(2)}, u32[]{:S(2)}) collective-permute-start(bf16[2,384,256]{2,1,0:T(8,128)(2,1)S(1)} %convolution_convert_fusion.2), channel_id=1, source_target_pairs={{0,64},{16,80},{32,96},{48,112},{64,0},{80,16},{96,32},{112,48},{1... | collective-permute-start | bytes 1179656 | tf_op jit(solution)/shard_map/ppermute | solution.py:17
  154.4 8.6 %copy-start.15 = (bf16[2,2,256,256]{3,2,1,0:T(8,128)(2,1)S(1)}, bf16[2,2,256,256]{3,2,1,0:T(8,128)(2,1)}, u32[]{:S(2)}) copy-start(bf16[2,2,256,256]{3,2,1,0:T(8,128)(2,1)} %copy-done.14) | copy-start | bytes 1572868
  154.4 8.9 %copy-start.8 = (bf16[2,2,256,256]{3,2,1,0:T(8,128)(2,1)S(1)}, bf16[2,2,256,256]{3,2,1,0:T(8,128)(2,1)}, u32[]{:S(2)}) copy-start(bf16[2,2,256,256]{3,2,1,0:T(8,128)(2,1)} %copy-done.7) | copy-start | bytes 1572868
  154.5 14.6 %copy-start.12 = (bf16[2,384,256]{2,1,0:T(8,128)(2,1)S(1)}, bf16[2,384,256]{2,1,0:T(8,128)(2,1)}, u32[]{:S(2)}) copy-start(bf16[2,384,256]{2,1,0:T(8,128)(2,1)} %copy-done.11) | copy-start | bytes 1179652
  154.5 15.6 %copy-start.19 = (bf16[2,384,256]{2,1,0:T(8,128)(2,1)S(1)}, bf16[2,384,256]{2,1,0:T(8,128)(2,1)}, u32[]{:S(2)}) copy-start(bf16[2,384,256]{2,1,0:T(8,128)(2,1)} %copy-done.18) | copy-start | bytes 1179652
  154.6 16.7 %collective-permute-start.9 = (bf16[8,3,2,2,16,256]{5,4,3,2,1,0:T(8,128)(2,1)S(1)}, bf16[8,3,2,2,16,256]{5,4,3,2,1,0:T(8,128)(2,1)S(1)}, u32[]{:S(2)}, u32[]{:S(2)}) collective-permute-start(bf16[8,3,2,2,16,256]{5,4,3,2,1,0:T(8,128)(2,1)S(1)} %select_bitcast_fusion.1), channel_id=1, source_target_pairs={{0,1},{1,0},{2,3},{3,2},{4,5},{5,4},{6,7},{7,6},{8,9},{9,8},{10,11... | collective-permute-start | bytes 2359304 | tf_op jit(solution)/shard_map/ppermute | solution.py:171
  164.4 12.6 %collective-permute-start.11 = (bf16[2,384,256]{2,1,0:T(8,128)(2,1)}, bf16[2,384,256]{2,1,0:T(8,128)(2,1)}, u32[]{:S(2)}, u32[]{:S(2)}) collective-permute-start(bf16[2,384,256]{2,1,0:T(8,128)(2,1)} %convolution_convert_fusion.1), channel_id=1, source_target_pairs={{0,32},{16,48},{32,0},{48,16},{64,96},{80,112},{96,64},{112,80},{1... | collective-permute-start | bytes 1179656 | tf_op jit(solution)/shard_map/ppermute | solution.py:17
  172.5 26.3 %all-to-all-start = ((bf16[8,3,2,2,16,256]{5,4,3,2,1,0:T(8,128)(2,1)}), bf16[8,3,2,2,16,256]{5,4,3,2,1,0:T(8,128)(2,1)S(1)}, u32[]{:S(2)}, u32[]{:S(2)}) async-start(bf16[8,3,2,2,16,256]{5,4,3,2,1,0:T(8,128)(2,1)} %fusion.3), calls=%async_computation | async-start | bytes 1572864 | tf_op jit(solution)/shard_map/all_to_all | solution.py:178
  176.3 6.4 %copy-start.17 = (bf16[2,384,256]{2,1,0:T(8,128)(2,1)S(1)}, bf16[2,384,256]{2,1,0:T(8,128)(2,1)}, u32[]{:S(2)}) copy-start(bf16[2,384,256]{2,1,0:T(8,128)(2,1)} %copy-done.16) | copy-start | bytes 1179652
  178.6 10.8 %collective-permute-start.12 = (bf16[2,384,256]{2,1,0:T(8,128)(2,1)S(1)}, bf16[2,384,256]{2,1,0:T(8,128)(2,1)S(1)}, u32[]{:S(2)}, u32[]{:S(2)}) collective-permute-start(bf16[2,384,256]{2,1,0:T(8,128)(2,1)S(1)} %convolution_convert_fusion), channel_id=1, source_target_pairs={{0,16},{16,0},{32,48},{48,32},{64,80},{80,64},{96,112},{112,96},{1... | collective-permute-start | bytes 1179656 | tf_op jit(solution)/shard_map/ppermute | solution.py:17
  183.1 6.7 %copy-start.10 = (bf16[2,384,256]{2,1,0:T(8,128)(2,1)S(1)}, bf16[2,384,256]{2,1,0:T(8,128)(2,1)}, u32[]{:S(2)}) copy-start(bf16[2,384,256]{2,1,0:T(8,128)(2,1)} %copy-done.9) | copy-start | bytes 1179652
  184.5 6.1 %copy-start.25 = (bf16[2,256,256]{2,1,0:T(8,128)(2,1)S(1)}, bf16[2,256,256]{2,1,0:T(8,128)(2,1)}, u32[]{:S(2)}) copy-start(bf16[2,256,256]{2,1,0:T(8,128)(2,1)} %convolution_convert_fusion.4) | copy-start | bytes 786436
  184.5 6.1 %copy-start.26 = (bf16[2,256,256]{2,1,0:T(8,128)(2,1)S(1)}, bf16[2,256,256]{2,1,0:T(8,128)(2,1)}, u32[]{:S(2)}) copy-start(bf16[2,256,256]{2,1,0:T(8,128)(2,1)} %convolution_convert_fusion.3) | copy-start | bytes 786436
  191.9 7.2 %collective-permute-start.13 = (bf16[8,3,2,2,16,256]{5,4,3,2,1,0:T(8,128)(2,1)}, bf16[8,3,2,2,16,256]{5,4,3,2,1,0:T(8,128)(2,1)}, u32[]{:S(2)}, u32[]{:S(2)}) collective-permute-start(bf16[8,3,2,2,16,256]{5,4,3,2,1,0:T(8,128)(2,1)} %select_bitcast_fusion), channel_id=1, source_target_pairs={{0,1},{1,0},{2,3},{3,2},{4,5},{5,4},{6,7},{7,6},{8,9},{9,8},{10,11... | collective-permute-start | bytes 2359304 | tf_op jit(solution)/shard_map/ppermute | solution.py:171
  196.9 19.3 %collective-permute-start.14 = (bf16[384,256]{1,0:T(8,128)(2,1)}, bf16[384,256]{1,0:T(8,128)(2,1)S(1)}, u32[]{:S(2)}, u32[]{:S(2)}) collective-permute-start(bf16[384,256]{1,0:T(8,128)(2,1)} %get-tuple-element.28), channel_id=1, source_target_pairs={{0,256},{16,272},{32,288},{48,304},{64,320},{80,336},{96,352},{112... | collective-permute-start | bytes 589832 | tf_op jit(solution)/shard_map/ppermute | solution.py:17
  201.6 14.5 %copy-start.24 = (bf16[2,384,256]{2,1,0:T(8,128)(2,1)S(1)}, bf16[2,384,256]{2,1,0:T(8,128)(2,1)}, u32[]{:S(2)}) copy-start(bf16[2,384,256]{2,1,0:T(8,128)(2,1)} %copy-done.23) | copy-start | bytes 1179652
  201.6 30.4 %all-to-all-start.1 = ((bf16[8,3,2,2,16,256]{5,4,3,2,1,0:T(8,128)(2,1)}), bf16[8,3,2,2,16,256]{5,4,3,2,1,0:T(8,128)(2,1)S(1)}, u32[]{:S(2)}, u32[]{:S(2)}) async-start(bf16[8,3,2,2,16,256]{5,4,3,2,1,0:T(8,128)(2,1)} %copy-done.13), calls=%async_computation.1 | async-start | bytes 1572864 | tf_op jit(solution)/shard_map/all_to_all | solution.py:178
  209.1 11.0 %collective-permute-start.16 = (bf16[2,16,256]{2,1,0:T(8,128)(2,1)S(1)}, bf16[2,16,256]{2,1,0:T(8,128)(2,1)S(1)}, u32[]{:S(2)}, u32[]{:S(2)}) collective-permute-start(bf16[2,16,256]{2,1,0:T(8,128)(2,1)S(1)} %get-tuple-element.34), channel_id=1, source_target_pairs={{0,256},{16,272},{32,288},{48,304},{64,320},{80,336},{96,352},{112... | collective-permute-start | bytes 49160 | tf_op jit(solution)/shard_map/ppermute | solution.py:17
  216.3 14.5 %collective-permute-start.15 = (bf16[384,256]{1,0:T(8,128)(2,1)S(1)}, bf16[384,256]{1,0:T(8,128)(2,1)S(1)}, u32[]{:S(2)}, u32[]{:S(2)}) collective-permute-start(bf16[384,256]{1,0:T(8,128)(2,1)S(1)} %select_select_fusion), channel_id=1, source_target_pairs={{0,128},{16,144},{32,160},{48,176},{64,192},{80,208},{96,224},{112... | collective-permute-start | bytes 589832 | tf_op jit(solution)/shard_map/ppermute | solution.py:17
  220.0 11.7 %collective-permute-start.17 = (bf16[2,2,16,256]{3,2,1,0:T(8,128)(2,1)S(1)}, bf16[2,2,16,256]{3,2,1,0:T(8,128)(2,1)S(1)}, u32[]{:S(2)}, u32[]{:S(2)}) collective-permute-start(bf16[2,2,16,256]{3,2,1,0:T(8,128)(2,1)S(1)} %get-tuple-element.31), channel_id=1, source_target_pairs={{0,128},{16,144},{32,160},{48,176},{64,192},{80,208},{96,224},{112... | collective-permute-start | bytes 98312 | tf_op jit(solution)/shard_map/ppermute | solution.py:17
  (4 other events, 3.0 us)
Sparse Core Ops, SparseCore 0:
  10.7 47.2 all-gather.2
  64.0 39.0 all-gather.4

commit v10 on v9

--- a/solution.py
+++ b/solution.py
@@ -54,25 +54,26 @@
     return (matchings[section, block] != block).astype(jnp.int32) ^ turn
 
 
-def order_early(matchings, weights, first, rest):
+def order_early(matchings, weights, first, rest, keep, send):
     _, low, _ = bits()
+    depth = weights.shape[-2]
     for section in range(4):
         for row in range(2):
             at = choice(matchings, section, row)
             out = first.at[0] if section == 0 else rest.at[section - 1]
             out[0, row] = weights[section, row ^ low, at]
             out[1, row] = weights[section, row ^ low, 1 - at]
-
-
-def pack_late(matchings, weights, cotangent, keep, packed):
-    _, low, _ = bits()
-    width = weights.shape[-1]
-    depth = weights.shape[-2]
     for place in range(2):
         for both in range(2):
             keep[place, both] = weights[4 + place, low, both]
-            packed[pl.ds((2 * place + both) * depth, depth)] = weights[4 + place, 1 - low, both]
-    packed[4 * depth :] = jnp.where(low == 1, cotangent[:, :width], cotangent[:, width:])
+            send[pl.ds((2 * place + both) * depth, depth)] = weights[4 + place, 1 - low, both]
+
+
+def pack_late(send, cotangent, packed):
+    _, low, _ = bits()
+    rows, width = send.shape
+    packed[:rows] = send[...]
+    packed[rows:] = jnp.where(low == 1, cotangent[:, :width], cotangent[:, width:])
 
 
 def between(matchings, keep, came, cotangent, fourth, fifth, packed, cotan):
@@ -144,15 +145,16 @@
 
 def local(kernel, matchings, *arrays, outs):
     whole = pl.BlockSpec(memory_space=pltpu.VMEM)
+    scalars = () if matchings is None else (matchings,)
     moved = sum(math.prod(x.shape) * x.dtype.itemsize for x in (*arrays, *outs))
     result = pl.pallas_call(
         kernel,
         out_shape=outs,
-        in_specs=[pl.BlockSpec(memory_space=pltpu.SMEM)] + [whole] * len(arrays),
+        in_specs=[pl.BlockSpec(memory_space=pltpu.SMEM)] * len(scalars) + [whole] * len(arrays),
         out_specs=[whole] * len(outs),
         cost_estimate=pl.CostEstimate(flops=0, bytes_accessed=moved, transcendentals=0),
         compiler_params=pltpu.CompilerParams(vmem_limit_bytes=16 * 2**20),
-    )(matchings, *arrays)
+    )(*scalars, *arrays)
     return result[0] if len(outs) == 1 else result
 
 
@@ -188,10 +190,13 @@
     def shape(*dims, dtype=bf16):
         return jax.ShapeDtypeStruct((*dims, width), dtype)
 
-    first, rest = local(order_early, matchings, weights, outs=[shape(1, 2, 2, depth), shape(3, 2, 2, depth)])
-    keep, packed = local(
-        pack_late, matchings, weights, cotangent, outs=[shape(2, 2, depth), shape(4 * depth + tokens)]
+    first, rest, keep, send = local(
+        order_early,
+        matchings,
+        weights,
+        outs=[shape(1, 2, 2, depth), shape(3, 2, 2, depth), shape(2, 2, depth), shape(4 * depth)],
     )
+    packed = local(pack_late, None, send, cotangent, outs=[shape(4 * depth + tokens)])
     came = flip(packed, 3)
     full = list(lax.all_gather(first, "tok", axis=3, tiled=True))
     full += list(lax.all_gather(rest, "tok", axis=3, tiled=True))

time: 241 us -> 240 us (level)
  local copies, waits for them, and re-layouts: 5.63 us -> 3.06 us
  waiting for transfers between devices: 62.6 us -> 60.1 us
    ppermute x16, waiting for transfers between devices: 52.2 us -> 49.3 us  [flip(): return lax.ppermute(value, 'blk', pairs)]
    unnamed x60 -> x58, local copies, waits for them, and re-layouts: 5.24 us -> 2.73 us
  transfers between devices with their start and end apart: 22 -> 22, of which waited for: 12 -> 14; matrix products, arithmetic and copies ran while one was open for 11% -> 12% of each run, Pallas kernels for 1% -> 1%
where the time goes in v10:
time: 240 us; the launch traced here: 239 us
  starting transfers between devices  101 us (42%)
  waiting for transfers between devices  60.1 us (25%)
  matrix products  20.8 us (9%)
  blocking collectives  20.6 us (9%)
  between operations  15 us (6%)
  other arithmetic  12.5 us (5%)
  Pallas kernels  5.37 us (2%)
  local copies, waits for them, and re-layouts  3.06 us (1%)
    ppermute x16, starting transfers between devices, flip(): return lax.ppermute(value, 'blk', pairs)  82.2 us
    ppermute x16, waiting for transfers between devices, flip(): return lax.ppermute(value, 'blk', pairs)  49.3 us
    all_gather x1, blocking collectives, body(): full = list(lax.all_gather(first, 'tok', axis=3, tiled=True))  20.6 us
    all_to_all x2, starting transfers between devices, all_parts(): return lax.all_to_all(chip, 'tok', 0, 0, axis_index_groups=groups)  10.4 us
    all_gather x1, waiting for transfers between devices, body(): full += list(lax.all_gather(late, 'tok', axis=3, tiled=True))  9.43 us
    ppermute x2, starting transfers between devices, chip_sum(): lax.ppermute(core_half(terms, 1 - core), 'tok', [(source, source ^ 1) for...  8.59 us
    dot_general x18, matrix products, dot_back(): jnp.einsum('...tl,...kl->...tk', left, right, preferred_element_type=jnp....  7.43 us
    dot_general x16, matrix products, dot_rows(): jnp.einsum('...tk,...tl->...kl', left, right, preferred_element_type=jnp....  7.37 us
  transfers between devices with their start and end apart: 22, of which 14 were waited for; matrix products, arithmetic and copies ran while one was open for 12% of the time, Pallas kernels for 1%

profile of v10, /device:TPU:1, one launch (start us, length us, event | category | flops | bytes accessed | tf_op | source)
XLA Modules:
  0.0 238.7 jit_solution(11556281052996136510)
XLA Ops:
  8.8 1.3 shard_map.67
  11.2 6.6 %collective-permute-start.2 = (bf16[448,256]{1,0:T(8,128)(2,1)S(1)}, bf16[448,256]{1,0:T(8,128)(2,1)S(1)}, u32[]{:S(2)}, u32[]{:S(2)}) collective-permute-start(bf16[448,256]{1,0:T(8,128)(2,1)S(1)} %shard_map.68), channel_id=1, source_target_pairs={{0,128},{16,144},{32,160},{48,176},{64,192},{80,208},{96,224},{112... | collective-permute-start | bytes 688136 | tf_op jit(solution)/shard_map/ppermute | solution.py:17
  17.9 1.1 select_bitcast_fusion.3
  19.0 20.6 %all_gather.9 = bf16[1,2,2,256,256]{4,3,2,1,0:T(8,128)(2,1)S(1)} all-gather(bf16[1,2,2,16,256]{4,3,2,1,0:T(8,128)(2,1)S(1)} %get-tuple-element.11), channel_id=1, replica_groups=mesh['blk'=32,'tok'=16] {'tok'}, dimensions={3}, use_global_device_ids=true | all-gather | bytes 557056 | tf_op jit(solution)/shard_map/all_gather | solution.py:201
  40.6 8.4 %collective-permute-start.4 = (bf16[416,256]{1,0:T(8,128)(2,1)S(1)}, bf16[416,256]{1,0:T(8,128)(2,1)S(1)}, u32[]{:S(2)}, u32[]{:S(2)}) collective-permute-start(bf16[416,256]{1,0:T(8,128)(2,1)S(1)} %get-tuple-element.18), channel_id=1, source_target_pairs={{0,256},{16,272},{32,288},{48,304},{64,320},{80,336},{96,352},{112... | collective-permute-start | bytes 638984 | tf_op jit(solution)/shard_map/ppermute | solution.py:17
  49.3 3.1 %collective-permute-start = (bf16[2,384,256]{2,1,0:T(8,128)(2,1)S(1)}, bf16[2,384,256]{2,1,0:T(8,128)(2,1)}, u32[]{:S(2)}, u32[]{:S(2)}) collective-permute-start(bf16[2,384,256]{2,1,0:T(8,128)(2,1)S(1)} %fusion.4), channel_id=1, source_target_pairs={{0,16},{16,0},{32,48},{48,32},{64,80},{80,64},{96,112},{112,96},{1... | collective-permute-start | bytes 1179656 | tf_op jit(solution)/shard_map/ppermute | solution.py:17
  52.4 3.9 %collective-permute-done.4.came = bf16[416,256]{1,0:T(8,128)(2,1)S(1)} collective-permute-done((bf16[416,256]{1,0:T(8,128)(2,1)S(1)}, bf16[416,256]{1,0:T(8,128)(2,1)S(1)}, u32[]{:S(2)}, u32[]{:S(2)}) %collective-permute-start.4) | collective-permute-done | bytes 213024 | tf_op jit(solution)/shard_map/ppermute | solution.py:17
  56.4 1.2 shard_map.70
  58.5 1.1 fusion.26
  59.8 1.7 collective-permute-done
  61.6 1.3 fusion.5
  62.9 4.6 %collective-permute-start.1 = (bf16[2,384,256]{2,1,0:T(8,128)(2,1)S(1)}, bf16[2,384,256]{2,1,0:T(8,128)(2,1)S(1)}, u32[]{:S(2)}, u32[]{:S(2)}) collective-permute-start(bf16[2,384,256]{2,1,0:T(8,128)(2,1)S(1)} %fusion.5), channel_id=1, source_target_pairs={{0,32},{16,48},{32,0},{48,16},{64,96},{80,112},{96,64},{112,80},{1... | collective-permute-start | bytes 1179656 | tf_op jit(solution)/shard_map/ppermute | solution.py:17
  67.8 7.7 %collective-permute-done.1 = bf16[2,384,256]{2,1,0:T(8,128)(2,1)S(1)} collective-permute-done((bf16[2,384,256]{2,1,0:T(8,128)(2,1)S(1)}, bf16[2,384,256]{2,1,0:T(8,128)(2,1)S(1)}, u32[]{:S(2)}, u32[]{:S(2)}) %collective-permute-start.1) | collective-permute-done | bytes 393248 | tf_op jit(solution)/shard_map/ppermute | solution.py:17
  75.9 4.7 %collective-permute-start.3 = (bf16[2,384,256]{2,1,0:T(8,128)(2,1)S(1)}, bf16[2,384,256]{2,1,0:T(8,128)(2,1)S(1)}, u32[]{:S(2)}, u32[]{:S(2)}) collective-permute-start(bf16[2,384,256]{2,1,0:T(8,128)(2,1)S(1)} %fusion.6), channel_id=1, source_target_pairs={{0,64},{16,80},{32,96},{48,112},{64,0},{80,16},{96,32},{112,48},{1... | collective-permute-start | bytes 1179656 | tf_op jit(solution)/shard_map/ppermute | solution.py:17
  81.1 7.4 %collective-permute-done.3 = bf16[2,384,256]{2,1,0:T(8,128)(2,1)S(1)} collective-permute-done((bf16[2,384,256]{2,1,0:T(8,128)(2,1)S(1)}, bf16[2,384,256]{2,1,0:T(8,128)(2,1)S(1)}, u32[]{:S(2)}, u32[]{:S(2)}) %collective-permute-start.3) | collective-permute-done | bytes 393248 | tf_op jit(solution)/shard_map/ppermute | solution.py:17
  88.7 1.9 collective-permute-start.5
  90.9 9.4 %all-gather.5.cloned.1.call-done = bf16[2,2,2,256,256]{4,3,2,1,0:T(8,128)(2,1)} async-done(((bf16[2,2,2,16,256]{4,3,2,1,0:T(8,128)(2,1)}), bf16[2,2,2,256,256]{4,3,2,1,0:T(8,128)(2,1)}) %all-gather.5.cloned.1.call-update) | async-done | bytes 1048592 | tf_op jit(solution)/shard_map/all_gather | solution.py:221
  100.3 1.2 fusion.23
  102.2 7.8 %collective-permute-start.6 = (bf16[384,256]{1,0:T(8,128)(2,1)S(1)}, bf16[384,256]{1,0:T(8,128)(2,1)S(1)}, u32[]{:S(2)}, u32[]{:S(2)}) collective-permute-start(bf16[384,256]{1,0:T(8,128)(2,1)S(1)} %fusion.13), channel_id=1, source_target_pairs={{0,256},{16,272},{32,288},{48,304},{64,320},{80,336},{96,352},{112... | collective-permute-start | bytes 589832 | tf_op jit(solution)/shard_map/ppermute | solution.py:17
  110.7 3.8 %collective-permute-done.6 = bf16[384,256]{1,0:T(8,128)(2,1)S(1)} collective-permute-done((bf16[384,256]{1,0:T(8,128)(2,1)S(1)}, bf16[384,256]{1,0:T(8,128)(2,1)S(1)}, u32[]{:S(2)}, u32[]{:S(2)}) %collective-permute-start.6) | collective-permute-done | bytes 196640 | tf_op jit(solution)/shard_map/ppermute | solution.py:17
  115.2 1.2 fusion.34
  117.4 7.2 %collective-permute-start.7 = (bf16[384,256]{1,0:T(8,128)(2,1)S(1)}, bf16[384,256]{1,0:T(8,128)(2,1)S(1)}, u32[]{:S(2)}, u32[]{:S(2)}) collective-permute-start(bf16[384,256]{1,0:T(8,128)(2,1)S(1)} %fusion.14), channel_id=1, source_target_pairs={{0,256},{16,272},{32,288},{48,304},{64,320},{80,336},{96,352},{112... | collective-permute-start | bytes 589832 | tf_op jit(solution)/shard_map/ppermute | solution.py:17
  126.5 1.3 collective-permute-done.7
  128.0 12.5 %collective-permute-start.8 = (bf16[384,256]{1,0:T(8,128)(2,1)S(1)}, bf16[384,256]{1,0:T(8,128)(2,1)S(1)}, u32[]{:S(2)}, u32[]{:S(2)}) collective-permute-start(bf16[384,256]{1,0:T(8,128)(2,1)S(1)} %fusion.17), channel_id=1, source_target_pairs={{0,128},{16,144},{32,160},{48,176},{64,192},{80,208},{96,224},{112... | collective-permute-start | bytes 589832 | tf_op jit(solution)/shard_map/ppermute | solution.py:17
  141.3 7.0 %collective-permute-done.8 = bf16[384,256]{1,0:T(8,128)(2,1)S(1)} collective-permute-done((bf16[384,256]{1,0:T(8,128)(2,1)S(1)}, bf16[384,256]{1,0:T(8,128)(2,1)S(1)}, u32[]{:S(2)}, u32[]{:S(2)}) %collective-permute-start.8) | collective-permute-done | bytes 196640 | tf_op jit(solution)/shard_map/ppermute | solution.py:17
  148.9 1.9 collective-permute-start.10
  151.8 3.2 %collective-permute-start.9 = (bf16[8,3,2,2,16,256]{5,4,3,2,1,0:T(8,128)(2,1)S(1)}, bf16[8,3,2,2,16,256]{5,4,3,2,1,0:T(8,128)(2,1)S(1)}, u32[]{:S(2)}, u32[]{:S(2)}) collective-permute-start(bf16[8,3,2,2,16,256]{5,4,3,2,1,0:T(8,128)(2,1)S(1)} %select_bitcast_fusion.1), channel_id=1, source_target_pairs={{0,1},{1,0},{2,3},{3,2},{4,5},{5,4},{6,7},{7,6},{8,9},{9,8},{10,11... | collective-permute-start | bytes 2359304 | tf_op jit(solution)/shard_map/ppermute | solution.py:173
  155.0 5.3 %collective-permute-done.10 = bf16[2,384,256]{2,1,0:T(8,128)(2,1)S(1)} collective-permute-done((bf16[2,384,256]{2,1,0:T(8,128)(2,1)S(1)}, bf16[2,384,256]{2,1,0:T(8,128)(2,1)S(1)}, u32[]{:S(2)}, u32[]{:S(2)}) %collective-permute-start.10) | collective-permute-done | bytes 393248 | tf_op jit(solution)/shard_map/ppermute | solution.py:17
  160.6 1.0 convolution_convert_fusion.1
  161.7 4.8 %collective-permute-start.11 = (bf16[2,384,256]{2,1,0:T(8,128)(2,1)}, bf16[2,384,256]{2,1,0:T(8,128)(2,1)}, u32[]{:S(2)}, u32[]{:S(2)}) collective-permute-start(bf16[2,384,256]{2,1,0:T(8,128)(2,1)} %convolution_convert_fusion.1), channel_id=1, source_target_pairs={{0,32},{16,48},{32,0},{48,16},{64,96},{80,112},{96,64},{112,80},{1... | collective-permute-start | bytes 1179656 | tf_op jit(solution)/shard_map/ppermute | solution.py:17
  166.5 1.1 convolution_convert_fusion.4
  167.6 1.1 convolution_convert_fusion.3
  168.6 1.3 fusion.3
  169.9 3.7 %all-to-all-start = ((bf16[8,3,2,2,16,256]{5,4,3,2,1,0:T(8,128)(2,1)}), bf16[8,3,2,2,16,256]{5,4,3,2,1,0:T(8,128)(2,1)S(1)}, u32[]{:S(2)}, u32[]{:S(2)}) async-start(bf16[8,3,2,2,16,256]{5,4,3,2,1,0:T(8,128)(2,1)} %fusion.3), calls=%async_computation | async-start | bytes 1572864 | tf_op jit(solution)/shard_map/all_to_all | solution.py:180
  174.4 1.3 fusion.8
  175.7 1.3 convolution_convert_fusion
  177.0 3.6 %collective-permute-start.12 = (bf16[2,384,256]{2,1,0:T(8,128)(2,1)S(1)}, bf16[2,384,256]{2,1,0:T(8,128)(2,1)S(1)}, u32[]{:S(2)}, u32[]{:S(2)}) collective-permute-start(bf16[2,384,256]{2,1,0:T(8,128)(2,1)S(1)} %convolution_convert_fusion), channel_id=1, source_target_pairs={{0,16},{16,0},{32,48},{48,32},{64,80},{80,64},{96,112},{112,96},{1... | collective-permute-start | bytes 1179656 | tf_op jit(solution)/shard_map/ppermute | solution.py:17
  181.0 1.4 convolution_convert_fusion.5
  182.5 4.5 %collective-permute-done.12 = bf16[2,384,256]{2,1,0:T(8,128)(2,1)S(1)} collective-permute-done((bf16[2,384,256]{2,1,0:T(8,128)(2,1)S(1)}, bf16[2,384,256]{2,1,0:T(8,128)(2,1)S(1)}, u32[]{:S(2)}, u32[]{:S(2)}) %collective-permute-start.12) | collective-permute-done | bytes 393248 | tf_op jit(solution)/shard_map/ppermute | solution.py:17
  189.3 5.4 %collective-permute-start.13 = (bf16[8,3,2,2,16,256]{5,4,3,2,1,0:T(8,128)(2,1)}, bf16[8,3,2,2,16,256]{5,4,3,2,1,0:T(8,128)(2,1)}, u32[]{:S(2)}, u32[]{:S(2)}) collective-permute-start(bf16[8,3,2,2,16,256]{5,4,3,2,1,0:T(8,128)(2,1)} %select_bitcast_fusion), channel_id=1, source_target_pairs={{0,1},{1,0},{2,3},{3,2},{4,5},{5,4},{6,7},{7,6},{8,9},{9,8},{10,11... | collective-permute-start | bytes 2359304 | tf_op jit(solution)/shard_map/ppermute | solution.py:173
  194.8 1.9 collective-permute-start.14
  197.0 2.4 %fusion.21 = bf16[8,3,2,2,16,256]{5,4,3,2,1,0:T(8,128)(2,1)} fusion(bf16[8,3,2,2,16,256]{5,4,3,2,1,0:T(8,128)(2,1)} %collective-permute-done.13, pred[256]{0:T(512)(128)(4,1)S(1)} %compare_reduce_fusion.2, pred[]{:T(512)S(6)} %eq.15, bf16[3,2,2,8,1,16,256]{6,5,4,3,2,1,0:T(8,128)(2,1)S(1)} %get-tuple-element.20, ...), kind=kLoop, calls=%fused_computation.62 | loop fusion | flops 2359296 | bytes 3145985 | tf_op jit(solution)/shard_map/jit(_where)/select_n | solution.py:23
  200.2 6.6 %all-to-all-start.1 = ((bf16[8,3,2,2,16,256]{5,4,3,2,1,0:T(8,128)(2,1)}), bf16[8,3,2,2,16,256]{5,4,3,2,1,0:T(8,128)(2,1)S(1)}, u32[]{:S(2)}, u32[]{:S(2)}) async-start(bf16[8,3,2,2,16,256]{5,4,3,2,1,0:T(8,128)(2,1)} %fusion.21), calls=%async_computation.1 | async-start | bytes 1572864 | tf_op jit(solution)/shard_map/all_to_all | solution.py:180
  207.5 6.9 %collective-permute-start.16 = (bf16[2,16,256]{2,1,0:T(8,128)(2,1)S(1)}, bf16[2,16,256]{2,1,0:T(8,128)(2,1)S(1)}, u32[]{:S(2)}, u32[]{:S(2)}) collective-permute-start(bf16[2,16,256]{2,1,0:T(8,128)(2,1)S(1)} %get-tuple-element.34), channel_id=1, source_target_pairs={{0,256},{16,272},{32,288},{48,304},{64,320},{80,336},{96,352},{112... | collective-permute-start | bytes 49160 | tf_op jit(solution)/shard_map/ppermute | solution.py:17
  214.7 1.9 collective-permute-start.15
  218.4 4.3 %collective-permute-start.17 = (bf16[2,2,16,256]{3,2,1,0:T(8,128)(2,1)S(1)}, bf16[2,2,16,256]{3,2,1,0:T(8,128)(2,1)S(1)}, u32[]{:S(2)}, u32[]{:S(2)}) collective-permute-start(bf16[2,2,16,256]{3,2,1,0:T(8,128)(2,1)S(1)} %get-tuple-element.31), channel_id=1, source_target_pairs={{0,128},{16,144},{32,160},{48,176},{64,192},{80,208},{96,224},{112... | collective-permute-start | bytes 98312 | tf_op jit(solution)/shard_map/ppermute | solution.py:17
  222.7 6.5 %collective-permute-done.15 = bf16[384,256]{1,0:T(8,128)(2,1)S(1)} collective-permute-done((bf16[384,256]{1,0:T(8,128)(2,1)S(1)}, bf16[384,256]{1,0:T(8,128)(2,1)S(1)}, u32[]{:S(2)}, u32[]{:S(2)}) %collective-permute-start.15) | collective-permute-done | bytes 196640 | tf_op jit(solution)/shard_map/ppermute | solution.py:17
  230.4 1.5 shard_map.72
  (148 shorter events, 22.6 us)
Async XLA Ops:
  7.2 51.3 %all-gather.3.cloned.1.call-start = ((), (), s32[]{:S(2)}) async-start(), calls=%async_computation.2 | async-start | bytes 1671168 | tf_op jit(solution)/shard_map/all_gather | solution.py:202
  10.1 90.2 %all-gather.5.cloned.1.call-start = ((), (), s32[]{:S(2)}) async-start(), calls=%async_computation.3 | async-start | bytes 1114112 | tf_op jit(solution)/shard_map/all_gather | solution.py:221
  10.2 1.0 copy-start
  11.2 28.7 %collective-permute-start.2 = (bf16[448,256]{1,0:T(8,128)(2,1)S(1)}, bf16[448,256]{1,0:T(8,128)(2,1)S(1)}, u32[]{:S(2)}, u32[]{:S(2)}) collective-permute-start(bf16[448,256]{1,0:T(8,128)(2,1)S(1)} %shard_map.68), channel_id=1, source_target_pairs={{0,128},{16,144},{32,160},{48,176},{64,192},{80,208},{96,224},{112... | collective-permute-start | bytes 688136 | tf_op jit(solution)/shard_map/ppermute | solution.py:17
  18.9 21.0 %copy-start.13 = (bf16[1,384,256]{2,1,0:T(8,128)(2,1)}, bf16[1,384,256]{2,1,0:T(8,128)(2,1)S(1)}, u32[]{:S(2)}) copy-start(bf16[1,384,256]{2,1,0:T(8,128)(2,1)S(1)} %get-tuple-element.30) | copy-start | bytes 589828
  19.0 21.0 %copy-start.1 = (bf16[384,512]{1,0:T(8,128)(2,1)S(1)}, bf16[384,512]{1,0:T(8,128)(2,1)}, u32[]{:S(2)}) copy-start(bf16[384,512]{1,0:T(8,128)(2,1)} %cotangent.3) | copy-start | bytes 1179652
  19.0 21.0 %copy-start.4 = (s32[6,64]{1,0:T(8,128)S(1)}, s32[6,64]{1,0:T(8,128)}, u32[]{:S(2)}) copy-start(s32[6,64]{1,0:T(8,128)} %matchings.9) | copy-start | bytes 4612
  19.0 30.3 %copy-start.5 = (bf16[2,384,256]{2,1,0:T(8,128)(2,1)}, bf16[2,384,256]{2,1,0:T(8,128)(2,1)S(1)}, u32[]{:S(2)}) copy-start(bf16[2,384,256]{2,1,0:T(8,128)(2,1)S(1)} %rev.3) | copy-start | bytes 1179652
  40.6 15.7 %collective-permute-start.4 = (bf16[416,256]{1,0:T(8,128)(2,1)S(1)}, bf16[416,256]{1,0:T(8,128)(2,1)S(1)}, u32[]{:S(2)}, u32[]{:S(2)}) collective-permute-start(bf16[416,256]{1,0:T(8,128)(2,1)S(1)} %get-tuple-element.18), channel_id=1, source_target_pairs={{0,256},{16,272},{32,288},{48,304},{64,320},{80,336},{96,352},{112... | collective-permute-start | bytes 638984 | tf_op jit(solution)/shard_map/ppermute | solution.py:17
  49.3 13.5 %copy-start.15 = (bf16[2,384,256]{2,1,0:T(8,128)(2,1)}, bf16[2,384,256]{2,1,0:T(8,128)(2,1)S(1)}, u32[]{:S(2)}) copy-start(bf16[2,384,256]{2,1,0:T(8,128)(2,1)S(1)} %fusion.4) | copy-start | bytes 1179652
  49.3 12.2 %collective-permute-start = (bf16[2,384,256]{2,1,0:T(8,128)(2,1)S(1)}, bf16[2,384,256]{2,1,0:T(8,128)(2,1)}, u32[]{:S(2)}, u32[]{:S(2)}) collective-permute-start(bf16[2,384,256]{2,1,0:T(8,128)(2,1)S(1)} %fusion.4), channel_id=1, source_target_pairs={{0,16},{16,0},{32,48},{48,32},{64,80},{80,64},{96,112},{112,96},{1... | collective-permute-start | bytes 1179656 | tf_op jit(solution)/shard_map/ppermute | solution.py:17
  59.6 8.0 %copy-start.9 = (bf16[2,2,256,256]{3,2,1,0:T(8,128)(2,1)}, bf16[2,2,256,256]{3,2,1,0:T(8,128)(2,1)S(1)}, u32[]{:S(2)}) copy-start(bf16[2,2,256,256]{3,2,1,0:T(8,128)(2,1)S(1)} %fusion.26) | copy-start | bytes 1572868
  59.6 8.0 %copy-start.21 = (bf16[3,2,2,256,256]{4,3,2,1,0:T(8,128)(2,1)S(1)}, bf16[3,2,2,256,256]{4,3,2,1,0:T(8,128)(2,1)}, u32[]{:S(2)}) copy-start(bf16[3,2,2,256,256]{4,3,2,1,0:T(8,128)(2,1)} %all-gather.3.cloned.1.call-done) | copy-start | bytes 4718596
  62.8 13.0 %copy-start.7 = (bf16[2,384,256]{2,1,0:T(8,128)(2,1)}, bf16[2,384,256]{2,1,0:T(8,128)(2,1)S(1)}, u32[]{:S(2)}) copy-start(bf16[2,384,256]{2,1,0:T(8,128)(2,1)S(1)} %fusion.5) | copy-start | bytes 1179652
  62.9 12.7 %collective-permute-start.1 = (bf16[2,384,256]{2,1,0:T(8,128)(2,1)S(1)}, bf16[2,384,256]{2,1,0:T(8,128)(2,1)S(1)}, u32[]{:S(2)}, u32[]{:S(2)}) collective-permute-start(bf16[2,384,256]{2,1,0:T(8,128)(2,1)S(1)} %fusion.5), channel_id=1, source_target_pairs={{0,32},{16,48},{32,0},{48,16},{64,96},{80,112},{96,64},{112,80},{1... | collective-permute-start | bytes 1179656 | tf_op jit(solution)/shard_map/ppermute | solution.py:17
  75.6 5.3 %copy-start.17 = (bf16[2,384,256]{2,1,0:T(8,128)(2,1)}, bf16[2,384,256]{2,1,0:T(8,128)(2,1)S(1)}, u32[]{:S(2)}) copy-start(bf16[2,384,256]{2,1,0:T(8,128)(2,1)S(1)} %collective-permute-done.1) | copy-start | bytes 1179652
  75.9 12.9 %copy-start.19 = (bf16[2,384,256]{2,1,0:T(8,128)(2,1)}, bf16[2,384,256]{2,1,0:T(8,128)(2,1)S(1)}, u32[]{:S(2)}) copy-start(bf16[2,384,256]{2,1,0:T(8,128)(2,1)S(1)} %fusion.6) | copy-start | bytes 1179652
  75.9 12.6 %collective-permute-start.3 = (bf16[2,384,256]{2,1,0:T(8,128)(2,1)S(1)}, bf16[2,384,256]{2,1,0:T(8,128)(2,1)S(1)}, u32[]{:S(2)}, u32[]{:S(2)}) collective-permute-start(bf16[2,384,256]{2,1,0:T(8,128)(2,1)S(1)} %fusion.6), channel_id=1, source_target_pairs={{0,64},{16,80},{32,96},{48,112},{64,0},{80,16},{96,32},{112,48},{1... | collective-permute-start | bytes 1179656 | tf_op jit(solution)/shard_map/ppermute | solution.py:17
  80.6 10.3 %copy-start.11 = (bf16[2,2,256,256]{3,2,1,0:T(8,128)(2,1)}, bf16[2,2,256,256]{3,2,1,0:T(8,128)(2,1)S(1)}, u32[]{:S(2)}) copy-start(bf16[2,2,256,256]{3,2,1,0:T(8,128)(2,1)S(1)} %fusion.24) | copy-start | bytes 1572868
  88.5 2.2 copy-start.27
  88.7 13.2 %collective-permute-start.5 = (bf16[384,256]{1,0:T(8,128)(2,1)S(1)}, bf16[384,256]{1,0:T(8,128)(2,1)S(1)}, u32[]{:S(2)}, u32[]{:S(2)}) collective-permute-start(bf16[384,256]{1,0:T(8,128)(2,1)S(1)} %fusion.11), channel_id=1, source_target_pairs={{0,128},{16,144},{32,160},{48,176},{64,192},{80,208},{96,224},{112... | collective-permute-start | bytes 589832 | tf_op jit(solution)/shard_map/ppermute | solution.py:17
  100.3 9.7 %copy-start.26 = (bf16[2,2,2,256,256]{4,3,2,1,0:T(8,128)(2,1)S(1)}, bf16[2,2,2,256,256]{4,3,2,1,0:T(8,128)(2,1)}, u32[]{:S(2)}) copy-start(bf16[2,2,2,256,256]{4,3,2,1,0:T(8,128)(2,1)} %all-gather.5.cloned.1.call-done) | copy-start | bytes 3145732
  102.2 12.3 %collective-permute-start.6 = (bf16[384,256]{1,0:T(8,128)(2,1)S(1)}, bf16[384,256]{1,0:T(8,128)(2,1)S(1)}, u32[]{:S(2)}, u32[]{:S(2)}) collective-permute-start(bf16[384,256]{1,0:T(8,128)(2,1)S(1)} %fusion.13), channel_id=1, source_target_pairs={{0,256},{16,272},{32,288},{48,304},{64,320},{80,336},{96,352},{112... | collective-permute-start | bytes 589832 | tf_op jit(solution)/shard_map/ppermute | solution.py:17
  117.4 10.3 %collective-permute-start.7 = (bf16[384,256]{1,0:T(8,128)(2,1)S(1)}, bf16[384,256]{1,0:T(8,128)(2,1)S(1)}, u32[]{:S(2)}, u32[]{:S(2)}) collective-permute-start(bf16[384,256]{1,0:T(8,128)(2,1)S(1)} %fusion.14), channel_id=1, source_target_pairs={{0,256},{16,272},{32,288},{48,304},{64,320},{80,336},{96,352},{112... | collective-permute-start | bytes 589832 | tf_op jit(solution)/shard_map/ppermute | solution.py:17
  126.5 21.8 %copy-start.20 = (bf16[2,384,256]{2,1,0:T(8,128)(2,1)S(1)}, bf16[2,384,256]{2,1,0:T(8,128)(2,1)}, u32[]{:S(2)}) copy-start(bf16[2,384,256]{2,1,0:T(8,128)(2,1)} %copy-done.19) | copy-start | bytes 1179652
  128.0 20.6 %copy-start.12 = (bf16[2,2,256,256]{3,2,1,0:T(8,128)(2,1)S(1)}, bf16[2,2,256,256]{3,2,1,0:T(8,128)(2,1)}, u32[]{:S(2)}) copy-start(bf16[2,2,256,256]{3,2,1,0:T(8,128)(2,1)} %copy-done.11) | copy-start | bytes 1572868
  128.0 20.3 %collective-permute-start.8 = (bf16[384,256]{1,0:T(8,128)(2,1)S(1)}, bf16[384,256]{1,0:T(8,128)(2,1)S(1)}, u32[]{:S(2)}, u32[]{:S(2)}) collective-permute-start(bf16[384,256]{1,0:T(8,128)(2,1)S(1)} %fusion.17), channel_id=1, source_target_pairs={{0,128},{16,144},{32,160},{48,176},{64,192},{80,208},{96,224},{112... | collective-permute-start | bytes 589832 | tf_op jit(solution)/shard_map/ppermute | solution.py:17
  141.0 9.9 %copy-start.28 = (bf16[2,384,256]{2,1,0:T(8,128)(2,1)S(1)}, bf16[2,384,256]{2,1,0:T(8,128)(2,1)}, u32[]{:S(2)}) copy-start(bf16[2,384,256]{2,1,0:T(8,128)(2,1)} %copy-done.27) | copy-start | bytes 1179652
  148.9 11.4 %collective-permute-start.10 = (bf16[2,384,256]{2,1,0:T(8,128)(2,1)S(1)}, bf16[2,384,256]{2,1,0:T(8,128)(2,1)S(1)}, u32[]{:S(2)}, u32[]{:S(2)}) collective-permute-start(bf16[2,384,256]{2,1,0:T(8,128)(2,1)S(1)} %convolution_convert_fusion.2), channel_id=1, source_target_pairs={{0,64},{16,80},{32,96},{48,112},{64,0},{80,16},{96,32},{112,48},{1... | collective-permute-start | bytes 1179656 | tf_op jit(solution)/shard_map/ppermute | solution.py:17
  151.8 14.7 %copy-start.8 = (bf16[2,384,256]{2,1,0:T(8,128)(2,1)S(1)}, bf16[2,384,256]{2,1,0:T(8,128)(2,1)}, u32[]{:S(2)}) copy-start(bf16[2,384,256]{2,1,0:T(8,128)(2,1)} %copy-done.7) | copy-start | bytes 1179652
  151.8 15.8 %copy-start.18 = (bf16[2,384,256]{2,1,0:T(8,128)(2,1)S(1)}, bf16[2,384,256]{2,1,0:T(8,128)(2,1)}, u32[]{:S(2)}) copy-start(bf16[2,384,256]{2,1,0:T(8,128)(2,1)} %copy-done.17) | copy-start | bytes 1179652
  151.8 16.8 %collective-permute-start.9 = (bf16[8,3,2,2,16,256]{5,4,3,2,1,0:T(8,128)(2,1)S(1)}, bf16[8,3,2,2,16,256]{5,4,3,2,1,0:T(8,128)(2,1)S(1)}, u32[]{:S(2)}, u32[]{:S(2)}) collective-permute-start(bf16[8,3,2,2,16,256]{5,4,3,2,1,0:T(8,128)(2,1)S(1)} %select_bitcast_fusion.1), channel_id=1, source_target_pairs={{0,1},{1,0},{2,3},{3,2},{4,5},{5,4},{6,7},{7,6},{8,9},{9,8},{10,11... | collective-permute-start | bytes 2359304 | tf_op jit(solution)/shard_map/ppermute | solution.py:173
  161.7 12.7 %collective-permute-start.11 = (bf16[2,384,256]{2,1,0:T(8,128)(2,1)}, bf16[2,384,256]{2,1,0:T(8,128)(2,1)}, u32[]{:S(2)}, u32[]{:S(2)}) collective-permute-start(bf16[2,384,256]{2,1,0:T(8,128)(2,1)} %convolution_convert_fusion.1), channel_id=1, source_target_pairs={{0,32},{16,48},{32,0},{48,16},{64,96},{80,112},{96,64},{112,80},{1... | collective-permute-start | bytes 1179656 | tf_op jit(solution)/shard_map/ppermute | solution.py:17
  169.9 26.8 %all-to-all-start = ((bf16[8,3,2,2,16,256]{5,4,3,2,1,0:T(8,128)(2,1)}), bf16[8,3,2,2,16,256]{5,4,3,2,1,0:T(8,128)(2,1)S(1)}, u32[]{:S(2)}, u32[]{:S(2)}) async-start(bf16[8,3,2,2,16,256]{5,4,3,2,1,0:T(8,128)(2,1)} %fusion.3), calls=%async_computation | async-start | bytes 1572864 | tf_op jit(solution)/shard_map/all_to_all | solution.py:180
  173.6 7.0 %copy-start.16 = (bf16[2,384,256]{2,1,0:T(8,128)(2,1)S(1)}, bf16[2,384,256]{2,1,0:T(8,128)(2,1)}, u32[]{:S(2)}) copy-start(bf16[2,384,256]{2,1,0:T(8,128)(2,1)} %copy-done.15) | copy-start | bytes 1179652
  175.7 11.3 %copy-start.10 = (bf16[2,2,256,256]{3,2,1,0:T(8,128)(2,1)S(1)}, bf16[2,2,256,256]{3,2,1,0:T(8,128)(2,1)}, u32[]{:S(2)}) copy-start(bf16[2,2,256,256]{3,2,1,0:T(8,128)(2,1)} %copy-done.9) | copy-start | bytes 1572868
  177.0 10.0 %collective-permute-start.12 = (bf16[2,384,256]{2,1,0:T(8,128)(2,1)S(1)}, bf16[2,384,256]{2,1,0:T(8,128)(2,1)S(1)}, u32[]{:S(2)}, u32[]{:S(2)}) collective-permute-start(bf16[2,384,256]{2,1,0:T(8,128)(2,1)S(1)} %convolution_convert_fusion), channel_id=1, source_target_pairs={{0,16},{16,0},{32,48},{48,32},{64,80},{80,64},{96,112},{112,96},{1... | collective-permute-start | bytes 1179656 | tf_op jit(solution)/shard_map/ppermute | solution.py:17
  181.0 6.3 %copy-start.6 = (bf16[2,384,256]{2,1,0:T(8,128)(2,1)S(1)}, bf16[2,384,256]{2,1,0:T(8,128)(2,1)}, u32[]{:S(2)}) copy-start(bf16[2,384,256]{2,1,0:T(8,128)(2,1)} %copy-done.5) | copy-start | bytes 1179652
  182.4 5.2 %copy-start.14 = (bf16[1,384,256]{2,1,0:T(8,128)(2,1)S(1)}, bf16[1,384,256]{2,1,0:T(8,128)(2,1)}, u32[]{:S(2)}) copy-start(bf16[1,384,256]{2,1,0:T(8,128)(2,1)} %copy-done.13) | copy-start | bytes 589828
  182.5 5.6 %copy-start.24 = (bf16[2,256,256]{2,1,0:T(8,128)(2,1)S(1)}, bf16[2,256,256]{2,1,0:T(8,128)(2,1)}, u32[]{:S(2)}) copy-start(bf16[2,256,256]{2,1,0:T(8,128)(2,1)} %convolution_convert_fusion.4) | copy-start | bytes 786436
  182.5 5.6 %copy-start.25 = (bf16[2,256,256]{2,1,0:T(8,128)(2,1)S(1)}, bf16[2,256,256]{2,1,0:T(8,128)(2,1)}, u32[]{:S(2)}) copy-start(bf16[2,256,256]{2,1,0:T(8,128)(2,1)} %convolution_convert_fusion.3) | copy-start | bytes 786436
  189.3 7.7 %collective-permute-start.13 = (bf16[8,3,2,2,16,256]{5,4,3,2,1,0:T(8,128)(2,1)}, bf16[8,3,2,2,16,256]{5,4,3,2,1,0:T(8,128)(2,1)}, u32[]{:S(2)}, u32[]{:S(2)}) collective-permute-start(bf16[8,3,2,2,16,256]{5,4,3,2,1,0:T(8,128)(2,1)} %select_bitcast_fusion), channel_id=1, source_target_pairs={{0,1},{1,0},{2,3},{3,2},{4,5},{5,4},{6,7},{7,6},{8,9},{9,8},{10,11... | collective-permute-start | bytes 2359304 | tf_op jit(solution)/shard_map/ppermute | solution.py:173
  194.8 19.7 %collective-permute-start.14 = (bf16[384,256]{1,0:T(8,128)(2,1)}, bf16[384,256]{1,0:T(8,128)(2,1)S(1)}, u32[]{:S(2)}, u32[]{:S(2)}) collective-permute-start(bf16[384,256]{1,0:T(8,128)(2,1)} %get-tuple-element.28), channel_id=1, source_target_pairs={{0,256},{16,272},{32,288},{48,304},{64,320},{80,336},{96,352},{112... | collective-permute-start | bytes 589832 | tf_op jit(solution)/shard_map/ppermute | solution.py:17
  199.4 15.0 %copy-start.23 = (bf16[2,384,256]{2,1,0:T(8,128)(2,1)S(1)}, bf16[2,384,256]{2,1,0:T(8,128)(2,1)}, u32[]{:S(2)}) copy-start(bf16[2,384,256]{2,1,0:T(8,128)(2,1)} %copy-done.22) | copy-start | bytes 1179652
  200.2 30.2 %all-to-all-start.1 = ((bf16[8,3,2,2,16,256]{5,4,3,2,1,0:T(8,128)(2,1)}), bf16[8,3,2,2,16,256]{5,4,3,2,1,0:T(8,128)(2,1)S(1)}, u32[]{:S(2)}, u32[]{:S(2)}) async-start(bf16[8,3,2,2,16,256]{5,4,3,2,1,0:T(8,128)(2,1)} %fusion.21), calls=%async_computation.1 | async-start | bytes 1572864 | tf_op jit(solution)/shard_map/all_to_all | solution.py:180
  207.5 10.9 %collective-permute-start.16 = (bf16[2,16,256]{2,1,0:T(8,128)(2,1)S(1)}, bf16[2,16,256]{2,1,0:T(8,128)(2,1)S(1)}, u32[]{:S(2)}, u32[]{:S(2)}) collective-permute-start(bf16[2,16,256]{2,1,0:T(8,128)(2,1)S(1)} %get-tuple-element.34), channel_id=1, source_target_pairs={{0,256},{16,272},{32,288},{48,304},{64,320},{80,336},{96,352},{112... | collective-permute-start | bytes 49160 | tf_op jit(solution)/shard_map/ppermute | solution.py:17
  214.7 14.5 %collective-permute-start.15 = (bf16[384,256]{1,0:T(8,128)(2,1)S(1)}, bf16[384,256]{1,0:T(8,128)(2,1)S(1)}, u32[]{:S(2)}, u32[]{:S(2)}) collective-permute-start(bf16[384,256]{1,0:T(8,128)(2,1)S(1)} %select_select_fusion), channel_id=1, source_target_pairs={{0,128},{16,144},{32,160},{48,176},{64,192},{80,208},{96,224},{112... | collective-permute-start | bytes 589832 | tf_op jit(solution)/shard_map/ppermute | solution.py:17
  218.4 11.8 %collective-permute-start.17 = (bf16[2,2,16,256]{3,2,1,0:T(8,128)(2,1)S(1)}, bf16[2,2,16,256]{3,2,1,0:T(8,128)(2,1)S(1)}, u32[]{:S(2)}, u32[]{:S(2)}) collective-permute-start(bf16[2,2,16,256]{3,2,1,0:T(8,128)(2,1)S(1)} %get-tuple-element.31), channel_id=1, source_target_pairs={{0,128},{16,144},{32,160},{48,176},{64,192},{80,208},{96,224},{112... | collective-permute-start | bytes 98312 | tf_op jit(solution)/shard_map/ppermute | solution.py:17
  (3 other events, 2.4 us)
Sparse Core Ops, SparseCore 0:
  10.7 47.7 all-gather.2
  60.6 39.6 all-gather.4

commit v11 on v10

--- a/solution.py
+++ b/solution.py
@@ -76,7 +76,7 @@
     packed[rows:] = jnp.where(low == 1, cotangent[:, :width], cotangent[:, width:])
 
 
-def between(matchings, keep, came, cotangent, fourth, fifth, packed, cotan):
+def between(matchings, keep, came, cotangent, fourth, fifth, send, cotan, cot_send):
     _, low, high = bits()
     width = keep.shape[-1]
     depth = keep.shape[-2]
@@ -93,11 +93,11 @@
     for both in range(2):
         mine5, yours5 = keep[1, both], came_at(1, both)
         fifth[both] = jnp.where(same, mine5, yours5)
-        packed[pl.ds(both * depth, depth)] = jnp.where(same, yours5, mine5)
+        send[both] = jnp.where(same, yours5, mine5)
     cot_keep = jnp.where(low == 1, cotangent[:, width:], cotangent[:, :width])
     cot_came = came[4 * depth :]
     cotan[...] = jnp.where(same, cot_keep, cot_came)
-    packed[2 * depth :] = jnp.where(same, cot_came, cot_keep)
+    cot_send[...] = jnp.where(same, cot_came, cot_keep)
 
 
 def gather_late(matchings, fourth, fifth, came, late):
@@ -109,7 +109,7 @@
             if row == 0:
                 late[1, slot, row] = fifth[both]
             else:
-                late[1, slot, row] = came[pl.ds(pl.multiple_of(both * depth, depth), depth)]
+                late[1, slot, row] = came[both]
 
 
 def total(parts, place, slot, row):
@@ -207,16 +207,16 @@
     inputs = [(value, other)]
     value = (dot(value, full[0][0]) + dot(other, full[0][1])).astype(bf16)
 
-    fourth, fifth, packed, cotan0 = local(
+    fourth, fifth, send, cotan0, cot_send = local(
         between,
         matchings,
         keep,
         came,
         cotangent,
-        outs=[shape(2, 2, depth), shape(2, depth), shape(2 * depth + tokens), shape(tokens)],
+        outs=[shape(2, 2, depth), shape(2, depth), shape(2, depth), shape(tokens), shape(tokens)],
     )
-    came = flip(packed, 4)
-    cotan1 = came[2 * depth :]
+    came = flip(send, 4)
+    cotan1 = flip(cot_send, 4)
     late = local(gather_late, matchings, fourth, fifth, came, outs=[shape(2, 2, 2, depth)])
     full += list(lax.all_gather(late, "tok", axis=3, tiled=True))
 
@@ -227,6 +227,8 @@
         own_w, other_w = full[section][0], full[section][1]
         if section < 3:
             value = (dot(value, own_w) + dot(other, other_w)).astype(bf16)
+            if section == 1:
+                value = after(value, cotan1)
         else:
             send = (dot(value[1], own_w[1]) + dot(other[1], other_w[1])).astype(bf16)
             keep = (dot(value[0], own_w[0]) + dot(other[0], other_w[0])).astype(bf16)

time: 240 us -> 247 us (1.029)
  waiting for transfers between devices: 60.1 us -> 68.7 us
  starting transfers between devices: 101 us -> 97.5 us
    ppermute x16 -> x17, waiting for transfers between devices: 49.3 us -> 62.2 us  [flip(): return lax.ppermute(value, 'blk', pairs)]
    ppermute x16 -> x17, starting transfers between devices: 82.2 us -> 75 us  [flip(): return lax.ppermute(value, 'blk', pairs)]
    all_gather x1, waiting for transfers between devices: 9.43 us -> 3.46 us  [body(): full += list(lax.all_gather(late, 'tok', axis=3, tiled=True))]
    all_to_all x2, starting transfers between devices: 10.4 us -> 13.5 us  [all_parts(): return lax.all_to_all(chip, 'tok', 0, 0, axis_index_groups=groups)]
    all_to_all x2, waiting for transfers between devices: 0.21 us -> 2.93 us  [all_parts(): return lax.all_to_all(chip, 'tok', 0, 0, axis_index_groups=groups)]
  transfers between devices with their start and end apart: 22 -> 23, of which waited for: 14 -> 12; matrix products, arithmetic and copies ran while one was open for 12% -> 13% of each run, Pallas kernels for 1% -> 1%
where the time goes in v11:
time: 247 us; the launch traced here: 245 us
  starting transfers between devices  97.5 us (39%)
  waiting for transfers between devices  68.7 us (28%)
  matrix products  21.8 us (9%)
  blocking collectives  20.6 us (8%)
  between operations  15.1 us (6%)
  other arithmetic  13.2 us (5%)
  Pallas kernels  5.37 us (2%)
  local copies, waits for them, and re-layouts  3.06 us (1%)
    ppermute x17, starting transfers between devices, flip(): return lax.ppermute(value, 'blk', pairs)  75 us
    ppermute x17, waiting for transfers between devices, flip(): return lax.ppermute(value, 'blk', pairs)  62.2 us
    all_gather x1, blocking collectives, body(): full = list(lax.all_gather(first, 'tok', axis=3, tiled=True))  20.6 us
    all_to_all x2, starting transfers between devices, all_parts(): return lax.all_to_all(chip, 'tok', 0, 0, axis_index_groups=groups)  13.5 us
    ppermute x2, starting transfers between devices, chip_sum(): lax.ppermute(core_half(terms, 1 - core), 'tok', [(source, source ^ 1) for...  9 us
    dot_general x18, matrix products, dot_back(): jnp.einsum('...tl,...kl->...tk', left, right, preferred_element_type=jnp....  7.44 us
    dot_general x16, matrix products, dot_rows(): jnp.einsum('...tk,...tl->...kl', left, right, preferred_element_type=jnp....  7.39 us
    dot_general x18, matrix products, dot(): jnp.einsum('...tk,...kl->...tl', left, right, preferred_element_type=jnp....  7 us
  transfers between devices with their start and end apart: 23, of which 12 were waited for; matrix products, arithmetic and copies ran while one was open for 13% of the time, Pallas kernels for 1%

profile of v11, /device:TPU:1, one launch (start us, length us, event | category | flops | bytes accessed | tf_op | source)
XLA Modules:
  0.0 245.4 jit_solution(9311177704923124996)
XLA Ops:
  8.8 1.3 shard_map.67
  11.2 6.6 %collective-permute-start = (bf16[448,256]{1,0:T(8,128)(2,1)S(1)}, bf16[448,256]{1,0:T(8,128)(2,1)S(1)}, u32[]{:S(2)}, u32[]{:S(2)}) collective-permute-start(bf16[448,256]{1,0:T(8,128)(2,1)S(1)} %shard_map.68), channel_id=1, source_target_pairs={{0,128},{16,144},{32,160},{48,176},{64,192},{80,208},{96,224},{112... | collective-permute-start | bytes 688136 | tf_op jit(solution)/shard_map/ppermute | solution.py:17
  19.0 20.6 %all_gather.9 = bf16[1,2,2,256,256]{4,3,2,1,0:T(8,128)(2,1)S(1)} all-gather(bf16[1,2,2,16,256]{4,3,2,1,0:T(8,128)(2,1)S(1)} %get-tuple-element.15), channel_id=1, replica_groups=mesh['blk'=32,'tok'=16] {'tok'}, dimensions={3}, use_global_device_ids=true | all-gather | bytes 557056 | tf_op jit(solution)/shard_map/all_gather | solution.py:201
  40.6 8.4 %collective-permute-start.1 = (bf16[384,256]{1,0:T(8,128)(2,1)S(1)}, bf16[384,256]{1,0:T(8,128)(2,1)S(1)}, u32[]{:S(2)}, u32[]{:S(2)}) collective-permute-start(bf16[384,256]{1,0:T(8,128)(2,1)S(1)} %get-tuple-element.14), channel_id=1, source_target_pairs={{0,256},{16,272},{32,288},{48,304},{64,320},{80,336},{96,352},{112... | collective-permute-start | bytes 589832 | tf_op jit(solution)/shard_map/ppermute | solution.py:17
  49.3 3.1 %collective-permute-start.2 = (bf16[2,384,256]{2,1,0:T(8,128)(2,1)S(1)}, bf16[2,384,256]{2,1,0:T(8,128)(2,1)}, u32[]{:S(2)}, u32[]{:S(2)}) collective-permute-start(bf16[2,384,256]{2,1,0:T(8,128)(2,1)S(1)} %fusion.4), channel_id=1, source_target_pairs={{0,16},{16,0},{32,48},{48,32},{64,80},{80,64},{96,112},{112,96},{1... | collective-permute-start | bytes 1179656 | tf_op jit(solution)/shard_map/ppermute | solution.py:17
  52.4 1.9 collective-permute-start.5
  54.4 6.4 %collective-permute-done.5.came = bf16[2,16,256]{2,1,0:T(8,128)(2,1)S(1)} collective-permute-done((bf16[2,16,256]{2,1,0:T(8,128)(2,1)S(1)}, bf16[2,16,256]{2,1,0:T(8,128)(2,1)S(1)}, u32[]{:S(2)}, u32[]{:S(2)}) %collective-permute-start.5) | collective-permute-done | bytes 16416 | tf_op jit(solution)/shard_map/ppermute | solution.py:17
  60.8 1.2 shard_map.70
  62.1 1.1 fusion.26
  63.6 1.6 broadcast_select_fusion.2
  65.2 4.5 %collective-permute-start.3 = (bf16[2,384,256]{2,1,0:T(8,128)(2,1)S(1)}, bf16[2,384,256]{2,1,0:T(8,128)(2,1)S(1)}, u32[]{:S(2)}, u32[]{:S(2)}) collective-permute-start(bf16[2,384,256]{2,1,0:T(8,128)(2,1)S(1)} %broadcast_select_fusion.2), channel_id=1, source_target_pairs={{0,32},{16,48},{32,0},{48,16},{64,96},{80,112},{96,64},{112,80},{1... | collective-permute-start | bytes 1179656 | tf_op jit(solution)/shard_map/ppermute | solution.py:17
  70.0 7.3 %collective-permute-done.3 = bf16[2,384,256]{2,1,0:T(8,128)(2,1)S(1)} collective-permute-done((bf16[2,384,256]{2,1,0:T(8,128)(2,1)S(1)}, bf16[2,384,256]{2,1,0:T(8,128)(2,1)S(1)}, u32[]{:S(2)}, u32[]{:S(2)}) %collective-permute-start.3) | collective-permute-done | bytes 393248 | tf_op jit(solution)/shard_map/ppermute | solution.py:17
  77.6 3.2 %collective-permute-start.4 = (bf16[2,384,256]{2,1,0:T(8,128)(2,1)S(1)}, bf16[2,384,256]{2,1,0:T(8,128)(2,1)S(1)}, u32[]{:S(2)}, u32[]{:S(2)}) collective-permute-start(bf16[2,384,256]{2,1,0:T(8,128)(2,1)S(1)} %fusion.6), channel_id=1, source_target_pairs={{0,64},{16,80},{32,96},{48,112},{64,0},{80,16},{96,32},{112,48},{1... | collective-permute-start | bytes 1179656 | tf_op jit(solution)/shard_map/ppermute | solution.py:17
  81.4 6.1 %collective-permute-done.4 = bf16[2,384,256]{2,1,0:T(8,128)(2,1)S(1)} collective-permute-done((bf16[2,384,256]{2,1,0:T(8,128)(2,1)S(1)}, bf16[2,384,256]{2,1,0:T(8,128)(2,1)S(1)}, u32[]{:S(2)}, u32[]{:S(2)}) %collective-permute-start.4) | collective-permute-done | bytes 393248 | tf_op jit(solution)/shard_map/ppermute | solution.py:17
  88.3 8.2 %collective-permute-start.6 = (bf16[384,256]{1,0:T(8,128)(2,1)}, bf16[384,256]{1,0:T(8,128)(2,1)S(1)}, u32[]{:S(2)}, u32[]{:S(2)}) collective-permute-start(bf16[384,256]{1,0:T(8,128)(2,1)} %fusion.11), channel_id=1, source_target_pairs={{0,128},{16,144},{32,160},{48,176},{64,192},{80,208},{96,224},{112... | collective-permute-start | bytes 589832 | tf_op jit(solution)/shard_map/ppermute | solution.py:17
  97.5 3.5 %all-gather.5.cloned.1.call-done = bf16[2,2,2,256,256]{4,3,2,1,0:T(8,128)(2,1)} async-done(((bf16[2,2,2,16,256]{4,3,2,1,0:T(8,128)(2,1)}), bf16[2,2,2,256,256]{4,3,2,1,0:T(8,128)(2,1)}) %all-gather.5.cloned.1.call-update) | async-done | bytes 1048592 | tf_op jit(solution)/shard_map/all_gather | solution.py:221
  100.9 1.2 fusion.23
  102.5 2.8 %collective-permute-done.6 = bf16[384,256]{1,0:T(8,128)(2,1)S(1)} collective-permute-done((bf16[384,256]{1,0:T(8,128)(2,1)}, bf16[384,256]{1,0:T(8,128)(2,1)S(1)}, u32[]{:S(2)}, u32[]{:S(2)}) %collective-permute-start.6) | collective-permute-done | bytes 196640 | tf_op jit(solution)/shard_map/ppermute | solution.py:17
  105.6 4.9 %collective-permute-start.7 = (bf16[384,256]{1,0:T(8,128)(2,1)S(1)}, bf16[384,256]{1,0:T(8,128)(2,1)S(1)}, u32[]{:S(2)}, u32[]{:S(2)}) collective-permute-start(bf16[384,256]{1,0:T(8,128)(2,1)S(1)} %fusion.13), channel_id=1, source_target_pairs={{0,256},{16,272},{32,288},{48,304},{64,320},{80,336},{96,352},{112... | collective-permute-start | bytes 589832 | tf_op jit(solution)/shard_map/ppermute | solution.py:17
  111.2 9.2 %collective-permute-done.7 = bf16[384,256]{1,0:T(8,128)(2,1)S(1)} collective-permute-done((bf16[384,256]{1,0:T(8,128)(2,1)S(1)}, bf16[384,256]{1,0:T(8,128)(2,1)S(1)}, u32[]{:S(2)}, u32[]{:S(2)}) %collective-permute-start.7) | collective-permute-done | bytes 196640 | tf_op jit(solution)/shard_map/ppermute | solution.py:17
  121.2 1.2 fusion.34
  123.4 6.6 %collective-permute-start.8 = (bf16[384,256]{1,0:T(8,128)(2,1)S(1)}, bf16[384,256]{1,0:T(8,128)(2,1)S(1)}, u32[]{:S(2)}, u32[]{:S(2)}) collective-permute-start(bf16[384,256]{1,0:T(8,128)(2,1)S(1)} %fusion.14), channel_id=1, source_target_pairs={{0,256},{16,272},{32,288},{48,304},{64,320},{80,336},{96,352},{112... | collective-permute-start | bytes 589832 | tf_op jit(solution)/shard_map/ppermute | solution.py:17
  131.8 5.9 %collective-permute-done.8 = bf16[384,256]{1,0:T(8,128)(2,1)S(1)} collective-permute-done((bf16[384,256]{1,0:T(8,128)(2,1)S(1)}, bf16[384,256]{1,0:T(8,128)(2,1)S(1)}, u32[]{:S(2)}, u32[]{:S(2)}) %collective-permute-start.8) | collective-permute-done | bytes 196640 | tf_op jit(solution)/shard_map/ppermute | solution.py:17
  138.0 2.1 collective-permute-start.9
  140.9 9.4 %collective-permute-done.9 = bf16[384,256]{1,0:T(8,128)(2,1)S(1)} collective-permute-done((bf16[384,256]{1,0:T(8,128)(2,1)S(1)}, bf16[384,256]{1,0:T(8,128)(2,1)S(1)}, u32[]{:S(2)}, u32[]{:S(2)}) %collective-permute-start.9) | collective-permute-done | bytes 196640 | tf_op jit(solution)/shard_map/ppermute | solution.py:17
  150.9 1.9 collective-permute-start.11
  153.8 4.2 %collective-permute-start.10 = (bf16[8,3,2,2,16,256]{5,4,3,2,1,0:T(8,128)(2,1)S(1)}, bf16[8,3,2,2,16,256]{5,4,3,2,1,0:T(8,128)(2,1)S(1)}, u32[]{:S(2)}, u32[]{:S(2)}) collective-permute-start(bf16[8,3,2,2,16,256]{5,4,3,2,1,0:T(8,128)(2,1)S(1)} %select_bitcast_fusion.1), channel_id=1, source_target_pairs={{0,1},{1,0},{2,3},{3,2},{4,5},{5,4},{6,7},{7,6},{8,9},{9,8},{10,11... | collective-permute-start | bytes 2359304 | tf_op jit(solution)/shard_map/ppermute | solution.py:173
  158.0 3.2 %collective-permute-done.11 = bf16[2,384,256]{2,1,0:T(8,128)(2,1)S(1)} collective-permute-done((bf16[2,384,256]{2,1,0:T(8,128)(2,1)S(1)}, bf16[2,384,256]{2,1,0:T(8,128)(2,1)S(1)}, u32[]{:S(2)}, u32[]{:S(2)}) %collective-permute-start.11) | collective-permute-done | bytes 393248 | tf_op jit(solution)/shard_map/ppermute | solution.py:17
  162.6 6.0 %collective-permute-start.12 = (bf16[2,384,256]{2,1,0:T(8,128)(2,1)}, bf16[2,384,256]{2,1,0:T(8,128)(2,1)}, u32[]{:S(2)}, u32[]{:S(2)}) collective-permute-start(bf16[2,384,256]{2,1,0:T(8,128)(2,1)} %convolution_convert_fusion.1), channel_id=1, source_target_pairs={{0,32},{16,48},{32,0},{48,16},{64,96},{80,112},{96,64},{112,80},{1... | collective-permute-start | bytes 1179656 | tf_op jit(solution)/shard_map/ppermute | solution.py:17
  168.6 1.1 convolution_convert_fusion.4
  169.7 1.1 convolution_convert_fusion.3
  170.7 1.3 fusion.3
  172.0 6.8 %all-to-all-start = ((bf16[8,3,2,2,16,256]{5,4,3,2,1,0:T(8,128)(2,1)}), bf16[8,3,2,2,16,256]{5,4,3,2,1,0:T(8,128)(2,1)S(1)}, u32[]{:S(2)}, u32[]{:S(2)}) async-start(bf16[8,3,2,2,16,256]{5,4,3,2,1,0:T(8,128)(2,1)} %fusion.3), calls=%async_computation | async-start | bytes 1572864 | tf_op jit(solution)/shard_map/all_to_all | solution.py:180
  179.5 1.3 fusion.8
  180.8 1.3 convolution_convert_fusion
  182.2 2.2 collective-permute-start.13
  184.7 1.4 convolution_convert_fusion.5
  186.2 6.6 %collective-permute-done.13 = bf16[2,384,256]{2,1,0:T(8,128)(2,1)S(1)} collective-permute-done((bf16[2,384,256]{2,1,0:T(8,128)(2,1)S(1)}, bf16[2,384,256]{2,1,0:T(8,128)(2,1)S(1)}, u32[]{:S(2)}, u32[]{:S(2)}) %collective-permute-start.13) | collective-permute-done | bytes 393248 | tf_op jit(solution)/shard_map/ppermute | solution.py:17
  195.1 4.8 %collective-permute-start.14 = (bf16[8,3,2,2,16,256]{5,4,3,2,1,0:T(8,128)(2,1)}, bf16[8,3,2,2,16,256]{5,4,3,2,1,0:T(8,128)(2,1)}, u32[]{:S(2)}, u32[]{:S(2)}) collective-permute-start(bf16[8,3,2,2,16,256]{5,4,3,2,1,0:T(8,128)(2,1)} %select_bitcast_fusion), channel_id=1, source_target_pairs={{0,1},{1,0},{2,3},{3,2},{4,5},{5,4},{6,7},{7,6},{8,9},{9,8},{10,11... | collective-permute-start | bytes 2359304 | tf_op jit(solution)/shard_map/ppermute | solution.py:173
  199.8 3.8 %collective-permute-start.15 = (bf16[384,256]{1,0:T(8,128)(2,1)}, bf16[384,256]{1,0:T(8,128)(2,1)S(1)}, u32[]{:S(2)}, u32[]{:S(2)}) collective-permute-start(bf16[384,256]{1,0:T(8,128)(2,1)} %get-tuple-element.30), channel_id=1, source_target_pairs={{0,256},{16,272},{32,288},{48,304},{64,320},{80,336},{96,352},{112... | collective-permute-start | bytes 589832 | tf_op jit(solution)/shard_map/ppermute | solution.py:17
  203.6 2.4 fusion.21
  206.8 6.7 %all-to-all-start.1 = ((bf16[8,3,2,2,16,256]{5,4,3,2,1,0:T(8,128)(2,1)}), bf16[8,3,2,2,16,256]{5,4,3,2,1,0:T(8,128)(2,1)S(1)}, u32[]{:S(2)}, u32[]{:S(2)}) async-start(bf16[8,3,2,2,16,256]{5,4,3,2,1,0:T(8,128)(2,1)} %fusion.21), calls=%async_computation.1 | async-start | bytes 1572864 | tf_op jit(solution)/shard_map/all_to_all | solution.py:180
  214.1 5.4 %collective-permute-start.17 = (bf16[2,16,256]{2,1,0:T(8,128)(2,1)S(1)}, bf16[2,16,256]{2,1,0:T(8,128)(2,1)S(1)}, u32[]{:S(2)}, u32[]{:S(2)}) collective-permute-start(bf16[2,16,256]{2,1,0:T(8,128)(2,1)S(1)} %get-tuple-element.36), channel_id=1, source_target_pairs={{0,256},{16,272},{32,288},{48,304},{64,320},{80,336},{96,352},{112... | collective-permute-start | bytes 49160 | tf_op jit(solution)/shard_map/ppermute | solution.py:17
  219.8 4.3 %collective-permute-start.16 = (bf16[384,256]{1,0:T(8,128)(2,1)S(1)}, bf16[384,256]{1,0:T(8,128)(2,1)S(1)}, u32[]{:S(2)}, u32[]{:S(2)}) collective-permute-start(bf16[384,256]{1,0:T(8,128)(2,1)S(1)} %select_select_fusion), channel_id=1, source_target_pairs={{0,128},{16,144},{32,160},{48,176},{64,192},{80,208},{96,224},{112... | collective-permute-start | bytes 589832 | tf_op jit(solution)/shard_map/ppermute | solution.py:17
  225.9 1.9 collective-permute-start.18
  227.8 5.3 %collective-permute-done.16 = bf16[384,256]{1,0:T(8,128)(2,1)S(1)} collective-permute-done((bf16[384,256]{1,0:T(8,128)(2,1)S(1)}, bf16[384,256]{1,0:T(8,128)(2,1)S(1)}, u32[]{:S(2)}, u32[]{:S(2)}) %collective-permute-start.16) | collective-permute-done | bytes 196640 | tf_op jit(solution)/shard_map/ppermute | solution.py:17
  234.1 2.9 %all-to-all-done.1.parts_low = bf16[8,3,2,2,16,256]{5,4,3,2,1,0:T(8,128)(2,1)S(1)} async-done(((bf16[8,3,2,2,16,256]{5,4,3,2,1,0:T(8,128)(2,1)}), bf16[8,3,2,2,16,256]{5,4,3,2,1,0:T(8,128)(2,1)S(1)}, u32[]{:S(2)}, u32[]{:S(2)}) %all-to-all-start.1) | async-done | bytes 786464 | tf_op jit(solution)/shard_map/all_to_all | solution.py:180
  237.0 1.5 shard_map.72
  (151 shorter events, 24.8 us)
Async XLA Ops:
  7.2 55.0 %all-gather.3.cloned.1.call-start = ((), (), s32[]{:S(2)}) async-start(), calls=%async_computation.2 | async-start | bytes 1671168 | tf_op jit(solution)/shard_map/all_gather | solution.py:202
  10.1 90.8 %all-gather.5.cloned.1.call-start = ((), (), s32[]{:S(2)}) async-start(), calls=%async_computation.3 | async-start | bytes 1114112 | tf_op jit(solution)/shard_map/all_gather | solution.py:221
  11.2 28.7 %collective-permute-start = (bf16[448,256]{1,0:T(8,128)(2,1)S(1)}, bf16[448,256]{1,0:T(8,128)(2,1)S(1)}, u32[]{:S(2)}, u32[]{:S(2)}) collective-permute-start(bf16[448,256]{1,0:T(8,128)(2,1)S(1)} %shard_map.68), channel_id=1, source_target_pairs={{0,128},{16,144},{32,160},{48,176},{64,192},{80,208},{96,224},{112... | collective-permute-start | bytes 688136 | tf_op jit(solution)/shard_map/ppermute | solution.py:17
  18.9 21.0 %copy-start.11 = (bf16[1,384,256]{2,1,0:T(8,128)(2,1)}, bf16[1,384,256]{2,1,0:T(8,128)(2,1)S(1)}, u32[]{:S(2)}) copy-start(bf16[1,384,256]{2,1,0:T(8,128)(2,1)S(1)} %get-tuple-element.32) | copy-start | bytes 589828
  19.0 21.0 %copy-start.1 = (bf16[384,512]{1,0:T(8,128)(2,1)S(1)}, bf16[384,512]{1,0:T(8,128)(2,1)}, u32[]{:S(2)}) copy-start(bf16[384,512]{1,0:T(8,128)(2,1)} %cotangent.3) | copy-start | bytes 1179652
  19.0 21.0 %copy-start.4 = (s32[6,64]{1,0:T(8,128)S(1)}, s32[6,64]{1,0:T(8,128)}, u32[]{:S(2)}) copy-start(s32[6,64]{1,0:T(8,128)} %matchings.9) | copy-start | bytes 4612
  19.0 30.3 %copy-start.5 = (bf16[2,384,256]{2,1,0:T(8,128)(2,1)}, bf16[2,384,256]{2,1,0:T(8,128)(2,1)S(1)}, u32[]{:S(2)}) copy-start(bf16[2,384,256]{2,1,0:T(8,128)(2,1)S(1)} %rev.3) | copy-start | bytes 1179652
  40.6 21.5 %collective-permute-start.1 = (bf16[384,256]{1,0:T(8,128)(2,1)S(1)}, bf16[384,256]{1,0:T(8,128)(2,1)S(1)}, u32[]{:S(2)}, u32[]{:S(2)}) collective-permute-start(bf16[384,256]{1,0:T(8,128)(2,1)S(1)} %get-tuple-element.14), channel_id=1, source_target_pairs={{0,256},{16,272},{32,288},{48,304},{64,320},{80,336},{96,352},{112... | collective-permute-start | bytes 589832 | tf_op jit(solution)/shard_map/ppermute | solution.py:17
  49.3 15.8 %copy-start.13 = (bf16[2,384,256]{2,1,0:T(8,128)(2,1)}, bf16[2,384,256]{2,1,0:T(8,128)(2,1)S(1)}, u32[]{:S(2)}) copy-start(bf16[2,384,256]{2,1,0:T(8,128)(2,1)S(1)} %fusion.4) | copy-start | bytes 1179652
  49.3 14.2 %collective-permute-start.2 = (bf16[2,384,256]{2,1,0:T(8,128)(2,1)S(1)}, bf16[2,384,256]{2,1,0:T(8,128)(2,1)}, u32[]{:S(2)}, u32[]{:S(2)}) collective-permute-start(bf16[2,384,256]{2,1,0:T(8,128)(2,1)S(1)} %fusion.4), channel_id=1, source_target_pairs={{0,16},{16,0},{32,48},{48,32},{64,80},{80,64},{96,112},{112,96},{1... | collective-permute-start | bytes 1179656 | tf_op jit(solution)/shard_map/ppermute | solution.py:17
  52.4 8.4 %collective-permute-start.5 = (bf16[2,16,256]{2,1,0:T(8,128)(2,1)S(1)}, bf16[2,16,256]{2,1,0:T(8,128)(2,1)S(1)}, u32[]{:S(2)}, u32[]{:S(2)}) collective-permute-start(bf16[2,16,256]{2,1,0:T(8,128)(2,1)S(1)} %get-tuple-element.20), channel_id=1, source_target_pairs={{0,256},{16,272},{32,288},{48,304},{64,320},{80,336},{96,352},{112... | collective-permute-start | bytes 49160 | tf_op jit(solution)/shard_map/ppermute | solution.py:17
  62.1 3.1 %copy-start.27 = (bf16[384,256]{1,0:T(8,128)(2,1)}, bf16[384,256]{1,0:T(8,128)(2,1)S(1)}, u32[]{:S(2)}) copy-start(bf16[384,256]{1,0:T(8,128)(2,1)S(1)} %collective-permute-done.1) | copy-start | bytes 589828
  63.3 6.4 %copy-start.9 = (bf16[2,2,256,256]{3,2,1,0:T(8,128)(2,1)}, bf16[2,2,256,256]{3,2,1,0:T(8,128)(2,1)S(1)}, u32[]{:S(2)}) copy-start(bf16[2,2,256,256]{3,2,1,0:T(8,128)(2,1)S(1)} %fusion.26) | copy-start | bytes 1572868
  63.3 6.4 %copy-start.19 = (bf16[3,2,2,256,256]{4,3,2,1,0:T(8,128)(2,1)S(1)}, bf16[3,2,2,256,256]{4,3,2,1,0:T(8,128)(2,1)}, u32[]{:S(2)}) copy-start(bf16[3,2,2,256,256]{4,3,2,1,0:T(8,128)(2,1)} %all-gather.3.cloned.1.call-done) | copy-start | bytes 4718596
  65.2 12.1 %collective-permute-start.3 = (bf16[2,384,256]{2,1,0:T(8,128)(2,1)S(1)}, bf16[2,384,256]{2,1,0:T(8,128)(2,1)S(1)}, u32[]{:S(2)}, u32[]{:S(2)}) collective-permute-start(bf16[2,384,256]{2,1,0:T(8,128)(2,1)S(1)} %broadcast_select_fusion.2), channel_id=1, source_target_pairs={{0,32},{16,48},{32,0},{48,16},{64,96},{80,112},{96,64},{112,80},{1... | collective-permute-start | bytes 1179656 | tf_op jit(solution)/shard_map/ppermute | solution.py:17
  77.3 3.8 %copy-start.15 = (bf16[2,384,256]{2,1,0:T(8,128)(2,1)}, bf16[2,384,256]{2,1,0:T(8,128)(2,1)S(1)}, u32[]{:S(2)}) copy-start(bf16[2,384,256]{2,1,0:T(8,128)(2,1)S(1)} %collective-permute-done.3) | copy-start | bytes 1179652
  77.6 10.7 %copy-start.17 = (bf16[2,384,256]{2,1,0:T(8,128)(2,1)}, bf16[2,384,256]{2,1,0:T(8,128)(2,1)S(1)}, u32[]{:S(2)}) copy-start(bf16[2,384,256]{2,1,0:T(8,128)(2,1)S(1)} %fusion.6) | copy-start | bytes 1179652
  77.6 9.8 %collective-permute-start.4 = (bf16[2,384,256]{2,1,0:T(8,128)(2,1)S(1)}, bf16[2,384,256]{2,1,0:T(8,128)(2,1)S(1)}, u32[]{:S(2)}, u32[]{:S(2)}) collective-permute-start(bf16[2,384,256]{2,1,0:T(8,128)(2,1)S(1)} %fusion.6), channel_id=1, source_target_pairs={{0,64},{16,80},{32,96},{48,112},{64,0},{80,16},{96,32},{112,48},{1... | collective-permute-start | bytes 1179656 | tf_op jit(solution)/shard_map/ppermute | solution.py:17
  80.9 16.5 %copy-start.7 = (bf16[2,2,256,256]{3,2,1,0:T(8,128)(2,1)}, bf16[2,2,256,256]{3,2,1,0:T(8,128)(2,1)S(1)}, u32[]{:S(2)}) copy-start(bf16[2,2,256,256]{3,2,1,0:T(8,128)(2,1)S(1)} %fusion.24) | copy-start | bytes 1572868
  87.4 9.8 %copy-start.25 = (bf16[2,384,256]{2,1,0:T(8,128)(2,1)}, bf16[2,384,256]{2,1,0:T(8,128)(2,1)S(1)}, u32[]{:S(2)}) copy-start(bf16[2,384,256]{2,1,0:T(8,128)(2,1)S(1)} %collective-permute-done.4) | copy-start | bytes 1179652
  88.3 17.0 %collective-permute-start.6 = (bf16[384,256]{1,0:T(8,128)(2,1)}, bf16[384,256]{1,0:T(8,128)(2,1)S(1)}, u32[]{:S(2)}, u32[]{:S(2)}) collective-permute-start(bf16[384,256]{1,0:T(8,128)(2,1)} %fusion.11), channel_id=1, source_target_pairs={{0,128},{16,144},{32,160},{48,176},{64,192},{80,208},{96,224},{112... | collective-permute-start | bytes 589832 | tf_op jit(solution)/shard_map/ppermute | solution.py:17
  100.9 9.6 %copy-start.24 = (bf16[2,2,2,256,256]{4,3,2,1,0:T(8,128)(2,1)S(1)}, bf16[2,2,2,256,256]{4,3,2,1,0:T(8,128)(2,1)}, u32[]{:S(2)}) copy-start(bf16[2,2,2,256,256]{4,3,2,1,0:T(8,128)(2,1)} %all-gather.5.cloned.1.call-done) | copy-start | bytes 3145732
  105.6 14.9 %collective-permute-start.7 = (bf16[384,256]{1,0:T(8,128)(2,1)S(1)}, bf16[384,256]{1,0:T(8,128)(2,1)S(1)}, u32[]{:S(2)}, u32[]{:S(2)}) collective-permute-start(bf16[384,256]{1,0:T(8,128)(2,1)S(1)} %fusion.13), channel_id=1, source_target_pairs={{0,256},{16,272},{32,288},{48,304},{64,320},{80,336},{96,352},{112... | collective-permute-start | bytes 589832 | tf_op jit(solution)/shard_map/ppermute | solution.py:17
  111.0 10.2 %copy-start.28 = (bf16[384,256]{1,0:T(8,128)(2,1)S(1)}, bf16[384,256]{1,0:T(8,128)(2,1)}, u32[]{:S(2)}) copy-start(bf16[384,256]{1,0:T(8,128)(2,1)} %copy-done.27) | copy-start | bytes 589828
  123.4 14.3 %collective-permute-start.8 = (bf16[384,256]{1,0:T(8,128)(2,1)S(1)}, bf16[384,256]{1,0:T(8,128)(2,1)S(1)}, u32[]{:S(2)}, u32[]{:S(2)}) collective-permute-start(bf16[384,256]{1,0:T(8,128)(2,1)S(1)} %fusion.14), channel_id=1, source_target_pairs={{0,256},{16,272},{32,288},{48,304},{64,320},{80,336},{96,352},{112... | collective-permute-start | bytes 589832 | tf_op jit(solution)/shard_map/ppermute | solution.py:17
  131.8 18.4 %copy-start.18 = (bf16[2,384,256]{2,1,0:T(8,128)(2,1)S(1)}, bf16[2,384,256]{2,1,0:T(8,128)(2,1)}, u32[]{:S(2)}) copy-start(bf16[2,384,256]{2,1,0:T(8,128)(2,1)} %copy-done.17) | copy-start | bytes 1179652
  138.0 12.6 %copy-start.8 = (bf16[2,2,256,256]{3,2,1,0:T(8,128)(2,1)S(1)}, bf16[2,2,256,256]{3,2,1,0:T(8,128)(2,1)}, u32[]{:S(2)}) copy-start(bf16[2,2,256,256]{3,2,1,0:T(8,128)(2,1)} %copy-done.7) | copy-start | bytes 1572868
  138.0 12.2 %collective-permute-start.9 = (bf16[384,256]{1,0:T(8,128)(2,1)S(1)}, bf16[384,256]{1,0:T(8,128)(2,1)S(1)}, u32[]{:S(2)}, u32[]{:S(2)}) collective-permute-start(bf16[384,256]{1,0:T(8,128)(2,1)S(1)} %fusion.17), channel_id=1, source_target_pairs={{0,128},{16,144},{32,160},{48,176},{64,192},{80,208},{96,224},{112... | collective-permute-start | bytes 589832 | tf_op jit(solution)/shard_map/ppermute | solution.py:17
  140.6 12.3 %copy-start.26 = (bf16[2,384,256]{2,1,0:T(8,128)(2,1)S(1)}, bf16[2,384,256]{2,1,0:T(8,128)(2,1)}, u32[]{:S(2)}) copy-start(bf16[2,384,256]{2,1,0:T(8,128)(2,1)} %copy-done.25) | copy-start | bytes 1179652
  150.9 10.3 %collective-permute-start.11 = (bf16[2,384,256]{2,1,0:T(8,128)(2,1)S(1)}, bf16[2,384,256]{2,1,0:T(8,128)(2,1)S(1)}, u32[]{:S(2)}, u32[]{:S(2)}) collective-permute-start(bf16[2,384,256]{2,1,0:T(8,128)(2,1)S(1)} %convolution_convert_fusion.2), channel_id=1, source_target_pairs={{0,64},{16,80},{32,96},{48,112},{64,0},{80,16},{96,32},{112,48},{1... | collective-permute-start | bytes 1179656 | tf_op jit(solution)/shard_map/ppermute | solution.py:17
  153.8 15.9 %copy-start.16 = (bf16[2,384,256]{2,1,0:T(8,128)(2,1)S(1)}, bf16[2,384,256]{2,1,0:T(8,128)(2,1)}, u32[]{:S(2)}) copy-start(bf16[2,384,256]{2,1,0:T(8,128)(2,1)} %copy-done.15) | copy-start | bytes 1179652
  153.8 16.9 %collective-permute-start.10 = (bf16[8,3,2,2,16,256]{5,4,3,2,1,0:T(8,128)(2,1)S(1)}, bf16[8,3,2,2,16,256]{5,4,3,2,1,0:T(8,128)(2,1)S(1)}, u32[]{:S(2)}, u32[]{:S(2)}) collective-permute-start(bf16[8,3,2,2,16,256]{5,4,3,2,1,0:T(8,128)(2,1)S(1)} %select_bitcast_fusion.1), channel_id=1, source_target_pairs={{0,1},{1,0},{2,3},{3,2},{4,5},{5,4},{6,7},{7,6},{8,9},{9,8},{10,11... | collective-permute-start | bytes 2359304 | tf_op jit(solution)/shard_map/ppermute | solution.py:173
  162.6 17.0 %collective-permute-start.12 = (bf16[2,384,256]{2,1,0:T(8,128)(2,1)}, bf16[2,384,256]{2,1,0:T(8,128)(2,1)}, u32[]{:S(2)}, u32[]{:S(2)}) collective-permute-start(bf16[2,384,256]{2,1,0:T(8,128)(2,1)} %convolution_convert_fusion.1), channel_id=1, source_target_pairs={{0,32},{16,48},{32,0},{48,16},{64,96},{80,112},{96,64},{112,80},{1... | collective-permute-start | bytes 1179656 | tf_op jit(solution)/shard_map/ppermute | solution.py:17
  172.0 31.6 %all-to-all-start = ((bf16[8,3,2,2,16,256]{5,4,3,2,1,0:T(8,128)(2,1)}), bf16[8,3,2,2,16,256]{5,4,3,2,1,0:T(8,128)(2,1)S(1)}, u32[]{:S(2)}, u32[]{:S(2)}) async-start(bf16[8,3,2,2,16,256]{5,4,3,2,1,0:T(8,128)(2,1)} %fusion.3), calls=%async_computation | async-start | bytes 1572864 | tf_op jit(solution)/shard_map/all_to_all | solution.py:180
  178.8 5.6 %copy-start.14 = (bf16[2,384,256]{2,1,0:T(8,128)(2,1)S(1)}, bf16[2,384,256]{2,1,0:T(8,128)(2,1)}, u32[]{:S(2)}) copy-start(bf16[2,384,256]{2,1,0:T(8,128)(2,1)} %copy-done.13) | copy-start | bytes 1179652
  180.8 11.9 %copy-start.10 = (bf16[2,2,256,256]{3,2,1,0:T(8,128)(2,1)S(1)}, bf16[2,2,256,256]{3,2,1,0:T(8,128)(2,1)}, u32[]{:S(2)}) copy-start(bf16[2,2,256,256]{3,2,1,0:T(8,128)(2,1)} %copy-done.9) | copy-start | bytes 1572868
  182.2 10.6 %collective-permute-start.13 = (bf16[2,384,256]{2,1,0:T(8,128)(2,1)S(1)}, bf16[2,384,256]{2,1,0:T(8,128)(2,1)S(1)}, u32[]{:S(2)}, u32[]{:S(2)}) collective-permute-start(bf16[2,384,256]{2,1,0:T(8,128)(2,1)S(1)} %convolution_convert_fusion), channel_id=1, source_target_pairs={{0,16},{16,0},{32,48},{48,32},{64,80},{80,64},{96,112},{112,96},{1... | collective-permute-start | bytes 1179656 | tf_op jit(solution)/shard_map/ppermute | solution.py:17
  184.7 8.3 %copy-start.6 = (bf16[2,384,256]{2,1,0:T(8,128)(2,1)S(1)}, bf16[2,384,256]{2,1,0:T(8,128)(2,1)}, u32[]{:S(2)}) copy-start(bf16[2,384,256]{2,1,0:T(8,128)(2,1)} %copy-done.5) | copy-start | bytes 1179652
  186.1 7.3 %copy-start.12 = (bf16[1,384,256]{2,1,0:T(8,128)(2,1)S(1)}, bf16[1,384,256]{2,1,0:T(8,128)(2,1)}, u32[]{:S(2)}) copy-start(bf16[1,384,256]{2,1,0:T(8,128)(2,1)} %copy-done.11) | copy-start | bytes 589828
  186.1 7.7 %copy-start.22 = (bf16[2,256,256]{2,1,0:T(8,128)(2,1)S(1)}, bf16[2,256,256]{2,1,0:T(8,128)(2,1)}, u32[]{:S(2)}) copy-start(bf16[2,256,256]{2,1,0:T(8,128)(2,1)} %convolution_convert_fusion.4) | copy-start | bytes 786436
  186.1 7.7 %copy-start.23 = (bf16[2,256,256]{2,1,0:T(8,128)(2,1)S(1)}, bf16[2,256,256]{2,1,0:T(8,128)(2,1)}, u32[]{:S(2)}) copy-start(bf16[2,256,256]{2,1,0:T(8,128)(2,1)} %convolution_convert_fusion.3) | copy-start | bytes 786436
  195.1 8.6 %collective-permute-start.14 = (bf16[8,3,2,2,16,256]{5,4,3,2,1,0:T(8,128)(2,1)}, bf16[8,3,2,2,16,256]{5,4,3,2,1,0:T(8,128)(2,1)}, u32[]{:S(2)}, u32[]{:S(2)}) collective-permute-start(bf16[8,3,2,2,16,256]{5,4,3,2,1,0:T(8,128)(2,1)} %select_bitcast_fusion), channel_id=1, source_target_pairs={{0,1},{1,0},{2,3},{3,2},{4,5},{5,4},{6,7},{7,6},{8,9},{9,8},{10,11... | collective-permute-start | bytes 2359304 | tf_op jit(solution)/shard_map/ppermute | solution.py:173
  199.8 19.8 %collective-permute-start.15 = (bf16[384,256]{1,0:T(8,128)(2,1)}, bf16[384,256]{1,0:T(8,128)(2,1)S(1)}, u32[]{:S(2)}, u32[]{:S(2)}) collective-permute-start(bf16[384,256]{1,0:T(8,128)(2,1)} %get-tuple-element.30), channel_id=1, source_target_pairs={{0,256},{16,272},{32,288},{48,304},{64,320},{80,336},{96,352},{112... | collective-permute-start | bytes 589832 | tf_op jit(solution)/shard_map/ppermute | solution.py:17
  206.0 13.5 %copy-start.21 = (bf16[2,384,256]{2,1,0:T(8,128)(2,1)S(1)}, bf16[2,384,256]{2,1,0:T(8,128)(2,1)}, u32[]{:S(2)}) copy-start(bf16[2,384,256]{2,1,0:T(8,128)(2,1)} %copy-done.20) | copy-start | bytes 1179652
  206.8 30.2 %all-to-all-start.1 = ((bf16[8,3,2,2,16,256]{5,4,3,2,1,0:T(8,128)(2,1)}), bf16[8,3,2,2,16,256]{5,4,3,2,1,0:T(8,128)(2,1)S(1)}, u32[]{:S(2)}, u32[]{:S(2)}) async-start(bf16[8,3,2,2,16,256]{5,4,3,2,1,0:T(8,128)(2,1)} %fusion.21), calls=%async_computation.1 | async-start | bytes 1572864 | tf_op jit(solution)/shard_map/all_to_all | solution.py:180
  214.1 11.7 %collective-permute-start.17 = (bf16[2,16,256]{2,1,0:T(8,128)(2,1)S(1)}, bf16[2,16,256]{2,1,0:T(8,128)(2,1)S(1)}, u32[]{:S(2)}, u32[]{:S(2)}) collective-permute-start(bf16[2,16,256]{2,1,0:T(8,128)(2,1)S(1)} %get-tuple-element.36), channel_id=1, source_target_pairs={{0,256},{16,272},{32,288},{48,304},{64,320},{80,336},{96,352},{112... | collective-permute-start | bytes 49160 | tf_op jit(solution)/shard_map/ppermute | solution.py:17
  219.8 13.3 %collective-permute-start.16 = (bf16[384,256]{1,0:T(8,128)(2,1)S(1)}, bf16[384,256]{1,0:T(8,128)(2,1)S(1)}, u32[]{:S(2)}, u32[]{:S(2)}) collective-permute-start(bf16[384,256]{1,0:T(8,128)(2,1)S(1)} %select_select_fusion), channel_id=1, source_target_pairs={{0,128},{16,144},{32,160},{48,176},{64,192},{80,208},{96,224},{112... | collective-permute-start | bytes 589832 | tf_op jit(solution)/shard_map/ppermute | solution.py:17
  225.9 8.2 %collective-permute-start.18 = (bf16[2,2,16,256]{3,2,1,0:T(8,128)(2,1)S(1)}, bf16[2,2,16,256]{3,2,1,0:T(8,128)(2,1)S(1)}, u32[]{:S(2)}, u32[]{:S(2)}) collective-permute-start(bf16[2,2,16,256]{3,2,1,0:T(8,128)(2,1)S(1)} %get-tuple-element.33), channel_id=1, source_target_pairs={{0,128},{16,144},{32,160},{48,176},{64,192},{80,208},{96,224},{112... | collective-permute-start | bytes 98312 | tf_op jit(solution)/shard_map/ppermute | solution.py:17
  (4 other events, 3.4 us)
Sparse Core Ops, SparseCore 0:
  10.7 47.7 all-gather.2
  62.2 38.6 all-gather.4

commit v12 on v10

--- a/solution.py
+++ b/solution.py
@@ -232,10 +232,11 @@
             keep = (dot(value[0], own_w[0]) + dot(other[0], other_w[0])).astype(bf16)
     came = flip(send, 3)
     inputs.append((keep, came))
-    full[4] = after(full[4], send)
-    own_w, other_w = full[4][0], full[4][1]
-    send = (dot(keep, own_w[1]) + dot(came, other_w[1])).astype(bf16)
-    keep = (dot(keep, own_w[0]) + dot(came, other_w[0])).astype(bf16)
+    send_w = after(full[4][:, 1], send)
+    send = (dot(keep, send_w[0]) + dot(came, send_w[1])).astype(bf16)
+    keep_w = after(full[4][:, 0], send)
+    keep = (dot(keep, keep_w[0]) + dot(came, keep_w[1])).astype(bf16)
+    full[4] = [[keep_w[slot], send_w[slot]] for slot in range(2)]
     came = flip(send, 4)
     inputs.append((keep, came))
     full[5] = after(full[5], send)

time: 240 us -> 317 us (1.32)
  waiting for transfers between devices: 60.1 us -> 147 us
  starting transfers between devices: 101 us -> 91.4 us
  local copies, waits for them, and re-layouts: 3.06 us -> 6.71 us
    all_gather x1, waiting for transfers between devices: 0.84 us -> 42.1 us  [body(): full += list(lax.all_gather(rest, 'tok', axis=3, tiled=True))]
    ppermute x16, waiting for transfers between devices: 49.3 us -> 84.1 us  [flip(): return lax.ppermute(value, 'blk', pairs)]
    ppermute x16, starting transfers between devices: 82.2 us -> 72.9 us  [flip(): return lax.ppermute(value, 'blk', pairs)]
    all_gather x1, waiting for transfers between devices: 9.43 us -> 18.1 us  [body(): full += list(lax.all_gather(late, 'tok', axis=3, tiled=True))]
  transfers between devices with their start and end apart: 22 -> 22, of which waited for: 14 -> 14; matrix products, arithmetic and copies ran while one was open for 12% -> 8% of each run, Pallas kernels for 1% -> 0%
where the time goes in v12:
time: 317 us; the launch traced here: 316 us
  waiting for transfers between devices  147 us (46%)
  starting transfers between devices  91.4 us (29%)
  blocking collectives  21.3 us (7%)
  matrix products  19.9 us (6%)
  between operations  14.8 us (5%)
  other arithmetic  9.7 us (3%)
  local copies, waits for them, and re-layouts  6.71 us (2%)
  Pallas kernels  5.36 us (2%)
    ppermute x16, waiting for transfers between devices, flip(): return lax.ppermute(value, 'blk', pairs)  84.1 us
    ppermute x16, starting transfers between devices, flip(): return lax.ppermute(value, 'blk', pairs)  72.9 us
    all_gather x1, waiting for transfers between devices, body(): full += list(lax.all_gather(rest, 'tok', axis=3, tiled=True))  42.1 us
    all_gather x1, blocking collectives, body(): full = list(lax.all_gather(first, 'tok', axis=3, tiled=True))  21.3 us
    all_gather x1, waiting for transfers between devices, body(): full += list(lax.all_gather(late, 'tok', axis=3, tiled=True))  18.1 us
    all_to_all x2, starting transfers between devices, all_parts(): return lax.all_to_all(chip, 'tok', 0, 0, axis_index_groups=groups)  11 us
    ppermute x2, starting transfers between devices, chip_sum(): lax.ppermute(core_half(terms, 1 - core), 'tok', [(source, source ^ 1) for...  7.5 us
    dot_general x16, matrix products, dot_rows(): jnp.einsum('...tk,...tl->...kl', left, right, preferred_element_type=jnp....  7.35 us
  transfers between devices with their start and end apart: 22, of which 14 were waited for; matrix products, arithmetic and copies ran while one was open for 8% of the time, Pallas kernels for 0%

profile of v12, /device:TPU:1, one launch (start us, length us, event | category | flops | bytes accessed | tf_op | source)
XLA Modules:
  0.0 315.8 jit_solution(77154274709948877)
XLA Ops:
  8.8 1.3 shard_map.67
  11.1 6.8 %collective-permute-start.2 = (bf16[448,256]{1,0:T(8,128)(2,1)S(1)}, bf16[448,256]{1,0:T(8,128)(2,1)S(1)}, u32[]{:S(2)}, u32[]{:S(2)}) collective-permute-start(bf16[448,256]{1,0:T(8,128)(2,1)S(1)} %shard_map.68), channel_id=1, source_target_pairs={{0,128},{16,144},{32,160},{48,176},{64,192},{80,208},{96,224},{112... | collective-permute-start | bytes 688136 | tf_op jit(solution)/shard_map/ppermute | solution.py:17
  17.9 9.1 %collective-permute-done.2.came = bf16[448,256]{1,0:T(8,128)(2,1)S(1)} collective-permute-done((bf16[448,256]{1,0:T(8,128)(2,1)S(1)}, bf16[448,256]{1,0:T(8,128)(2,1)S(1)}, u32[]{:S(2)}, u32[]{:S(2)}) %collective-permute-start.2) | collective-permute-done | bytes 229408 | tf_op jit(solution)/shard_map/ppermute | solution.py:17
  29.4 10.0 %collective-permute-start.4 = (bf16[416,256]{1,0:T(8,128)(2,1)S(1)}, bf16[416,256]{1,0:T(8,128)(2,1)S(1)}, u32[]{:S(2)}, u32[]{:S(2)}) collective-permute-start(bf16[416,256]{1,0:T(8,128)(2,1)S(1)} %get-tuple-element.18), channel_id=1, source_target_pairs={{0,256},{16,272},{32,288},{48,304},{64,320},{80,336},{96,352},{112... | collective-permute-start | bytes 638984 | tf_op jit(solution)/shard_map/ppermute | solution.py:17
  39.4 7.0 %collective-permute-done.4.came = bf16[416,256]{1,0:T(8,128)(2,1)S(1)} collective-permute-done((bf16[416,256]{1,0:T(8,128)(2,1)S(1)}, bf16[416,256]{1,0:T(8,128)(2,1)S(1)}, u32[]{:S(2)}, u32[]{:S(2)}) %collective-permute-start.4) | collective-permute-done | bytes 213024 | tf_op jit(solution)/shard_map/ppermute | solution.py:17
  46.4 1.2 shard_map.70
  48.6 21.3 %all_gather.9 = bf16[1,2,2,256,256]{4,3,2,1,0:T(8,128)(2,1)S(1)} all-gather(bf16[1,2,2,16,256]{4,3,2,1,0:T(8,128)(2,1)S(1)} %get-tuple-element.11), channel_id=1, replica_groups=mesh['blk'=32,'tok'=16] {'tok'}, dimensions={3}, use_global_device_ids=true | all-gather | bytes 557056 | tf_op jit(solution)/shard_map/all_gather | solution.py:201
  70.5 3.1 collective-permute-start
  73.6 18.1 %all-gather.5.cloned.1.call-done = bf16[2,2,2,256,256]{4,3,2,1,0:T(8,128)(2,1)} async-done(((bf16[2,2,2,16,256]{4,3,2,1,0:T(8,128)(2,1)}), bf16[2,2,2,256,256]{4,3,2,1,0:T(8,128)(2,1)}) %all-gather.5.cloned.1.call-update) | async-done | bytes 1048592 | tf_op jit(solution)/shard_map/all_gather | solution.py:221
  91.7 1.1 slice_bitcast_fusion.1
  92.8 42.1 %all-gather.3.cloned.1.call-done = bf16[3,2,2,256,256]{4,3,2,1,0:T(8,128)(2,1)} async-done(((bf16[3,2,2,16,256]{4,3,2,1,0:T(8,128)(2,1)}), bf16[3,2,2,256,256]{4,3,2,1,0:T(8,128)(2,1)}) %all-gather.3.cloned.1.call-update) | async-done | bytes 1572880 | tf_op jit(solution)/shard_map/all_gather | solution.py:202
  134.9 1.1 fusion.25
  136.3 1.4 fusion.5
  137.7 4.6 %collective-permute-start.1 = (bf16[2,384,256]{2,1,0:T(8,128)(2,1)S(1)}, bf16[2,384,256]{2,1,0:T(8,128)(2,1)S(1)}, u32[]{:S(2)}, u32[]{:S(2)}) collective-permute-start(bf16[2,384,256]{2,1,0:T(8,128)(2,1)S(1)} %fusion.5), channel_id=1, source_target_pairs={{0,32},{16,48},{32,0},{48,16},{64,96},{80,112},{96,64},{112,80},{1... | collective-permute-start | bytes 1179656 | tf_op jit(solution)/shard_map/ppermute | solution.py:17
  142.7 8.9 %collective-permute-done.1 = bf16[2,384,256]{2,1,0:T(8,128)(2,1)S(1)} collective-permute-done((bf16[2,384,256]{2,1,0:T(8,128)(2,1)S(1)}, bf16[2,384,256]{2,1,0:T(8,128)(2,1)S(1)}, u32[]{:S(2)}, u32[]{:S(2)}) %collective-permute-start.1) | collective-permute-done | bytes 393248 | tf_op jit(solution)/shard_map/ppermute | solution.py:17
  151.9 3.3 %collective-permute-start.3 = (bf16[2,384,256]{2,1,0:T(8,128)(2,1)S(1)}, bf16[2,384,256]{2,1,0:T(8,128)(2,1)S(1)}, u32[]{:S(2)}, u32[]{:S(2)}) collective-permute-start(bf16[2,384,256]{2,1,0:T(8,128)(2,1)S(1)} %fusion.6), channel_id=1, source_target_pairs={{0,64},{16,80},{32,96},{48,112},{64,0},{80,16},{96,32},{112,48},{1... | collective-permute-start | bytes 1179656 | tf_op jit(solution)/shard_map/ppermute | solution.py:17
  155.6 7.6 %collective-permute-done.3 = bf16[2,384,256]{2,1,0:T(8,128)(2,1)S(1)} collective-permute-done((bf16[2,384,256]{2,1,0:T(8,128)(2,1)S(1)}, bf16[2,384,256]{2,1,0:T(8,128)(2,1)S(1)}, u32[]{:S(2)}, u32[]{:S(2)}) %collective-permute-start.3) | collective-permute-done | bytes 393248 | tf_op jit(solution)/shard_map/ppermute | solution.py:17
  163.5 4.4 %collective-permute-start.5 = (bf16[384,256]{1,0:T(8,128)(2,1)S(1)}, bf16[384,256]{1,0:T(8,128)(2,1)S(1)}, u32[]{:S(2)}, u32[]{:S(2)}) collective-permute-start(bf16[384,256]{1,0:T(8,128)(2,1)S(1)} %fusion.11), channel_id=1, source_target_pairs={{0,128},{16,144},{32,160},{48,176},{64,192},{80,208},{96,224},{112... | collective-permute-start | bytes 589832 | tf_op jit(solution)/shard_map/ppermute | solution.py:17
  168.4 7.9 %collective-permute-done.5 = bf16[384,256]{1,0:T(8,128)(2,1)S(1)} collective-permute-done((bf16[384,256]{1,0:T(8,128)(2,1)S(1)}, bf16[384,256]{1,0:T(8,128)(2,1)S(1)}, u32[]{:S(2)}, u32[]{:S(2)}) %collective-permute-start.5) | collective-permute-done | bytes 196640 | tf_op jit(solution)/shard_map/ppermute | solution.py:17
  176.5 8.5 %collective-permute-start.6 = (bf16[384,256]{1,0:T(8,128)(2,1)S(1)}, bf16[384,256]{1,0:T(8,128)(2,1)S(1)}, u32[]{:S(2)}, u32[]{:S(2)}) collective-permute-start(bf16[384,256]{1,0:T(8,128)(2,1)S(1)} %fusion.12), channel_id=1, source_target_pairs={{0,256},{16,272},{32,288},{48,304},{64,320},{80,336},{96,352},{112... | collective-permute-start | bytes 589832 | tf_op jit(solution)/shard_map/ppermute | solution.py:17
  186.0 6.5 %collective-permute-done.6 = bf16[384,256]{1,0:T(8,128)(2,1)S(1)} collective-permute-done((bf16[384,256]{1,0:T(8,128)(2,1)S(1)}, bf16[384,256]{1,0:T(8,128)(2,1)S(1)}, u32[]{:S(2)}, u32[]{:S(2)}) %collective-permute-start.6) | collective-permute-done | bytes 196640 | tf_op jit(solution)/shard_map/ppermute | solution.py:17
  193.3 1.2 fusion.33
  195.5 5.3 %collective-permute-start.7 = (bf16[384,256]{1,0:T(8,128)(2,1)S(1)}, bf16[384,256]{1,0:T(8,128)(2,1)S(1)}, u32[]{:S(2)}, u32[]{:S(2)}) collective-permute-start(bf16[384,256]{1,0:T(8,128)(2,1)S(1)} %fusion.14), channel_id=1, source_target_pairs={{0,256},{16,272},{32,288},{48,304},{64,320},{80,336},{96,352},{112... | collective-permute-start | bytes 589832 | tf_op jit(solution)/shard_map/ppermute | solution.py:17
  202.6 7.8 %collective-permute-done.7 = bf16[384,256]{1,0:T(8,128)(2,1)S(1)} collective-permute-done((bf16[384,256]{1,0:T(8,128)(2,1)S(1)}, bf16[384,256]{1,0:T(8,128)(2,1)S(1)}, u32[]{:S(2)}, u32[]{:S(2)}) %collective-permute-start.7) | collective-permute-done | bytes 196640 | tf_op jit(solution)/shard_map/ppermute | solution.py:17
  210.7 1.9 collective-permute-start.8
  213.4 10.3 %collective-permute-done.8 = bf16[384,256]{1,0:T(8,128)(2,1)S(1)} collective-permute-done((bf16[384,256]{1,0:T(8,128)(2,1)S(1)}, bf16[384,256]{1,0:T(8,128)(2,1)S(1)}, u32[]{:S(2)}, u32[]{:S(2)}) %collective-permute-start.8) | collective-permute-done | bytes 196640 | tf_op jit(solution)/shard_map/ppermute | solution.py:17
  224.4 1.9 collective-permute-start.10
  227.2 2.4 collective-permute-start.9
  229.6 6.8 %collective-permute-done.10 = bf16[2,384,256]{2,1,0:T(8,128)(2,1)S(1)} collective-permute-done((bf16[2,384,256]{2,1,0:T(8,128)(2,1)S(1)}, bf16[2,384,256]{2,1,0:T(8,128)(2,1)S(1)}, u32[]{:S(2)}, u32[]{:S(2)}) %collective-permute-start.10) | collective-permute-done | bytes 393248 | tf_op jit(solution)/shard_map/ppermute | solution.py:17
  237.8 4.6 %collective-permute-start.11 = (bf16[2,384,256]{2,1,0:T(8,128)(2,1)}, bf16[2,384,256]{2,1,0:T(8,128)(2,1)}, u32[]{:S(2)}, u32[]{:S(2)}) collective-permute-start(bf16[2,384,256]{2,1,0:T(8,128)(2,1)} %convolution_convert_fusion.1), channel_id=1, source_target_pairs={{0,32},{16,48},{32,0},{48,16},{64,96},{80,112},{96,64},{112,80},{1... | collective-permute-start | bytes 1179656 | tf_op jit(solution)/shard_map/ppermute | solution.py:17
  243.5 1.1 convolution_convert_fusion.3
  244.5 1.3 fusion.3
  245.8 4.2 %all-to-all-start = ((bf16[8,3,2,2,16,256]{5,4,3,2,1,0:T(8,128)(2,1)}), bf16[8,3,2,2,16,256]{5,4,3,2,1,0:T(8,128)(2,1)S(1)}, u32[]{:S(2)}, u32[]{:S(2)}) async-start(bf16[8,3,2,2,16,256]{5,4,3,2,1,0:T(8,128)(2,1)} %fusion.3), calls=%async_computation | async-start | bytes 1572864 | tf_op jit(solution)/shard_map/all_to_all | solution.py:180
  250.8 1.3 fusion.8
  252.4 3.0 collective-permute-start.12
  255.7 1.4 convolution_convert_fusion.5
  257.2 5.5 %collective-permute-done.12 = bf16[2,384,256]{2,1,0:T(8,128)(2,1)S(1)} collective-permute-done((bf16[2,384,256]{2,1,0:T(8,128)(2,1)S(1)}, bf16[2,384,256]{2,1,0:T(8,128)(2,1)S(1)}, u32[]{:S(2)}, u32[]{:S(2)}) %collective-permute-start.12) | collective-permute-done | bytes 393248 | tf_op jit(solution)/shard_map/ppermute | solution.py:17
  265.0 5.1 %collective-permute-start.13 = (bf16[8,3,2,2,16,256]{5,4,3,2,1,0:T(8,128)(2,1)}, bf16[8,3,2,2,16,256]{5,4,3,2,1,0:T(8,128)(2,1)}, u32[]{:S(2)}, u32[]{:S(2)}) collective-permute-start(bf16[8,3,2,2,16,256]{5,4,3,2,1,0:T(8,128)(2,1)} %select_bitcast_fusion), channel_id=1, source_target_pairs={{0,1},{1,0},{2,3},{3,2},{4,5},{5,4},{6,7},{7,6},{8,9},{9,8},{10,11... | collective-permute-start | bytes 2359304 | tf_op jit(solution)/shard_map/ppermute | solution.py:173
  270.1 4.5 %collective-permute-start.14 = (bf16[384,256]{1,0:T(8,128)(2,1)}, bf16[384,256]{1,0:T(8,128)(2,1)}, u32[]{:S(2)}, u32[]{:S(2)}) collective-permute-start(bf16[384,256]{1,0:T(8,128)(2,1)} %get-tuple-element.28), channel_id=1, source_target_pairs={{0,256},{16,272},{32,288},{48,304},{64,320},{80,336},{96,352},{112... | collective-permute-start | bytes 589832 | tf_op jit(solution)/shard_map/ppermute | solution.py:17
  274.7 1.5 fusion.21
  277.1 6.8 %all-to-all-start.1 = ((bf16[8,3,2,2,16,256]{5,4,3,2,1,0:T(8,128)(2,1)}), bf16[8,3,2,2,16,256]{5,4,3,2,1,0:T(8,128)(2,1)S(1)}, u32[]{:S(2)}, u32[]{:S(2)}) async-start(bf16[8,3,2,2,16,256]{5,4,3,2,1,0:T(8,128)(2,1)} %copy-done.8), calls=%async_computation.1 | async-start | bytes 1572864 | tf_op jit(solution)/shard_map/all_to_all | solution.py:180
  284.6 4.7 %collective-permute-start.16 = (bf16[2,16,256]{2,1,0:T(8,128)(2,1)S(1)}, bf16[2,16,256]{2,1,0:T(8,128)(2,1)S(1)}, u32[]{:S(2)}, u32[]{:S(2)}) collective-permute-start(bf16[2,16,256]{2,1,0:T(8,128)(2,1)S(1)} %get-tuple-element.34), channel_id=1, source_target_pairs={{0,256},{16,272},{32,288},{48,304},{64,320},{80,336},{96,352},{112... | collective-permute-start | bytes 49160 | tf_op jit(solution)/shard_map/ppermute | solution.py:17
  289.3 1.1 select_select_fusion
  290.4 1.9 collective-permute-start.15
  294.2 4.3 %collective-permute-start.17 = (bf16[2,2,16,256]{3,2,1,0:T(8,128)(2,1)S(1)}, bf16[2,2,16,256]{3,2,1,0:T(8,128)(2,1)S(1)}, u32[]{:S(2)}, u32[]{:S(2)}) collective-permute-start(bf16[2,2,16,256]{3,2,1,0:T(8,128)(2,1)S(1)} %get-tuple-element.31), channel_id=1, source_target_pairs={{0,128},{16,144},{32,160},{48,176},{64,192},{80,208},{96,224},{112... | collective-permute-start | bytes 98312 | tf_op jit(solution)/shard_map/ppermute | solution.py:17
  298.4 6.5 %collective-permute-done.15 = bf16[384,256]{1,0:T(8,128)(2,1)S(1)} collective-permute-done((bf16[384,256]{1,0:T(8,128)(2,1)S(1)}, bf16[384,256]{1,0:T(8,128)(2,1)S(1)}, u32[]{:S(2)}, u32[]{:S(2)}) %collective-permute-start.15) | collective-permute-done | bytes 196640 | tf_op jit(solution)/shard_map/ppermute | solution.py:17
  305.9 1.5 all-to-all-done.1.parts_low
  307.5 1.5 shard_map.72
  (128 shorter events, 26.2 us)
Async XLA Ops:
  7.2 84.6 %all-gather.5.cloned.1.call-start = ((), (), s32[]{:S(2)}) async-start(), calls=%async_computation.3 | async-start | bytes 1114112 | tf_op jit(solution)/shard_map/all_gather | solution.py:221
  7.2 0.9 copy-start.2
  8.1 0.7 copy-start.3
  10.1 1.0 copy-start
  11.1 37.4 %copy-start.17 = (bf16[384,512]{1,0:T(8,128)(2,1)S(1)}, bf16[384,512]{1,0:T(8,128)(2,1)}, u32[]{:S(2)}) copy-start(bf16[384,512]{1,0:T(8,128)(2,1)} %param.4) | copy-start | bytes 1179652
  11.1 15.9 %collective-permute-start.2 = (bf16[448,256]{1,0:T(8,128)(2,1)S(1)}, bf16[448,256]{1,0:T(8,128)(2,1)S(1)}, u32[]{:S(2)}, u32[]{:S(2)}) collective-permute-start(bf16[448,256]{1,0:T(8,128)(2,1)S(1)} %shard_map.68), channel_id=1, source_target_pairs={{0,128},{16,144},{32,160},{48,176},{64,192},{80,208},{96,224},{112... | collective-permute-start | bytes 688136 | tf_op jit(solution)/shard_map/ppermute | solution.py:17
  27.0 1.0 copy-start.1
  28.0 0.7 copy-start.4
  29.4 17.1 %collective-permute-start.4 = (bf16[416,256]{1,0:T(8,128)(2,1)S(1)}, bf16[416,256]{1,0:T(8,128)(2,1)S(1)}, u32[]{:S(2)}, u32[]{:S(2)}) collective-permute-start(bf16[416,256]{1,0:T(8,128)(2,1)S(1)} %get-tuple-element.18), channel_id=1, source_target_pairs={{0,256},{16,272},{32,288},{48,304},{64,320},{80,336},{96,352},{112... | collective-permute-start | bytes 638984 | tf_op jit(solution)/shard_map/ppermute | solution.py:17
  47.7 87.2 %all-gather.3.cloned.1.call-start = ((), (), s32[]{:S(2)}) async-start(), calls=%async_computation.2 | async-start | bytes 1671168 | tf_op jit(solution)/shard_map/all_gather | solution.py:202
  48.6 21.8 %copy-start.6 = (bf16[2,384,256]{2,1,0:T(8,128)(2,1)}, bf16[2,384,256]{2,1,0:T(8,128)(2,1)S(1)}, u32[]{:S(2)}) copy-start(bf16[2,384,256]{2,1,0:T(8,128)(2,1)S(1)} %rev.3) | copy-start | bytes 1179652
  70.4 65.8 %copy-start.9 = (bf16[2,384,256]{2,1,0:T(8,128)(2,1)}, bf16[2,384,256]{2,1,0:T(8,128)(2,1)S(1)}, u32[]{:S(2)}) copy-start(bf16[2,384,256]{2,1,0:T(8,128)(2,1)S(1)} %fusion.4) | copy-start | bytes 1179652
  70.5 65.8 %collective-permute-start = (bf16[2,384,256]{2,1,0:T(8,128)(2,1)S(1)}, bf16[2,384,256]{2,1,0:T(8,128)(2,1)}, u32[]{:S(2)}, u32[]{:S(2)}) collective-permute-start(bf16[2,384,256]{2,1,0:T(8,128)(2,1)S(1)} %fusion.4), channel_id=1, source_target_pairs={{0,16},{16,0},{32,48},{48,32},{64,80},{80,64},{96,112},{112,96},{1... | collective-permute-start | bytes 1179656 | tf_op jit(solution)/shard_map/ppermute | solution.py:17
  136.0 6.3 %copy-start.11 = (bf16[3,2,2,256,256]{4,3,2,1,0:T(8,128)(2,1)S(1)}, bf16[3,2,2,256,256]{4,3,2,1,0:T(8,128)(2,1)}, u32[]{:S(2)}) copy-start(bf16[3,2,2,256,256]{4,3,2,1,0:T(8,128)(2,1)} %all-gather.3.cloned.1.call-done) | copy-start | bytes 4718596
  137.7 13.8 %collective-permute-start.1 = (bf16[2,384,256]{2,1,0:T(8,128)(2,1)S(1)}, bf16[2,384,256]{2,1,0:T(8,128)(2,1)S(1)}, u32[]{:S(2)}, u32[]{:S(2)}) collective-permute-start(bf16[2,384,256]{2,1,0:T(8,128)(2,1)S(1)} %fusion.5), channel_id=1, source_target_pairs={{0,32},{16,48},{32,0},{48,16},{64,96},{80,112},{96,64},{112,80},{1... | collective-permute-start | bytes 1179656 | tf_op jit(solution)/shard_map/ppermute | solution.py:17
  151.9 11.4 %collective-permute-start.3 = (bf16[2,384,256]{2,1,0:T(8,128)(2,1)S(1)}, bf16[2,384,256]{2,1,0:T(8,128)(2,1)S(1)}, u32[]{:S(2)}, u32[]{:S(2)}) collective-permute-start(bf16[2,384,256]{2,1,0:T(8,128)(2,1)S(1)} %fusion.6), channel_id=1, source_target_pairs={{0,64},{16,80},{32,96},{48,112},{64,0},{80,16},{96,32},{112,48},{1... | collective-permute-start | bytes 1179656 | tf_op jit(solution)/shard_map/ppermute | solution.py:17
  163.5 12.8 %collective-permute-start.5 = (bf16[384,256]{1,0:T(8,128)(2,1)S(1)}, bf16[384,256]{1,0:T(8,128)(2,1)S(1)}, u32[]{:S(2)}, u32[]{:S(2)}) collective-permute-start(bf16[384,256]{1,0:T(8,128)(2,1)S(1)} %fusion.11), channel_id=1, source_target_pairs={{0,128},{16,144},{32,160},{48,176},{64,192},{80,208},{96,224},{112... | collective-permute-start | bytes 589832 | tf_op jit(solution)/shard_map/ppermute | solution.py:17
  168.1 17.2 %copy-start.16 = (bf16[2,2,2,256,256]{4,3,2,1,0:T(8,128)(2,1)S(1)}, bf16[2,2,2,256,256]{4,3,2,1,0:T(8,128)(2,1)}, u32[]{:S(2)}) copy-start(bf16[2,2,2,256,256]{4,3,2,1,0:T(8,128)(2,1)} %all-gather.5.cloned.1.call-done) | copy-start | bytes 3145732
  176.5 16.0 %collective-permute-start.6 = (bf16[384,256]{1,0:T(8,128)(2,1)S(1)}, bf16[384,256]{1,0:T(8,128)(2,1)S(1)}, u32[]{:S(2)}, u32[]{:S(2)}) collective-permute-start(bf16[384,256]{1,0:T(8,128)(2,1)S(1)} %fusion.12), channel_id=1, source_target_pairs={{0,256},{16,272},{32,288},{48,304},{64,320},{80,336},{96,352},{112... | collective-permute-start | bytes 589832 | tf_op jit(solution)/shard_map/ppermute | solution.py:17
  195.5 15.0 %collective-permute-start.7 = (bf16[384,256]{1,0:T(8,128)(2,1)S(1)}, bf16[384,256]{1,0:T(8,128)(2,1)S(1)}, u32[]{:S(2)}, u32[]{:S(2)}) collective-permute-start(bf16[384,256]{1,0:T(8,128)(2,1)S(1)} %fusion.14), channel_id=1, source_target_pairs={{0,256},{16,272},{32,288},{48,304},{64,320},{80,336},{96,352},{112... | collective-permute-start | bytes 589832 | tf_op jit(solution)/shard_map/ppermute | solution.py:17
  210.7 13.0 %collective-permute-start.8 = (bf16[384,256]{1,0:T(8,128)(2,1)S(1)}, bf16[384,256]{1,0:T(8,128)(2,1)S(1)}, u32[]{:S(2)}, u32[]{:S(2)}) collective-permute-start(bf16[384,256]{1,0:T(8,128)(2,1)S(1)} %fusion.17), channel_id=1, source_target_pairs={{0,128},{16,144},{32,160},{48,176},{64,192},{80,208},{96,224},{112... | collective-permute-start | bytes 589832 | tf_op jit(solution)/shard_map/ppermute | solution.py:17
  224.4 12.1 %collective-permute-start.10 = (bf16[2,384,256]{2,1,0:T(8,128)(2,1)S(1)}, bf16[2,384,256]{2,1,0:T(8,128)(2,1)S(1)}, u32[]{:S(2)}, u32[]{:S(2)}) collective-permute-start(bf16[2,384,256]{2,1,0:T(8,128)(2,1)S(1)} %convolution_convert_fusion.2), channel_id=1, source_target_pairs={{0,64},{16,80},{32,96},{48,112},{64,0},{80,16},{96,32},{112,48},{1... | collective-permute-start | bytes 1179656 | tf_op jit(solution)/shard_map/ppermute | solution.py:17
  227.2 17.3 %collective-permute-start.9 = (bf16[8,3,2,2,16,256]{5,4,3,2,1,0:T(8,128)(2,1)S(1)}, bf16[8,3,2,2,16,256]{5,4,3,2,1,0:T(8,128)(2,1)S(1)}, u32[]{:S(2)}, u32[]{:S(2)}) collective-permute-start(bf16[8,3,2,2,16,256]{5,4,3,2,1,0:T(8,128)(2,1)S(1)} %select_bitcast_fusion.1), channel_id=1, source_target_pairs={{0,1},{1,0},{2,3},{3,2},{4,5},{5,4},{6,7},{7,6},{8,9},{9,8},{10,11... | collective-permute-start | bytes 2359304 | tf_op jit(solution)/shard_map/ppermute | solution.py:173
  237.8 13.0 %collective-permute-start.11 = (bf16[2,384,256]{2,1,0:T(8,128)(2,1)}, bf16[2,384,256]{2,1,0:T(8,128)(2,1)}, u32[]{:S(2)}, u32[]{:S(2)}) collective-permute-start(bf16[2,384,256]{2,1,0:T(8,128)(2,1)} %convolution_convert_fusion.1), channel_id=1, source_target_pairs={{0,32},{16,48},{32,0},{48,16},{64,96},{80,112},{96,64},{112,80},{1... | collective-permute-start | bytes 1179656 | tf_op jit(solution)/shard_map/ppermute | solution.py:17
  245.8 28.8 %all-to-all-start = ((bf16[8,3,2,2,16,256]{5,4,3,2,1,0:T(8,128)(2,1)}), bf16[8,3,2,2,16,256]{5,4,3,2,1,0:T(8,128)(2,1)S(1)}, u32[]{:S(2)}, u32[]{:S(2)}) async-start(bf16[8,3,2,2,16,256]{5,4,3,2,1,0:T(8,128)(2,1)} %fusion.3), calls=%async_computation | async-start | bytes 1572864 | tf_op jit(solution)/shard_map/all_to_all | solution.py:180
  250.0 5.4 %copy-start.10 = (bf16[2,384,256]{2,1,0:T(8,128)(2,1)S(1)}, bf16[2,384,256]{2,1,0:T(8,128)(2,1)}, u32[]{:S(2)}) copy-start(bf16[2,384,256]{2,1,0:T(8,128)(2,1)} %copy-done.9) | copy-start | bytes 1179652
  252.4 10.2 %collective-permute-start.12 = (bf16[2,384,256]{2,1,0:T(8,128)(2,1)S(1)}, bf16[2,384,256]{2,1,0:T(8,128)(2,1)S(1)}, u32[]{:S(2)}, u32[]{:S(2)}) collective-permute-start(bf16[2,384,256]{2,1,0:T(8,128)(2,1)S(1)} %convolution_convert_fusion), channel_id=1, source_target_pairs={{0,16},{16,0},{32,48},{48,32},{64,80},{80,64},{96,112},{112,96},{1... | collective-permute-start | bytes 1179656 | tf_op jit(solution)/shard_map/ppermute | solution.py:17
  255.7 7.2 %copy-start.7 = (bf16[2,384,256]{2,1,0:T(8,128)(2,1)S(1)}, bf16[2,384,256]{2,1,0:T(8,128)(2,1)}, u32[]{:S(2)}) copy-start(bf16[2,384,256]{2,1,0:T(8,128)(2,1)} %copy-done.6) | copy-start | bytes 1179652
  257.1 6.5 %copy-start.14 = (bf16[2,256,256]{2,1,0:T(8,128)(2,1)S(1)}, bf16[2,256,256]{2,1,0:T(8,128)(2,1)}, u32[]{:S(2)}) copy-start(bf16[2,256,256]{2,1,0:T(8,128)(2,1)} %convolution_convert_fusion.4) | copy-start | bytes 786436
  257.1 6.5 %copy-start.15 = (bf16[2,256,256]{2,1,0:T(8,128)(2,1)S(1)}, bf16[2,256,256]{2,1,0:T(8,128)(2,1)}, u32[]{:S(2)}) copy-start(bf16[2,256,256]{2,1,0:T(8,128)(2,1)} %convolution_convert_fusion.3) | copy-start | bytes 786436
  262.9 0.7 copy-start.12
  265.0 9.6 %collective-permute-start.13 = (bf16[8,3,2,2,16,256]{5,4,3,2,1,0:T(8,128)(2,1)}, bf16[8,3,2,2,16,256]{5,4,3,2,1,0:T(8,128)(2,1)}, u32[]{:S(2)}, u32[]{:S(2)}) collective-permute-start(bf16[8,3,2,2,16,256]{5,4,3,2,1,0:T(8,128)(2,1)} %select_bitcast_fusion), channel_id=1, source_target_pairs={{0,1},{1,0},{2,3},{3,2},{4,5},{5,4},{6,7},{7,6},{8,9},{9,8},{10,11... | collective-permute-start | bytes 2359304 | tf_op jit(solution)/shard_map/ppermute | solution.py:173
  270.1 19.2 %collective-permute-start.14 = (bf16[384,256]{1,0:T(8,128)(2,1)}, bf16[384,256]{1,0:T(8,128)(2,1)}, u32[]{:S(2)}, u32[]{:S(2)}) collective-permute-start(bf16[384,256]{1,0:T(8,128)(2,1)} %get-tuple-element.28), channel_id=1, source_target_pairs={{0,256},{16,272},{32,288},{48,304},{64,320},{80,336},{96,352},{112... | collective-permute-start | bytes 589832 | tf_op jit(solution)/shard_map/ppermute | solution.py:17
  276.2 0.9 copy-start.8
  277.1 6.8 %copy-start.5 = (s32[6,64]{1,0:T(8,128)S(1)}, s32[6,64]{1,0:T(8,128)}, u32[]{:S(2)}) copy-start(s32[6,64]{1,0:T(8,128)} %matchings.9) | copy-start | bytes 4612
  277.1 12.2 %copy-start.13 = (bf16[2,384,256]{2,1,0:T(8,128)(2,1)S(1)}, bf16[2,384,256]{2,1,0:T(8,128)(2,1)}, u32[]{:S(2)}) copy-start(bf16[2,384,256]{2,1,0:T(8,128)(2,1)} %copy-done.12) | copy-start | bytes 1179652
  277.1 30.4 %all-to-all-start.1 = ((bf16[8,3,2,2,16,256]{5,4,3,2,1,0:T(8,128)(2,1)}), bf16[8,3,2,2,16,256]{5,4,3,2,1,0:T(8,128)(2,1)S(1)}, u32[]{:S(2)}, u32[]{:S(2)}) async-start(bf16[8,3,2,2,16,256]{5,4,3,2,1,0:T(8,128)(2,1)} %copy-done.8), calls=%async_computation.1 | async-start | bytes 1572864 | tf_op jit(solution)/shard_map/all_to_all | solution.py:180
  284.6 9.6 %collective-permute-start.16 = (bf16[2,16,256]{2,1,0:T(8,128)(2,1)S(1)}, bf16[2,16,256]{2,1,0:T(8,128)(2,1)S(1)}, u32[]{:S(2)}, u32[]{:S(2)}) collective-permute-start(bf16[2,16,256]{2,1,0:T(8,128)(2,1)S(1)} %get-tuple-element.34), channel_id=1, source_target_pairs={{0,256},{16,272},{32,288},{48,304},{64,320},{80,336},{96,352},{112... | collective-permute-start | bytes 49160 | tf_op jit(solution)/shard_map/ppermute | solution.py:17
  290.4 14.5 %collective-permute-start.15 = (bf16[384,256]{1,0:T(8,128)(2,1)S(1)}, bf16[384,256]{1,0:T(8,128)(2,1)S(1)}, u32[]{:S(2)}, u32[]{:S(2)}) collective-permute-start(bf16[384,256]{1,0:T(8,128)(2,1)S(1)} %select_select_fusion), channel_id=1, source_target_pairs={{0,128},{16,144},{32,160},{48,176},{64,192},{80,208},{96,224},{112... | collective-permute-start | bytes 589832 | tf_op jit(solution)/shard_map/ppermute | solution.py:17
  294.2 11.8 %collective-permute-start.17 = (bf16[2,2,16,256]{3,2,1,0:T(8,128)(2,1)S(1)}, bf16[2,2,16,256]{3,2,1,0:T(8,128)(2,1)S(1)}, u32[]{:S(2)}, u32[]{:S(2)}) collective-permute-start(bf16[2,2,16,256]{3,2,1,0:T(8,128)(2,1)S(1)} %get-tuple-element.31), channel_id=1, source_target_pairs={{0,128},{16,144},{32,160},{48,176},{64,192},{80,208},{96,224},{112... | collective-permute-start | bytes 98312 | tf_op jit(solution)/shard_map/ppermute | solution.py:17
Sparse Core Ops, SparseCore 0:
  47.8 43.8 all-gather.4
  94.5 40.4 all-gather.2
